TPU v7x, 32 devices: a whole 2x2x4 slice. The times are simulated.
32 devices in a mesh: batch: 4 (over x, core), ctx: 2 (over y), head: 4 (over z).
Axes of the slice: x: 2, y: 2, z: 4, core: 2. Of those that a mesh axis runs over, the one named last changes fastest.
Arguments:
- query_raw: bfloat16 [4096, 2560], P(('batch', 'ctx'), 'head'), parts along dimension 0, may hold values from -400 to 400
- key_raw: bfloat16 [4096, 2560], P(('batch', 'ctx'), 'head'), parts along dimension 0, may hold values from -400 to 400
- value_rows: bfloat16 [4096, 2560], P(('batch', 'ctx'), 'head'), parts along dimension 0, may hold values from -6 to 6
- query_gain: float32 [2560], P('head'), may hold values from 1.2 to 2
- key_gain: float32 [2560], P('head'), may hold values from 1.2 to 2
- segment: int32 [4096], P(('batch', 'ctx')), parts along dimension 0, may hold values from 0 to 5, never falling along the last dimension, each value on 1 to 512 neighbouring positions
- destination: int32 [4096], P(('batch', 'ctx')), parts along dimension 0, may hold values from 0 to 1023, as said below
- timestep: int32 [24], P('batch'), parts along dimension 0, may hold values from 0 to 49
- out_weight: bfloat16 [2560, 5120], P('head'), may hold values from -0.3125 to 0.3125
- gate_table: float32 [50, 5120], P(None, 'head'), may hold values from 0.5 to 1.5
Outputs:
- gated: bfloat16 [4096, 5120], P(('batch', 'ctx'), 'head'), parts along dimension 0
There are 4 independent parts, one for each index of `batch`. A program takes and returns all parts, laid end to end along the dimension named above; an argument that names none is the same for every part. Nothing has to cross between parts.
Inputs may be any that keep to these rules, and one draw needn't show every extreme that they name: `segment`: the positions of one video are contiguous and the numbers never fall; each of the 6 videos has 1 to 512 positions, some video exactly 512. `destination`: A permutation of the 1024 rows. The 512 positions of each block b of 512 go 256 to every block c, and fill rows c*512 + b*256 to c*512 + (b+1)*256 - 1.
All inputs are finite; a program needn't handle non-finite values.
Results may differ from a plain program's by a relative error of at most 0.01555.
Values may be sent and summed in bfloat16 or wider, within the bound.
No kernel may reach another device: no remote copies, remote signals or barrier semaphores. Data moves between devices by JAX's collectives and lax.ppermute only.
A program may use at most 192 MiB of HBM per device.

v0:
```python
import math

import jax
import jax.numpy as jnp
from jax import lax
from jax.sharding import PartitionSpec as P

HD = 128


def for_sending(array):

    def short(part):
        return part.astype(jnp.bfloat16) if part.dtype == jnp.float32 else part

    return jax.tree.map(short, array)


def attend(running, queries, query_mark, key_rows, value_part, key_mark, head_count, score_scale):
    maxima, totals, accumulated = running
    query_count = queries.shape[0]
    query_heads = queries.reshape(query_count, head_count, HD)
    key_heads = key_rows.reshape(key_rows.shape[0], head_count, HD)
    value_heads = value_part.reshape(value_part.shape[0], head_count, HD)
    scores = (
        jnp.einsum("qhd,khd->hqk", query_heads, key_heads, preferred_element_type=jnp.float32)
        * score_scale
    )
    allowed = (query_mark[:, None] == key_mark[None, :])[None]
    scores = jnp.where(allowed, scores, -1e30)
    new_max = jnp.maximum(maxima, jnp.max(scores, axis=2))
    factor = jnp.exp(maxima - new_max)
    weights = jnp.where(allowed, jnp.exp(scores - new_max[:, :, None]), 0.0)
    totals = totals * factor + jnp.sum(weights, axis=2)
    update = jnp.einsum(
        "hqk,khd->qhd",
        weights.astype(jnp.bfloat16),
        value_heads,
        preferred_element_type=jnp.float32,
    )
    accumulated = accumulated * jnp.transpose(factor)[:, :, None] + update
    return (new_max, totals, accumulated)


def attend_blocks(
    running, queries, query_mark, key_rows, value_part, key_mark, head_count, score_scale
):
    block_rows = queries.shape[0]
    block_count = key_rows.shape[0] // block_rows
    stacked = (
        key_rows.reshape(block_count, block_rows, key_rows.shape[1]),
        value_part.reshape(block_count, block_rows, value_part.shape[1]),
        key_mark.reshape(block_count, block_rows),
    )

    def advance(state, shard_piece):
        return (
            attend(
                state,
                queries,
                query_mark,
                shard_piece[0],
                shard_piece[1],
                shard_piece[2],
                head_count,
                score_scale,
            ),
            None,
        )

    running, unused = lax.scan(advance, running, stacked)
    return running


def local(
    query_raw,
    key_raw,
    value_rows,
    query_gain,
    key_gain,
    segment,
    destination,
    timestep,
    out_weight,
    gate_table,
):
    row_count = query_raw.shape[0]
    row_width = query_raw.shape[1]
    head_count = row_width // HD
    ctx_size = lax.axis_size("ctx")
    total_width = row_width * lax.axis_size("head")
    score_scale = 1.0 / math.sqrt(HD)
    query_float = query_raw.astype(jnp.float32)
    key_float = key_raw.astype(jnp.float32)
    query_sum, key_sum = lax.psum(
        (jnp.sum(query_float * query_float, axis=1), jnp.sum(key_float * key_float, axis=1)), "head"
    )
    queries = (
        query_float * lax.rsqrt(query_sum / total_width + 1e-06)[:, None] * query_gain
    ).astype(jnp.bfloat16)
    normed_keys = (key_float * lax.rsqrt(key_sum / total_width + 1e-06)[:, None] * key_gain).astype(
        jnp.bfloat16
    )
    slot_count = row_count // ctx_size
    target = destination // row_count * slot_count + destination % slot_count

    def placed(array):
        return jnp.zeros_like(array).at[target].set(array)

    initial = (
        jnp.full((head_count, row_count), -1e30, jnp.float32),
        jnp.zeros((head_count, row_count), jnp.float32),
        jnp.zeros((row_count, head_count, HD), jnp.float32),
    )
    own_queries, own_keys, own_values, own_segment = (
        lax.all_to_all(placed(queries), "ctx", split_axis=0, concat_axis=0, tiled=True),
        lax.all_to_all(placed(normed_keys), "ctx", split_axis=0, concat_axis=0, tiled=True),
        lax.all_to_all(placed(value_rows), "ctx", split_axis=0, concat_axis=0, tiled=True),
        lax.all_to_all(placed(segment), "ctx", split_axis=0, concat_axis=0, tiled=True),
    )
    running = attend_blocks(
        initial,
        own_queries,
        own_segment,
        lax.all_gather(own_keys, "ctx", axis=0, tiled=True),
        lax.all_gather(own_values, "ctx", axis=0, tiled=True),
        lax.all_gather(for_sending(own_segment), "ctx", axis=0, tiled=True),
        head_count,
        score_scale,
    )
    attended = (
        (running[2] / jnp.transpose(running[1])[:, :, None])
        .reshape(row_count, row_width)
        .astype(jnp.bfloat16)
    )
    head_terms = jnp.dot(attended, out_weight, preferred_element_type=jnp.float32)
    mixed_rows = lax.psum_scatter(
        head_terms.astype(jnp.bfloat16), "head", scatter_dimension=1, tiled=True
    ).astype(jnp.float32)
    video_gates = jnp.dot(
        jax.nn.one_hot(timestep, gate_table.shape[0], dtype=jnp.float32),
        gate_table,
        precision=lax.Precision.HIGHEST,
    )
    token_gates = jnp.dot(
        jax.nn.one_hot(own_segment, timestep.shape[0], dtype=jnp.float32),
        video_gates,
        precision=lax.Precision.HIGHEST,
    )
    return (mixed_rows * token_gates).astype(jnp.bfloat16)


def solution(mesh):
    placed = (
        P(("batch", "ctx"), "head"),
        P(("batch", "ctx"), "head"),
        P(("batch", "ctx"), "head"),
        P("head"),
        P("head"),
        P(("batch", "ctx")),
        P(("batch", "ctx")),
        P("batch"),
        P("head", None),
        P(None, "head"),
    )
    return jax.shard_map(
        local, mesh=mesh, in_specs=placed, out_specs=P(("batch", "ctx"), "head"), check_vma=False
    )
```

profile of v0, /device:TPU:0, one launch (start us, length us, event | category | flops | bytes accessed | tf_op | source)
XLA Modules:
  0.0 230.7 jit_solution(1796277568046913709)
XLA Ops:
  6.5 0.0 copy-start
  6.5 0.0 copy-start.1
  6.5 0.0 copy-start.5
  6.5 0.0 copy-start.3
  6.5 0.0 all-gather.4.cloned.1.call-start
  6.6 1.4 fusion.18
  7.9 1.3 fusion.21
  9.2 0.0 copy-done.5
  9.3 13.5 %all-reduce = (f32[512]{0:T(512)S(1)}, f32[512]{0:T(512)S(1)}) all-reduce(f32[512]{0:T(512)S(1)} %fusion.18, f32[512]{0:T(512)S(1)} %fusion.21), channel_id=1, replica_groups=mesh['batch'=4,'ctx'=2,'head'=4] {'head'}, use_global_device_ids=true, to_apply=%region_1.0 | all-reduce | flops 1024 | bytes 8192 | tf_op jit(solution)/shard_map/psum | solution.py:95
  22.7 0.0 copy-done.1
  22.7 0.0 copy-done.3
  22.7 2.9 %scatter_custom_fusion.1 = bf16[512,640]{1,0:T(8,128)(2,1)S(1)} fusion(s32[512]{0:T(512)S(1)} %compare_select_fusion, bf16[512,640]{1,0:T(8,128)(2,1)S(1)} %copy-done.1, f32[640]{0:T(1024)S(1)} %copy-done.3, f32[512]{0:T(512)S(1)} %get-tuple-element.139, bf16[]{:T(256)} %constant.57.clone.1), kind=kCustom, calls=%fused_computation.41 | custom fusion | flops 1310720 | bytes 1316866 | tf_op jit(solution)/shard_map/scatter | solution.py:108
  25.7 10.7 %all_to_all.48 = bf16[2,256,640]{2,1,0:T(8,128)(2,1)} all-to-all(bf16[2,256,640]{2,1,0:T(8,128)(2,1)S(1)} %bitcast.82), channel_id=1, replica_groups=mesh['batch'=4,'ctx'=2,'head'=4] {'ctx'}, dimensions={0} | all-to-all | bytes 1310720 | tf_op jit(solution)/shard_map/all_to_all | solution.py:117
  36.4 0.0 all-gather.4.cloned.1.call-update
  36.4 0.0 copy-start.2
  36.4 0.0 copy-start.4
  36.4 0.0 all-gather.6.cloned.1.call-start
  36.5 3.4 %scatter_custom_fusion.3 = bf16[512,640]{1,0:T(8,128)(2,1)S(1)} fusion(s32[512]{0:T(512)S(1)} %compare_select_fusion, bf16[512,640]{1,0:T(8,128)(2,1)} %param.14, bf16[]{:T(256)} %constant.57.clone.1), kind=kCustom, calls=%fused_computation.46 | custom fusion | bytes 655872 | tf_op jit(solution)/shard_map/scatter | solution.py:108
  39.9 18.7 %all_to_all.49 = bf16[2,256,640]{2,1,0:T(8,128)(2,1)} all-to-all(bf16[2,256,640]{2,1,0:T(8,128)(2,1)S(1)} %bitcast.83), channel_id=1, replica_groups=mesh['batch'=4,'ctx'=2,'head'=4] {'ctx'}, dimensions={0} | all-to-all | bytes 1310720 | tf_op jit(solution)/shard_map/all_to_all | solution.py:118
  58.6 0.0 all-gather.6.cloned.1.call-update
  58.6 3.2 %scatter_custom_fusion = s32[512]{0:T(512)} fusion(s32[512]{0:T(512)S(1)} %compare_select_fusion, s32[512]{0:T(512)} %param.17, s32[]{:T(128)} %constant.54.clone.1), kind=kCustom, calls=%fused_computation.71 | custom fusion | bytes 2560 | tf_op jit(solution)/shard_map/scatter | solution.py:108
  61.8 3.2 %all-to-all-start = ((s32[2,256,1]{1,2,0:T(1,128)}), s32[2,256,1]{1,2,0:T(1,128)S(1)}, u32[]{:S(2)}, u32[]{:S(2)}) async-start(s32[2,256,1]{1,2,0:T(1,128)} %bitcast), calls=%async_computation | async-start | bytes 4096 | tf_op jit(solution)/shard_map/all_to_all | solution.py:119
  65.0 0.0 copy-done.2
  65.0 0.0 copy-done.4
  65.0 3.6 %scatter_custom_fusion.2 = bf16[512,640]{1,0:T(8,128)(2,1)} fusion(s32[512]{0:T(512)S(1)} %compare_select_fusion, bf16[512,640]{1,0:T(8,128)(2,1)S(1)} %copy-done.2, f32[640]{0:T(1024)S(1)} %copy-done.4, f32[512]{0:T(512)S(1)} %get-tuple-element.138, bf16[]{:T(256)} %constant.57.clone.1), kind=kCustom, calls=%fused_computation.40 | custom fusion | flops 1310720 | bytes 1316866 | tf_op jit(solution)/shard_map/scatter | solution.py:108
  68.6 0.2 all-to-all-done
  68.8 3.5 %all-to-all-start.2 = ((bf16[2,256,640]{2,1,0:T(8,128)(2,1)}), bf16[2,256,640]{2,1,0:T(8,128)(2,1)S(1)}, u32[]{:S(2)}, u32[]{:S(2)}) async-start(bf16[2,256,640]{2,1,0:T(8,128)(2,1)} %bitcast.6), calls=%async_computation.2 | async-start | bytes 1310720 | tf_op jit(solution)/shard_map/all_to_all | solution.py:116
  72.3 0.0 reduce-scatter.2.cloned.1.call-start
  72.4 14.3 %all-gather = s32[2,1,512]{2,1,0:T(1,128)S(1)} all-gather(s32[1,1,512]{2,1,0:T(1,128)S(1)} %bitcast.87), channel_id=1, replica_groups=mesh['batch'=4,'ctx'=2,'head'=4] {'ctx'}, dimensions={0}, use_global_device_ids=true | all-gather | bytes 6144 | tf_op jit(solution)/shard_map/all_gather | solution.py:127
  86.7 0.0 all-to-all-done.2
  86.7 1.2 copy.33
  87.9 0.0 all-gather.4.cloned.1.call-done
  87.9 3.6 %all-gather.6.cloned.1.call-done = bf16[1024,640]{1,0:T(8,128)(2,1)} async-done(((bf16[512,640]{1,0:T(8,128)(2,1)}), bf16[1024,640]{1,0:T(8,128)(2,1)}) %all-gather.6.cloned.1.call-update) | async-done | bytes 1310736 | tf_op jit(solution)/shard_map/all_gather | solution.py:126
  91.5 27.3 %while.15 = (s32[]{:T(128)}, f32[5,512]{1,0:T(8,128)S(1)}, f32[5,512]{1,0:T(8,128)S(1)}, f32[512,5,128]{0,2,1:T(8,128)}, s32[512]{0:T(512)S(1)}, /*index=5*/s32[...) while((s32[]{:T(128)}, f32[5,512]{1,0:T(8,128)S(1)}, ...), condition=%wide.region_11.12_spmd.clone, body=%wide.region_8.11_spmd.clone.sunk | while | flops 689388544 | bytes 42508464 | solution.py:71
  91.5 0.2 broadcast_compare_fusion.2
  91.7 1.4 constant_dynamic-slice_fusion.6
  93.1 0.3 copy.41
  93.4 4.5 %fusion.66 = (f32[5,512]{1,0:T(8,128)S(1)}, f32[5,512,512]{2,1,0:T(8,128)}) fusion(pred[512,512]{0,1:T(8,128)(4,1)S(1)} %broadcast_compare_fusion.2, bf16[512,5,128]{0,2,1:T(8,128)(2,1)S(1)} %bitcast.74, bf16[512,5,128]{0,2,1:T(8,128)(2,1)} %bitcast.75), kind=kOutput, calls=%fused_computation.6.clone.1 | convolution fusion | flops 339473920 | bytes 6825984 | tf_op jit(solution)/shard_map/while/body/eval_jaxpr/qhd,khd->hqk/dot_general | solution.py:26
  97.9 0.0 slice-start
  97.9 0.3 copy.42
  98.2 0.0 slice-start.1
  98.2 5.4 %fusion.70 = f32[512,5,128]{0,2,1:T(8,128)} fusion(bf16[512,5,128]{0,2,1:T(8,128)(2,1)S(1)} %bitcast.76, f32[5,512,512]{2,1,0:T(8,128)} %get-tuple-element.204, f32[5,512]{1,0:T(8,128)S(1)} %get-tuple-element.230, pred[512,512]{0,1:T(8,128)(4,1)S(1)} %broadcast_compare_fusion.2, f32[512,5,128]{0,2,1:T(8,128)} %get-tuple-element.221, ...), kind=kOutput, calls=%fused_computation.12.clone.1 | convolution fusion | flops 343080960 | bytes 8802305 | tf_op jit(solution)/shard_map/while/body/eval_jaxpr/hqk,khd->qhd/dot_general | solution.py:35
  103.6 0.0 slice-done
  103.6 0.0 slice-done.1
  103.6 1.3 fusion.68
  105.0 0.2 broadcast_compare_fusion.2
  105.2 1.4 constant_dynamic-slice_fusion.6
  106.6 0.3 copy.41
  106.9 4.5 %fusion.66 = (f32[5,512]{1,0:T(8,128)S(1)}, f32[5,512,512]{2,1,0:T(8,128)}) fusion(pred[512,512]{0,1:T(8,128)(4,1)S(1)} %broadcast_compare_fusion.2, bf16[512,5,128]{0,2,1:T(8,128)(2,1)S(1)} %bitcast.74, bf16[512,5,128]{0,2,1:T(8,128)(2,1)} %bitcast.75), kind=kOutput, calls=%fused_computation.6.clone.1 | convolution fusion | flops 339473920 | bytes 6825984 | tf_op jit(solution)/shard_map/while/body/eval_jaxpr/qhd,khd->hqk/dot_general | solution.py:26
  111.4 0.0 slice-start
  111.4 0.3 copy.42
  111.7 0.0 slice-start.1
  111.7 5.8 %fusion.70 = f32[512,5,128]{0,2,1:T(8,128)} fusion(bf16[512,5,128]{0,2,1:T(8,128)(2,1)S(1)} %bitcast.76, f32[5,512,512]{2,1,0:T(8,128)} %get-tuple-element.204, f32[5,512]{1,0:T(8,128)S(1)} %get-tuple-element.230, pred[512,512]{0,1:T(8,128)(4,1)S(1)} %broadcast_compare_fusion.2, f32[512,5,128]{0,2,1:T(8,128)} %get-tuple-element.221, ...), kind=kOutput, calls=%fused_computation.12.clone.1 | convolution fusion | flops 343080960 | bytes 8802305 | tf_op jit(solution)/shard_map/while/body/eval_jaxpr/hqk,khd->qhd/dot_general | solution.py:35
  117.5 0.0 slice-done
  117.5 0.0 slice-done.1
  117.5 1.3 fusion.68
  118.8 1.5 divide_convert_fusion
  120.3 8.9 %convolution_convert_fusion = bf16[512,5120]{1,0:T(8,128)(2,1)} fusion(bf16[512,640]{0,1:T(8,128)(2,1)S(1)} %bitcast.84, bf16[640,5120]{1,0:T(8,128)(2,1)} %param.20), kind=kOutput, calls=%fused_computation.26 | convolution fusion | flops 3358064640 | bytes 12451840 | tf_op jit(solution)/shard_map/dot_general | solution.py:136
  129.2 0.0 reduce-scatter.2.cloned.1.call-update
  129.2 0.0 copy-done
  129.2 0.6 copy-done.6
  129.9 0.2 fusion.37
  130.1 90.4 %reduce-scatter.2.cloned.1.call-done = bf16[512,1280]{1,0:T(8,128)(2,1)} async-done(((bf16[512,5120]{1,0:T(8,128)(2,1)}), bf16[512,1280]{1,0:T(8,128)(2,1)}) %reduce-scatter.2.cloned.1.call-update) | async-done | bytes 1310736 | tf_op jit(solution)/shard_map/reduce_scatter | solution.py:137
  220.5 3.6 %fusion.17 = bf16[512,1280]{1,0:T(8,128)(2,1)} fusion(f32[6,1280]{1,0:T(8,128)S(1)} %fusion.37, bf16[512,1280]{1,0:T(8,128)(2,1)} %reduce-scatter.2.cloned.1.call-done, s32[512]{0:T(512)S(1)} %get-tuple-element.254), kind=kOutput, calls=%fused_computation.28 | convolution fusion | flops 49155072 | bytes 2654208 | tf_op jit(solution)/shard_map/dot_general | solution.py:145
  (17 shorter events, 0.1 us)
Async XLA Ops:
  6.5 122.7 %copy-start = (f32[50,1280]{1,0:T(8,128)S(1)}, f32[50,1280]{1,0:T(8,128)}, u32[]{:S(2)}) copy-start(f32[50,1280]{1,0:T(8,128)} %param.21) | copy-start | bytes 768004
  6.5 16.2 %copy-start.1 = (bf16[512,640]{1,0:T(8,128)(2,1)S(1)}, bf16[512,640]{1,0:T(8,128)(2,1)}, u32[]{:S(2)}) copy-start(bf16[512,640]{1,0:T(8,128)(2,1)} %param.13) | copy-start | bytes 1966084
  6.5 2.7 %copy-start.5 = (s32[512]{0:T(512)S(1)}, s32[512]{0:T(512)}, u32[]{:S(2)}) copy-start(s32[512]{0:T(512)} %param.18) | copy-start | bytes 6148
  6.5 16.2 %copy-start.3 = (f32[640]{0:T(1024)S(1)}, f32[640]{0:T(1024)}, u32[]{:S(2)}) copy-start(f32[640]{0:T(1024)} %param.16) | copy-start | bytes 7684
  6.5 81.3 %all-gather.4.cloned.1.call-start = ((), (), s32[]{:S(2)}) async-start(), calls=%async_computation.5 | async-start | bytes 1966080 | tf_op jit(solution)/shard_map/all_gather | solution.py:125
  36.4 28.6 %copy-start.2 = (bf16[512,640]{1,0:T(8,128)(2,1)S(1)}, bf16[512,640]{1,0:T(8,128)(2,1)}, u32[]{:S(2)}) copy-start(bf16[512,640]{1,0:T(8,128)(2,1)} %param.12) | copy-start | bytes 1966084
  36.4 28.6 %copy-start.4 = (f32[640]{0:T(1024)S(1)}, f32[640]{0:T(1024)}, u32[]{:S(2)}) copy-start(f32[640]{0:T(1024)} %param.15) | copy-start | bytes 7684
  36.4 55.0 %all-gather.6.cloned.1.call-start = ((), (), s32[]{:S(2)}) async-start(), calls=%async_computation.6 | async-start | bytes 1966080 | tf_op jit(solution)/shard_map/all_gather | solution.py:126
  61.8 7.0 %all-to-all-start = ((s32[2,256,1]{1,2,0:T(1,128)}), s32[2,256,1]{1,2,0:T(1,128)S(1)}, u32[]{:S(2)}, u32[]{:S(2)}) async-start(s32[2,256,1]{1,2,0:T(1,128)} %bitcast), calls=%async_computation | async-start | bytes 4096 | tf_op jit(solution)/shard_map/all_to_all | solution.py:119
  68.8 17.9 %all-to-all-start.2 = ((bf16[2,256,640]{2,1,0:T(8,128)(2,1)}), bf16[2,256,640]{2,1,0:T(8,128)(2,1)S(1)}, u32[]{:S(2)}, u32[]{:S(2)}) async-start(bf16[2,256,640]{2,1,0:T(8,128)(2,1)} %bitcast.6), calls=%async_computation.2 | async-start | bytes 1310720 | tf_op jit(solution)/shard_map/all_to_all | solution.py:116
  72.3 148.2 %reduce-scatter.2.cloned.1.call-start = ((), (), s32[]{:S(2)}) async-start(), calls=%async_computation.7 | async-start | bytes 6553600 | tf_op jit(solution)/shard_map/reduce_scatter | solution.py:137
  97.9 5.7 %slice-start = ((s8[5242880]{0:T(1024)(128)(4,1)}), s8[1048576]{0:T(1024)(128)(4,1)S(1)}, s32[]{:S(2)}) async-start(s8[5242880]{0:T(1024)(128)(4,1)} %bitcast.72), calls=%async_computation.8 | async-start | bytes 2097152 | tf_op jit(solution)/shard_map/while
  98.2 5.4 %slice-start.1 = ((s8[5242880]{0:T(1024)(128)(4,1)}), s8[4194304]{0:T(1024)(128)(4,1)S(1)}, s32[]{:S(2)}) async-start(s8[5242880]{0:T(1024)(128)(4,1)} %bitcast.72), calls=%async_computation.9 | async-start | bytes 8388608 | tf_op jit(solution)/shard_map/while
  111.4 6.1 %slice-start = ((s8[5242880]{0:T(1024)(128)(4,1)}), s8[1048576]{0:T(1024)(128)(4,1)S(1)}, s32[]{:S(2)}) async-start(s8[5242880]{0:T(1024)(128)(4,1)} %bitcast.72), calls=%async_computation.8 | async-start | bytes 2097152 | tf_op jit(solution)/shard_map/while
  111.7 5.8 %slice-start.1 = ((s8[5242880]{0:T(1024)(128)(4,1)}), s8[4194304]{0:T(1024)(128)(4,1)S(1)}, s32[]{:S(2)}) async-start(s8[5242880]{0:T(1024)(128)(4,1)} %bitcast.72), calls=%async_computation.9 | async-start | bytes 8388608 | tf_op jit(solution)/shard_map/while
  129.2 0.7 copy-start.6
Sparse Core Ops, SparseCore 0:
  36.5 27.3 all-gather.3
  65.4 25.9 all-gather.5
  129.3 91.1 reduce-scatter.1
where the time goes:
time: 231 us
  waiting for transfers between devices  94.2 us (41%)
  blocking collectives  57.2 us (25%)
  matrix products  33 us (14%)
  other arithmetic  13.7 us (6%)
  between operations  13.3 us (6%)
  local copies, waits for them, and re-layouts  12.3 us (5%)
  starting transfers between devices  6.86 us (3%)
    reduce_scatter x1, waiting for transfers between devices, local(): lax.psum_scatter(head_terms.astype(jnp.bfloat16), 'head', scatter_dimensi...  90.4 us
    all_to_all x1, blocking collectives, local(): lax.all_to_all(placed(value_rows), 'ctx', split_axis=0, concat_axis=0, ti...  18.7 us
    all_gather x1, blocking collectives, local(): lax.all_gather(for_sending(own_segment), 'ctx', axis=0, tiled=True)  14.3 us
    psum x1, blocking collectives, local(): lax.psum((jnp.sum(query_float * query_float, axis=1), jnp.sum(key_float *...  13.5 us
    dot_general x2, matrix products, attend(): jnp.einsum('hqk,khd->qhd', weights.astype(jnp.bfloat16), value_heads, pre...  11.2 us
    all_to_all x1, blocking collectives, local(): lax.all_to_all(placed(normed_keys), 'ctx', split_axis=0, concat_axis=0, t...  10.7 us
    dot_general x2, matrix products, attend(): jnp.einsum('qhd,khd->hqk', query_heads, key_heads, preferred_element_type...  9.03 us
    dot_general x1, matrix products, local(): jnp.dot(attended, out_weight, preferred_element_type=jnp.float32)  8.89 us
  transfers between devices with their start and end apart: 5, of which 3 were waited for; matrix products, arithmetic and copies ran while one was open for 5% of the time, Pallas kernels for 0%

commit v1 on v0

--- a/solution.py
+++ b/solution.py
@@ -1,11 +1,283 @@
+import functools
 import math
 
 import jax
 import jax.numpy as jnp
 from jax import lax
+from jax.experimental import pallas as pl
+from jax.experimental.pallas import tpu as pltpu
 from jax.sharding import PartitionSpec as P
 
 HD = 128
+F32 = jnp.float32
+BF16 = jnp.bfloat16
+VMEM = pl.BlockSpec(memory_space=pltpu.VMEM)
+SMEM = pl.BlockSpec(memory_space=pltpu.SMEM)
+ANY = pl.BlockSpec(memory_space=pl.ANY)
+LIMIT = 48 * 1024 * 1024
+HEAD_SPLIT = (2, 2, 1)
+
+SWAP_CTX = ((0, 1), (1, 0))
+SWAP_CORE = ((0, 1), (1, 0), (2, 3), (3, 2))
+SWAP_X = ((0, 2), (2, 0), (1, 3), (3, 1))
+
+
+def xor_pairs(size, step):
+    return tuple((i, i ^ step) for i in range(size))
+
+
+def params(**more):
+    return pltpu.CompilerParams(vmem_limit_bytes=LIMIT, **more)
+
+
+def cost(flops, moved):
+    return pl.CostEstimate(flops=int(flops), bytes_accessed=int(moved), transcendentals=0)
+
+
+def prepare_kernel(cuts, place, q_ref, k_ref, v_ref, dest_ref, seg_ref, own_ref, *outs):
+    packed, stats_ref = outs[:-1], outs[-1]
+    rows, width = q_ref.shape
+    half = rows // 2
+    me = place[0]
+    dest = dest_ref[...]
+    block = (dest >= rows).astype(jnp.int32)
+    slot = dest - block * rows - me * half + jnp.where(block == me, 0, half)
+    spread = (lax.broadcasted_iota(jnp.int32, (rows, rows), 0) == slot).astype(BF16)
+    moved = jnp.dot(spread, q_ref[...], preferred_element_type=F32)
+    moved_short = moved.astype(BF16)
+    own_ref[...] = moved_short[:half]
+    for ref, (low, high) in zip(packed, cuts):
+        ref[0:half, :] = moved_short[half:, low:high]
+        ref[half : half + rows, :] = k_ref[:, low:high]
+        ref[half + rows :, :] = v_ref[:, low:high]
+    keys = k_ref[...].astype(F32)
+    ones = jnp.ones((8, width), F32)
+
+    def row_sums(values):
+        return lax.dot_general(
+            ones, values * values, (((1,), (1,)), ((), ())),
+            precision=lax.Precision.HIGHEST, preferred_element_type=F32,
+        )
+
+    marks = seg_ref[...].astype(F32)
+    moved_marks = lax.dot_general(
+        jnp.broadcast_to(marks, (8, rows)).astype(BF16), spread, (((1,), (1,)), ((), ())),
+        preferred_element_type=F32,
+    )
+    stats_ref[0:1, :] = row_sums(moved)[0:1]
+    stats_ref[1:2, :] = row_sums(keys)[0:1]
+    stats_ref[2:3, :] = moved_marks[0:1]
+    stats_ref[3:4, :] = marks
+    stats_ref[4:8, :] = jnp.zeros((4, rows), F32)
+
+
+def attend_kernel(
+    heads, low, total_width, place, near_ref, far_ref, q_ref, remote_ref, k_ref, v_ref, qg_ref, kg_ref, out_ref
+):
+    rows = k_ref.shape[0]
+    half = rows // 2
+    me = place[0]
+    stats = near_ref[...] + far_ref[...]
+    q_sum = jnp.concatenate([stats[0:1, :half], stats[8:9, half:]], axis=1)
+    q_mark = jnp.concatenate([stats[2:3, :half], stats[10:11, half:]], axis=1)
+    k_sum = jnp.concatenate([stats[1:2], stats[9:10]], axis=1)
+    k_mark = jnp.concatenate([stats[3:4], stats[11:12]], axis=1)
+
+    def column(row):
+        return jnp.transpose(jnp.broadcast_to(row, (8, row.shape[1])))[:, 0:1]
+
+    q_factor = column(lax.rsqrt(q_sum / total_width + 1e-06))
+    k_factor = column(lax.rsqrt(k_sum / total_width + 1e-06))
+    allowed = column(q_mark) == k_mark
+    scale = math.log2(math.e) / math.sqrt(HD)
+    for head in range(heads):
+        cut = slice(head * HD, (head + 1) * HD)
+        wide = slice(low + head * HD, low + (head + 1) * HD)
+        queries = jnp.concatenate([q_ref[:, wide], remote_ref[0:half, cut]], axis=0)
+        keys = jnp.concatenate([k_ref[:, wide], remote_ref[half : half + rows, cut]], axis=0)
+        values = jnp.concatenate([v_ref[:, wide], remote_ref[half + rows :, cut]], axis=0)
+        queries = (queries.astype(F32) * q_factor * qg_ref[0:1, wide]).astype(BF16)
+        keys = (keys.astype(F32) * k_factor * kg_ref[0:1, wide]).astype(BF16)
+        for part in range(2):
+            piece = slice(part * half, (part + 1) * half)
+            scores = lax.dot_general(
+                queries[piece], keys, (((1,), (1,)), ((), ())), preferred_element_type=F32
+            )
+            scores = jnp.where(allowed[piece], scores, -1e30)
+            largest = jnp.max(scores, axis=1, keepdims=True)
+            weights = jnp.exp2((scores - largest) * scale)
+            totals = jnp.sum(weights, axis=1, keepdims=True)
+            mixed = jnp.dot(weights.astype(BF16), values, preferred_element_type=F32)
+            start = me * half if part == 0 else (1 - me) * half
+            out_ref[pl.ds(pl.multiple_of(start, half), half), cut] = (mixed / totals).astype(BF16)
+
+
+def cut_kernel(place, weight_ref, *refs):
+    outs, sems = refs[:3], refs[3]
+    rows, width = outs[0].shape
+    first = pl.multiple_of(place[2] * rows, rows)
+    copies = []
+    for step in range(1, 4):
+        column = pl.multiple_of((place[1] ^ step) * width, width)
+        copies.append(
+            pltpu.make_async_copy(
+                weight_ref.at[pl.ds(first, rows), pl.ds(column, width)], outs[step - 1], sems.at[step - 1]
+            )
+        )
+    for copy in copies:
+        copy.start()
+    for copy in copies:
+        copy.wait()
+
+
+def project_kernel(cuts, place, near_ref, far_ref, times, gate_ref, weight_ref, *refs):
+    chunk_count = len(cuts)
+    parts = refs[: 5 * chunk_count]
+    shares = refs[5 * chunk_count : 5 * chunk_count + 8]
+    out_ref, own_w, w_all, sems, total = refs[5 * chunk_count + 8 :]
+    rows, width = out_ref.shape
+    half = rows // 2
+    group = own_w.shape[0]
+    share = group // 8
+    me, head, mine = place[0], place[1], place[2]
+    own_copy = pltpu.make_async_copy(
+        weight_ref.at[:, pl.ds(pl.multiple_of(head * width, width), width)], own_w, sems.at[0]
+    )
+    own_copy.start()
+    copies = []
+    for index in range(8):
+        start = pl.multiple_of((mine ^ index) * share, share)
+        for step in range(3):
+            copies.append(
+                pltpu.make_async_copy(
+                    shares[index].at[pl.ds(step * share, share), :],
+                    w_all.at[step, pl.ds(start, share), :],
+                    sems.at[1 + index * 3 + step],
+                )
+            )
+    for copy in copies:
+        copy.start()
+    own_copy.wait()
+    total[...] = jnp.dot(parts[0][...], own_w[cuts[0][0] : cuts[0][1]], preferred_element_type=F32)
+    for chunk, (low, high) in enumerate(cuts):
+        if chunk > 0:
+            total[...] += jnp.dot(parts[5 * chunk][...], own_w[low:high], preferred_element_type=F32)
+    for copy in copies:
+        copy.wait()
+    inner = jnp.logical_or(head == 1, head == 2)
+    for chunk, (low, high) in enumerate(cuts):
+        own, one, two, three_near, three_far = parts[5 * chunk : 5 * chunk + 5]
+        total[...] += jnp.dot(one[...], w_all[0, low:high], preferred_element_type=F32)
+        total[...] += jnp.dot(two[...], w_all[1, low:high], preferred_element_type=F32)
+        three = jnp.where(inner, three_near[...], three_far[...])
+        total[...] += jnp.dot(three, w_all[2, low:high], preferred_element_type=F32)
+    stats = near_ref[...] + far_ref[...]
+    own_mark = stats[2:3, :half]
+    other_mark = stats[10:11, half:]
+    for part in range(2):
+        row = own_mark if part == 0 else other_mark
+        marks = jnp.transpose(jnp.broadcast_to(row, (8, half)))[:, 0:1]
+        start = me * half if part == 0 else (1 - me) * half
+        at = pl.ds(pl.multiple_of(start, half), half)
+        gates = jnp.zeros((half, width), F32)
+        for video in range(times.shape[0]):
+            gate = gate_ref[pl.ds(times[video], 1), :]
+            gates = jnp.where(marks == 4.0 * video, gate, gates)
+        out_ref[at, :] = (total[at, :] * gates).astype(BF16)
+
+
+def fast_local(
+    query_raw, key_raw, value_rows, query_gain, key_gain, segment, destination, timestep, out_weight, gate_table
+):
+    rows, width = query_raw.shape
+    half = rows // 2
+    out_width = gate_table.shape[1]
+    total_width = width * lax.axis_size("head")
+    ctx, head, batch = lax.axis_index("ctx"), lax.axis_index("head"), lax.axis_index("batch")
+    mine = batch * 2 + ctx
+    place = jnp.stack([ctx, head, mine]).astype(jnp.int32)
+    cuts, low = [], 0
+    for count in HEAD_SPLIT:
+        cuts.append((low * HD, (low + count) * HD))
+        low += count
+    assert low * HD == width
+    share = width // 8
+
+    cut_weights = pl.pallas_call(
+        cut_kernel,
+        in_specs=[SMEM, ANY],
+        out_specs=[VMEM] * 3,
+        out_shape=[jax.ShapeDtypeStruct((share, out_width), BF16)] * 3,
+        scratch_shapes=[pltpu.SemaphoreType.DMA((3,))],
+        compiler_params=params(),
+        cost_estimate=cost(0, 6 * share * out_width * 2),
+        name="cut_weights",
+    )(place, out_weight)
+    from_head = [lax.ppermute(cut_weights[s - 1], "head", xor_pairs(4, s)) for s in (1, 2, 3)]
+    share0 = jnp.concatenate(from_head, axis=0)
+    share_y = lax.ppermute(share0, "ctx", SWAP_CTX)
+    share_x = lax.ppermute(share0, "batch", SWAP_X)
+    share_xy = lax.ppermute(share_y, "batch", SWAP_X)
+    shares = [None] * 8
+    for index, value in ((0, share0), (1, share_y), (4, share_x), (5, share_xy)):
+        shares[index] = value
+        shares[index ^ 2] = lax.ppermute(value, "batch", SWAP_CORE)
+
+    packed_shapes = [jax.ShapeDtypeStruct((half + 2 * rows, high - low), BF16) for low, high in cuts]
+    own_queries, *packed, stats = pl.pallas_call(
+        functools.partial(prepare_kernel, cuts),
+        in_specs=[SMEM] + [VMEM] * 5,
+        out_specs=[VMEM] * (2 + len(cuts)),
+        out_shape=[jax.ShapeDtypeStruct((half, width), BF16)]
+        + packed_shapes
+        + [jax.ShapeDtypeStruct((8, rows), F32)],
+        compiler_params=params(),
+        cost_estimate=cost(2 * rows * rows * width, 6 * rows * width * 2),
+        name="prepare",
+    )(place, query_raw, key_raw, value_rows, destination.reshape(1, rows), segment.reshape(1, rows))
+
+    other_stats = lax.ppermute(stats, "ctx", SWAP_CTX)
+    both = jnp.concatenate([stats, other_stats], axis=0)
+    near = both + lax.ppermute(both, "head", xor_pairs(4, 1))
+    far = lax.ppermute(near, "head", xor_pairs(4, 2))
+
+    arrived = [lax.ppermute(piece, "ctx", SWAP_CTX) for piece in packed]
+    parts = []
+    for (low, high), piece in zip(cuts, arrived):
+        heads = (high - low) // HD
+        attended = pl.pallas_call(
+            functools.partial(attend_kernel, heads, low, total_width),
+            in_specs=[SMEM] + [VMEM] * 8,
+            out_specs=VMEM,
+            out_shape=jax.ShapeDtypeStruct((rows, high - low), BF16),
+            compiler_params=params(),
+            cost_estimate=cost(heads * 3 * 4 * rows * 2 * rows * HD, 4 * rows * width * 2),
+            name="attend",
+        )(
+            place, near, far, own_queries, piece, key_raw, value_rows,
+            query_gain.reshape(1, width), key_gain.reshape(1, width),
+        )
+        one = lax.ppermute(attended, "head", xor_pairs(4, 1))
+        three_near = lax.ppermute(attended, "head", ((1, 2), (2, 1)))
+        two = lax.ppermute(attended, "head", xor_pairs(4, 2))
+        three_far = lax.ppermute(two, "head", ((2, 3), (1, 0)))
+        parts += [attended, one, two, three_near, three_far]
+
+    return pl.pallas_call(
+        functools.partial(project_kernel, cuts),
+        in_specs=[SMEM, VMEM, VMEM, SMEM, VMEM, ANY] + [VMEM] * len(parts) + [ANY] * 8,
+        out_specs=VMEM,
+        out_shape=jax.ShapeDtypeStruct((rows, out_width), BF16),
+        scratch_shapes=[
+            pltpu.VMEM((width, out_width), BF16),
+            pltpu.VMEM((3, width, out_width), BF16),
+            pltpu.SemaphoreType.DMA((25,)),
+            pltpu.VMEM((rows, out_width), F32),
+        ],
+        compiler_params=params(),
+        cost_estimate=cost(2 * rows * 4 * width * out_width, 5 * width * out_width * 2),
+        name="project",
+    )(place, near, far, timestep, gate_table, out_weight, *parts, *shares)
 
 
 def for_sending(array):
@@ -72,7 +344,7 @@
     return running
 
 
-def local(
+def general_local(
     query_raw,
     key_raw,
     value_rows,
@@ -163,6 +435,9 @@
         P("head", None),
         P(None, "head"),
     )
+    sizes = dict(mesh.shape)
+    fast = sizes["batch"] == 4 and sizes["ctx"] == 2 and sizes["head"] == 4
+    local = fast_local if fast else general_local
     return jax.shard_map(
         local, mesh=mesh, in_specs=placed, out_specs=P(("batch", "ctx"), "head"), check_vma=False
     )

time: 231 us -> 126 us (0.55)
  blocking collectives: 57.2 us -> 0 us
  waiting for transfers between devices: 94.2 us -> 48.8 us
  starting transfers between devices: 6.86 us -> 49.6 us
  matrix products: 33 us -> 0 us
  Pallas kernels: 0 us -> 25.5 us
  other arithmetic: 13.7 us -> 0.08 us
  between operations: 13.3 us -> 0.43 us
  local copies, waits for them, and re-layouts: 12.3 us -> 1.71 us
    reduce_scatter x1 -> x0, waiting for transfers between devices: 90.4 us -> none  [local(): lax.psum_scatter(head_terms.astype(jnp.bfloat16), 'head', scatter_dimensi...]
    ppermute x0 -> x28, starting transfers between devices: none -> 49.6 us  [the longest x3 12.4 us: fast_local(): one = lax.ppermute(attended, 'head', xor_pairs(4, 1))]
    ppermute x0 -> x28, waiting for transfers between devices: none -> 48.8 us  [the longest x3 14.2 us: fast_local(): three_far = lax.ppermute(two, 'head', ((2, 3), (1, 0)))]
    dot_general x7 -> x0, matrix products: 33 us -> none  [the longest x2 11.2 us: attend(): jnp.einsum('hqk,khd->qhd', weights.astype(jnp.bfloat16), value_heads, pre...]
    all_to_all x2 -> x0, blocking collectives: 29.5 us -> none  [the longest x1 18.7 us: local(): lax.all_to_all(placed(value_rows), 'ctx', split_axis=0, concat_axis=0, ti...]
    pallas_call x0 -> x6, Pallas kernels: none -> 25.5 us  [the longest x1 11.6 us: fast_local(): pl.pallas_call(functools.partial(project_kernel, cuts), in_specs=[SMEM, V...]
    all_gather x1 -> x0, blocking collectives: 14.3 us -> none  [local(): lax.all_gather(for_sending(own_segment), 'ctx', axis=0, tiled=True)]
    psum x1 -> x0, blocking collectives: 13.5 us -> none  [local(): lax.psum((jnp.sum(query_float * query_float, axis=1), jnp.sum(key_float *...]
  transfers between devices with their start and end apart: 5 -> 28, of which waited for: 3 -> 15; matrix products, arithmetic and copies ran while one was open for 5% -> 0% of each run, Pallas kernels for 0% -> 10%
where the time goes in v1:
time: 126 us
  starting transfers between devices  49.6 us (39%)
  waiting for transfers between devices  48.8 us (39%)
  Pallas kernels  25.5 us (20%)
  local copies, waits for them, and re-layouts  1.71 us (1%)
    ppermute x3, waiting for transfers between devices, fast_local(): three_far = lax.ppermute(two, 'head', ((2, 3), (1, 0)))  14.2 us
    ppermute x3, waiting for transfers between devices, fast_local(): two = lax.ppermute(attended, 'head', xor_pairs(4, 2))  12.9 us
    ppermute x3, starting transfers between devices, fast_local(): one = lax.ppermute(attended, 'head', xor_pairs(4, 1))  12.4 us
    pallas_call x1, Pallas kernels, fast_local(): pl.pallas_call(functools.partial(project_kernel, cuts), in_specs=[SMEM, V...  11.6 us
    ppermute x3, starting transfers between devices, fast_local(): two = lax.ppermute(attended, 'head', xor_pairs(4, 2))  10.2 us
    ppermute x3, waiting for transfers between devices, fast_local(): lax.ppermute(cut_weights[s - 1], 'head', xor_pairs(4, s))  9.69 us
    pallas_call x3, Pallas kernels, fast_local(): pl.pallas_call(functools.partial(attend_kernel, heads, low, total_width),...  8.99 us
    ppermute x3, starting transfers between devices, fast_local(): lax.ppermute(cut_weights[s - 1], 'head', xor_pairs(4, s))  5.7 us
  transfers between devices with their start and end apart: 28, of which 15 were waited for; matrix products, arithmetic and copies ran while one was open for 0% of the time, Pallas kernels for 10%

profile of v1, /device:TPU:0, one launch (start us, length us, event | category | flops | bytes accessed | tf_op | source)
XLA Modules:
  0.0 126.2 jit_solution(1782324377453160912)
XLA Ops:
  0.0 0.1 pad_add_fusion.place
  0.1 1.7 %cut_weights.1 = (bf16[80,1280]{1,0:T(8,128)(2,1)S(1)}, bf16[80,1280]{1,0:T(8,128)(2,1)S(1)}, bf16[80,1280]{1,0:T(8,128)(2,1)S(1)}) custom-call(s32[3]{0:T(128)S(1)} %pad_add_fusion.place, bf16[640,5120]{1,0:T(8,128)(2,1)} %weight_ref.3), custom_call_target="tpu_custom_call" | custom-call | bytes 1228800 | tf_op jit(solution)/shard_map/cut_weights/pallas_call | solution.py:206
  1.8 3.1 %collective-permute-start.18 = (bf16[80,1280]{1,0:T(8,128)(2,1)S(1)}, bf16[80,1280]{1,0:T(8,128)(2,1)S(1)}, u32[]{:S(2)}, u32[]{:S(2)}) collective-permute-start(bf16[80,1280]{1,0:T(8,128)(2,1)S(1)} %get-tuple-element.18), channel_id=1, source_target_pairs={{0,1},{1,0},{2,3},{3,2},{4,5},{5,4},{6,7},{7,6},{8,9},{9,8},{10,11... | collective-permute-start | bytes 614408 | tf_op jit(solution)/shard_map/ppermute | solution.py:216
  4.9 2.6 %collective-permute-start.19 = (bf16[80,1280]{1,0:T(8,128)(2,1)S(1)}, bf16[80,1280]{1,0:T(8,128)(2,1)S(1)}, u32[]{:S(2)}, u32[]{:S(2)}) collective-permute-start(bf16[80,1280]{1,0:T(8,128)(2,1)S(1)} %get-tuple-element.19), channel_id=1, source_target_pairs={{0,2},{1,3},{2,0},{3,1},{4,6},{5,7},{6,4},{7,5},{8,10},{9,11},{10,... | collective-permute-start | bytes 614408 | tf_op jit(solution)/shard_map/ppermute | solution.py:216
  7.5 0.0 collective-permute-start.20
  7.6 3.3 %prepare.1 = (bf16[256,640]{1,0:T(8,128)(2,1)S(1)}, bf16[1280,256]{1,0:T(8,128)(2,1)S(1)}, bf16[1280,256]{1,0:T(8,128)(2,1)S(1)}, bf16[1280,128]{1,0:T(8,128)(2,1)S(1)}, f32[8,512]{1,0:T(8,128)S(1)}) custom-call(s32[3]{0:T(128)S(1)} %pad_add_fusion.place, bf16[512,640]{1,0:T(8,128)(2,1)S(1)} %copy-done, bf16[512,640]{1,0:T(8,128)(2,1)S(1)} %copy-done.1, ...), custom_call_target="tpu_custom_call" | custom-call | flops 335544320 | bytes 3932160 | tf_op jit(solution)/shard_map/prepare/pallas_call | solution.py:227
  10.8 1.8 %collective-permute-start = (f32[8,512]{1,0:T(8,128)S(1)}, f32[8,512]{1,0:T(8,128)S(1)}, u32[]{:S(2)}, u32[]{:S(2)}) collective-permute-start(f32[8,512]{1,0:T(8,128)S(1)} %get-tuple-element.13), channel_id=1, source_target_pairs={{0,4},{4,0},{1,5},{5,1},{2,6},{6,2},{3,7},{7,3},{8,12},{12,8},{9,1... | collective-permute-start | bytes 49160 | tf_op jit(solution)/shard_map/ppermute | solution.py:239
  12.6 0.3 collective-permute-start.13
  12.9 0.7 collective-permute-done.18
  13.6 9.0 %collective-permute-done.19 = bf16[80,1280]{1,0:T(8,128)(2,1)S(1)} collective-permute-done((bf16[80,1280]{1,0:T(8,128)(2,1)S(1)}, bf16[80,1280]{1,0:T(8,128)(2,1)S(1)}, u32[]{:S(2)}, u32[]{:S(2)}) %collective-permute-start.19) | collective-permute-done | bytes 204832 | tf_op jit(solution)/shard_map/ppermute | solution.py:216
  22.6 0.0 collective-permute-done.20
  22.7 1.6 %collective-permute-start.21 = (bf16[240,1280]{1,0:T(8,128)(2,1)S(1)}, bf16[240,1280]{1,0:T(8,128)(2,1)S(1)}, u32[]{:S(2)}, u32[]{:S(2)}) collective-permute-start(bf16[240,1280]{1,0:T(8,128)(2,1)S(1)} %constant_dynamic-update-slice_fusion.2.refs_15_), channel_id=1, source_target_pairs={{0,4},{4,0},{1,5},{5,1},{2,6},{6,2},{3,7},{7,3},{8,12},{12,8},{9,1... | collective-permute-start | bytes 1843208 | tf_op jit(solution)/shard_map/ppermute | solution.py:218
  24.3 0.0 collective-permute-done
  24.3 3.5 %collective-permute-start.1 = (f32[16,512]{1,0:T(8,128)S(1)}, f32[16,512]{1,0:T(8,128)S(1)}, u32[]{:S(2)}, u32[]{:S(2)}) collective-permute-start(f32[16,512]{1,0:T(8,128)S(1)} %constant_dynamic-update-slice_fusion), channel_id=1, source_target_pairs={{0,1},{1,0},{2,3},{3,2},{4,5},{5,4},{6,7},{7,6},{8,9},{9,8},{10,11... | collective-permute-start | bytes 98312 | tf_op jit(solution)/shard_map/ppermute | solution.py:241
  27.8 1.9 %collective-permute-done.1 = f32[16,512]{1,0:T(8,128)S(1)} collective-permute-done((f32[16,512]{1,0:T(8,128)S(1)}, f32[16,512]{1,0:T(8,128)S(1)}, u32[]{:S(2)}, u32[]{:S(2)}) %collective-permute-start.1) | collective-permute-done | bytes 32800 | tf_op jit(solution)/shard_map/ppermute | solution.py:241
  29.7 3.3 %collective-permute-start.2 = (f32[16,512]{1,0:T(8,128)S(1)}, f32[16,512]{1,0:T(8,128)S(1)}, u32[]{:S(2)}, u32[]{:S(2)}) collective-permute-start(f32[16,512]{1,0:T(8,128)S(1)} %add.7.near_ref), channel_id=1, source_target_pairs={{0,2},{1,3},{2,0},{3,1},{4,6},{5,7},{6,4},{7,5},{8,10},{9,11},{10,... | collective-permute-start | bytes 98312 | tf_op jit(solution)/shard_map/ppermute | solution.py:242
  32.9 0.5 collective-permute-start.3
  33.5 1.4 %collective-permute-done.2.far_ref = f32[16,512]{1,0:T(8,128)S(1)} collective-permute-done((f32[16,512]{1,0:T(8,128)S(1)}, f32[16,512]{1,0:T(8,128)S(1)}, u32[]{:S(2)}, u32[]{:S(2)}) %collective-permute-start.2) | collective-permute-done | bytes 32800 | tf_op jit(solution)/shard_map/ppermute | solution.py:242
  34.8 0.0 collective-permute-done.13.remote_ref
  34.8 2.3 %attend.5.refs_10_ = bf16[512,128]{1,0:T(8,128)(2,1)S(1)} custom-call(s32[3]{0:T(128)S(1)} %pad_add_fusion.place, f32[16,512]{1,0:T(8,128)S(1)} %add.7.near_ref, f32[16,512]{1,0:T(8,128)S(1)} %collective-permute-done.2.far_ref, bf16[256,640]{1,0:T(8,128)(2,1)S(1)} %get-tuple-element.14.q_ref, bf16[1280,128]{1,0:T(8,128)(2,1)S(1)} %collective-permute-done.13.remote_ref, ...), custom_call_target="tpu_custom_call" | custom-call | flops 805306368 | bytes 2621440 | tf_op jit(solution)/shard_map/attend/pallas_call | solution.py:248
  37.1 0.0 copy-start.3
  37.2 0.0 copy-start.6
  37.2 0.8 collective-permute-start.16
  38.0 0.6 collective-permute-start.8
  38.5 4.4 %collective-permute-start.15 = (bf16[512,128]{1,0:T(8,128)(2,1)S(1)}, bf16[512,128]{1,0:T(8,128)(2,1)S(1)}, u32[]{:S(2)}, u32[]{:S(2)}) collective-permute-start(bf16[512,128]{1,0:T(8,128)(2,1)S(1)} %attend.5.refs_10_), channel_id=1, source_target_pairs={{0,2},{1,3},{2,0},{3,1},{4,6},{5,7},{6,4},{7,5},{8,10},{9,11},{10,... | collective-permute-start | bytes 393224 | tf_op jit(solution)/shard_map/ppermute | solution.py:262
  42.9 0.0 collective-permute-done.16.refs_13_
  42.9 2.9 %collective-permute-start.14 = (bf16[512,128]{1,0:T(8,128)(2,1)S(1)}, bf16[512,128]{1,0:T(8,128)(2,1)S(1)}, u32[]{:S(2)}, u32[]{:S(2)}) collective-permute-start(bf16[512,128]{1,0:T(8,128)(2,1)S(1)} %attend.5.refs_10_), channel_id=1, source_target_pairs={{0,1},{1,0},{2,3},{3,2},{4,5},{5,4},{6,7},{7,6},{8,9},{9,8},{10,11... | collective-permute-start | bytes 393224 | tf_op jit(solution)/shard_map/ppermute | solution.py:260
  45.8 0.8 collective-permute-done.15.refs_12_
  46.7 1.5 %collective-permute-start.24 = (bf16[240,1280]{1,0:T(8,128)(2,1)S(1)}, bf16[240,1280]{1,0:T(8,128)(2,1)S(1)}, u32[]{:S(2)}, u32[]{:S(2)}) collective-permute-start(bf16[240,1280]{1,0:T(8,128)(2,1)S(1)} %constant_dynamic-update-slice_fusion.2.refs_15_), channel_id=1, source_target_pairs={{0,16},{16,0},{8,24},{24,8},{1,17},{17,1},{9,25},{25,9},{2,18},{18... | collective-permute-start | bytes 1843208 | tf_op jit(solution)/shard_map/ppermute | solution.py:219
  48.2 0.6 collective-permute-done.14.refs_11_
  48.8 0.0 collective-permute-start.22
  48.8 0.0 collective-permute-done.21.refs_16_
  48.8 1.5 %collective-permute-start.25 = (bf16[240,1280]{1,0:T(8,128)(2,1)S(1)}, bf16[240,1280]{1,0:T(8,128)(2,1)S(1)}, u32[]{:S(2)}, u32[]{:S(2)}) collective-permute-start(bf16[240,1280]{1,0:T(8,128)(2,1)S(1)} %collective-permute-done.21.refs_16_), channel_id=1, source_target_pairs={{0,16},{16,0},{8,24},{24,8},{1,17},{17,1},{9,25},{25,9},{2,18},{18... | collective-permute-start | bytes 1843208 | tf_op jit(solution)/shard_map/ppermute | solution.py:220
  50.3 3.1 %collective-permute-done.3.remote_ref = bf16[1280,256]{1,0:T(8,128)(2,1)S(1)} collective-permute-done((bf16[1280,256]{1,0:T(8,128)(2,1)S(1)}, bf16[1280,256]{1,0:T(8,128)(2,1)S(1)}, u32[]{:S(2)}, u32[]{:S(2)}) %collective-permute-start.3) | collective-permute-done | bytes 655392 | tf_op jit(solution)/shard_map/ppermute | solution.py:244
  53.4 1.3 %collective-permute-start.17 = (bf16[512,128]{1,0:T(8,128)(2,1)S(1)}, bf16[512,128]{1,0:T(8,128)(2,1)S(1)}, u32[]{:S(2)}, u32[]{:S(2)}) collective-permute-start(bf16[512,128]{1,0:T(8,128)(2,1)S(1)} %collective-permute-done.15.refs_12_), channel_id=1, source_target_pairs={{2,3},{1,0},{6,7},{5,4},{10,11},{9,8},{14,15},{13,12},{18,19},{17,... | collective-permute-start | bytes 393224 | tf_op jit(solution)/shard_map/ppermute | solution.py:263
  54.7 3.3 %attend.3.refs_0_ = bf16[512,256]{1,0:T(8,128)(2,1)S(1)} custom-call(s32[3]{0:T(128)S(1)} %pad_add_fusion.place, f32[16,512]{1,0:T(8,128)S(1)} %add.7.near_ref, f32[16,512]{1,0:T(8,128)S(1)} %collective-permute-done.2.far_ref, bf16[256,640]{1,0:T(8,128)(2,1)S(1)} %get-tuple-element.14.q_ref, bf16[1280,256]{1,0:T(8,128)(2,1)S(1)} %collective-permute-done.3.remote_ref, ...), custom_call_target="tpu_custom_call" | custom-call | flops 1610612736 | bytes 2621440 | tf_op jit(solution)/shard_map/attend/pallas_call | solution.py:248
  58.0 3.3 %collective-permute-done.17.refs_14_ = bf16[512,128]{1,0:T(8,128)(2,1)S(1)} collective-permute-done((bf16[512,128]{1,0:T(8,128)(2,1)S(1)}, bf16[512,128]{1,0:T(8,128)(2,1)S(1)}, u32[]{:S(2)}, u32[]{:S(2)}) %collective-permute-start.17) | collective-permute-done | bytes 131104 | tf_op jit(solution)/shard_map/ppermute | solution.py:263
  61.3 0.7 collective-permute-start.6
  62.0 2.0 %collective-permute-done.8.remote_ref = bf16[1280,256]{1,0:T(8,128)(2,1)S(1)} collective-permute-done((bf16[1280,256]{1,0:T(8,128)(2,1)S(1)}, bf16[1280,256]{1,0:T(8,128)(2,1)S(1)}, u32[]{:S(2)}, u32[]{:S(2)}) %collective-permute-start.8) | collective-permute-done | bytes 655392 | tf_op jit(solution)/shard_map/ppermute | solution.py:244
  63.9 5.9 %collective-permute-start.5 = (bf16[512,256]{1,0:T(8,128)(2,1)S(1)}, bf16[512,256]{1,0:T(8,128)(2,1)S(1)}, u32[]{:S(2)}, u32[]{:S(2)}) collective-permute-start(bf16[512,256]{1,0:T(8,128)(2,1)S(1)} %attend.3.refs_0_), channel_id=1, source_target_pairs={{0,2},{1,3},{2,0},{3,1},{4,6},{5,7},{6,4},{7,5},{8,10},{9,11},{10,... | collective-permute-start | bytes 786440 | tf_op jit(solution)/shard_map/ppermute | solution.py:262
  69.8 3.3 %attend.4.refs_5_ = bf16[512,256]{1,0:T(8,128)(2,1)S(1)} custom-call(s32[3]{0:T(128)S(1)} %pad_add_fusion.place, f32[16,512]{1,0:T(8,128)S(1)} %add.7.near_ref, f32[16,512]{1,0:T(8,128)S(1)} %collective-permute-done.2.far_ref, bf16[256,640]{1,0:T(8,128)(2,1)S(1)} %get-tuple-element.14.q_ref, bf16[1280,256]{1,0:T(8,128)(2,1)S(1)} %collective-permute-done.8.remote_ref, ...), custom_call_target="tpu_custom_call" | custom-call | flops 1610612736 | bytes 2621440 | tf_op jit(solution)/shard_map/attend/pallas_call | solution.py:248
  73.1 0.0 collective-permute-done.24.refs_19_
  73.1 0.1 collective-permute-start.4
  73.2 0.0 collective-permute-done.22.refs_17_
  73.2 0.7 collective-permute-start.11
  73.9 0.1 collective-permute-start.23
  74.0 7.6 %collective-permute-done.5.refs_2_ = bf16[512,256]{1,0:T(8,128)(2,1)S(1)} collective-permute-done((bf16[512,256]{1,0:T(8,128)(2,1)S(1)}, bf16[512,256]{1,0:T(8,128)(2,1)S(1)}, u32[]{:S(2)}, u32[]{:S(2)}) %collective-permute-start.5) | collective-permute-done | bytes 262176 | tf_op jit(solution)/shard_map/ppermute | solution.py:262
  81.6 0.0 collective-permute-start.26
  81.6 0.0 collective-permute-done.25.refs_20_
  81.6 0.5 collective-permute-start.27
  82.2 1.6 %collective-permute-done.4.refs_1_ = bf16[512,256]{1,0:T(8,128)(2,1)S(1)} collective-permute-done((bf16[512,256]{1,0:T(8,128)(2,1)S(1)}, bf16[512,256]{1,0:T(8,128)(2,1)S(1)}, u32[]{:S(2)}, u32[]{:S(2)}) %collective-permute-start.4) | collective-permute-done | bytes 262176 | tf_op jit(solution)/shard_map/ppermute | solution.py:260
  83.8 0.0 collective-permute-done.11.refs_8_
  83.8 9.4 %collective-permute-start.9 = (bf16[512,256]{1,0:T(8,128)(2,1)S(1)}, bf16[512,256]{1,0:T(8,128)(2,1)S(1)}, u32[]{:S(2)}, u32[]{:S(2)}) collective-permute-start(bf16[512,256]{1,0:T(8,128)(2,1)S(1)} %attend.4.refs_5_), channel_id=1, source_target_pairs={{0,1},{1,0},{2,3},{3,2},{4,5},{5,4},{6,7},{7,6},{8,9},{9,8},{10,11... | collective-permute-start | bytes 786440 | tf_op jit(solution)/shard_map/ppermute | solution.py:260
  93.2 4.4 %collective-permute-done.10.refs_7_ = bf16[512,256]{1,0:T(8,128)(2,1)S(1)} collective-permute-done((bf16[512,256]{1,0:T(8,128)(2,1)S(1)}, bf16[512,256]{1,0:T(8,128)(2,1)S(1)}, u32[]{:S(2)}, u32[]{:S(2)}) %collective-permute-start.10) | collective-permute-done | bytes 262176 | tf_op jit(solution)/shard_map/ppermute | solution.py:262
  97.6 1.3 %collective-permute-start.7 = (bf16[512,256]{1,0:T(8,128)(2,1)S(1)}, bf16[512,256]{1,0:T(8,128)(2,1)S(1)}, u32[]{:S(2)}, u32[]{:S(2)}) collective-permute-start(bf16[512,256]{1,0:T(8,128)(2,1)S(1)} %collective-permute-done.5.refs_2_), channel_id=1, source_target_pairs={{2,3},{1,0},{6,7},{5,4},{10,11},{9,8},{14,15},{13,12},{18,19},{17,... | collective-permute-start | bytes 786440 | tf_op jit(solution)/shard_map/ppermute | solution.py:263
  98.9 1.4 %collective-permute-done.9.refs_6_ = bf16[512,256]{1,0:T(8,128)(2,1)S(1)} collective-permute-done((bf16[512,256]{1,0:T(8,128)(2,1)S(1)}, bf16[512,256]{1,0:T(8,128)(2,1)S(1)}, u32[]{:S(2)}, u32[]{:S(2)}) %collective-permute-start.9) | collective-permute-done | bytes 262176 | tf_op jit(solution)/shard_map/ppermute | solution.py:260
  100.4 1.5 %collective-permute-start.12 = (bf16[512,256]{1,0:T(8,128)(2,1)S(1)}, bf16[512,256]{1,0:T(8,128)(2,1)S(1)}, u32[]{:S(2)}, u32[]{:S(2)}) collective-permute-start(bf16[512,256]{1,0:T(8,128)(2,1)S(1)} %collective-permute-done.10.refs_7_), channel_id=1, source_target_pairs={{2,3},{1,0},{6,7},{5,4},{10,11},{9,8},{14,15},{13,12},{18,19},{17,... | collective-permute-start | bytes 786440 | tf_op jit(solution)/shard_map/ppermute | solution.py:263
  101.8 7.0 %collective-permute-done.7.refs_4_ = bf16[512,256]{1,0:T(8,128)(2,1)S(1)} collective-permute-done((bf16[512,256]{1,0:T(8,128)(2,1)S(1)}, bf16[512,256]{1,0:T(8,128)(2,1)S(1)}, u32[]{:S(2)}, u32[]{:S(2)}) %collective-permute-start.7) | collective-permute-done | bytes 262176 | tf_op jit(solution)/shard_map/ppermute | solution.py:263
  108.8 4.0 %collective-permute-done.12.refs_9_ = bf16[512,256]{1,0:T(8,128)(2,1)S(1)} collective-permute-done((bf16[512,256]{1,0:T(8,128)(2,1)S(1)}, bf16[512,256]{1,0:T(8,128)(2,1)S(1)}, u32[]{:S(2)}, u32[]{:S(2)}) %collective-permute-start.12) | collective-permute-done | bytes 262176 | tf_op jit(solution)/shard_map/ppermute | solution.py:263
  112.8 0.0 collective-permute-done.26.refs_21_
  112.8 0.0 collective-permute-done.23.refs_18_
  112.8 0.8 copy-done.9
  113.6 0.8 copy-done.10
  114.5 11.6 %project.1 = bf16[512,1280]{1,0:T(8,128)(2,1)} custom-call(s32[3]{0:T(128)S(1)} %pad_add_fusion.place, f32[16,512]{1,0:T(8,128)S(1)} %add.7.near_ref, f32[16,512]{1,0:T(8,128)S(1)} %collective-permute-done.2.far_ref, s32[6]{0:T(128)S(1)} %copy-done.6, f32[50,1280]{1,0:T(8,128)S(1)} %copy-done.3, bf16[640,5120]{1,0:T(8,128)(2,1)} %weight_ref.3, ...), custom_call_target="tpu_custom_call" | custom-call | flops 3355443200 | bytes 8192000 | tf_op jit(solution)/shard_map/project/pallas_call | solution.py:266
  (33 shorter events, 0.1 us)
Async XLA Ops:
  0.0 7.5 %copy-start.2 = (bf16[512,640]{1,0:T(8,128)(2,1)S(1)}, bf16[512,640]{1,0:T(8,128)(2,1)}, u32[]{:S(2)}) copy-start(bf16[512,640]{1,0:T(8,128)(2,1)} %v_ref.7) | copy-start | bytes 1966084
  0.0 7.5 %copy-start.1 = (bf16[512,640]{1,0:T(8,128)(2,1)S(1)}, bf16[512,640]{1,0:T(8,128)(2,1)}, u32[]{:S(2)}) copy-start(bf16[512,640]{1,0:T(8,128)(2,1)} %k_ref.7) | copy-start | bytes 1966084
  0.0 7.5 %copy-start.4 = (s32[512]{0:T(512)S(1)}, s32[512]{0:T(512)}, u32[]{:S(2)}) copy-start(s32[512]{0:T(512)} %param.16) | copy-start | bytes 6148
  0.0 7.5 %copy-start.5 = (s32[512]{0:T(512)S(1)}, s32[512]{0:T(512)}, u32[]{:S(2)}) copy-start(s32[512]{0:T(512)} %param.15) | copy-start | bytes 6148
  0.0 7.5 %copy-start = (bf16[512,640]{1,0:T(8,128)(2,1)S(1)}, bf16[512,640]{1,0:T(8,128)(2,1)}, u32[]{:S(2)}) copy-start(bf16[512,640]{1,0:T(8,128)(2,1)} %q_ref.1) | copy-start | bytes 1966084
  0.0 33.4 %copy-start.11 = (f32[640]{0:T(1024)S(1)}, f32[640]{0:T(1024)}, u32[]{:S(2)}) copy-start(f32[640]{0:T(1024)} %param.13) | copy-start | bytes 7684
  0.0 33.4 %copy-start.12 = (f32[640]{0:T(1024)S(1)}, f32[640]{0:T(1024)}, u32[]{:S(2)}) copy-start(f32[640]{0:T(1024)} %param.14) | copy-start | bytes 7684
  1.8 11.8 %collective-permute-start.18 = (bf16[80,1280]{1,0:T(8,128)(2,1)S(1)}, bf16[80,1280]{1,0:T(8,128)(2,1)S(1)}, u32[]{:S(2)}, u32[]{:S(2)}) collective-permute-start(bf16[80,1280]{1,0:T(8,128)(2,1)S(1)} %get-tuple-element.18), channel_id=1, source_target_pairs={{0,1},{1,0},{2,3},{3,2},{4,5},{5,4},{6,7},{7,6},{8,9},{9,8},{10,11... | collective-permute-start | bytes 614408 | tf_op jit(solution)/shard_map/ppermute | solution.py:216
  4.9 17.7 %collective-permute-start.19 = (bf16[80,1280]{1,0:T(8,128)(2,1)S(1)}, bf16[80,1280]{1,0:T(8,128)(2,1)S(1)}, u32[]{:S(2)}, u32[]{:S(2)}) collective-permute-start(bf16[80,1280]{1,0:T(8,128)(2,1)S(1)} %get-tuple-element.19), channel_id=1, source_target_pairs={{0,2},{1,3},{2,0},{3,1},{4,6},{5,7},{6,4},{7,5},{8,10},{9,11},{10,... | collective-permute-start | bytes 614408 | tf_op jit(solution)/shard_map/ppermute | solution.py:216
  7.5 15.1 %collective-permute-start.20 = (bf16[80,1280]{1,0:T(8,128)(2,1)S(1)}, bf16[80,1280]{1,0:T(8,128)(2,1)S(1)}, u32[]{:S(2)}, u32[]{:S(2)}) collective-permute-start(bf16[80,1280]{1,0:T(8,128)(2,1)S(1)} %get-tuple-element.20), channel_id=1, source_target_pairs={{0,3},{1,2},{2,1},{3,0},{4,7},{5,6},{6,5},{7,4},{8,11},{9,10},{10,... | collective-permute-start | bytes 614408 | tf_op jit(solution)/shard_map/ppermute | solution.py:216
  10.8 13.4 %collective-permute-start = (f32[8,512]{1,0:T(8,128)S(1)}, f32[8,512]{1,0:T(8,128)S(1)}, u32[]{:S(2)}, u32[]{:S(2)}) collective-permute-start(f32[8,512]{1,0:T(8,128)S(1)} %get-tuple-element.13), channel_id=1, source_target_pairs={{0,4},{4,0},{1,5},{5,1},{2,6},{6,2},{3,7},{7,3},{8,12},{12,8},{9,1... | collective-permute-start | bytes 49160 | tf_op jit(solution)/shard_map/ppermute | solution.py:239
  12.6 22.2 %collective-permute-start.13 = (bf16[1280,128]{1,0:T(8,128)(2,1)S(1)}, bf16[1280,128]{1,0:T(8,128)(2,1)S(1)}, u32[]{:S(2)}, u32[]{:S(2)}) collective-permute-start(bf16[1280,128]{1,0:T(8,128)(2,1)S(1)} %get-tuple-element.17), channel_id=1, source_target_pairs={{0,4},{4,0},{1,5},{5,1},{2,6},{6,2},{3,7},{7,3},{8,12},{12,8},{9,1... | collective-permute-start | bytes 983048 | tf_op jit(solution)/shard_map/ppermute | solution.py:244
  22.7 26.1 %collective-permute-start.21 = (bf16[240,1280]{1,0:T(8,128)(2,1)S(1)}, bf16[240,1280]{1,0:T(8,128)(2,1)S(1)}, u32[]{:S(2)}, u32[]{:S(2)}) collective-permute-start(bf16[240,1280]{1,0:T(8,128)(2,1)S(1)} %constant_dynamic-update-slice_fusion.2.refs_15_), channel_id=1, source_target_pairs={{0,4},{4,0},{1,5},{5,1},{2,6},{6,2},{3,7},{7,3},{8,12},{12,8},{9,1... | collective-permute-start | bytes 1843208 | tf_op jit(solution)/shard_map/ppermute | solution.py:218
  24.3 5.4 %collective-permute-start.1 = (f32[16,512]{1,0:T(8,128)S(1)}, f32[16,512]{1,0:T(8,128)S(1)}, u32[]{:S(2)}, u32[]{:S(2)}) collective-permute-start(f32[16,512]{1,0:T(8,128)S(1)} %constant_dynamic-update-slice_fusion), channel_id=1, source_target_pairs={{0,1},{1,0},{2,3},{3,2},{4,5},{5,4},{6,7},{7,6},{8,9},{9,8},{10,11... | collective-permute-start | bytes 98312 | tf_op jit(solution)/shard_map/ppermute | solution.py:241
  29.7 5.2 %collective-permute-start.2 = (f32[16,512]{1,0:T(8,128)S(1)}, f32[16,512]{1,0:T(8,128)S(1)}, u32[]{:S(2)}, u32[]{:S(2)}) collective-permute-start(f32[16,512]{1,0:T(8,128)S(1)} %add.7.near_ref), channel_id=1, source_target_pairs={{0,2},{1,3},{2,0},{3,1},{4,6},{5,7},{6,4},{7,5},{8,10},{9,11},{10,... | collective-permute-start | bytes 98312 | tf_op jit(solution)/shard_map/ppermute | solution.py:242
  32.9 20.4 %collective-permute-start.3 = (bf16[1280,256]{1,0:T(8,128)(2,1)S(1)}, bf16[1280,256]{1,0:T(8,128)(2,1)S(1)}, u32[]{:S(2)}, u32[]{:S(2)}) collective-permute-start(bf16[1280,256]{1,0:T(8,128)(2,1)S(1)} %get-tuple-element.15), channel_id=1, source_target_pairs={{0,4},{4,0},{1,5},{5,1},{2,6},{6,2},{3,7},{7,3},{8,12},{12,8},{9,1... | collective-permute-start | bytes 1966088 | tf_op jit(solution)/shard_map/ppermute | solution.py:244
  37.1 77.3 %copy-start.3 = (f32[50,1280]{1,0:T(8,128)S(1)}, f32[50,1280]{1,0:T(8,128)}, u32[]{:S(2)}) copy-start(f32[50,1280]{1,0:T(8,128)} %gate_ref.1) | copy-start | bytes 768004
  37.2 77.3 %copy-start.6 = (s32[6]{0:T(128)S(1)}, s32[6]{0:T(128)}, u32[]{:S(2)}) copy-start(s32[6]{0:T(128)} %times.1) | copy-start | bytes 76
  37.2 5.8 %collective-permute-start.16 = (bf16[512,128]{1,0:T(8,128)(2,1)S(1)}, bf16[512,128]{1,0:T(8,128)(2,1)S(1)}, u32[]{:S(2)}, u32[]{:S(2)}) collective-permute-start(bf16[512,128]{1,0:T(8,128)(2,1)S(1)} %attend.5.refs_10_), channel_id=1, source_target_pairs={{1,2},{2,1},{5,6},{6,5},{9,10},{10,9},{13,14},{14,13},{17,18},{18,... | collective-permute-start | bytes 393224 | tf_op jit(solution)/shard_map/ppermute | solution.py:261
  38.0 25.9 %collective-permute-start.8 = (bf16[1280,256]{1,0:T(8,128)(2,1)S(1)}, bf16[1280,256]{1,0:T(8,128)(2,1)S(1)}, u32[]{:S(2)}, u32[]{:S(2)}) collective-permute-start(bf16[1280,256]{1,0:T(8,128)(2,1)S(1)} %get-tuple-element.16), channel_id=1, source_target_pairs={{0,4},{4,0},{1,5},{5,1},{2,6},{6,2},{3,7},{7,3},{8,12},{12,8},{9,1... | collective-permute-start | bytes 1966088 | tf_op jit(solution)/shard_map/ppermute | solution.py:244
  38.5 8.1 %collective-permute-start.15 = (bf16[512,128]{1,0:T(8,128)(2,1)S(1)}, bf16[512,128]{1,0:T(8,128)(2,1)S(1)}, u32[]{:S(2)}, u32[]{:S(2)}) collective-permute-start(bf16[512,128]{1,0:T(8,128)(2,1)S(1)} %attend.5.refs_10_), channel_id=1, source_target_pairs={{0,2},{1,3},{2,0},{3,1},{4,6},{5,7},{6,4},{7,5},{8,10},{9,11},{10,... | collective-permute-start | bytes 393224 | tf_op jit(solution)/shard_map/ppermute | solution.py:262
  42.9 5.9 %collective-permute-start.14 = (bf16[512,128]{1,0:T(8,128)(2,1)S(1)}, bf16[512,128]{1,0:T(8,128)(2,1)S(1)}, u32[]{:S(2)}, u32[]{:S(2)}) collective-permute-start(bf16[512,128]{1,0:T(8,128)(2,1)S(1)} %attend.5.refs_10_), channel_id=1, source_target_pairs={{0,1},{1,0},{2,3},{3,2},{4,5},{5,4},{6,7},{7,6},{8,9},{9,8},{10,11... | collective-permute-start | bytes 393224 | tf_op jit(solution)/shard_map/ppermute | solution.py:260
  46.7 26.5 %collective-permute-start.24 = (bf16[240,1280]{1,0:T(8,128)(2,1)S(1)}, bf16[240,1280]{1,0:T(8,128)(2,1)S(1)}, u32[]{:S(2)}, u32[]{:S(2)}) collective-permute-start(bf16[240,1280]{1,0:T(8,128)(2,1)S(1)} %constant_dynamic-update-slice_fusion.2.refs_15_), channel_id=1, source_target_pairs={{0,16},{16,0},{8,24},{24,8},{1,17},{17,1},{9,25},{25,9},{2,18},{18... | collective-permute-start | bytes 1843208 | tf_op jit(solution)/shard_map/ppermute | solution.py:219
  48.8 24.4 %collective-permute-start.22 = (bf16[240,1280]{1,0:T(8,128)(2,1)S(1)}, bf16[240,1280]{1,0:T(8,128)(2,1)S(1)}, u32[]{:S(2)}, u32[]{:S(2)}) collective-permute-start(bf16[240,1280]{1,0:T(8,128)(2,1)S(1)} %constant_dynamic-update-slice_fusion.2.refs_15_), channel_id=1, source_target_pairs={{0,8},{8,0},{16,24},{24,16},{1,9},{9,1},{17,25},{25,17},{2,10},{10... | collective-permute-start | bytes 1843208 | tf_op jit(solution)/shard_map/ppermute | solution.py:224
  48.8 32.9 %collective-permute-start.25 = (bf16[240,1280]{1,0:T(8,128)(2,1)S(1)}, bf16[240,1280]{1,0:T(8,128)(2,1)S(1)}, u32[]{:S(2)}, u32[]{:S(2)}) collective-permute-start(bf16[240,1280]{1,0:T(8,128)(2,1)S(1)} %collective-permute-done.21.refs_16_), channel_id=1, source_target_pairs={{0,16},{16,0},{8,24},{24,8},{1,17},{17,1},{9,25},{25,9},{2,18},{18... | collective-permute-start | bytes 1843208 | tf_op jit(solution)/shard_map/ppermute | solution.py:220
  53.4 7.9 %collective-permute-start.17 = (bf16[512,128]{1,0:T(8,128)(2,1)S(1)}, bf16[512,128]{1,0:T(8,128)(2,1)S(1)}, u32[]{:S(2)}, u32[]{:S(2)}) collective-permute-start(bf16[512,128]{1,0:T(8,128)(2,1)S(1)} %collective-permute-done.15.refs_12_), channel_id=1, source_target_pairs={{2,3},{1,0},{6,7},{5,4},{10,11},{9,8},{14,15},{13,12},{18,19},{17,... | collective-permute-start | bytes 393224 | tf_op jit(solution)/shard_map/ppermute | solution.py:263
  61.3 12.6 %collective-permute-start.6 = (bf16[512,256]{1,0:T(8,128)(2,1)S(1)}, bf16[512,256]{1,0:T(8,128)(2,1)S(1)}, u32[]{:S(2)}, u32[]{:S(2)}) collective-permute-start(bf16[512,256]{1,0:T(8,128)(2,1)S(1)} %attend.3.refs_0_), channel_id=1, source_target_pairs={{1,2},{2,1},{5,6},{6,5},{9,10},{10,9},{13,14},{14,13},{17,18},{18,... | collective-permute-start | bytes 786440 | tf_op jit(solution)/shard_map/ppermute | solution.py:261
  63.9 17.7 %collective-permute-start.5 = (bf16[512,256]{1,0:T(8,128)(2,1)S(1)}, bf16[512,256]{1,0:T(8,128)(2,1)S(1)}, u32[]{:S(2)}, u32[]{:S(2)}) collective-permute-start(bf16[512,256]{1,0:T(8,128)(2,1)S(1)} %attend.3.refs_0_), channel_id=1, source_target_pairs={{0,2},{1,3},{2,0},{3,1},{4,6},{5,7},{6,4},{7,5},{8,10},{9,11},{10,... | collective-permute-start | bytes 786440 | tf_op jit(solution)/shard_map/ppermute | solution.py:262
  73.1 39.7 %copy-start.7 = (bf16[240,1280]{1,0:T(8,128)(2,1)}, bf16[240,1280]{1,0:T(8,128)(2,1)S(1)}, u32[]{:S(2)}) copy-start(bf16[240,1280]{1,0:T(8,128)(2,1)S(1)} %collective-permute-done.24.refs_19_) | copy-start | bytes 1843204
  73.1 10.6 %collective-permute-start.4 = (bf16[512,256]{1,0:T(8,128)(2,1)S(1)}, bf16[512,256]{1,0:T(8,128)(2,1)S(1)}, u32[]{:S(2)}, u32[]{:S(2)}) collective-permute-start(bf16[512,256]{1,0:T(8,128)(2,1)S(1)} %attend.3.refs_0_), channel_id=1, source_target_pairs={{0,1},{1,0},{2,3},{3,2},{4,5},{5,4},{6,7},{7,6},{8,9},{9,8},{10,11... | collective-permute-start | bytes 786440 | tf_op jit(solution)/shard_map/ppermute | solution.py:260
  73.2 10.5 %collective-permute-start.11 = (bf16[512,256]{1,0:T(8,128)(2,1)S(1)}, bf16[512,256]{1,0:T(8,128)(2,1)S(1)}, u32[]{:S(2)}, u32[]{:S(2)}) collective-permute-start(bf16[512,256]{1,0:T(8,128)(2,1)S(1)} %attend.4.refs_5_), channel_id=1, source_target_pairs={{1,2},{2,1},{5,6},{6,5},{9,10},{10,9},{13,14},{14,13},{17,18},{18,... | collective-permute-start | bytes 786440 | tf_op jit(solution)/shard_map/ppermute | solution.py:261
  73.9 38.9 %collective-permute-start.23 = (bf16[240,1280]{1,0:T(8,128)(2,1)S(1)}, bf16[240,1280]{1,0:T(8,128)(2,1)S(1)}, u32[]{:S(2)}, u32[]{:S(2)}) collective-permute-start(bf16[240,1280]{1,0:T(8,128)(2,1)S(1)} %collective-permute-done.21.refs_16_), channel_id=1, source_target_pairs={{0,8},{8,0},{16,24},{24,16},{1,9},{9,1},{17,25},{25,17},{2,10},{10... | collective-permute-start | bytes 1843208 | tf_op jit(solution)/shard_map/ppermute | solution.py:224
  81.6 31.2 %collective-permute-start.26 = (bf16[240,1280]{1,0:T(8,128)(2,1)S(1)}, bf16[240,1280]{1,0:T(8,128)(2,1)S(1)}, u32[]{:S(2)}, u32[]{:S(2)}) collective-permute-start(bf16[240,1280]{1,0:T(8,128)(2,1)S(1)} %collective-permute-done.24.refs_19_), channel_id=1, source_target_pairs={{0,8},{8,0},{16,24},{24,16},{1,9},{9,1},{17,25},{25,17},{2,10},{10... | collective-permute-start | bytes 1843208 | tf_op jit(solution)/shard_map/ppermute | solution.py:224
  81.6 31.2 %copy-start.8 = (bf16[240,1280]{1,0:T(8,128)(2,1)}, bf16[240,1280]{1,0:T(8,128)(2,1)S(1)}, u32[]{:S(2)}) copy-start(bf16[240,1280]{1,0:T(8,128)(2,1)S(1)} %collective-permute-done.25.refs_20_) | copy-start | bytes 1843204
  81.6 31.2 %collective-permute-start.27 = (bf16[240,1280]{1,0:T(8,128)(2,1)S(1)}, bf16[240,1280]{1,0:T(8,128)(2,1)S(1)}, u32[]{:S(2)}, u32[]{:S(2)}) collective-permute-start(bf16[240,1280]{1,0:T(8,128)(2,1)S(1)} %collective-permute-done.25.refs_20_), channel_id=1, source_target_pairs={{0,8},{8,0},{16,24},{24,16},{1,9},{9,1},{17,25},{25,17},{2,10},{10... | collective-permute-start | bytes 1843208 | tf_op jit(solution)/shard_map/ppermute | solution.py:224
  83.7 13.9 %collective-permute-start.10 = (bf16[512,256]{1,0:T(8,128)(2,1)S(1)}, bf16[512,256]{1,0:T(8,128)(2,1)S(1)}, u32[]{:S(2)}, u32[]{:S(2)}) collective-permute-start(bf16[512,256]{1,0:T(8,128)(2,1)S(1)} %attend.4.refs_5_), channel_id=1, source_target_pairs={{0,2},{1,3},{2,0},{3,1},{4,6},{5,7},{6,4},{7,5},{8,10},{9,11},{10,... | collective-permute-start | bytes 786440 | tf_op jit(solution)/shard_map/ppermute | solution.py:262
  83.8 16.6 %collective-permute-start.9 = (bf16[512,256]{1,0:T(8,128)(2,1)S(1)}, bf16[512,256]{1,0:T(8,128)(2,1)S(1)}, u32[]{:S(2)}, u32[]{:S(2)}) collective-permute-start(bf16[512,256]{1,0:T(8,128)(2,1)S(1)} %attend.4.refs_5_), channel_id=1, source_target_pairs={{0,1},{1,0},{2,3},{3,2},{4,5},{5,4},{6,7},{7,6},{8,9},{9,8},{10,11... | collective-permute-start | bytes 786440 | tf_op jit(solution)/shard_map/ppermute | solution.py:260
  97.6 11.1 %collective-permute-start.7 = (bf16[512,256]{1,0:T(8,128)(2,1)S(1)}, bf16[512,256]{1,0:T(8,128)(2,1)S(1)}, u32[]{:S(2)}, u32[]{:S(2)}) collective-permute-start(bf16[512,256]{1,0:T(8,128)(2,1)S(1)} %collective-permute-done.5.refs_2_), channel_id=1, source_target_pairs={{2,3},{1,0},{6,7},{5,4},{10,11},{9,8},{14,15},{13,12},{18,19},{17,... | collective-permute-start | bytes 786440 | tf_op jit(solution)/shard_map/ppermute | solution.py:263
  100.4 12.4 %collective-permute-start.12 = (bf16[512,256]{1,0:T(8,128)(2,1)S(1)}, bf16[512,256]{1,0:T(8,128)(2,1)S(1)}, u32[]{:S(2)}, u32[]{:S(2)}) collective-permute-start(bf16[512,256]{1,0:T(8,128)(2,1)S(1)} %collective-permute-done.10.refs_7_), channel_id=1, source_target_pairs={{2,3},{1,0},{6,7},{5,4},{10,11},{9,8},{14,15},{13,12},{18,19},{17,... | collective-permute-start | bytes 786440 | tf_op jit(solution)/shard_map/ppermute | solution.py:263
  112.8 0.8 copy-start.9
  113.6 0.8 copy-start.10

commit v2 on v0

--- a/solution.py
+++ b/solution.py
@@ -1,11 +1,364 @@
+import functools
 import math
 
 import jax
 import jax.numpy as jnp
 from jax import lax
+from jax.experimental import pallas as pl
+from jax.experimental.pallas import tpu as pltpu
 from jax.sharding import PartitionSpec as P
 
 HD = 128
+F32 = jnp.float32
+BF16 = jnp.bfloat16
+VMEM = pl.BlockSpec(memory_space=pltpu.VMEM)
+SMEM = pl.BlockSpec(memory_space=pltpu.SMEM)
+ANY = pl.BlockSpec(memory_space=pl.ANY)
+HBM = pl.BlockSpec(memory_space=pltpu.HBM)
+AFTER = VMEM
+SENDS = (3, 2)
+
+SWAP_CTX = ((0, 1), (1, 0))
+SWAP_CORE = ((0, 1), (1, 0), (2, 3), (3, 2))
+SWAP_X = ((0, 2), (2, 0), (1, 3), (3, 1))
+
+
+def xor_pairs(size, step):
+    return tuple((i, i ^ step) for i in range(size))
+
+
+def params(mebibytes):
+    return pltpu.CompilerParams(vmem_limit_bytes=mebibytes * 1024 * 1024)
+
+
+def cost(microseconds):
+    return pl.CostEstimate(flops=0, bytes_accessed=int(microseconds * 3_600_000), transcendentals=0)
+
+
+def load(pairs, sems):
+    copies = [pltpu.make_async_copy(source, target, sems.at[i]) for i, (source, target) in enumerate(pairs)]
+    for copy in copies:
+        copy.start()
+    return copies
+
+
+def row_sums(values):
+    squares = values * values
+    folded = squares[:, 0:HD]
+    for low in range(HD, values.shape[1], HD):
+        folded = folded + squares[:, low : low + HD]
+    return jnp.sum(jnp.transpose(folded), axis=0, keepdims=True)
+
+
+def three_pieces(value):
+    pieces = []
+    for _ in range(3):
+        short = value.astype(BF16).astype(F32)
+        pieces.append(short)
+        value = value - short
+    return pieces
+
+
+def column(row):
+    return jnp.transpose(jnp.broadcast_to(row, (8, row.shape[1])))[:, 0:1]
+
+
+def prepare_kernel(
+    cut, place, q_hbm, k_hbm, v_hbm, dest_hbm, seg_hbm, own_ref, other_ref, packed_ref, stats_ref, k_ref, v_ref,
+    q_ref, dest_ref, seg_ref, sems,
+):
+    copies = load(
+        ((dest_hbm, dest_ref), (seg_hbm, seg_ref), (q_hbm, q_ref), (k_hbm, k_ref), (v_hbm, v_ref)), sems
+    )
+    rows = q_ref.shape[0]
+    half = rows // 2
+    low, high = cut
+    me = place[0]
+    copies[0].wait()
+    copies[1].wait()
+    dest = dest_ref[...]
+    block = (dest >= rows).astype(jnp.int32)
+    slot = dest - block * rows - me * half + jnp.where(block == me, 0, half)
+    spread = (lax.broadcasted_iota(jnp.int32, (rows, rows), 0) == slot).astype(BF16)
+    marks = seg_ref[...].astype(F32)
+    moved_marks = lax.dot_general(
+        jnp.broadcast_to(marks, (8, rows)).astype(BF16), spread, (((1,), (1,)), ((), ())),
+        preferred_element_type=F32,
+    )[0:1]
+    copies[2].wait()
+    moved = jnp.dot(spread, q_ref[...], preferred_element_type=F32)
+    moved_short = moved.astype(BF16)
+    own_ref[...] = moved_short[:half]
+    other_ref[...] = moved_short[half:]
+    packed_ref[0:half, :] = moved_short[half:, low:high]
+    query_sums = row_sums(moved)
+    copies[3].wait()
+    packed_ref[half : half + rows, :] = k_ref[:, low:high]
+    key_sums = row_sums(k_ref[...].astype(F32))
+    stats_ref[...] = jnp.concatenate(
+        [query_sums, key_sums, moved_marks, marks, jnp.zeros((4, rows), F32)], axis=0
+    )
+    copies[4].wait()
+    packed_ref[half + rows :, :] = v_ref[:, low:high]
+
+
+def settle_kernel(near_ref, far_ref, *refs):
+    refs[-1][...] = near_ref[...] + far_ref[...]
+
+
+def pack_kernel(cut, other_ref, k_ref, v_ref, after_ref, out_ref):
+    low, high = cut
+    half, rows = other_ref.shape[0], k_ref.shape[0]
+    out_ref[0:half, :] = other_ref[:, low:high]
+    out_ref[half : half + rows, :] = k_ref[:, low:high]
+    out_ref[half + rows :, :] = v_ref[:, low:high]
+
+
+def attend_kernel(
+    cut, total_width, place, near_ref, far_ref, q_ref, k_ref, v_ref, qg_ref, kg_ref, remote_ref, after_ref, out_ref
+):
+    rows = k_ref.shape[0]
+    half = rows // 2
+    me = place[0]
+    near, far = near_ref[...], far_ref[...]
+    near_factors = lax.rsqrt(near[0:2] / total_width + 1e-06)
+    far_factors = lax.rsqrt(far[0:2] / total_width + 1e-06)
+    q_mark = jnp.concatenate([near[2:3, :half], far[2:3, half:]], axis=1)
+    k_mark = jnp.concatenate([near[3:4], far[3:4]], axis=1)
+    q_factor = column(jnp.concatenate([near_factors[0:1, :half], far_factors[0:1, half:]], axis=1))
+    k_factor = column(jnp.concatenate([near_factors[1:2], far_factors[1:2]], axis=1))
+    allowed = column(q_mark) == k_mark
+    scale = math.log2(math.e) / math.sqrt(HD)
+    first, last = cut
+    for low in range(first, last, HD):
+        here = slice(low - first, low - first + HD)
+        wide = slice(low, low + HD)
+        queries = jnp.concatenate([q_ref[:, wide], remote_ref[0:half, here]], axis=0)
+        keys = jnp.concatenate([k_ref[:, wide], remote_ref[half : half + rows, here]], axis=0)
+        values = jnp.concatenate([v_ref[:, wide], remote_ref[half + rows :, here]], axis=0)
+        queries = (queries.astype(F32) * q_factor * qg_ref[0:1, wide]).astype(BF16)
+        keys = (keys.astype(F32) * k_factor * kg_ref[0:1, wide]).astype(BF16)
+        for part in range(2):
+            piece = slice(part * half, (part + 1) * half)
+            scores = lax.dot_general(
+                queries[piece], keys, (((1,), (1,)), ((), ())), preferred_element_type=F32
+            )
+            scores = jnp.where(allowed[piece], scores, -1e30)
+            largest = jnp.max(scores, axis=1, keepdims=True)
+            weights = jnp.exp2((scores - largest) * scale)
+            totals = jnp.sum(weights, axis=1, keepdims=True)
+            mixed = jnp.dot(weights.astype(BF16), values, preferred_element_type=F32)
+            start = me * half if part == 0 else (1 - me) * half
+            at = pl.ds(pl.multiple_of(start, half), half)
+            out_ref[at, here] = (mixed / totals).astype(BF16)
+
+
+def cut_kernel(place, weight_ref, *refs):
+    outs, sems = refs[:3], refs[3]
+    rows, width = outs[0].shape
+    first = pl.multiple_of(place[2] * rows, rows)
+    pairs = []
+    for step in range(1, 4):
+        start = pl.multiple_of((place[1] ^ step) * width, width)
+        pairs.append((weight_ref.at[pl.ds(first, rows), pl.ds(start, width)], outs[step - 1]))
+    for copy in load(pairs, sems):
+        copy.wait()
+
+
+def join_kernel(one_ref, two_ref, three_ref, after_ref, out_ref):
+    share = one_ref.shape[0]
+    for step, ref in enumerate((one_ref, two_ref, three_ref)):
+        out_ref[step * share : (step + 1) * share, :] = ref[...]
+
+
+def project_kernel(chunks, place, times, near_ref, far_ref, gate_ref, weight_ref, *refs):
+    parts, shares = refs[: 4 * chunks], refs[4 * chunks : 4 * chunks + 8]
+    out_hbm, rows_all, w_all, gates_ref, total, out_ref, sems = refs[4 * chunks + 8 :]
+    rows, width = out_ref.shape
+    half = rows // 2
+    group = w_all.shape[0] // 4
+    share = group // 8
+    me, head, mine = place[0], place[1], place[2]
+    own_start = pl.multiple_of(head * width, width)
+    own_copy = pltpu.make_async_copy(
+        weight_ref.at[:, pl.ds(own_start, width)], w_all.at[pl.ds(0, group), :], sems.at[0]
+    )
+    own_copy.start()
+    low = 0
+    for slot in range(4):
+        for chunk in range(chunks):
+            part = parts[4 * chunk + slot]
+            rows_all[:, low : low + part.shape[1]] = part[...]
+            low += part.shape[1]
+    for step in range(3):
+        for index in range(8):
+            start = pl.multiple_of((1 + step) * group + (mine ^ index) * share, share)
+            w_all[pl.ds(start, share), :] = shares[index][step * share : (step + 1) * share, :]
+    gates_ref[...] = jnp.zeros(gates_ref.shape, BF16)
+    for video in range(times.shape[0]):
+        for index, piece in enumerate(three_pieces(gate_ref[pl.ds(times[video], 1), :])):
+            gates_ref[index * 16 + video : index * 16 + video + 1, :] = piece.astype(BF16)
+    videos = lax.rem(lax.broadcasted_iota(jnp.int32, (rows, gates_ref.shape[0]), 1), 16).astype(F32)
+    own_mark, other_mark = near_ref[2:3, :half], far_ref[2:3, half:]
+    marks = jnp.concatenate(
+        [jnp.where(me == 0, own_mark, other_mark), jnp.where(me == 0, other_mark, own_mark)], axis=1
+    )
+    picked = (column(marks) == 4.0 * videos).astype(BF16)
+    own_copy.wait()
+    middle = 2 * group
+    blocks = [slice(low, low + 256) for low in range(0, width, 256)]
+    for block in blocks:
+        total[:, block] = jnp.dot(rows_all[:, 0:middle], w_all[0:middle, block], preferred_element_type=F32)
+    out_copies = []
+    for index, block in enumerate(blocks):
+        gates = jnp.dot(picked, gates_ref[:, block], preferred_element_type=F32)
+        mixed = total[:, block] + jnp.dot(
+            rows_all[:, middle:], w_all[middle:, block], preferred_element_type=F32
+        )
+        out_ref[:, block] = (mixed * gates).astype(BF16)
+        out_copies.append(
+            pltpu.make_async_copy(out_ref.at[:, block], out_hbm.at[:, block], sems.at[1 + index])
+        )
+        out_copies[-1].start()
+    for copy in out_copies:
+        copy.wait()
+
+
+def fast_local(
+    query_raw, key_raw, value_rows, query_gain, key_gain, segment, destination, timestep, out_weight, gate_table
+):
+    rows, width = query_raw.shape
+    half = rows // 2
+    out_width = gate_table.shape[1]
+    total_width = width * lax.axis_size("head")
+    ctx, head, batch = lax.axis_index("ctx"), lax.axis_index("head"), lax.axis_index("batch")
+    mine = batch * 2 + ctx
+    place = jnp.stack([ctx, head, mine]).astype(jnp.int32)
+    cuts, low = [], 0
+    for count in SENDS:
+        cuts.append((low * HD, (low + count) * HD))
+        low += count
+    assert low * HD == width
+    share = width // 8
+    packed_shapes = [jax.ShapeDtypeStruct((half + 2 * rows, high - low), BF16) for low, high in cuts]
+    in_hbm = functools.partial(pltpu.with_memory_space_constraint, memory_space=pltpu.HBM)
+    weight_hbm = in_hbm(out_weight)
+
+    cut_weights = pl.pallas_call(
+        cut_kernel,
+        in_specs=[SMEM, HBM],
+        out_specs=[VMEM] * 3,
+        out_shape=[jax.ShapeDtypeStruct((share, out_width), BF16)] * 3,
+        scratch_shapes=[pltpu.SemaphoreType.DMA((3,))],
+        compiler_params=params(4),
+        cost_estimate=cost(1),
+        name="cut_weights",
+    )(place, weight_hbm)
+    from_head = [lax.ppermute(cut_weights[s - 1], "head", xor_pairs(4, s)) for s in (1, 2, 3)]
+
+    own_queries, other_queries, packed, stats, keys, values = pl.pallas_call(
+        functools.partial(prepare_kernel, cuts[0]),
+        in_specs=[SMEM] + [HBM] * 5,
+        out_specs=[VMEM] * 6,
+        out_shape=[
+            jax.ShapeDtypeStruct((half, width), BF16),
+            jax.ShapeDtypeStruct((half, width), BF16),
+            packed_shapes[0],
+            jax.ShapeDtypeStruct((8, rows), F32),
+            jax.ShapeDtypeStruct((rows, width), BF16),
+            jax.ShapeDtypeStruct((rows, width), BF16),
+        ],
+        scratch_shapes=[
+            pltpu.VMEM((rows, width), BF16),
+            pltpu.VMEM((1, rows), jnp.int32),
+            pltpu.VMEM((1, rows), jnp.int32),
+            pltpu.SemaphoreType.DMA((5,)),
+        ],
+        compiler_params=params(14),
+        cost_estimate=cost(2),
+        name="prepare",
+    )(
+        place, in_hbm(query_raw), in_hbm(key_raw), in_hbm(value_rows),
+        in_hbm(destination.reshape(1, rows)), in_hbm(segment.reshape(1, rows)),
+    )
+    arrived = [lax.ppermute(packed, "ctx", SWAP_CTX)]
+    stats = stats + lax.ppermute(stats, "head", xor_pairs(4, 1))
+    near = pl.pallas_call(
+        settle_kernel,
+        in_specs=[VMEM] * 2 + [AFTER] * 4,
+        out_specs=VMEM,
+        out_shape=jax.ShapeDtypeStruct((8, rows), F32),
+        compiler_params=params(4),
+        cost_estimate=cost(1),
+        name="settle",
+    )(stats, lax.ppermute(stats, "head", xor_pairs(4, 2)), arrived[0], *from_head)
+    far = lax.ppermute(near, "ctx", SWAP_CTX)
+    packed = pl.pallas_call(
+        functools.partial(pack_kernel, cuts[1]),
+        in_specs=[VMEM] * 3 + [AFTER],
+        out_specs=VMEM,
+        out_shape=packed_shapes[1],
+        compiler_params=params(4),
+        cost_estimate=cost(1),
+        name="pack",
+    )(other_queries, keys, values, far)
+    arrived.append(lax.ppermute(packed, "ctx", SWAP_CTX))
+
+    parts = []
+    before = near
+    for cut, piece in zip(cuts, arrived):
+        attended = pl.pallas_call(
+            functools.partial(attend_kernel, cut, total_width),
+            in_specs=[SMEM] + [VMEM] * 8 + [AFTER],
+            out_specs=VMEM,
+            out_shape=jax.ShapeDtypeStruct((rows, cut[1] - cut[0]), BF16),
+            compiler_params=params(14),
+            cost_estimate=cost(8),
+            name="attend",
+        )(
+            place, near, far, own_queries, keys, values, query_gain.reshape(1, width),
+            key_gain.reshape(1, width), piece, before,
+        )
+        one = lax.ppermute(attended, "head", xor_pairs(4, 1))
+        two = lax.ppermute(attended, "head", xor_pairs(4, 2))
+        three = lax.ppermute(two, "head", xor_pairs(4, 1))
+        parts += [attended, one, two, three]
+        before = attended
+
+    share0 = pl.pallas_call(
+        join_kernel,
+        in_specs=[VMEM] * 3 + [AFTER],
+        out_specs=VMEM,
+        out_shape=jax.ShapeDtypeStruct((3 * share, out_width), BF16),
+        compiler_params=params(4),
+        cost_estimate=cost(1),
+        name="join",
+    )(*from_head, parts[0])
+    share_y = lax.ppermute(share0, "ctx", SWAP_CTX)
+    share_x = lax.ppermute(share0, "batch", SWAP_X)
+    share_xy = lax.ppermute(share_y, "batch", SWAP_X)
+    shares = [None] * 8
+    for index, value in ((0, share0), (1, share_y), (4, share_x), (5, share_xy)):
+        shares[index] = value
+        shares[index ^ 2] = lax.ppermute(value, "batch", SWAP_CORE)
+
+    return pl.pallas_call(
+        functools.partial(project_kernel, 2),
+        in_specs=[SMEM, SMEM] + [VMEM] * 3 + [HBM] + [VMEM] * (len(parts) + 8),
+        out_specs=ANY,
+        out_shape=jax.ShapeDtypeStruct((rows, out_width), BF16),
+        scratch_shapes=[
+            pltpu.VMEM((rows, 4 * width), BF16),
+            pltpu.VMEM((4 * width, out_width), BF16),
+            pltpu.VMEM((48, out_width), BF16),
+            pltpu.VMEM((rows, out_width), F32),
+            pltpu.VMEM((rows, out_width), BF16),
+            pltpu.SemaphoreType.DMA((1 + out_width // 256,)),
+        ],
+        compiler_params=params(28),
+        cost_estimate=cost(8),
+        name="project",
+    )(place, timestep, near, far, gate_table, weight_hbm, *parts, *shares)
 
 
 def for_sending(array):
@@ -72,7 +425,7 @@
     return running
 
 
-def local(
+def general_local(
     query_raw,
     key_raw,
     value_rows,
@@ -163,6 +516,9 @@
         P("head", None),
         P(None, "head"),
     )
+    sizes = dict(mesh.shape)
+    fast = sizes["batch"] == 4 and sizes["ctx"] == 2 and sizes["head"] == 4
+    local = fast_local if fast else general_local
     return jax.shard_map(
         local, mesh=mesh, in_specs=placed, out_specs=P(("batch", "ctx"), "head"), check_vma=False
     )

time: 231 us -> 104 us (0.45)
  blocking collectives: 57.2 us -> 0 us
  matrix products: 33 us -> 0 us
  waiting for transfers between devices: 94.2 us -> 62 us
  Pallas kernels: 0 us -> 18.9 us
  starting transfers between devices: 6.86 us -> 22.8 us
  other arithmetic: 13.7 us -> 0.08 us
  between operations: 13.3 us -> 0.13 us
  local copies, waits for them, and re-layouts: 12.3 us -> 0.03 us
    reduce_scatter x1 -> x0, waiting for transfers between devices: 90.4 us -> none  [local(): lax.psum_scatter(head_terms.astype(jnp.bfloat16), 'head', scatter_dimensi...]
    ppermute x0 -> x21, waiting for transfers between devices: none -> 62 us  [the longest x2 15.7 us: fast_local(): one = lax.ppermute(attended, 'head', xor_pairs(4, 1))]
    dot_general x7 -> x0, matrix products: 33 us -> none  [the longest x2 11.2 us: attend(): jnp.einsum('hqk,khd->qhd', weights.astype(jnp.bfloat16), value_heads, pre...]
    all_to_all x2 -> x0, blocking collectives: 29.5 us -> none  [the longest x1 18.7 us: local(): lax.all_to_all(placed(value_rows), 'ctx', split_axis=0, concat_axis=0, ti...]
    ppermute x0 -> x21, starting transfers between devices: none -> 22.8 us  [the longest x3 4.45 us: fast_local(): lax.ppermute(cut_weights[s - 1], 'head', xor_pairs(4, s))]
    pallas_call x0 -> x8, Pallas kernels: none -> 18.9 us  [the longest x2 7.68 us: fast_local(): pl.pallas_call(functools.partial(attend_kernel, cut, total_width), in_spe...]
    all_gather x1 -> x0, blocking collectives: 14.3 us -> none  [local(): lax.all_gather(for_sending(own_segment), 'ctx', axis=0, tiled=True)]
    psum x1 -> x0, blocking collectives: 13.5 us -> none  [local(): lax.psum((jnp.sum(query_float * query_float, axis=1), jnp.sum(key_float *...]
  transfers between devices with their start and end apart: 5 -> 21, of which waited for: 3 -> 9; matrix products, arithmetic and copies ran while one was open for 5% -> 0% of each run, Pallas kernels for 0% -> 5%
where the time goes in v2:
time: 104 us
  waiting for transfers between devices  62 us (60%)
  starting transfers between devices  22.8 us (22%)
  Pallas kernels  18.9 us (18%)
    ppermute x2, waiting for transfers between devices, fast_local(): one = lax.ppermute(attended, 'head', xor_pairs(4, 1))  15.7 us
    ppermute x1, waiting for transfers between devices, fast_local(): share_y = lax.ppermute(share0, 'ctx', SWAP_CTX)  11.8 us
    ppermute x2, waiting for transfers between devices, fast_local(): three = lax.ppermute(two, 'head', xor_pairs(4, 1))  11.4 us
    ppermute x1, waiting for transfers between devices, fast_local(): stats = stats + lax.ppermute(stats, 'head', xor_pairs(4, 1))  9.74 us
    pallas_call x2, Pallas kernels, fast_local(): pl.pallas_call(functools.partial(attend_kernel, cut, total_width), in_spe...  7.68 us
    pallas_call x1, Pallas kernels, fast_local(): pl.pallas_call(functools.partial(project_kernel, 2), in_specs=[SMEM, SMEM...  6.81 us
    ppermute x2, waiting for transfers between devices, fast_local(): two = lax.ppermute(attended, 'head', xor_pairs(4, 2))  5.7 us
    ppermute x3, starting transfers between devices, fast_local(): lax.ppermute(cut_weights[s - 1], 'head', xor_pairs(4, s))  4.45 us
  transfers between devices with their start and end apart: 21, of which 9 were waited for; matrix products, arithmetic and copies ran while one was open for 0% of the time, Pallas kernels for 5%

profile of v2, /device:TPU:0, one launch (start us, length us, event | category | flops | bytes accessed | tf_op | source)
XLA Modules:
  0.0 103.9 jit_solution(14257374444393650426)
XLA Ops:
  0.0 0.0 copy-start.2
  0.0 0.0 copy-start.3
  0.0 0.1 pad_add_fusion.place
  0.1 2.6 %prepare.1 = (bf16[256,640]{1,0:T(8,128)(2,1)S(1)}, bf16[256,640]{1,0:T(8,128)(2,1)S(1)}, bf16[1280,384]{1,0:T(8,128)(2,1)S(1)}, f32[8,512]{1,0:T(8,128)S(1)}, b...) custom-call(s32[3]{0:T(128)S(1)} %pad_add_fusion.place, bf16[512,640]{1,0:T(8,128)(2,1)} %q_hbm.1, ...), custom_call_target="tpu_custom_call" | custom-call | bytes 7200000 | tf_op jit(solution)/shard_map/prepare/pallas_call | solution.py:259
  2.7 3.0 %collective-permute-start.2 = (bf16[1280,384]{1,0:T(8,128)(2,1)S(1)}, bf16[1280,384]{1,0:T(8,128)(2,1)S(1)}, u32[]{:S(2)}, u32[]{:S(2)}) collective-permute-start(bf16[1280,384]{1,0:T(8,128)(2,1)S(1)} %get-tuple-element.15), channel_id=1, source_target_pairs={{0,4},{4,0},{1,5},{5,1},{2,6},{6,2},{3,7},{7,3},{8,12},{12,8},{9,1... | collective-permute-start | bytes 2949128 | tf_op jit(solution)/shard_map/ppermute | solution.py:284
  5.7 1.7 %cut_weights.1 = (bf16[80,1280]{1,0:T(8,128)(2,1)S(1)}, bf16[80,1280]{1,0:T(8,128)(2,1)S(1)}, bf16[80,1280]{1,0:T(8,128)(2,1)S(1)}) custom-call(s32[3]{0:T(128)S(1)} %pad_add_fusion.place, bf16[640,5120]{1,0:T(8,128)(2,1)} %weight_ref.3), custom_call_target="tpu_custom_call" | custom-call | bytes 3600000 | tf_op jit(solution)/shard_map/cut_weights/pallas_call | solution.py:247
  7.4 0.0 copy-start
  7.5 0.0 copy-start.1
  7.5 1.6 %collective-permute-start.3 = (bf16[80,1280]{1,0:T(8,128)(2,1)S(1)}, bf16[80,1280]{1,0:T(8,128)(2,1)S(1)}, u32[]{:S(2)}, u32[]{:S(2)}) collective-permute-start(bf16[80,1280]{1,0:T(8,128)(2,1)S(1)} %get-tuple-element.16), channel_id=1, source_target_pairs={{0,1},{1,0},{2,3},{3,2},{4,5},{5,4},{6,7},{7,6},{8,9},{9,8},{10,11... | collective-permute-start | bytes 614408 | tf_op jit(solution)/shard_map/ppermute | solution.py:257
  9.1 2.6 %collective-permute-start.4 = (bf16[80,1280]{1,0:T(8,128)(2,1)S(1)}, bf16[80,1280]{1,0:T(8,128)(2,1)S(1)}, u32[]{:S(2)}, u32[]{:S(2)}) collective-permute-start(bf16[80,1280]{1,0:T(8,128)(2,1)S(1)} %get-tuple-element.17), channel_id=1, source_target_pairs={{0,2},{1,3},{2,0},{3,1},{4,6},{5,7},{6,4},{7,5},{8,10},{9,11},{10,... | collective-permute-start | bytes 614408 | tf_op jit(solution)/shard_map/ppermute | solution.py:257
  11.7 0.2 collective-permute-start.5
  11.9 0.7 collective-permute-start
  12.6 9.7 %collective-permute-done = f32[8,512]{1,0:T(8,128)S(1)} collective-permute-done((f32[8,512]{1,0:T(8,128)S(1)}, f32[8,512]{1,0:T(8,128)S(1)}, u32[]{:S(2)}, u32[]{:S(2)}) %collective-permute-start) | collective-permute-done | bytes 16416 | tf_op jit(solution)/shard_map/ppermute | solution.py:285
  22.3 3.5 %collective-permute-start.1 = (f32[8,512]{1,0:T(8,128)S(1)}, f32[8,512]{1,0:T(8,128)S(1)}, u32[]{:S(2)}, u32[]{:S(2)}) collective-permute-start(f32[8,512]{1,0:T(8,128)S(1)} %add.7.near_ref), channel_id=1, source_target_pairs={{0,2},{1,3},{2,0},{3,1},{4,6},{5,7},{6,4},{7,5},{8,10},{9,11},{10,... | collective-permute-start | bytes 49160 | tf_op jit(solution)/shard_map/ppermute | solution.py:294
  25.8 4.3 %collective-permute-done.1.far_ref = f32[8,512]{1,0:T(8,128)S(1)} collective-permute-done((f32[8,512]{1,0:T(8,128)S(1)}, f32[8,512]{1,0:T(8,128)S(1)}, u32[]{:S(2)}, u32[]{:S(2)}) %collective-permute-start.1) | collective-permute-done | bytes 16416 | tf_op jit(solution)/shard_map/ppermute | solution.py:294
  30.2 0.0 collective-permute-done.3.refs_1_.one_ref
  30.2 0.0 collective-permute-done.4.refs_2_.two_ref
  30.2 0.0 collective-permute-done.5.refs_3_.three_ref
  30.2 0.0 collective-permute-done.2.refs_0_.remote_ref
  30.2 0.6 collective-permute-start.6
  30.8 0.0 copy-done.2
  30.8 0.0 copy-done.3
  30.8 3.2 %collective-permute-done.6.far_ref.after_ref = f32[8,512]{1,0:T(8,128)S(1)} collective-permute-done((f32[8,512]{1,0:T(8,128)S(1)}, f32[8,512]{1,0:T(8,128)S(1)}, u32[]{:S(2)}, u32[]{:S(2)}) %collective-permute-start.6) | collective-permute-done | bytes 16416 | tf_op jit(solution)/shard_map/ppermute | solution.py:295
  34.0 4.3 %attend.2.after_ref.refs_0_ = bf16[512,384]{1,0:T(8,128)(2,1)S(1)} custom-call(s32[3]{0:T(128)S(1)} %pad_add_fusion.place, f32[8,512]{1,0:T(8,128)S(1)} %settle.1.near_ref.after_ref, f32[8,512]{1,0:T(8,128)S(1)} %collective-permute-done.6.far_ref.after_ref, bf16[256,640]{1,0:T(8,128)(2,1)S(1)} %get-tuple-element.19.q_ref, ...), custom_call_target="tpu_custom_call" | custom-call | bytes 28800000 | tf_op jit(solution)/shard_map/attend/pallas_call | solution.py:310
  38.4 0.6 collective-permute-start.14
  39.0 1.4 %collective-permute-start.8 = (bf16[512,384]{1,0:T(8,128)(2,1)S(1)}, bf16[512,384]{1,0:T(8,128)(2,1)S(1)}, u32[]{:S(2)}, u32[]{:S(2)}) collective-permute-start(bf16[512,384]{1,0:T(8,128)(2,1)S(1)} %attend.2.after_ref.refs_0_), channel_id=1, source_target_pairs={{0,2},{1,3},{2,0},{3,1},{4,6},{5,7},{6,4},{7,5},{8,10},{9,11},{10,... | collective-permute-start | bytes 1179656 | tf_op jit(solution)/shard_map/ppermute | solution.py:323
  40.4 1.6 %collective-permute-start.10 = (bf16[1280,256]{1,0:T(8,128)(2,1)S(1)}, bf16[1280,256]{1,0:T(8,128)(2,1)S(1)}, u32[]{:S(2)}, u32[]{:S(2)}) collective-permute-start(bf16[1280,256]{1,0:T(8,128)(2,1)S(1)} %pack.1), channel_id=1, source_target_pairs={{0,4},{4,0},{1,5},{5,1},{2,6},{6,2},{3,7},{7,3},{8,12},{12,8},{9,1... | collective-permute-start | bytes 1966088 | tf_op jit(solution)/shard_map/ppermute | solution.py:305
  42.0 1.5 %collective-permute-start.17 = (bf16[240,1280]{1,0:T(8,128)(2,1)S(1)}, bf16[240,1280]{1,0:T(8,128)(2,1)S(1)}, u32[]{:S(2)}, u32[]{:S(2)}) collective-permute-start(bf16[240,1280]{1,0:T(8,128)(2,1)S(1)} %join.1.refs_8_), channel_id=1, source_target_pairs={{0,16},{16,0},{8,24},{24,8},{1,17},{17,1},{9,25},{25,9},{2,18},{18... | collective-permute-start | bytes 1843208 | tf_op jit(solution)/shard_map/ppermute | solution.py:338
  43.5 11.8 %collective-permute-done.14.refs_9_ = bf16[240,1280]{1,0:T(8,128)(2,1)S(1)} collective-permute-done((bf16[240,1280]{1,0:T(8,128)(2,1)S(1)}, bf16[240,1280]{1,0:T(8,128)(2,1)S(1)}, u32[]{:S(2)}, u32[]{:S(2)}) %collective-permute-start.14) | collective-permute-done | bytes 614432 | tf_op jit(solution)/shard_map/ppermute | solution.py:337
  55.3 1.5 %collective-permute-start.18 = (bf16[240,1280]{1,0:T(8,128)(2,1)S(1)}, bf16[240,1280]{1,0:T(8,128)(2,1)S(1)}, u32[]{:S(2)}, u32[]{:S(2)}) collective-permute-start(bf16[240,1280]{1,0:T(8,128)(2,1)S(1)} %collective-permute-done.14.refs_9_), channel_id=1, source_target_pairs={{0,16},{16,0},{8,24},{24,8},{1,17},{17,1},{9,25},{25,9},{2,18},{18... | collective-permute-start | bytes 1843208 | tf_op jit(solution)/shard_map/ppermute | solution.py:339
  56.8 0.0 collective-permute-start.15
  56.8 0.0 collective-permute-done.8.refs_2_
  56.8 0.4 collective-permute-start.7
  57.1 11.2 %collective-permute-done.7.refs_1_ = bf16[512,384]{1,0:T(8,128)(2,1)S(1)} collective-permute-done((bf16[512,384]{1,0:T(8,128)(2,1)S(1)}, bf16[512,384]{1,0:T(8,128)(2,1)S(1)}, u32[]{:S(2)}, u32[]{:S(2)}) %collective-permute-start.7) | collective-permute-done | bytes 393248 | tf_op jit(solution)/shard_map/ppermute | solution.py:322
  68.3 0.4 collective-permute-start.9
  68.7 0.0 collective-permute-done.17.refs_12_
  68.7 0.0 collective-permute-start.16
  68.7 0.0 collective-permute-done.10.remote_ref
  68.7 0.5 collective-permute-start.19
  69.2 0.0 collective-permute-done.18.refs_13_
  69.2 0.1 collective-permute-start.20
  69.3 3.3 %attend.3.refs_4_ = bf16[512,256]{1,0:T(8,128)(2,1)S(1)} custom-call(s32[3]{0:T(128)S(1)} %pad_add_fusion.place, f32[8,512]{1,0:T(8,128)S(1)} %settle.1.near_ref.after_ref, f32[8,512]{1,0:T(8,128)S(1)} %collective-permute-done.6.far_ref.after_ref, bf16[256,640]{1,0:T(8,128)(2,1)S(1)} %get-tuple-element.19.q_ref, ...), custom_call_target="tpu_custom_call" | custom-call | bytes 28800000 | tf_op jit(solution)/shard_map/attend/pallas_call | solution.py:310
  72.6 0.0 collective-permute-done.15.refs_10_
  72.6 2.7 %collective-permute-start.12 = (bf16[512,256]{1,0:T(8,128)(2,1)S(1)}, bf16[512,256]{1,0:T(8,128)(2,1)S(1)}, u32[]{:S(2)}, u32[]{:S(2)}) collective-permute-start(bf16[512,256]{1,0:T(8,128)(2,1)S(1)} %attend.3.refs_4_), channel_id=1, source_target_pairs={{0,2},{1,3},{2,0},{3,1},{4,6},{5,7},{6,4},{7,5},{8,10},{9,11},{10,... | collective-permute-start | bytes 786440 | tf_op jit(solution)/shard_map/ppermute | solution.py:323
  75.3 7.0 %collective-permute-done.9.refs_3_ = bf16[512,384]{1,0:T(8,128)(2,1)S(1)} collective-permute-done((bf16[512,384]{1,0:T(8,128)(2,1)S(1)}, bf16[512,384]{1,0:T(8,128)(2,1)S(1)}, u32[]{:S(2)}, u32[]{:S(2)}) %collective-permute-start.9) | collective-permute-done | bytes 393248 | tf_op jit(solution)/shard_map/ppermute | solution.py:324
  82.3 0.0 collective-permute-start.11
  82.3 5.7 %collective-permute-done.12.refs_6_ = bf16[512,256]{1,0:T(8,128)(2,1)S(1)} collective-permute-done((bf16[512,256]{1,0:T(8,128)(2,1)S(1)}, bf16[512,256]{1,0:T(8,128)(2,1)S(1)}, u32[]{:S(2)}, u32[]{:S(2)}) %collective-permute-start.12) | collective-permute-done | bytes 262176 | tf_op jit(solution)/shard_map/ppermute | solution.py:323
  88.0 0.0 collective-permute-start.13
  88.0 4.5 %collective-permute-done.11.refs_5_ = bf16[512,256]{1,0:T(8,128)(2,1)S(1)} collective-permute-done((bf16[512,256]{1,0:T(8,128)(2,1)S(1)}, bf16[512,256]{1,0:T(8,128)(2,1)S(1)}, u32[]{:S(2)}, u32[]{:S(2)}) %collective-permute-start.11) | collective-permute-done | bytes 262176 | tf_op jit(solution)/shard_map/ppermute | solution.py:322
  92.6 4.5 %collective-permute-done.13.refs_7_ = bf16[512,256]{1,0:T(8,128)(2,1)S(1)} collective-permute-done((bf16[512,256]{1,0:T(8,128)(2,1)S(1)}, bf16[512,256]{1,0:T(8,128)(2,1)S(1)}, u32[]{:S(2)}, u32[]{:S(2)}) %collective-permute-start.13) | collective-permute-done | bytes 262176 | tf_op jit(solution)/shard_map/ppermute | solution.py:324
  97.0 0.0 collective-permute-done.16.refs_11_
  97.0 0.0 collective-permute-done.19.refs_14_
  97.0 0.0 collective-permute-done.20.refs_15_
  97.1 0.0 copy-done
  97.1 0.0 copy-done.1
  97.1 6.8 %project.1 = bf16[512,1280]{1,0:T(8,128)(2,1)} custom-call(s32[3]{0:T(128)S(1)} %pad_add_fusion.place, s32[6]{0:T(128)S(1)} %copy-done.1, f32[8,512]{1,0:T(8,128)S(1)} %settle.1.near_ref.after_ref, f32[8,512]{1,0:T(8,128)S(1)} %collective-permute-done.6.far_ref.after_ref, f32[50,1280]{1,0:T(8,128)S(1)} %copy-done, bf16[640,5120]{1,0:T(8,128)(2,1)} %weight_ref.3, ...), custom_call_target="tpu_custom_call" | custom-call | bytes 28800000 | tf_op jit(solution)/shard_map/project/pallas_call | solution.py:345
  (6 shorter events, 0.1 us)
Async XLA Ops:
  0.0 30.8 %copy-start.2 = (f32[640]{0:T(1024)S(1)}, f32[640]{0:T(1024)}, u32[]{:S(2)}) copy-start(f32[640]{0:T(1024)} %param.13) | copy-start | bytes 7684
  0.0 30.8 %copy-start.3 = (f32[640]{0:T(1024)S(1)}, f32[640]{0:T(1024)}, u32[]{:S(2)}) copy-start(f32[640]{0:T(1024)} %param.14) | copy-start | bytes 7684
  2.7 27.5 %collective-permute-start.2 = (bf16[1280,384]{1,0:T(8,128)(2,1)S(1)}, bf16[1280,384]{1,0:T(8,128)(2,1)S(1)}, u32[]{:S(2)}, u32[]{:S(2)}) collective-permute-start(bf16[1280,384]{1,0:T(8,128)(2,1)S(1)} %get-tuple-element.15), channel_id=1, source_target_pairs={{0,4},{4,0},{1,5},{5,1},{2,6},{6,2},{3,7},{7,3},{8,12},{12,8},{9,1... | collective-permute-start | bytes 2949128 | tf_op jit(solution)/shard_map/ppermute | solution.py:284
  7.4 89.6 %copy-start = (f32[50,1280]{1,0:T(8,128)S(1)}, f32[50,1280]{1,0:T(8,128)}, u32[]{:S(2)}) copy-start(f32[50,1280]{1,0:T(8,128)} %gate_ref.1) | copy-start | bytes 768004
  7.5 89.6 %copy-start.1 = (s32[6]{0:T(128)S(1)}, s32[6]{0:T(128)}, u32[]{:S(2)}) copy-start(s32[6]{0:T(128)} %times.1) | copy-start | bytes 76
  7.5 22.7 %collective-permute-start.3 = (bf16[80,1280]{1,0:T(8,128)(2,1)S(1)}, bf16[80,1280]{1,0:T(8,128)(2,1)S(1)}, u32[]{:S(2)}, u32[]{:S(2)}) collective-permute-start(bf16[80,1280]{1,0:T(8,128)(2,1)S(1)} %get-tuple-element.16), channel_id=1, source_target_pairs={{0,1},{1,0},{2,3},{3,2},{4,5},{5,4},{6,7},{7,6},{8,9},{9,8},{10,11... | collective-permute-start | bytes 614408 | tf_op jit(solution)/shard_map/ppermute | solution.py:257
  9.1 21.1 %collective-permute-start.4 = (bf16[80,1280]{1,0:T(8,128)(2,1)S(1)}, bf16[80,1280]{1,0:T(8,128)(2,1)S(1)}, u32[]{:S(2)}, u32[]{:S(2)}) collective-permute-start(bf16[80,1280]{1,0:T(8,128)(2,1)S(1)} %get-tuple-element.17), channel_id=1, source_target_pairs={{0,2},{1,3},{2,0},{3,1},{4,6},{5,7},{6,4},{7,5},{8,10},{9,11},{10,... | collective-permute-start | bytes 614408 | tf_op jit(solution)/shard_map/ppermute | solution.py:257
  11.7 18.5 %collective-permute-start.5 = (bf16[80,1280]{1,0:T(8,128)(2,1)S(1)}, bf16[80,1280]{1,0:T(8,128)(2,1)S(1)}, u32[]{:S(2)}, u32[]{:S(2)}) collective-permute-start(bf16[80,1280]{1,0:T(8,128)(2,1)S(1)} %get-tuple-element.18), channel_id=1, source_target_pairs={{0,3},{1,2},{2,1},{3,0},{4,7},{5,6},{6,5},{7,4},{8,11},{9,10},{10,... | collective-permute-start | bytes 614408 | tf_op jit(solution)/shard_map/ppermute | solution.py:257
  11.9 10.4 %collective-permute-start = (f32[8,512]{1,0:T(8,128)S(1)}, f32[8,512]{1,0:T(8,128)S(1)}, u32[]{:S(2)}, u32[]{:S(2)}) collective-permute-start(f32[8,512]{1,0:T(8,128)S(1)} %get-tuple-element.14), channel_id=1, source_target_pairs={{0,1},{1,0},{2,3},{3,2},{4,5},{5,4},{6,7},{7,6},{8,9},{9,8},{10,11... | collective-permute-start | bytes 49160 | tf_op jit(solution)/shard_map/ppermute | solution.py:285
  22.3 7.8 %collective-permute-start.1 = (f32[8,512]{1,0:T(8,128)S(1)}, f32[8,512]{1,0:T(8,128)S(1)}, u32[]{:S(2)}, u32[]{:S(2)}) collective-permute-start(f32[8,512]{1,0:T(8,128)S(1)} %add.7.near_ref), channel_id=1, source_target_pairs={{0,2},{1,3},{2,0},{3,1},{4,6},{5,7},{6,4},{7,5},{8,10},{9,11},{10,... | collective-permute-start | bytes 49160 | tf_op jit(solution)/shard_map/ppermute | solution.py:294
  30.2 3.8 %collective-permute-start.6 = (f32[8,512]{1,0:T(8,128)S(1)}, f32[8,512]{1,0:T(8,128)S(1)}, u32[]{:S(2)}, u32[]{:S(2)}) collective-permute-start(f32[8,512]{1,0:T(8,128)S(1)} %settle.1.near_ref.after_ref), channel_id=1, source_target_pairs={{0,4},{4,0},{1,5},{5,1},{2,6},{6,2},{3,7},{7,3},{8,12},{12,8},{9,1... | collective-permute-start | bytes 49160 | tf_op jit(solution)/shard_map/ppermute | solution.py:295
  38.4 16.9 %collective-permute-start.14 = (bf16[240,1280]{1,0:T(8,128)(2,1)S(1)}, bf16[240,1280]{1,0:T(8,128)(2,1)S(1)}, u32[]{:S(2)}, u32[]{:S(2)}) collective-permute-start(bf16[240,1280]{1,0:T(8,128)(2,1)S(1)} %join.1.refs_8_), channel_id=1, source_target_pairs={{0,4},{4,0},{1,5},{5,1},{2,6},{6,2},{3,7},{7,3},{8,12},{12,8},{9,1... | collective-permute-start | bytes 1843208 | tf_op jit(solution)/shard_map/ppermute | solution.py:337
  39.0 17.8 %collective-permute-start.8 = (bf16[512,384]{1,0:T(8,128)(2,1)S(1)}, bf16[512,384]{1,0:T(8,128)(2,1)S(1)}, u32[]{:S(2)}, u32[]{:S(2)}) collective-permute-start(bf16[512,384]{1,0:T(8,128)(2,1)S(1)} %attend.2.after_ref.refs_0_), channel_id=1, source_target_pairs={{0,2},{1,3},{2,0},{3,1},{4,6},{5,7},{6,4},{7,5},{8,10},{9,11},{10,... | collective-permute-start | bytes 1179656 | tf_op jit(solution)/shard_map/ppermute | solution.py:323
  40.4 28.3 %collective-permute-start.10 = (bf16[1280,256]{1,0:T(8,128)(2,1)S(1)}, bf16[1280,256]{1,0:T(8,128)(2,1)S(1)}, u32[]{:S(2)}, u32[]{:S(2)}) collective-permute-start(bf16[1280,256]{1,0:T(8,128)(2,1)S(1)} %pack.1), channel_id=1, source_target_pairs={{0,4},{4,0},{1,5},{5,1},{2,6},{6,2},{3,7},{7,3},{8,12},{12,8},{9,1... | collective-permute-start | bytes 1966088 | tf_op jit(solution)/shard_map/ppermute | solution.py:305
  42.0 26.7 %collective-permute-start.17 = (bf16[240,1280]{1,0:T(8,128)(2,1)S(1)}, bf16[240,1280]{1,0:T(8,128)(2,1)S(1)}, u32[]{:S(2)}, u32[]{:S(2)}) collective-permute-start(bf16[240,1280]{1,0:T(8,128)(2,1)S(1)} %join.1.refs_8_), channel_id=1, source_target_pairs={{0,16},{16,0},{8,24},{24,8},{1,17},{17,1},{9,25},{25,9},{2,18},{18... | collective-permute-start | bytes 1843208 | tf_op jit(solution)/shard_map/ppermute | solution.py:338
  55.3 13.9 %collective-permute-start.18 = (bf16[240,1280]{1,0:T(8,128)(2,1)S(1)}, bf16[240,1280]{1,0:T(8,128)(2,1)S(1)}, u32[]{:S(2)}, u32[]{:S(2)}) collective-permute-start(bf16[240,1280]{1,0:T(8,128)(2,1)S(1)} %collective-permute-done.14.refs_9_), channel_id=1, source_target_pairs={{0,16},{16,0},{8,24},{24,8},{1,17},{17,1},{9,25},{25,9},{2,18},{18... | collective-permute-start | bytes 1843208 | tf_op jit(solution)/shard_map/ppermute | solution.py:339
  56.8 15.8 %collective-permute-start.15 = (bf16[240,1280]{1,0:T(8,128)(2,1)S(1)}, bf16[240,1280]{1,0:T(8,128)(2,1)S(1)}, u32[]{:S(2)}, u32[]{:S(2)}) collective-permute-start(bf16[240,1280]{1,0:T(8,128)(2,1)S(1)} %join.1.refs_8_), channel_id=1, source_target_pairs={{0,8},{8,0},{16,24},{24,16},{1,9},{9,1},{17,25},{25,17},{2,10},{10... | collective-permute-start | bytes 1843208 | tf_op jit(solution)/shard_map/ppermute | solution.py:343
  56.8 11.5 %collective-permute-start.7 = (bf16[512,384]{1,0:T(8,128)(2,1)S(1)}, bf16[512,384]{1,0:T(8,128)(2,1)S(1)}, u32[]{:S(2)}, u32[]{:S(2)}) collective-permute-start(bf16[512,384]{1,0:T(8,128)(2,1)S(1)} %attend.2.after_ref.refs_0_), channel_id=1, source_target_pairs={{0,1},{1,0},{2,3},{3,2},{4,5},{5,4},{6,7},{7,6},{8,9},{9,8},{10,11... | collective-permute-start | bytes 1179656 | tf_op jit(solution)/shard_map/ppermute | solution.py:322
  68.3 14.0 %collective-permute-start.9 = (bf16[512,384]{1,0:T(8,128)(2,1)S(1)}, bf16[512,384]{1,0:T(8,128)(2,1)S(1)}, u32[]{:S(2)}, u32[]{:S(2)}) collective-permute-start(bf16[512,384]{1,0:T(8,128)(2,1)S(1)} %collective-permute-done.8.refs_2_), channel_id=1, source_target_pairs={{0,1},{1,0},{2,3},{3,2},{4,5},{5,4},{6,7},{7,6},{8,9},{9,8},{10,11... | collective-permute-start | bytes 1179656 | tf_op jit(solution)/shard_map/ppermute | solution.py:324
  68.7 28.4 %collective-permute-start.16 = (bf16[240,1280]{1,0:T(8,128)(2,1)S(1)}, bf16[240,1280]{1,0:T(8,128)(2,1)S(1)}, u32[]{:S(2)}, u32[]{:S(2)}) collective-permute-start(bf16[240,1280]{1,0:T(8,128)(2,1)S(1)} %collective-permute-done.14.refs_9_), channel_id=1, source_target_pairs={{0,8},{8,0},{16,24},{24,16},{1,9},{9,1},{17,25},{25,17},{2,10},{10... | collective-permute-start | bytes 1843208 | tf_op jit(solution)/shard_map/ppermute | solution.py:343
  68.7 28.4 %collective-permute-start.19 = (bf16[240,1280]{1,0:T(8,128)(2,1)S(1)}, bf16[240,1280]{1,0:T(8,128)(2,1)S(1)}, u32[]{:S(2)}, u32[]{:S(2)}) collective-permute-start(bf16[240,1280]{1,0:T(8,128)(2,1)S(1)} %collective-permute-done.17.refs_12_), channel_id=1, source_target_pairs={{0,8},{8,0},{16,24},{24,16},{1,9},{9,1},{17,25},{25,17},{2,10},{10... | collective-permute-start | bytes 1843208 | tf_op jit(solution)/shard_map/ppermute | solution.py:343
  69.2 27.9 %collective-permute-start.20 = (bf16[240,1280]{1,0:T(8,128)(2,1)S(1)}, bf16[240,1280]{1,0:T(8,128)(2,1)S(1)}, u32[]{:S(2)}, u32[]{:S(2)}) collective-permute-start(bf16[240,1280]{1,0:T(8,128)(2,1)S(1)} %collective-permute-done.18.refs_13_), channel_id=1, source_target_pairs={{0,8},{8,0},{16,24},{24,16},{1,9},{9,1},{17,25},{25,17},{2,10},{10... | collective-permute-start | bytes 1843208 | tf_op jit(solution)/shard_map/ppermute | solution.py:343
  72.6 15.4 %collective-permute-start.12 = (bf16[512,256]{1,0:T(8,128)(2,1)S(1)}, bf16[512,256]{1,0:T(8,128)(2,1)S(1)}, u32[]{:S(2)}, u32[]{:S(2)}) collective-permute-start(bf16[512,256]{1,0:T(8,128)(2,1)S(1)} %attend.3.refs_4_), channel_id=1, source_target_pairs={{0,2},{1,3},{2,0},{3,1},{4,6},{5,7},{6,4},{7,5},{8,10},{9,11},{10,... | collective-permute-start | bytes 786440 | tf_op jit(solution)/shard_map/ppermute | solution.py:323
  82.3 10.3 %collective-permute-start.11 = (bf16[512,256]{1,0:T(8,128)(2,1)S(1)}, bf16[512,256]{1,0:T(8,128)(2,1)S(1)}, u32[]{:S(2)}, u32[]{:S(2)}) collective-permute-start(bf16[512,256]{1,0:T(8,128)(2,1)S(1)} %attend.3.refs_4_), channel_id=1, source_target_pairs={{0,1},{1,0},{2,3},{3,2},{4,5},{5,4},{6,7},{7,6},{8,9},{9,8},{10,11... | collective-permute-start | bytes 786440 | tf_op jit(solution)/shard_map/ppermute | solution.py:322
  88.0 9.0 %collective-permute-start.13 = (bf16[512,256]{1,0:T(8,128)(2,1)S(1)}, bf16[512,256]{1,0:T(8,128)(2,1)S(1)}, u32[]{:S(2)}, u32[]{:S(2)}) collective-permute-start(bf16[512,256]{1,0:T(8,128)(2,1)S(1)} %collective-permute-done.12.refs_6_), channel_id=1, source_target_pairs={{0,1},{1,0},{2,3},{3,2},{4,5},{5,4},{6,7},{7,6},{8,9},{9,8},{10,11... | collective-permute-start | bytes 786440 | tf_op jit(solution)/shard_map/ppermute | solution.py:324

commit v3 on v2

--- a/solution.py
+++ b/solution.py
@@ -64,12 +64,17 @@
 
 
 def prepare_kernel(
-    cut, place, q_hbm, k_hbm, v_hbm, dest_hbm, seg_hbm, own_ref, other_ref, packed_ref, stats_ref, k_ref, v_ref,
+    cut, place, q_hbm, k_hbm, v_hbm, dest_hbm, seg_hbm, weight_ref,
+    own_ref, other_ref, packed_ref, stats_ref, k_ref, v_ref, one_ref, two_ref, three_ref,
     q_ref, dest_ref, seg_ref, sems,
 ):
-    copies = load(
-        ((dest_hbm, dest_ref), (seg_hbm, seg_ref), (q_hbm, q_ref), (k_hbm, k_ref), (v_hbm, v_ref)), sems
-    )
+    pairs = [(dest_hbm, dest_ref), (seg_hbm, seg_ref), (q_hbm, q_ref), (k_hbm, k_ref), (v_hbm, v_ref)]
+    for step, (ref, index) in enumerate(((one_ref, place[3]), (two_ref, place[2]), (three_ref, place[2]))):
+        count, columns = ref.shape
+        first = pl.multiple_of(index * count, count)
+        start = pl.multiple_of((place[1] ^ (step + 1)) * columns, columns)
+        pairs.append((weight_ref.at[pl.ds(first, count), pl.ds(start, columns)], ref))
+    copies = load(pairs, sems)
     rows = q_ref.shape[0]
     half = rows // 2
     low, high = cut
@@ -100,6 +105,8 @@
     )
     copies[4].wait()
     packed_ref[half + rows :, :] = v_ref[:, low:high]
+    for copy in copies[5:]:
+        copy.wait()
 
 
 def settle_kernel(near_ref, far_ref, *refs):
@@ -115,8 +122,9 @@
 
 
 def attend_kernel(
-    cut, total_width, place, near_ref, far_ref, q_ref, k_ref, v_ref, qg_ref, kg_ref, remote_ref, after_ref, out_ref
+    cut, total_width, place, near_ref, far_ref, q_ref, k_ref, v_ref, qg_ref, kg_ref, remote_ref, *refs
 ):
+    out_ref = refs[-1]
     rows = k_ref.shape[0]
     half = rows // 2
     me = place[0]
@@ -153,74 +161,91 @@
             out_ref[at, here] = (mixed / totals).astype(BF16)
 
 
-def cut_kernel(place, weight_ref, *refs):
-    outs, sems = refs[:3], refs[3]
-    rows, width = outs[0].shape
-    first = pl.multiple_of(place[2] * rows, rows)
-    pairs = []
-    for step in range(1, 4):
-        start = pl.multiple_of((place[1] ^ step) * width, width)
-        pairs.append((weight_ref.at[pl.ds(first, rows), pl.ds(start, width)], outs[step - 1]))
-    for copy in load(pairs, sems):
-        copy.wait()
-
-
-def join_kernel(one_ref, two_ref, three_ref, after_ref, out_ref):
-    share = one_ref.shape[0]
-    for step, ref in enumerate((one_ref, two_ref, three_ref)):
-        out_ref[step * share : (step + 1) * share, :] = ref[...]
-
-
-def project_kernel(chunks, place, times, near_ref, far_ref, gate_ref, weight_ref, *refs):
-    parts, shares = refs[: 4 * chunks], refs[4 * chunks : 4 * chunks + 8]
-    out_hbm, rows_all, w_all, gates_ref, total, out_ref, sems = refs[4 * chunks + 8 :]
-    rows, width = out_ref.shape
-    half = rows // 2
-    group = w_all.shape[0] // 4
+def join_kernel(count, *refs):
+    low = 0
+    for ref in refs[:count]:
+        refs[-1][low : low + ref.shape[0], :] = ref[...]
+        low += ref.shape[0]
+
+
+def join(pieces, after, name):
+    return pl.pallas_call(
+        functools.partial(join_kernel, len(pieces)),
+        in_specs=[VMEM] * len(pieces) + [AFTER] * len(after),
+        out_specs=VMEM,
+        out_shape=jax.ShapeDtypeStruct((sum([piece.shape[0] for piece in pieces]), pieces[0].shape[1]), BF16),
+        compiler_params=params(4),
+        cost_estimate=cost(1),
+        name=name,
+    )(*pieces, *after)
+
+
+def project_kernel(place, times, gate_ref, weight_ref, *refs):
+    first, own_last, shares = refs[:4], refs[4], refs[5:13]
+    total, tail_ref, gates_ref, rows_all, w_all, sems = refs[13:]
+    width = total.shape[1]
+    group = w_all.shape[1]
     share = group // 8
-    me, head, mine = place[0], place[1], place[2]
+    early = first[0].shape[1]
+    head, mine = place[1], place[2]
     own_start = pl.multiple_of(head * width, width)
-    own_copy = pltpu.make_async_copy(
-        weight_ref.at[:, pl.ds(own_start, width)], w_all.at[pl.ds(0, group), :], sems.at[0]
-    )
+    own_copy = pltpu.make_async_copy(weight_ref.at[:, pl.ds(own_start, width)], w_all.at[0], sems.at[0])
     own_copy.start()
-    low = 0
     for slot in range(4):
-        for chunk in range(chunks):
-            part = parts[4 * chunk + slot]
-            rows_all[:, low : low + part.shape[1]] = part[...]
-            low += part.shape[1]
-    for step in range(3):
-        for index in range(8):
-            start = pl.multiple_of((1 + step) * group + (mine ^ index) * share, share)
-            w_all[pl.ds(start, share), :] = shares[index][step * share : (step + 1) * share, :]
+        rows_all[:, slot * early : (slot + 1) * early] = first[slot][...]
+    rows_all[:, 4 * early :] = own_last[...]
     gates_ref[...] = jnp.zeros(gates_ref.shape, BF16)
     for video in range(times.shape[0]):
         for index, piece in enumerate(three_pieces(gate_ref[pl.ds(times[video], 1), :])):
             gates_ref[index * 16 + video : index * 16 + video + 1, :] = piece.astype(BF16)
+    for core in range(2):
+        near, far, other, diagonal = shares[4 * core : 4 * core + 4]
+        pieces = [(near, 0, 0, 0), (far, 0, 0, 4)]
+        for step in (1, 2):
+            pieces += [
+                (near, (step + 1) * share, step, 0),
+                (far, (step + 1) * share, step, 4),
+                (other, (step - 1) * share, step, 1),
+                (diagonal, (step - 1) * share, step, 5),
+            ]
+        for ref, low, step, flip in pieces:
+            count = share if step else 2 * share
+            index = mine ^ (flip + 2 * core) if step else place[3] ^ (flip // 2 + core)
+            w_all[1 + step, pl.ds(pl.multiple_of(index * count, count), count), :] = ref[low : low + count, :]
+    for step in range(3):
+        tail_ref[step * (group - early) : (step + 1) * (group - early), :] = w_all[1 + step, early:group, :]
+    own_copy.wait()
+    for low in range(0, width, 256):
+        block = slice(low, low + 256)
+        mixed = jnp.dot(rows_all[:, 4 * early :], w_all[0, early:group, block], preferred_element_type=F32)
+        for slot in range(4):
+            mixed += jnp.dot(
+                rows_all[:, slot * early : (slot + 1) * early], w_all[slot, 0:early, block],
+                preferred_element_type=F32,
+            )
+        total[:, block] = mixed
+
+
+def finish_kernel(place, near_ref, far_ref, total, tail_ref, gates_ref, one, two, three, out_hbm, out_ref, sems):
+    rows, width = out_ref.shape
+    half = rows // 2
+    me = place[0]
     videos = lax.rem(lax.broadcasted_iota(jnp.int32, (rows, gates_ref.shape[0]), 1), 16).astype(F32)
     own_mark, other_mark = near_ref[2:3, :half], far_ref[2:3, half:]
     marks = jnp.concatenate(
         [jnp.where(me == 0, own_mark, other_mark), jnp.where(me == 0, other_mark, own_mark)], axis=1
     )
     picked = (column(marks) == 4.0 * videos).astype(BF16)
-    own_copy.wait()
-    middle = 2 * group
-    blocks = [slice(low, low + 256) for low in range(0, width, 256)]
-    for block in blocks:
-        total[:, block] = jnp.dot(rows_all[:, 0:middle], w_all[0:middle, block], preferred_element_type=F32)
-    out_copies = []
-    for index, block in enumerate(blocks):
+    late = jnp.concatenate([one[...], two[...], three[...]], axis=1)
+    copies = []
+    for index, low in enumerate(range(0, width, 256)):
+        block = slice(low, low + 256)
         gates = jnp.dot(picked, gates_ref[:, block], preferred_element_type=F32)
-        mixed = total[:, block] + jnp.dot(
-            rows_all[:, middle:], w_all[middle:, block], preferred_element_type=F32
-        )
+        mixed = total[:, block] + jnp.dot(late, tail_ref[:, block], preferred_element_type=F32)
         out_ref[:, block] = (mixed * gates).astype(BF16)
-        out_copies.append(
-            pltpu.make_async_copy(out_ref.at[:, block], out_hbm.at[:, block], sems.at[1 + index])
-        )
-        out_copies[-1].start()
-    for copy in out_copies:
+        copies.append(pltpu.make_async_copy(out_ref.at[:, block], out_hbm.at[:, block], sems.at[index]))
+        copies[-1].start()
+    for copy in copies:
         copy.wait()
 
 
@@ -233,7 +258,7 @@
     total_width = width * lax.axis_size("head")
     ctx, head, batch = lax.axis_index("ctx"), lax.axis_index("head"), lax.axis_index("batch")
     mine = batch * 2 + ctx
-    place = jnp.stack([ctx, head, mine]).astype(jnp.int32)
+    place = jnp.stack([ctx, head, mine, batch]).astype(jnp.int32)
     cuts, low = [], 0
     for count in SENDS:
         cuts.append((low * HD, (low + count) * HD))
@@ -244,22 +269,10 @@
     in_hbm = functools.partial(pltpu.with_memory_space_constraint, memory_space=pltpu.HBM)
     weight_hbm = in_hbm(out_weight)
 
-    cut_weights = pl.pallas_call(
-        cut_kernel,
-        in_specs=[SMEM, HBM],
-        out_specs=[VMEM] * 3,
-        out_shape=[jax.ShapeDtypeStruct((share, out_width), BF16)] * 3,
-        scratch_shapes=[pltpu.SemaphoreType.DMA((3,))],
-        compiler_params=params(4),
-        cost_estimate=cost(1),
-        name="cut_weights",
-    )(place, weight_hbm)
-    from_head = [lax.ppermute(cut_weights[s - 1], "head", xor_pairs(4, s)) for s in (1, 2, 3)]
-
-    own_queries, other_queries, packed, stats, keys, values = pl.pallas_call(
+    own_queries, other_queries, packed, stats, keys, values, *cut_weights = pl.pallas_call(
         functools.partial(prepare_kernel, cuts[0]),
-        in_specs=[SMEM] + [HBM] * 5,
-        out_specs=[VMEM] * 6,
+        in_specs=[SMEM] + [HBM] * 6,
+        out_specs=[VMEM] * 9,
         out_shape=[
             jax.ShapeDtypeStruct((half, width), BF16),
             jax.ShapeDtypeStruct((half, width), BF16),
@@ -267,20 +280,24 @@
             jax.ShapeDtypeStruct((8, rows), F32),
             jax.ShapeDtypeStruct((rows, width), BF16),
             jax.ShapeDtypeStruct((rows, width), BF16),
+            jax.ShapeDtypeStruct((2 * share, out_width), BF16),
+            jax.ShapeDtypeStruct((share, out_width), BF16),
+            jax.ShapeDtypeStruct((share, out_width), BF16),
         ],
         scratch_shapes=[
             pltpu.VMEM((rows, width), BF16),
             pltpu.VMEM((1, rows), jnp.int32),
             pltpu.VMEM((1, rows), jnp.int32),
-            pltpu.SemaphoreType.DMA((5,)),
+            pltpu.SemaphoreType.DMA((8,)),
         ],
-        compiler_params=params(14),
+        compiler_params=params(16),
         cost_estimate=cost(2),
         name="prepare",
     )(
         place, in_hbm(query_raw), in_hbm(key_raw), in_hbm(value_rows),
-        in_hbm(destination.reshape(1, rows)), in_hbm(segment.reshape(1, rows)),
-    )
+        in_hbm(destination.reshape(1, rows)), in_hbm(segment.reshape(1, rows)), weight_hbm,
+    )
+    from_head = [lax.ppermute(cut_weights[s - 1], "head", xor_pairs(4, s)) for s in (1, 2, 3)]
     arrived = [lax.ppermute(packed, "ctx", SWAP_CTX)]
     stats = stats + lax.ppermute(stats, "head", xor_pairs(4, 1))
     near = pl.pallas_call(
@@ -293,6 +310,33 @@
         name="settle",
     )(stats, lax.ppermute(stats, "head", xor_pairs(4, 2)), arrived[0], *from_head)
     far = lax.ppermute(near, "ctx", SWAP_CTX)
+
+    two_three = join(from_head[1:], [far], "join_two")
+    share0 = join(from_head, [two_three], "join_all")
+    share_y = lax.ppermute(two_three, "ctx", SWAP_CTX)
+    share_x = lax.ppermute(share0, "batch", SWAP_X)
+
+    def attend(cut, piece, after):
+        return pl.pallas_call(
+            functools.partial(attend_kernel, cut, total_width),
+            in_specs=[SMEM] + [VMEM] * 8 + [AFTER] * len(after),
+            out_specs=VMEM,
+            out_shape=jax.ShapeDtypeStruct((rows, cut[1] - cut[0]), BF16),
+            compiler_params=params(14),
+            cost_estimate=cost(8),
+            name="attend",
+        )(
+            place, near, far, own_queries, keys, values, query_gain.reshape(1, width),
+            key_gain.reshape(1, width), piece, *after,
+        )
+
+    def spread(attended):
+        one = lax.ppermute(attended, "head", xor_pairs(4, 1))
+        two = lax.ppermute(attended, "head", xor_pairs(4, 2))
+        three = lax.ppermute(two, "head", xor_pairs(4, 1))
+        return [attended, one, two, three]
+
+    first = spread(attend(cuts[0], arrived[0], [share0]))
     packed = pl.pallas_call(
         functools.partial(pack_kernel, cuts[1]),
         in_specs=[VMEM] * 3 + [AFTER],
@@ -301,64 +345,46 @@
         compiler_params=params(4),
         cost_estimate=cost(1),
         name="pack",
-    )(other_queries, keys, values, far)
+    )(other_queries, keys, values, first[0])
     arrived.append(lax.ppermute(packed, "ctx", SWAP_CTX))
-
-    parts = []
-    before = near
-    for cut, piece in zip(cuts, arrived):
-        attended = pl.pallas_call(
-            functools.partial(attend_kernel, cut, total_width),
-            in_specs=[SMEM] + [VMEM] * 8 + [AFTER],
-            out_specs=VMEM,
-            out_shape=jax.ShapeDtypeStruct((rows, cut[1] - cut[0]), BF16),
-            compiler_params=params(14),
-            cost_estimate=cost(8),
-            name="attend",
-        )(
-            place, near, far, own_queries, keys, values, query_gain.reshape(1, width),
-            key_gain.reshape(1, width), piece, before,
-        )
-        one = lax.ppermute(attended, "head", xor_pairs(4, 1))
-        two = lax.ppermute(attended, "head", xor_pairs(4, 2))
-        three = lax.ppermute(two, "head", xor_pairs(4, 1))
-        parts += [attended, one, two, three]
-        before = attended
-
-    share0 = pl.pallas_call(
-        join_kernel,
-        in_specs=[VMEM] * 3 + [AFTER],
-        out_specs=VMEM,
-        out_shape=jax.ShapeDtypeStruct((3 * share, out_width), BF16),
-        compiler_params=params(4),
-        cost_estimate=cost(1),
-        name="join",
-    )(*from_head, parts[0])
-    share_y = lax.ppermute(share0, "ctx", SWAP_CTX)
-    share_x = lax.ppermute(share0, "batch", SWAP_X)
+    share_y = join([share_y], first[1:3] + [packed], "hold")
     share_xy = lax.ppermute(share_y, "batch", SWAP_X)
-    shares = [None] * 8
-    for index, value in ((0, share0), (1, share_y), (4, share_x), (5, share_xy)):
-        shares[index] = value
-        shares[index ^ 2] = lax.ppermute(value, "batch", SWAP_CORE)
-
+    last = spread(attend(cuts[1], arrived[1], [share_y]))
+    shares = [share0, share_x, share_y, share_xy]
+    shares += [lax.ppermute(value, "batch", SWAP_CORE) for value in shares]
+
+    tail = width - cuts[0][1]
+    total, tail_weights, gates = pl.pallas_call(
+        project_kernel,
+        in_specs=[SMEM, SMEM, VMEM, HBM] + [VMEM] * 13,
+        out_specs=[VMEM] * 3,
+        out_shape=[
+            jax.ShapeDtypeStruct((rows, out_width), F32),
+            jax.ShapeDtypeStruct((3 * tail, out_width), BF16),
+            jax.ShapeDtypeStruct((48, out_width), BF16),
+        ],
+        scratch_shapes=[
+            pltpu.VMEM((rows, 3 * cuts[0][1] + width), BF16),
+            pltpu.VMEM((4, width, out_width), BF16),
+            pltpu.SemaphoreType.DMA((1,)),
+        ],
+        compiler_params=params(24),
+        cost_estimate=cost(0),
+        name="project",
+    )(place, timestep, gate_table, weight_hbm, *first, last[0], *shares)
     return pl.pallas_call(
-        functools.partial(project_kernel, 2),
-        in_specs=[SMEM, SMEM] + [VMEM] * 3 + [HBM] + [VMEM] * (len(parts) + 8),
+        finish_kernel,
+        in_specs=[SMEM] + [VMEM] * 8,
         out_specs=ANY,
         out_shape=jax.ShapeDtypeStruct((rows, out_width), BF16),
         scratch_shapes=[
-            pltpu.VMEM((rows, 4 * width), BF16),
-            pltpu.VMEM((4 * width, out_width), BF16),
-            pltpu.VMEM((48, out_width), BF16),
-            pltpu.VMEM((rows, out_width), F32),
             pltpu.VMEM((rows, out_width), BF16),
-            pltpu.SemaphoreType.DMA((1 + out_width // 256,)),
+            pltpu.SemaphoreType.DMA((out_width // 256,)),
         ],
-        compiler_params=params(28),
-        cost_estimate=cost(8),
-        name="project",
-    )(place, timestep, near, far, gate_table, weight_hbm, *parts, *shares)
+        compiler_params=params(14),
+        cost_estimate=cost(0),
+        name="finish",
+    )(place, near, far, total, tail_weights, gates, *last[1:])
 
 
 def for_sending(array):

time: 104 us -> 92.9 us (0.89)
  waiting for transfers between devices: 62 us -> 47.9 us
  starting transfers between devices: 22.8 us -> 25.6 us
    ppermute x11, waiting for transfers between devices: 44.7 us -> 27.7 us  [the longest x2 20.2 us: spread(): two = lax.ppermute(attended, 'head', xor_pairs(4, 2))]
    ppermute x11, starting transfers between devices: 5.98 us -> 10.7 us  [the longest x2 5.35 us: spread(): two = lax.ppermute(attended, 'head', xor_pairs(4, 2))]
    ppermute x1, waiting for transfers between devices: 9.74 us -> 14.1 us  [fast_local(): stats = stats + lax.ppermute(stats, 'head', xor_pairs(4, 1))]
    ppermute x1, waiting for transfers between devices: 4.34 us -> 1.72 us  [fast_local(): lax.ppermute(stats, 'head', xor_pairs(4, 2))]
    ppermute x1, waiting for transfers between devices: 0.01 us -> 1.15 us  [fast_local(): share_xy = lax.ppermute(share_y, 'batch', SWAP_X)]
    pallas_call x5 -> x7, Pallas kernels: 16.2 us -> 16.2 us  [the longest x2 7.68 us: attend(): pl.pallas_call(functools.partial(attend_kernel, cut, total_width), in_spe...]
  transfers between devices with their start and end apart: 21 -> 21, of which waited for: 9 -> 10; matrix products, arithmetic and copies ran while one was open for 0% -> 0% of each run, Pallas kernels for 5% -> 14%
where the time goes in v3:
time: 92.9 us; the launch traced here: 92.7 us
  waiting for transfers between devices  47.9 us (52%)
  starting transfers between devices  25.6 us (28%)
  Pallas kernels  18.9 us (20%)
    ppermute x2, waiting for transfers between devices, spread(): two = lax.ppermute(attended, 'head', xor_pairs(4, 2))  20.2 us
    ppermute x1, waiting for transfers between devices, fast_local(): stats = stats + lax.ppermute(stats, 'head', xor_pairs(4, 1))  14.1 us
    pallas_call x2, Pallas kernels, attend(): pl.pallas_call(functools.partial(attend_kernel, cut, total_width), in_spe...  7.68 us
    ppermute x2, starting transfers between devices, spread(): two = lax.ppermute(attended, 'head', xor_pairs(4, 2))  5.35 us
    pallas_call x1, Pallas kernels, fast_local(): pl.pallas_call(project_kernel, in_specs=[SMEM, SMEM, VMEM, HBM] + [VMEM]...  5.19 us
    ppermute x3, starting transfers between devices, fast_local(): lax.ppermute(cut_weights[s - 1], 'head', xor_pairs(4, s))  4.39 us
    ppermute x1, starting transfers between devices, fast_local(): lax.ppermute(stats, 'head', xor_pairs(4, 2))  3.49 us
    ppermute x2, waiting for transfers between devices, spread(): three = lax.ppermute(two, 'head', xor_pairs(4, 1))  3.38 us
  transfers between devices with their start and end apart: 21, of which 10 were waited for; matrix products, arithmetic and copies ran while one was open for 0% of the time, Pallas kernels for 14%

profile of v3, /device:TPU:0, one launch (start us, length us, event | category | flops | bytes accessed | tf_op | source)
XLA Modules:
  0.0 92.7 jit_solution(4724354854367583883)
XLA Ops:
  0.0 0.1 pad_add_fusion.place
  0.1 2.6 %prepare.1 = (bf16[256,640]{1,0:T(8,128)(2,1)S(1)}, bf16[256,640]{1,0:T(8,128)(2,1)S(1)}, bf16[1280,384]{1,0:T(8,128)(2,1)S(1)}, f32[8,512]{1,0:T(8,128)S(1)}, b...) custom-call(s32[4]{0:T(128)S(1)} %pad_add_fusion.place, ...), custom_call_target="tpu_custom_call" | custom-call | bytes 7200000 | tf_op jit(solution)/shard_map/prepare/pallas_call | solution.py:272
  2.7 0.0 copy-start.2
  2.7 0.0 copy-start.3
  2.8 3.0 %collective-permute-start.2 = (bf16[1280,384]{1,0:T(8,128)(2,1)S(1)}, bf16[1280,384]{1,0:T(8,128)(2,1)S(1)}, u32[]{:S(2)}, u32[]{:S(2)}) collective-permute-start(bf16[1280,384]{1,0:T(8,128)(2,1)S(1)} %get-tuple-element.18), channel_id=1, source_target_pairs={{0,4},{4,0},{1,5},{5,1},{2,6},{6,2},{3,7},{7,3},{8,12},{12,8},{9,1... | collective-permute-start | bytes 2949128 | tf_op jit(solution)/shard_map/ppermute | solution.py:301
  5.8 1.6 %collective-permute-start.3 = (bf16[160,1280]{1,0:T(8,128)(2,1)S(1)}, bf16[160,1280]{1,0:T(8,128)(2,1)S(1)}, u32[]{:S(2)}, u32[]{:S(2)}) collective-permute-start(bf16[160,1280]{1,0:T(8,128)(2,1)S(1)} %get-tuple-element.19), channel_id=1, source_target_pairs={{0,1},{1,0},{2,3},{3,2},{4,5},{5,4},{6,7},{7,6},{8,9},{9,8},{10,11... | collective-permute-start | bytes 1228808 | tf_op jit(solution)/shard_map/ppermute | solution.py:300
  7.4 2.6 %collective-permute-start.4 = (bf16[80,1280]{1,0:T(8,128)(2,1)S(1)}, bf16[80,1280]{1,0:T(8,128)(2,1)S(1)}, u32[]{:S(2)}, u32[]{:S(2)}) collective-permute-start(bf16[80,1280]{1,0:T(8,128)(2,1)S(1)} %get-tuple-element.20), channel_id=1, source_target_pairs={{0,2},{1,3},{2,0},{3,1},{4,6},{5,7},{6,4},{7,5},{8,10},{9,11},{10,... | collective-permute-start | bytes 614408 | tf_op jit(solution)/shard_map/ppermute | solution.py:300
  10.0 0.2 collective-permute-start.5
  10.2 0.7 collective-permute-start
  10.9 14.1 %collective-permute-done = f32[8,512]{1,0:T(8,128)S(1)} collective-permute-done((f32[8,512]{1,0:T(8,128)S(1)}, f32[8,512]{1,0:T(8,128)S(1)}, u32[]{:S(2)}, u32[]{:S(2)}) %collective-permute-start) | collective-permute-done | bytes 16416 | tf_op jit(solution)/shard_map/ppermute | solution.py:302
  25.0 3.5 %collective-permute-start.1 = (f32[8,512]{1,0:T(8,128)S(1)}, f32[8,512]{1,0:T(8,128)S(1)}, u32[]{:S(2)}, u32[]{:S(2)}) collective-permute-start(f32[8,512]{1,0:T(8,128)S(1)} %add.7.near_ref), channel_id=1, source_target_pairs={{0,2},{1,3},{2,0},{3,1},{4,6},{5,7},{6,4},{7,5},{8,10},{9,11},{10,... | collective-permute-start | bytes 49160 | tf_op jit(solution)/shard_map/ppermute | solution.py:311
  28.5 1.7 %collective-permute-done.1.far_ref = f32[8,512]{1,0:T(8,128)S(1)} collective-permute-done((f32[8,512]{1,0:T(8,128)S(1)}, f32[8,512]{1,0:T(8,128)S(1)}, u32[]{:S(2)}, u32[]{:S(2)}) %collective-permute-start.1) | collective-permute-done | bytes 16416 | tf_op jit(solution)/shard_map/ppermute | solution.py:311
  30.2 0.0 collective-permute-done.4.refs_2_.refs_0_.refs_1_
  30.2 0.0 collective-permute-done.5.refs_3_.refs_1_.refs_2_
  30.2 0.0 collective-permute-done.3.refs_1_.refs_0_
  30.2 0.0 collective-permute-done.2.refs_0_.remote_ref
  30.2 0.6 collective-permute-start.6
  30.8 3.2 %collective-permute-done.6.refs_2_.far_ref = f32[8,512]{1,0:T(8,128)S(1)} collective-permute-done((f32[8,512]{1,0:T(8,128)S(1)}, f32[8,512]{1,0:T(8,128)S(1)}, u32[]{:S(2)}, u32[]{:S(2)}) %collective-permute-start.6) | collective-permute-done | bytes 16416 | tf_op jit(solution)/shard_map/ppermute | solution.py:312
  34.1 0.1 join_all.1.refs_0_.refs_5_
  34.1 1.6 %collective-permute-start.12 = (bf16[320,1280]{1,0:T(8,128)(2,1)S(1)}, bf16[320,1280]{1,0:T(8,128)(2,1)S(1)}, u32[]{:S(2)}, u32[]{:S(2)}) collective-permute-start(bf16[320,1280]{1,0:T(8,128)(2,1)S(1)} %join_all.1.refs_0_.refs_5_), channel_id=1, source_target_pairs={{0,16},{16,0},{8,24},{24,8},{1,17},{17,1},{9,25},{25,9},{2,18},{18... | collective-permute-start | bytes 2457608 | tf_op jit(solution)/shard_map/ppermute | solution.py:317
  35.7 0.0 copy-done.2
  35.7 0.0 copy-done.3
  35.7 4.3 %attend.2.after_ref.refs_0_ = bf16[512,384]{1,0:T(8,128)(2,1)S(1)} custom-call(s32[4]{0:T(128)S(1)} %pad_add_fusion.place, f32[8,512]{1,0:T(8,128)S(1)} %settle.1.near_ref, f32[8,512]{1,0:T(8,128)S(1)} %collective-permute-done.6.refs_2_.far_ref, bf16[256,640]{1,0:T(8,128)(2,1)S(1)} %get-tuple-element.22.q_ref, bf16[512,640]{1,0:T(8,128)(2,1)S(1)} %get-tuple-element.23.k_ref, ...), custom_call_target="tpu_custom_call" | custom-call | bytes 28800000 | tf_op jit(solution)/shard_map/attend/pallas_call | solution.py:320
  40.1 0.0 copy-start
  40.1 0.0 copy-start.1
  40.1 0.6 collective-permute-start.10
  40.7 2.9 %collective-permute-start.8 = (bf16[512,384]{1,0:T(8,128)(2,1)S(1)}, bf16[512,384]{1,0:T(8,128)(2,1)S(1)}, u32[]{:S(2)}, u32[]{:S(2)}) collective-permute-start(bf16[512,384]{1,0:T(8,128)(2,1)S(1)} %attend.2.after_ref.refs_0_), channel_id=1, source_target_pairs={{0,2},{1,3},{2,0},{3,1},{4,6},{5,7},{6,4},{7,5},{8,10},{9,11},{10,... | collective-permute-start | bytes 1179656 | tf_op jit(solution)/shard_map/ppermute | solution.py:335
  43.6 1.5 %collective-permute-start.11 = (bf16[160,1280]{1,0:T(8,128)(2,1)S(1)}, bf16[160,1280]{1,0:T(8,128)(2,1)S(1)}, u32[]{:S(2)}, u32[]{:S(2)}) collective-permute-start(bf16[160,1280]{1,0:T(8,128)(2,1)S(1)} %join_two.1.refs_3_), channel_id=1, source_target_pairs={{0,4},{4,0},{1,5},{5,1},{2,6},{6,2},{3,7},{7,3},{8,12},{12,8},{9,1... | collective-permute-start | bytes 1228808 | tf_op jit(solution)/shard_map/ppermute | solution.py:316
  45.2 1.6 %collective-permute-start.7 = (bf16[512,384]{1,0:T(8,128)(2,1)S(1)}, bf16[512,384]{1,0:T(8,128)(2,1)S(1)}, u32[]{:S(2)}, u32[]{:S(2)}) collective-permute-start(bf16[512,384]{1,0:T(8,128)(2,1)S(1)} %attend.2.after_ref.refs_0_), channel_id=1, source_target_pairs={{0,1},{1,0},{2,3},{3,2},{4,5},{5,4},{6,7},{7,6},{8,9},{9,8},{10,11... | collective-permute-start | bytes 1179656 | tf_op jit(solution)/shard_map/ppermute | solution.py:334
  46.8 10.4 %collective-permute-done.8.refs_2_ = bf16[512,384]{1,0:T(8,128)(2,1)S(1)} collective-permute-done((bf16[512,384]{1,0:T(8,128)(2,1)S(1)}, bf16[512,384]{1,0:T(8,128)(2,1)S(1)}, u32[]{:S(2)}, u32[]{:S(2)}) %collective-permute-start.8) | collective-permute-done | bytes 393248 | tf_op jit(solution)/shard_map/ppermute | solution.py:335
  57.2 0.7 collective-permute-start.9
  57.9 0.8 collective-permute-done.7.refs_1_
  58.7 0.0 collective-permute-start.14
  58.7 3.3 %collective-permute-done.11.refs_0_ = bf16[160,1280]{1,0:T(8,128)(2,1)S(1)} collective-permute-done((bf16[160,1280]{1,0:T(8,128)(2,1)S(1)}, bf16[160,1280]{1,0:T(8,128)(2,1)S(1)}, u32[]{:S(2)}, u32[]{:S(2)}) %collective-permute-start.11) | collective-permute-done | bytes 409632 | tf_op jit(solution)/shard_map/ppermute | solution.py:316
  62.0 0.6 collective-permute-start.13
  62.6 0.0 collective-permute-done.12.refs_6_
  62.6 0.0 collective-permute-start.15
  62.6 0.0 collective-permute-done.10.remote_ref
  62.6 0.5 collective-permute-start.16
  63.1 3.3 %attend.3.refs_4_ = bf16[512,256]{1,0:T(8,128)(2,1)S(1)} custom-call(s32[4]{0:T(128)S(1)} %pad_add_fusion.place, f32[8,512]{1,0:T(8,128)S(1)} %settle.1.near_ref, f32[8,512]{1,0:T(8,128)S(1)} %collective-permute-done.6.refs_2_.far_ref, bf16[256,640]{1,0:T(8,128)(2,1)S(1)} %get-tuple-element.22.q_ref, bf16[512,640]{1,0:T(8,128)(2,1)S(1)} %get-tuple-element.23.k_ref, ...), custom_call_target="tpu_custom_call" | custom-call | bytes 28800000 | tf_op jit(solution)/shard_map/attend/pallas_call | solution.py:320
  66.4 0.6 collective-permute-done.9.refs_3_
  67.1 2.4 %collective-permute-start.19 = (bf16[512,256]{1,0:T(8,128)(2,1)S(1)}, bf16[512,256]{1,0:T(8,128)(2,1)S(1)}, u32[]{:S(2)}, u32[]{:S(2)}) collective-permute-start(bf16[512,256]{1,0:T(8,128)(2,1)S(1)} %attend.3.refs_4_), channel_id=1, source_target_pairs={{0,2},{1,3},{2,0},{3,1},{4,6},{5,7},{6,4},{7,5},{8,10},{9,11},{10,... | collective-permute-start | bytes 786440 | tf_op jit(solution)/shard_map/ppermute | solution.py:335
  69.5 1.1 %collective-permute-done.13.refs_8_ = bf16[160,1280]{1,0:T(8,128)(2,1)S(1)} collective-permute-done((bf16[160,1280]{1,0:T(8,128)(2,1)S(1)}, bf16[160,1280]{1,0:T(8,128)(2,1)S(1)}, u32[]{:S(2)}, u32[]{:S(2)}) %collective-permute-start.13) | collective-permute-done | bytes 409632 | tf_op jit(solution)/shard_map/ppermute | solution.py:351
  70.6 0.0 collective-permute-start.17
  70.6 0.0 collective-permute-done.16.refs_11_
  70.6 1.0 %collective-permute-start.18 = (bf16[512,256]{1,0:T(8,128)(2,1)S(1)}, bf16[512,256]{1,0:T(8,128)(2,1)S(1)}, u32[]{:S(2)}, u32[]{:S(2)}) collective-permute-start(bf16[512,256]{1,0:T(8,128)(2,1)S(1)} %attend.3.refs_4_), channel_id=1, source_target_pairs={{0,1},{1,0},{2,3},{3,2},{4,5},{5,4},{6,7},{7,6},{8,9},{9,8},{10,11... | collective-permute-start | bytes 786440 | tf_op jit(solution)/shard_map/ppermute | solution.py:334
  71.6 9.8 %collective-permute-done.19.two = bf16[512,256]{1,0:T(8,128)(2,1)S(1)} collective-permute-done((bf16[512,256]{1,0:T(8,128)(2,1)S(1)}, bf16[512,256]{1,0:T(8,128)(2,1)S(1)}, u32[]{:S(2)}, u32[]{:S(2)}) %collective-permute-start.19) | collective-permute-done | bytes 262176 | tf_op jit(solution)/shard_map/ppermute | solution.py:335
  81.4 0.0 collective-permute-start.20
  81.4 0.0 collective-permute-done.14.refs_9_
  81.4 0.0 collective-permute-done.17.refs_12_
  81.4 0.0 collective-permute-done.15.refs_10_
  81.4 0.0 copy-done
  81.5 0.0 copy-done.1
  81.5 5.2 %project.1 = (f32[512,1280]{1,0:T(8,128)S(1)}, bf16[768,1280]{1,0:T(8,128)(2,1)S(1)}, bf16[48,1280]{1,0:T(8,128)(2,1)S(1)}) custom-call(s32[4]{0:T(128)S(1)} %pad_add_fusion.place, s32[6]{0:T(128)S(1)} %copy-done.1, f32[50,1280]{1,0:T(8,128)S(1)} %copy-done, bf16[640,5120]{1,0:T(8,128)(2,1)} %weight_ref.3, bf16[512,384]{1,0:T(8,128)(2,1)S(1)} %attend.2.after_ref.refs_0_, ...), custom_call_target="tpu_custom_call" | custom-call | tf_op jit(solution)/shard_map/project/pallas_call | solution.py:357
  86.7 0.0 collective-permute-done.18.one
  86.7 2.7 %collective-permute-done.20.three = bf16[512,256]{1,0:T(8,128)(2,1)S(1)} collective-permute-done((bf16[512,256]{1,0:T(8,128)(2,1)S(1)}, bf16[512,256]{1,0:T(8,128)(2,1)S(1)}, u32[]{:S(2)}, u32[]{:S(2)}) %collective-permute-start.20) | collective-permute-done | bytes 262176 | tf_op jit(solution)/shard_map/ppermute | solution.py:336
  89.4 3.3 %finish.1 = bf16[512,1280]{1,0:T(8,128)(2,1)} custom-call(s32[4]{0:T(128)S(1)} %pad_add_fusion.place, f32[8,512]{1,0:T(8,128)S(1)} %settle.1.near_ref, f32[8,512]{1,0:T(8,128)S(1)} %collective-permute-done.6.refs_2_.far_ref, f32[512,1280]{1,0:T(8,128)S(1)} %get-tuple-element.26.total, bf16[768,1280]{1,0:T(8,128)(2,1)S(1)} %get-tuple-element.27.tail_ref, ...), custom_call_target="tpu_custom_call" | custom-call | tf_op jit(solution)/shard_map/finish/pallas_call | solution.py:375
  (7 shorter events, 0.1 us)
Async XLA Ops:
  2.7 33.0 %copy-start.2 = (f32[640]{0:T(1024)S(1)}, f32[640]{0:T(1024)}, u32[]{:S(2)}) copy-start(f32[640]{0:T(1024)} %param.13) | copy-start | bytes 7684
  2.7 33.0 %copy-start.3 = (f32[640]{0:T(1024)S(1)}, f32[640]{0:T(1024)}, u32[]{:S(2)}) copy-start(f32[640]{0:T(1024)} %param.14) | copy-start | bytes 7684
  2.8 27.5 %collective-permute-start.2 = (bf16[1280,384]{1,0:T(8,128)(2,1)S(1)}, bf16[1280,384]{1,0:T(8,128)(2,1)S(1)}, u32[]{:S(2)}, u32[]{:S(2)}) collective-permute-start(bf16[1280,384]{1,0:T(8,128)(2,1)S(1)} %get-tuple-element.18), channel_id=1, source_target_pairs={{0,4},{4,0},{1,5},{5,1},{2,6},{6,2},{3,7},{7,3},{8,12},{12,8},{9,1... | collective-permute-start | bytes 2949128 | tf_op jit(solution)/shard_map/ppermute | solution.py:301
  5.8 24.4 %collective-permute-start.3 = (bf16[160,1280]{1,0:T(8,128)(2,1)S(1)}, bf16[160,1280]{1,0:T(8,128)(2,1)S(1)}, u32[]{:S(2)}, u32[]{:S(2)}) collective-permute-start(bf16[160,1280]{1,0:T(8,128)(2,1)S(1)} %get-tuple-element.19), channel_id=1, source_target_pairs={{0,1},{1,0},{2,3},{3,2},{4,5},{5,4},{6,7},{7,6},{8,9},{9,8},{10,11... | collective-permute-start | bytes 1228808 | tf_op jit(solution)/shard_map/ppermute | solution.py:300
  7.4 22.8 %collective-permute-start.4 = (bf16[80,1280]{1,0:T(8,128)(2,1)S(1)}, bf16[80,1280]{1,0:T(8,128)(2,1)S(1)}, u32[]{:S(2)}, u32[]{:S(2)}) collective-permute-start(bf16[80,1280]{1,0:T(8,128)(2,1)S(1)} %get-tuple-element.20), channel_id=1, source_target_pairs={{0,2},{1,3},{2,0},{3,1},{4,6},{5,7},{6,4},{7,5},{8,10},{9,11},{10,... | collective-permute-start | bytes 614408 | tf_op jit(solution)/shard_map/ppermute | solution.py:300
  10.0 20.2 %collective-permute-start.5 = (bf16[80,1280]{1,0:T(8,128)(2,1)S(1)}, bf16[80,1280]{1,0:T(8,128)(2,1)S(1)}, u32[]{:S(2)}, u32[]{:S(2)}) collective-permute-start(bf16[80,1280]{1,0:T(8,128)(2,1)S(1)} %get-tuple-element.21), channel_id=1, source_target_pairs={{0,3},{1,2},{2,1},{3,0},{4,7},{5,6},{6,5},{7,4},{8,11},{9,10},{10,... | collective-permute-start | bytes 614408 | tf_op jit(solution)/shard_map/ppermute | solution.py:300
  10.2 14.8 %collective-permute-start = (f32[8,512]{1,0:T(8,128)S(1)}, f32[8,512]{1,0:T(8,128)S(1)}, u32[]{:S(2)}, u32[]{:S(2)}) collective-permute-start(f32[8,512]{1,0:T(8,128)S(1)} %get-tuple-element.17), channel_id=1, source_target_pairs={{0,1},{1,0},{2,3},{3,2},{4,5},{5,4},{6,7},{7,6},{8,9},{9,8},{10,11... | collective-permute-start | bytes 49160 | tf_op jit(solution)/shard_map/ppermute | solution.py:302
  25.0 5.2 %collective-permute-start.1 = (f32[8,512]{1,0:T(8,128)S(1)}, f32[8,512]{1,0:T(8,128)S(1)}, u32[]{:S(2)}, u32[]{:S(2)}) collective-permute-start(f32[8,512]{1,0:T(8,128)S(1)} %add.7.near_ref), channel_id=1, source_target_pairs={{0,2},{1,3},{2,0},{3,1},{4,6},{5,7},{6,4},{7,5},{8,10},{9,11},{10,... | collective-permute-start | bytes 49160 | tf_op jit(solution)/shard_map/ppermute | solution.py:311
  30.2 3.8 %collective-permute-start.6 = (f32[8,512]{1,0:T(8,128)S(1)}, f32[8,512]{1,0:T(8,128)S(1)}, u32[]{:S(2)}, u32[]{:S(2)}) collective-permute-start(f32[8,512]{1,0:T(8,128)S(1)} %settle.1.near_ref), channel_id=1, source_target_pairs={{0,4},{4,0},{1,5},{5,1},{2,6},{6,2},{3,7},{7,3},{8,12},{12,8},{9,1... | collective-permute-start | bytes 49160 | tf_op jit(solution)/shard_map/ppermute | solution.py:312
  34.1 28.5 %collective-permute-start.12 = (bf16[320,1280]{1,0:T(8,128)(2,1)S(1)}, bf16[320,1280]{1,0:T(8,128)(2,1)S(1)}, u32[]{:S(2)}, u32[]{:S(2)}) collective-permute-start(bf16[320,1280]{1,0:T(8,128)(2,1)S(1)} %join_all.1.refs_0_.refs_5_), channel_id=1, source_target_pairs={{0,16},{16,0},{8,24},{24,8},{1,17},{17,1},{9,25},{25,9},{2,18},{18... | collective-permute-start | bytes 2457608 | tf_op jit(solution)/shard_map/ppermute | solution.py:317
  40.1 41.3 %copy-start = (f32[50,1280]{1,0:T(8,128)S(1)}, f32[50,1280]{1,0:T(8,128)}, u32[]{:S(2)}) copy-start(f32[50,1280]{1,0:T(8,128)} %gate_ref.1) | copy-start | bytes 768004
  40.1 41.3 %copy-start.1 = (s32[6]{0:T(128)S(1)}, s32[6]{0:T(128)}, u32[]{:S(2)}) copy-start(s32[6]{0:T(128)} %times.1) | copy-start | bytes 76
  40.1 22.5 %collective-permute-start.10 = (bf16[1280,256]{1,0:T(8,128)(2,1)S(1)}, bf16[1280,256]{1,0:T(8,128)(2,1)S(1)}, u32[]{:S(2)}, u32[]{:S(2)}) collective-permute-start(bf16[1280,256]{1,0:T(8,128)(2,1)S(1)} %pack.1.refs_3_), channel_id=1, source_target_pairs={{0,4},{4,0},{1,5},{5,1},{2,6},{6,2},{3,7},{7,3},{8,12},{12,8},{9,1... | collective-permute-start | bytes 1966088 | tf_op jit(solution)/shard_map/ppermute | solution.py:349
  40.7 16.5 %collective-permute-start.8 = (bf16[512,384]{1,0:T(8,128)(2,1)S(1)}, bf16[512,384]{1,0:T(8,128)(2,1)S(1)}, u32[]{:S(2)}, u32[]{:S(2)}) collective-permute-start(bf16[512,384]{1,0:T(8,128)(2,1)S(1)} %attend.2.after_ref.refs_0_), channel_id=1, source_target_pairs={{0,2},{1,3},{2,0},{3,1},{4,6},{5,7},{6,4},{7,5},{8,10},{9,11},{10,... | collective-permute-start | bytes 1179656 | tf_op jit(solution)/shard_map/ppermute | solution.py:335
  43.6 18.3 %collective-permute-start.11 = (bf16[160,1280]{1,0:T(8,128)(2,1)S(1)}, bf16[160,1280]{1,0:T(8,128)(2,1)S(1)}, u32[]{:S(2)}, u32[]{:S(2)}) collective-permute-start(bf16[160,1280]{1,0:T(8,128)(2,1)S(1)} %join_two.1.refs_3_), channel_id=1, source_target_pairs={{0,4},{4,0},{1,5},{5,1},{2,6},{6,2},{3,7},{7,3},{8,12},{12,8},{9,1... | collective-permute-start | bytes 1228808 | tf_op jit(solution)/shard_map/ppermute | solution.py:316
  45.2 13.5 %collective-permute-start.7 = (bf16[512,384]{1,0:T(8,128)(2,1)S(1)}, bf16[512,384]{1,0:T(8,128)(2,1)S(1)}, u32[]{:S(2)}, u32[]{:S(2)}) collective-permute-start(bf16[512,384]{1,0:T(8,128)(2,1)S(1)} %attend.2.after_ref.refs_0_), channel_id=1, source_target_pairs={{0,1},{1,0},{2,3},{3,2},{4,5},{5,4},{6,7},{7,6},{8,9},{9,8},{10,11... | collective-permute-start | bytes 1179656 | tf_op jit(solution)/shard_map/ppermute | solution.py:334
  57.2 9.9 %collective-permute-start.9 = (bf16[512,384]{1,0:T(8,128)(2,1)S(1)}, bf16[512,384]{1,0:T(8,128)(2,1)S(1)}, u32[]{:S(2)}, u32[]{:S(2)}) collective-permute-start(bf16[512,384]{1,0:T(8,128)(2,1)S(1)} %collective-permute-done.8.refs_2_), channel_id=1, source_target_pairs={{0,1},{1,0},{2,3},{3,2},{4,5},{5,4},{6,7},{7,6},{8,9},{9,8},{10,11... | collective-permute-start | bytes 1179656 | tf_op jit(solution)/shard_map/ppermute | solution.py:336
  58.7 22.8 %collective-permute-start.14 = (bf16[320,1280]{1,0:T(8,128)(2,1)S(1)}, bf16[320,1280]{1,0:T(8,128)(2,1)S(1)}, u32[]{:S(2)}, u32[]{:S(2)}) collective-permute-start(bf16[320,1280]{1,0:T(8,128)(2,1)S(1)} %join_all.1.refs_0_.refs_5_), channel_id=1, source_target_pairs={{0,8},{8,0},{16,24},{24,16},{1,9},{9,1},{17,25},{25,17},{2,10},{10... | collective-permute-start | bytes 2457608 | tf_op jit(solution)/shard_map/ppermute | solution.py:354
  62.0 8.6 %collective-permute-start.13 = (bf16[160,1280]{1,0:T(8,128)(2,1)S(1)}, bf16[160,1280]{1,0:T(8,128)(2,1)S(1)}, u32[]{:S(2)}, u32[]{:S(2)}) collective-permute-start(bf16[160,1280]{1,0:T(8,128)(2,1)S(1)} %hold.1.refs_0_.refs_7_), channel_id=1, source_target_pairs={{0,16},{16,0},{8,24},{24,8},{1,17},{17,1},{9,25},{25,9},{2,18},{18... | collective-permute-start | bytes 1228808 | tf_op jit(solution)/shard_map/ppermute | solution.py:351
  62.6 18.8 %collective-permute-start.15 = (bf16[320,1280]{1,0:T(8,128)(2,1)S(1)}, bf16[320,1280]{1,0:T(8,128)(2,1)S(1)}, u32[]{:S(2)}, u32[]{:S(2)}) collective-permute-start(bf16[320,1280]{1,0:T(8,128)(2,1)S(1)} %collective-permute-done.12.refs_6_), channel_id=1, source_target_pairs={{0,8},{8,0},{16,24},{24,16},{1,9},{9,1},{17,25},{25,17},{2,10},{10... | collective-permute-start | bytes 2457608 | tf_op jit(solution)/shard_map/ppermute | solution.py:354
  62.6 8.0 %collective-permute-start.16 = (bf16[160,1280]{1,0:T(8,128)(2,1)S(1)}, bf16[160,1280]{1,0:T(8,128)(2,1)S(1)}, u32[]{:S(2)}, u32[]{:S(2)}) collective-permute-start(bf16[160,1280]{1,0:T(8,128)(2,1)S(1)} %hold.1.refs_0_.refs_7_), channel_id=1, source_target_pairs={{0,8},{8,0},{16,24},{24,16},{1,9},{9,1},{17,25},{25,17},{2,10},{10... | collective-permute-start | bytes 1228808 | tf_op jit(solution)/shard_map/ppermute | solution.py:354
  67.1 14.3 %collective-permute-start.19 = (bf16[512,256]{1,0:T(8,128)(2,1)S(1)}, bf16[512,256]{1,0:T(8,128)(2,1)S(1)}, u32[]{:S(2)}, u32[]{:S(2)}) collective-permute-start(bf16[512,256]{1,0:T(8,128)(2,1)S(1)} %attend.3.refs_4_), channel_id=1, source_target_pairs={{0,2},{1,3},{2,0},{3,1},{4,6},{5,7},{6,4},{7,5},{8,10},{9,11},{10,... | collective-permute-start | bytes 786440 | tf_op jit(solution)/shard_map/ppermute | solution.py:335
  70.6 10.8 %collective-permute-start.17 = (bf16[160,1280]{1,0:T(8,128)(2,1)S(1)}, bf16[160,1280]{1,0:T(8,128)(2,1)S(1)}, u32[]{:S(2)}, u32[]{:S(2)}) collective-permute-start(bf16[160,1280]{1,0:T(8,128)(2,1)S(1)} %collective-permute-done.13.refs_8_), channel_id=1, source_target_pairs={{0,8},{8,0},{16,24},{24,16},{1,9},{9,1},{17,25},{25,17},{2,10},{10... | collective-permute-start | bytes 1228808 | tf_op jit(solution)/shard_map/ppermute | solution.py:354
  70.6 16.0 %collective-permute-start.18 = (bf16[512,256]{1,0:T(8,128)(2,1)S(1)}, bf16[512,256]{1,0:T(8,128)(2,1)S(1)}, u32[]{:S(2)}, u32[]{:S(2)}) collective-permute-start(bf16[512,256]{1,0:T(8,128)(2,1)S(1)} %attend.3.refs_4_), channel_id=1, source_target_pairs={{0,1},{1,0},{2,3},{3,2},{4,5},{5,4},{6,7},{7,6},{8,9},{9,8},{10,11... | collective-permute-start | bytes 786440 | tf_op jit(solution)/shard_map/ppermute | solution.py:334
  81.4 8.0 %collective-permute-start.20 = (bf16[512,256]{1,0:T(8,128)(2,1)S(1)}, bf16[512,256]{1,0:T(8,128)(2,1)S(1)}, u32[]{:S(2)}, u32[]{:S(2)}) collective-permute-start(bf16[512,256]{1,0:T(8,128)(2,1)S(1)} %collective-permute-done.19.two), channel_id=1, source_target_pairs={{0,1},{1,0},{2,3},{3,2},{4,5},{5,4},{6,7},{7,6},{8,9},{9,8},{10,11... | collective-permute-start | bytes 786440 | tf_op jit(solution)/shard_map/ppermute | solution.py:336

commit v4 on v3

--- a/solution.py
+++ b/solution.py
@@ -64,16 +64,11 @@
 
 
 def prepare_kernel(
-    cut, place, q_hbm, k_hbm, v_hbm, dest_hbm, seg_hbm, weight_ref,
-    own_ref, other_ref, packed_ref, stats_ref, k_ref, v_ref, one_ref, two_ref, three_ref,
+    cut, place, q_hbm, k_hbm, v_hbm, dest_hbm, seg_hbm,
+    own_ref, other_ref, packed_ref, stats_ref, k_ref, v_ref,
     q_ref, dest_ref, seg_ref, sems,
 ):
     pairs = [(dest_hbm, dest_ref), (seg_hbm, seg_ref), (q_hbm, q_ref), (k_hbm, k_ref), (v_hbm, v_ref)]
-    for step, (ref, index) in enumerate(((one_ref, place[3]), (two_ref, place[2]), (three_ref, place[2]))):
-        count, columns = ref.shape
-        first = pl.multiple_of(index * count, count)
-        start = pl.multiple_of((place[1] ^ (step + 1)) * columns, columns)
-        pairs.append((weight_ref.at[pl.ds(first, count), pl.ds(start, columns)], ref))
     copies = load(pairs, sems)
     rows = q_ref.shape[0]
     half = rows // 2
@@ -105,15 +100,25 @@
     )
     copies[4].wait()
     packed_ref[half + rows :, :] = v_ref[:, low:high]
-    for copy in copies[5:]:
+
+
+def settle_kernel(near_ref, far_ref, out_ref):
+    out_ref[...] = near_ref[...] + far_ref[...]
+
+
+def cut_kernel(place, weight_ref, after_ref, one_ref, two_ref, three_ref, sems):
+    pairs = []
+    for step, (ref, index) in enumerate(((one_ref, place[3]), (two_ref, place[2]), (three_ref, place[2]))):
+        count, columns = ref.shape
+        first = pl.multiple_of(index * count, count)
+        start = pl.multiple_of((place[1] ^ (step + 1)) * columns, columns)
+        pairs.append((weight_ref.at[pl.ds(first, count), pl.ds(start, columns)], ref))
+    for copy in load(pairs, sems):
         copy.wait()
 
 
-def settle_kernel(near_ref, far_ref, *refs):
-    refs[-1][...] = near_ref[...] + far_ref[...]
-
-
-def pack_kernel(cut, other_ref, k_ref, v_ref, after_ref, out_ref):
+def pack_kernel(cut, other_ref, k_ref, v_ref, *refs):
+    out_ref = refs[-1]
     low, high = cut
     half, rows = other_ref.shape[0], k_ref.shape[0]
     out_ref[0:half, :] = other_ref[:, low:high]
@@ -135,7 +140,10 @@
     k_mark = jnp.concatenate([near[3:4], far[3:4]], axis=1)
     q_factor = column(jnp.concatenate([near_factors[0:1, :half], far_factors[0:1, half:]], axis=1))
     k_factor = column(jnp.concatenate([near_factors[1:2], far_factors[1:2]], axis=1))
-    allowed = column(q_mark) == k_mark
+    lane_video = 4.0 * lax.broadcasted_iota(jnp.int32, (2 * rows, HD), 1).astype(F32)
+    q_video = jnp.where(column(q_mark) == lane_video[:rows], 1.0, 0.0).astype(BF16)
+    k_video = jnp.where(column(k_mark) == lane_video, 0.0, -(2.0**20)).astype(BF16)
+    ones = jnp.ones((2 * rows, HD), BF16)
     scale = math.log2(math.e) / math.sqrt(HD)
     first, last = cut
     for low in range(first, last, HD):
@@ -146,16 +154,18 @@
         values = jnp.concatenate([v_ref[:, wide], remote_ref[half + rows :, here]], axis=0)
         queries = (queries.astype(F32) * q_factor * qg_ref[0:1, wide]).astype(BF16)
         keys = (keys.astype(F32) * k_factor * kg_ref[0:1, wide]).astype(BF16)
+        queries = jnp.concatenate([queries, q_video], axis=1)
+        keys = jnp.concatenate([keys, k_video], axis=1)
+        values = jnp.concatenate([values, ones], axis=1)
         for part in range(2):
             piece = slice(part * half, (part + 1) * half)
             scores = lax.dot_general(
                 queries[piece], keys, (((1,), (1,)), ((), ())), preferred_element_type=F32
             )
-            scores = jnp.where(allowed[piece], scores, -1e30)
             largest = jnp.max(scores, axis=1, keepdims=True)
-            weights = jnp.exp2((scores - largest) * scale)
-            totals = jnp.sum(weights, axis=1, keepdims=True)
-            mixed = jnp.dot(weights.astype(BF16), values, preferred_element_type=F32)
+            weights = jnp.exp2((scores - largest) * scale).astype(BF16)
+            mixed = jnp.dot(weights, values, preferred_element_type=F32)
+            mixed, totals = mixed[:, :HD], mixed[:, HD:]
             start = me * half if part == 0 else (1 - me) * half
             at = pl.ds(pl.multiple_of(start, half), half)
             out_ref[at, here] = (mixed / totals).astype(BF16)
@@ -166,6 +176,22 @@
     for ref in refs[:count]:
         refs[-1][low : low + ref.shape[0], :] = ref[...]
         low += ref.shape[0]
+
+
+def gate_kernel(*refs):
+    refs[-1][...] = jnp.zeros(refs[-1].shape, F32)
+
+
+def gate(after, weight, name):
+    return pl.pallas_call(
+        gate_kernel,
+        in_specs=[AFTER] * len(after),
+        out_specs=VMEM,
+        out_shape=jax.ShapeDtypeStruct((8, 128), F32),
+        compiler_params=params(4),
+        cost_estimate=pl.CostEstimate(flops=weight * 900_000_000, bytes_accessed=4096, transcendentals=0),
+        name=name,
+    )(*after)
 
 
 def join(pieces, after, name):
@@ -181,8 +207,8 @@
 
 
 def project_kernel(place, times, gate_ref, weight_ref, *refs):
-    first, own_last, shares = refs[:4], refs[4], refs[5:13]
-    total, tail_ref, gates_ref, rows_all, w_all, sems = refs[13:]
+    first, own_last, shares = refs[:4], refs[4], refs[5:11]
+    total, tail_ref, gates_ref, rows_all, w_all, sems = refs[11:]
     width = total.shape[1]
     group = w_all.shape[1]
     share = group // 8
@@ -199,14 +225,14 @@
         for index, piece in enumerate(three_pieces(gate_ref[pl.ds(times[video], 1), :])):
             gates_ref[index * 16 + video : index * 16 + video + 1, :] = piece.astype(BF16)
     for core in range(2):
-        near, far, other, diagonal = shares[4 * core : 4 * core + 4]
+        near, far, other = shares[3 * core : 3 * core + 3]
         pieces = [(near, 0, 0, 0), (far, 0, 0, 4)]
         for step in (1, 2):
             pieces += [
                 (near, (step + 1) * share, step, 0),
                 (far, (step + 1) * share, step, 4),
                 (other, (step - 1) * share, step, 1),
-                (diagonal, (step - 1) * share, step, 5),
+                (other, (step + 1) * share, step, 5),
             ]
         for ref, low, step, flip in pieces:
             count = share if step else 2 * share
@@ -269,10 +295,10 @@
     in_hbm = functools.partial(pltpu.with_memory_space_constraint, memory_space=pltpu.HBM)
     weight_hbm = in_hbm(out_weight)
 
-    own_queries, other_queries, packed, stats, keys, values, *cut_weights = pl.pallas_call(
+    own_queries, other_queries, packed, stats, keys, values = pl.pallas_call(
         functools.partial(prepare_kernel, cuts[0]),
-        in_specs=[SMEM] + [HBM] * 6,
-        out_specs=[VMEM] * 9,
+        in_specs=[SMEM] + [HBM] * 5,
+        out_specs=[VMEM] * 6,
         out_shape=[
             jax.ShapeDtypeStruct((half, width), BF16),
             jax.ShapeDtypeStruct((half, width), BF16),
@@ -280,41 +306,44 @@
             jax.ShapeDtypeStruct((8, rows), F32),
             jax.ShapeDtypeStruct((rows, width), BF16),
             jax.ShapeDtypeStruct((rows, width), BF16),
-            jax.ShapeDtypeStruct((2 * share, out_width), BF16),
-            jax.ShapeDtypeStruct((share, out_width), BF16),
-            jax.ShapeDtypeStruct((share, out_width), BF16),
         ],
         scratch_shapes=[
             pltpu.VMEM((rows, width), BF16),
             pltpu.VMEM((1, rows), jnp.int32),
             pltpu.VMEM((1, rows), jnp.int32),
-            pltpu.SemaphoreType.DMA((8,)),
+            pltpu.SemaphoreType.DMA((5,)),
         ],
         compiler_params=params(16),
         cost_estimate=cost(2),
         name="prepare",
     )(
         place, in_hbm(query_raw), in_hbm(key_raw), in_hbm(value_rows),
-        in_hbm(destination.reshape(1, rows)), in_hbm(segment.reshape(1, rows)), weight_hbm,
-    )
-    from_head = [lax.ppermute(cut_weights[s - 1], "head", xor_pairs(4, s)) for s in (1, 2, 3)]
+        in_hbm(destination.reshape(1, rows)), in_hbm(segment.reshape(1, rows)),
+    )
     arrived = [lax.ppermute(packed, "ctx", SWAP_CTX)]
     stats = stats + lax.ppermute(stats, "head", xor_pairs(4, 1))
     near = pl.pallas_call(
         settle_kernel,
-        in_specs=[VMEM] * 2 + [AFTER] * 4,
+        in_specs=[VMEM] * 2,
         out_specs=VMEM,
         out_shape=jax.ShapeDtypeStruct((8, rows), F32),
         compiler_params=params(4),
         cost_estimate=cost(1),
         name="settle",
-    )(stats, lax.ppermute(stats, "head", xor_pairs(4, 2)), arrived[0], *from_head)
+    )(stats, lax.ppermute(stats, "head", xor_pairs(4, 2)))
     far = lax.ppermute(near, "ctx", SWAP_CTX)
 
-    two_three = join(from_head[1:], [far], "join_two")
-    share0 = join(from_head, [two_three], "join_all")
-    share_y = lax.ppermute(two_three, "ctx", SWAP_CTX)
-    share_x = lax.ppermute(share0, "batch", SWAP_X)
+    cut_weights = pl.pallas_call(
+        cut_kernel,
+        in_specs=[SMEM, HBM, AFTER],
+        out_specs=[VMEM] * 3,
+        out_shape=[jax.ShapeDtypeStruct((count * share, out_width), BF16) for count in (2, 1, 1)],
+        scratch_shapes=[pltpu.SemaphoreType.DMA((3,))],
+        compiler_params=params(4),
+        cost_estimate=cost(1),
+        name="cut_weights",
+    )(place, weight_hbm, near)
+    from_head = [lax.ppermute(cut_weights[s - 1], "head", xor_pairs(4, s)) for s in (1, 2, 3)]
 
     def attend(cut, piece, after):
         return pl.pallas_call(
@@ -336,27 +365,37 @@
         three = lax.ppermute(two, "head", xor_pairs(4, 1))
         return [attended, one, two, three]
 
-    first = spread(attend(cuts[0], arrived[0], [share0]))
+    first = spread(attend(cuts[0], arrived[0], []))
+    landed = gate(from_head, 10, "landed")
     packed = pl.pallas_call(
         functools.partial(pack_kernel, cuts[1]),
-        in_specs=[VMEM] * 3 + [AFTER],
+        in_specs=[VMEM] * 3 + [AFTER] * 2,
         out_specs=VMEM,
         out_shape=packed_shapes[1],
         compiler_params=params(4),
         cost_estimate=cost(1),
         name="pack",
-    )(other_queries, keys, values, first[0])
+    )(other_queries, keys, values, first[0], landed)
     arrived.append(lax.ppermute(packed, "ctx", SWAP_CTX))
-    share_y = join([share_y], first[1:3] + [packed], "hold")
+    two_three = join(from_head[1:], [packed], "join_two")
+    share0 = join(from_head, [packed], "join_all")
+    share_y = lax.ppermute(two_three, "ctx", SWAP_CTX)
+    share_x = lax.ppermute(share0, "batch", SWAP_X)
+
+    token = gate(first[1:3], 10, "token")
+    attended = attend(cuts[1], arrived[1], [token])
+    share_y = join([share_y], [attended, share_x], "hold")
     share_xy = lax.ppermute(share_y, "batch", SWAP_X)
-    last = spread(attend(cuts[1], arrived[1], [share_y]))
-    shares = [share0, share_x, share_y, share_xy]
+    last = spread(attended)
+    passed = gate([first[3], *last[1:3]], 10, "passed")
+    share_yxy = join([share_y, share_xy], [passed], "join_y")
+    shares = [share0, share_x, share_yxy]
     shares += [lax.ppermute(value, "batch", SWAP_CORE) for value in shares]
 
     tail = width - cuts[0][1]
     total, tail_weights, gates = pl.pallas_call(
         project_kernel,
-        in_specs=[SMEM, SMEM, VMEM, HBM] + [VMEM] * 13,
+        in_specs=[SMEM, SMEM, VMEM, HBM] + [VMEM] * 11,
         out_specs=[VMEM] * 3,
         out_shape=[
             jax.ShapeDtypeStruct((rows, out_width), F32),

time: 92.9 us -> 84.5 us (0.910)
  waiting for transfers between devices: 47.9 us -> 38.3 us
    ppermute x1, waiting for transfers between devices: 14.1 us -> 2.16 us  [fast_local(): stats = stats + lax.ppermute(stats, 'head', xor_pairs(4, 1))]
    ppermute x2, waiting for transfers between devices: 20.2 us -> 12.9 us  [spread(): two = lax.ppermute(attended, 'head', xor_pairs(4, 2))]
    ppermute x2, waiting for transfers between devices: 3.38 us -> 9.03 us  [spread(): three = lax.ppermute(two, 'head', xor_pairs(4, 1))]
    ppermute x1, waiting for transfers between devices: 3.23 us -> 7.15 us  [fast_local(): far = lax.ppermute(near, 'ctx', SWAP_CTX)]
    ppermute x1, waiting for transfers between devices: 3.31 us -> 0.86 us  [fast_local(): share_y = lax.ppermute(two_three, 'ctx', SWAP_CTX)]
    ppermute x2, waiting for transfers between devices: 0.75 us -> 2.81 us  [spread(): one = lax.ppermute(attended, 'head', xor_pairs(4, 1))]
    pallas_call x1 -> x5, Pallas kernels: 0.01 us -> 1.74 us  [the longest x1 1.73 us: fast_local(): pl.pallas_call(cut_kernel, in_specs=[SMEM, HBM, AFTER], out_specs=[VMEM]...]
    ppermute x2, starting transfers between devices: 5.35 us -> 3.74 us  [spread(): two = lax.ppermute(attended, 'head', xor_pairs(4, 2))]
  transfers between devices with their start and end apart: 21 -> 20, of which waited for: 10 -> 10; matrix products, arithmetic and copies ran while one was open for 0% -> 0% of each run, Pallas kernels for 14% -> 16%
where the time goes in v4:
time: 84.5 us; the launch traced here: 84.3 us
  waiting for transfers between devices  38.3 us (45%)
  starting transfers between devices  26.1 us (31%)
  Pallas kernels  19.7 us (23%)
    ppermute x2, waiting for transfers between devices, spread(): two = lax.ppermute(attended, 'head', xor_pairs(4, 2))  12.9 us
    ppermute x2, waiting for transfers between devices, spread(): three = lax.ppermute(two, 'head', xor_pairs(4, 1))  9.03 us
    ppermute x1, waiting for transfers between devices, fast_local(): far = lax.ppermute(near, 'ctx', SWAP_CTX)  7.15 us
    pallas_call x2, Pallas kernels, attend(): pl.pallas_call(functools.partial(attend_kernel, cut, total_width), in_spe...  6.65 us
    pallas_call x1, Pallas kernels, fast_local(): pl.pallas_call(project_kernel, in_specs=[SMEM, SMEM, VMEM, HBM] + [VMEM]...  5.18 us
    ppermute x3, starting transfers between devices, fast_local(): lax.ppermute(cut_weights[s - 1], 'head', xor_pairs(4, s))  4.45 us
    ppermute x2, starting transfers between devices, spread(): two = lax.ppermute(attended, 'head', xor_pairs(4, 2))  3.74 us
    pallas_call x1, Pallas kernels, fast_local(): pl.pallas_call(finish_kernel, in_specs=[SMEM] + [VMEM] * 8, out_specs=ANY...  3.27 us
  transfers between devices with their start and end apart: 20, of which 10 were waited for; matrix products, arithmetic and copies ran while one was open for 0% of the time, Pallas kernels for 16%

profile of v4, /device:TPU:0, one launch (start us, length us, event | category | flops | bytes accessed | tf_op | source)
XLA Modules:
  0.0 84.3 jit_solution(3538893836199123245)
XLA Ops:
  0.0 0.1 pad_add_fusion.place
  0.1 2.6 %prepare.1 = (bf16[256,640]{1,0:T(8,128)(2,1)S(1)}, bf16[256,640]{1,0:T(8,128)(2,1)S(1)}, bf16[1280,384]{1,0:T(8,128)(2,1)S(1)}, f32[8,512]{1,0:T(8,128)S(1)}, b...) custom-call(s32[4]{0:T(128)S(1)} %pad_add_fusion.place, bf16[512,640]{1,0:T(8,128)(2,1)} %q_hbm.1, ...), custom_call_target="tpu_custom_call" | custom-call | bytes 7200000 | tf_op jit(solution)/shard_map/prepare/pallas_call | solution.py:298
  2.7 3.0 %collective-permute-start.3 = (bf16[1280,384]{1,0:T(8,128)(2,1)S(1)}, bf16[1280,384]{1,0:T(8,128)(2,1)S(1)}, u32[]{:S(2)}, u32[]{:S(2)}) collective-permute-start(bf16[1280,384]{1,0:T(8,128)(2,1)S(1)} %get-tuple-element.21), channel_id=1, source_target_pairs={{0,4},{4,0},{1,5},{5,1},{2,6},{6,2},{3,7},{7,3},{8,12},{12,8},{9,1... | collective-permute-start | bytes 2949128 | tf_op jit(solution)/shard_map/ppermute | solution.py:323
  5.7 1.6 %collective-permute-start = (f32[8,512]{1,0:T(8,128)S(1)}, f32[8,512]{1,0:T(8,128)S(1)}, u32[]{:S(2)}, u32[]{:S(2)}) collective-permute-start(f32[8,512]{1,0:T(8,128)S(1)} %get-tuple-element.17), channel_id=1, source_target_pairs={{0,1},{1,0},{2,3},{3,2},{4,5},{5,4},{6,7},{7,6},{8,9},{9,8},{10,11... | collective-permute-start | bytes 49160 | tf_op jit(solution)/shard_map/ppermute | solution.py:324
  7.3 2.2 %collective-permute-done = f32[8,512]{1,0:T(8,128)S(1)} collective-permute-done((f32[8,512]{1,0:T(8,128)S(1)}, f32[8,512]{1,0:T(8,128)S(1)}, u32[]{:S(2)}, u32[]{:S(2)}) %collective-permute-start) | collective-permute-done | bytes 16416 | tf_op jit(solution)/shard_map/ppermute | solution.py:324
  9.5 2.6 %collective-permute-start.1 = (f32[8,512]{1,0:T(8,128)S(1)}, f32[8,512]{1,0:T(8,128)S(1)}, u32[]{:S(2)}, u32[]{:S(2)}) collective-permute-start(f32[8,512]{1,0:T(8,128)S(1)} %add.7.near_ref), channel_id=1, source_target_pairs={{0,2},{1,3},{2,0},{3,1},{4,6},{5,7},{6,4},{7,5},{8,10},{9,11},{10,... | collective-permute-start | bytes 49160 | tf_op jit(solution)/shard_map/ppermute | solution.py:333
  12.1 2.0 %collective-permute-done.1.far_ref = f32[8,512]{1,0:T(8,128)S(1)} collective-permute-done((f32[8,512]{1,0:T(8,128)S(1)}, f32[8,512]{1,0:T(8,128)S(1)}, u32[]{:S(2)}, u32[]{:S(2)}) %collective-permute-start.1) | collective-permute-done | bytes 16416 | tf_op jit(solution)/shard_map/ppermute | solution.py:333
  14.1 0.0 copy-start.2
  14.1 0.0 copy-start.3
  14.1 1.7 %cut_weights.1 = (bf16[160,1280]{1,0:T(8,128)(2,1)S(1)}, bf16[80,1280]{1,0:T(8,128)(2,1)S(1)}, bf16[80,1280]{1,0:T(8,128)(2,1)S(1)}) custom-call(s32[4]{0:T(128)S(1)} %pad_add_fusion.place, bf16[640,5120]{1,0:T(8,128)(2,1)} %weight_ref.3, f32[8,512]{1,0:T(8,128)S(1)} %settle.1.near_ref.after_ref), custom_call_target="tpu_custom_call" | custom-call | bytes 3600000 | tf_op jit(solution)/shard_map/cut_weights/pallas_call | solution.py:336
  15.9 1.6 %collective-permute-start.7 = (bf16[160,1280]{1,0:T(8,128)(2,1)S(1)}, bf16[160,1280]{1,0:T(8,128)(2,1)S(1)}, u32[]{:S(2)}, u32[]{:S(2)}) collective-permute-start(bf16[160,1280]{1,0:T(8,128)(2,1)S(1)} %get-tuple-element.23), channel_id=1, source_target_pairs={{0,1},{1,0},{2,3},{3,2},{4,5},{5,4},{6,7},{7,6},{8,9},{9,8},{10,11... | collective-permute-start | bytes 1228808 | tf_op jit(solution)/shard_map/ppermute | solution.py:346
  17.5 2.7 %collective-permute-start.8 = (bf16[80,1280]{1,0:T(8,128)(2,1)S(1)}, bf16[80,1280]{1,0:T(8,128)(2,1)S(1)}, u32[]{:S(2)}, u32[]{:S(2)}) collective-permute-start(bf16[80,1280]{1,0:T(8,128)(2,1)S(1)} %get-tuple-element.24), channel_id=1, source_target_pairs={{0,2},{1,3},{2,0},{3,1},{4,6},{5,7},{6,4},{7,5},{8,10},{9,11},{10,... | collective-permute-start | bytes 614408 | tf_op jit(solution)/shard_map/ppermute | solution.py:346
  20.2 0.2 collective-permute-start.9
  20.3 0.3 collective-permute-start.2
  20.7 0.0 copy-done.2
  20.7 0.0 copy-done.3
  20.7 7.1 %collective-permute-done.2.far_ref = f32[8,512]{1,0:T(8,128)S(1)} collective-permute-done((f32[8,512]{1,0:T(8,128)S(1)}, f32[8,512]{1,0:T(8,128)S(1)}, u32[]{:S(2)}, u32[]{:S(2)}) %collective-permute-start.2) | collective-permute-done | bytes 16416 | tf_op jit(solution)/shard_map/ppermute | solution.py:334
  27.8 0.0 collective-permute-done.3.remote_ref
  27.8 3.7 %attend.2.refs_0_ = bf16[512,384]{1,0:T(8,128)(2,1)S(1)} custom-call(s32[4]{0:T(128)S(1)} %pad_add_fusion.place, f32[8,512]{1,0:T(8,128)S(1)} %settle.1.near_ref.after_ref, f32[8,512]{1,0:T(8,128)S(1)} %collective-permute-done.2.far_ref, bf16[256,640]{1,0:T(8,128)(2,1)S(1)} %get-tuple-element.18.q_ref, bf16[512,640]{1,0:T(8,128)(2,1)S(1)} %get-tuple-element.19.k_ref, ...), custom_call_target="tpu_custom_call" | custom-call | bytes 28800000 | tf_op jit(solution)/shard_map/attend/pallas_call | solution.py:349
  31.5 1.9 %collective-permute-start.4 = (bf16[512,384]{1,0:T(8,128)(2,1)S(1)}, bf16[512,384]{1,0:T(8,128)(2,1)S(1)}, u32[]{:S(2)}, u32[]{:S(2)}) collective-permute-start(bf16[512,384]{1,0:T(8,128)(2,1)S(1)} %attend.2.refs_0_), channel_id=1, source_target_pairs={{0,1},{1,0},{2,3},{3,2},{4,5},{5,4},{6,7},{7,6},{8,9},{9,8},{10,11... | collective-permute-start | bytes 1179656 | tf_op jit(solution)/shard_map/ppermute | solution.py:363
  33.4 2.6 %collective-permute-start.5 = (bf16[512,384]{1,0:T(8,128)(2,1)S(1)}, bf16[512,384]{1,0:T(8,128)(2,1)S(1)}, u32[]{:S(2)}, u32[]{:S(2)}) collective-permute-start(bf16[512,384]{1,0:T(8,128)(2,1)S(1)} %attend.2.refs_0_), channel_id=1, source_target_pairs={{0,2},{1,3},{2,0},{3,1},{4,6},{5,7},{6,4},{7,5},{8,10},{9,11},{10,... | collective-permute-start | bytes 1179656 | tf_op jit(solution)/shard_map/ppermute | solution.py:364
  36.0 0.0 collective-permute-done.8.refs_1_.refs_0_
  36.0 0.1 collective-permute-done.9.refs_2_.refs_1_
  36.0 0.0 collective-permute-done.7.refs_0_
  36.1 1.6 %collective-permute-start.10 = (bf16[1280,256]{1,0:T(8,128)(2,1)S(1)}, bf16[1280,256]{1,0:T(8,128)(2,1)S(1)}, u32[]{:S(2)}, u32[]{:S(2)}) collective-permute-start(bf16[1280,256]{1,0:T(8,128)(2,1)S(1)} %pack.1.refs_3_.refs_2_), channel_id=1, source_target_pairs={{0,4},{4,0},{1,5},{5,1},{2,6},{6,2},{3,7},{7,3},{8,12},{12,8},{9,1... | collective-permute-start | bytes 1966088 | tf_op jit(solution)/shard_map/ppermute | solution.py:379
  37.7 0.6 collective-permute-start.12
  38.3 0.1 join_all.1.refs_5_
  38.3 1.6 %collective-permute-start.11 = (bf16[320,1280]{1,0:T(8,128)(2,1)S(1)}, bf16[320,1280]{1,0:T(8,128)(2,1)S(1)}, u32[]{:S(2)}, u32[]{:S(2)}) collective-permute-start(bf16[320,1280]{1,0:T(8,128)(2,1)S(1)} %join_all.1.refs_5_), channel_id=1, source_target_pairs={{0,16},{16,0},{8,24},{24,8},{1,17},{17,1},{9,25},{25,9},{2,18},{18... | collective-permute-start | bytes 2457608 | tf_op jit(solution)/shard_map/ppermute | solution.py:383
  39.9 12.9 %collective-permute-done.5.refs_1_.refs_2_ = bf16[512,384]{1,0:T(8,128)(2,1)S(1)} collective-permute-done((bf16[512,384]{1,0:T(8,128)(2,1)S(1)}, bf16[512,384]{1,0:T(8,128)(2,1)S(1)}, u32[]{:S(2)}, u32[]{:S(2)}) %collective-permute-start.5) | collective-permute-done | bytes 393248 | tf_op jit(solution)/shard_map/ppermute | solution.py:364
  52.8 0.4 collective-permute-start.6
  53.3 0.0 collective-permute-done.4.refs_0_.refs_1_
  53.3 0.5 collective-permute-done.10.remote_ref
  53.8 3.0 %attend.3.refs_1_.refs_4_ = bf16[512,256]{1,0:T(8,128)(2,1)S(1)} custom-call(s32[4]{0:T(128)S(1)} %pad_add_fusion.place, f32[8,512]{1,0:T(8,128)S(1)} %settle.1.near_ref.after_ref, f32[8,512]{1,0:T(8,128)S(1)} %collective-permute-done.2.far_ref, bf16[256,640]{1,0:T(8,128)(2,1)S(1)} %get-tuple-element.18.q_ref, bf16[512,640]{1,0:T(8,128)(2,1)S(1)} %get-tuple-element.19.k_ref, ...), custom_call_target="tpu_custom_call" | custom-call | bytes 28800000 | tf_op jit(solution)/shard_map/attend/pallas_call | solution.py:349
  56.8 1.1 %collective-permute-start.14 = (bf16[512,256]{1,0:T(8,128)(2,1)S(1)}, bf16[512,256]{1,0:T(8,128)(2,1)S(1)}, u32[]{:S(2)}, u32[]{:S(2)}) collective-permute-start(bf16[512,256]{1,0:T(8,128)(2,1)S(1)} %attend.3.refs_1_.refs_4_), channel_id=1, source_target_pairs={{0,1},{1,0},{2,3},{3,2},{4,5},{5,4},{6,7},{7,6},{8,9},{9,8},{10,11... | collective-permute-start | bytes 786440 | tf_op jit(solution)/shard_map/ppermute | solution.py:363
  57.9 1.2 %collective-permute-start.15 = (bf16[512,256]{1,0:T(8,128)(2,1)S(1)}, bf16[512,256]{1,0:T(8,128)(2,1)S(1)}, u32[]{:S(2)}, u32[]{:S(2)}) collective-permute-start(bf16[512,256]{1,0:T(8,128)(2,1)S(1)} %attend.3.refs_1_.refs_4_), channel_id=1, source_target_pairs={{0,2},{1,3},{2,0},{3,1},{4,6},{5,7},{6,4},{7,5},{8,10},{9,11},{10,... | collective-permute-start | bytes 786440 | tf_op jit(solution)/shard_map/ppermute | solution.py:364
  59.1 0.9 %collective-permute-done.12.refs_0_ = bf16[160,1280]{1,0:T(8,128)(2,1)S(1)} collective-permute-done((bf16[160,1280]{1,0:T(8,128)(2,1)S(1)}, bf16[160,1280]{1,0:T(8,128)(2,1)S(1)}, u32[]{:S(2)}, u32[]{:S(2)}) %collective-permute-start.12) | collective-permute-done | bytes 409632 | tf_op jit(solution)/shard_map/ppermute | solution.py:382
  59.9 0.0 collective-permute-start.16
  59.9 0.0 collective-permute-done.11.refs_2_.refs_6_
  60.0 0.0 copy-start
  60.0 0.0 copy-start.1
  60.0 1.6 %collective-permute-start.13 = (bf16[160,1280]{1,0:T(8,128)(2,1)S(1)}, bf16[160,1280]{1,0:T(8,128)(2,1)S(1)}, u32[]{:S(2)}, u32[]{:S(2)}) collective-permute-start(bf16[160,1280]{1,0:T(8,128)(2,1)S(1)} %hold.1.refs_0_), channel_id=1, source_target_pairs={{0,16},{16,0},{8,24},{24,8},{1,17},{17,1},{9,25},{25,9},{2,18},{18... | collective-permute-start | bytes 1228808 | tf_op jit(solution)/shard_map/ppermute | solution.py:388
  61.5 7.8 %collective-permute-done.6.refs_0_.refs_3_ = bf16[512,384]{1,0:T(8,128)(2,1)S(1)} collective-permute-done((bf16[512,384]{1,0:T(8,128)(2,1)S(1)}, bf16[512,384]{1,0:T(8,128)(2,1)S(1)}, u32[]{:S(2)}, u32[]{:S(2)}) %collective-permute-start.6) | collective-permute-done | bytes 393248 | tf_op jit(solution)/shard_map/ppermute | solution.py:365
  69.4 0.0 collective-permute-start.17
  69.4 2.8 %collective-permute-done.14.refs_1_.one = bf16[512,256]{1,0:T(8,128)(2,1)S(1)} collective-permute-done((bf16[512,256]{1,0:T(8,128)(2,1)S(1)}, bf16[512,256]{1,0:T(8,128)(2,1)S(1)}, u32[]{:S(2)}, u32[]{:S(2)}) %collective-permute-start.14) | collective-permute-done | bytes 262176 | tf_op jit(solution)/shard_map/ppermute | solution.py:363
  72.2 0.0 collective-permute-done.15.refs_2_.two
  72.2 0.0 collective-permute-done.13.refs_1_
  72.2 0.1 join_y.1.refs_7_
  72.2 0.1 collective-permute-start.18
  72.3 1.6 %collective-permute-start.19 = (bf16[512,256]{1,0:T(8,128)(2,1)S(1)}, bf16[512,256]{1,0:T(8,128)(2,1)S(1)}, u32[]{:S(2)}, u32[]{:S(2)}) collective-permute-start(bf16[512,256]{1,0:T(8,128)(2,1)S(1)} %collective-permute-done.15.refs_2_.two), channel_id=1, source_target_pairs={{0,1},{1,0},{2,3},{3,2},{4,5},{5,4},{6,7},{7,6},{8,9},{9,8},{10,11... | collective-permute-start | bytes 786440 | tf_op jit(solution)/shard_map/ppermute | solution.py:365
  73.9 0.0 collective-permute-done.16.refs_8_
  74.0 0.0 collective-permute-done.17.refs_9_
  74.0 0.7 collective-permute-done.18.refs_10_
  74.6 0.0 copy-done
  74.7 0.0 copy-done.1
  74.7 5.2 %project.1 = (f32[512,1280]{1,0:T(8,128)S(1)}, bf16[768,1280]{1,0:T(8,128)(2,1)S(1)}, bf16[48,1280]{1,0:T(8,128)(2,1)S(1)}) custom-call(s32[4]{0:T(128)S(1)} %pad_add_fusion.place, s32[6]{0:T(128)S(1)} %copy-done.1, f32[50,1280]{1,0:T(8,128)S(1)} %copy-done, bf16[640,5120]{1,0:T(8,128)(2,1)} %weight_ref.3, bf16[512,384]{1,0:T(8,128)(2,1)S(1)} %attend.2.refs_0_, ...), custom_call_target="tpu_custom_call" | custom-call | tf_op jit(solution)/shard_map/project/pallas_call | solution.py:396
  79.8 1.2 %collective-permute-done.19.three = bf16[512,256]{1,0:T(8,128)(2,1)S(1)} collective-permute-done((bf16[512,256]{1,0:T(8,128)(2,1)S(1)}, bf16[512,256]{1,0:T(8,128)(2,1)S(1)}, u32[]{:S(2)}, u32[]{:S(2)}) %collective-permute-start.19) | collective-permute-done | bytes 262176 | tf_op jit(solution)/shard_map/ppermute | solution.py:365
  81.1 3.3 %finish.1 = bf16[512,1280]{1,0:T(8,128)(2,1)} custom-call(s32[4]{0:T(128)S(1)} %pad_add_fusion.place, f32[8,512]{1,0:T(8,128)S(1)} %settle.1.near_ref.after_ref, f32[8,512]{1,0:T(8,128)S(1)} %collective-permute-done.2.far_ref, f32[512,1280]{1,0:T(8,128)S(1)} %get-tuple-element.26.total, bf16[768,1280]{1,0:T(8,128)(2,1)S(1)} %get-tuple-element.27.tail_ref, ...), custom_call_target="tpu_custom_call" | custom-call | tf_op jit(solution)/shard_map/finish/pallas_call | solution.py:414
  (10 shorter events, 0.1 us)
Async XLA Ops:
  2.7 25.1 %collective-permute-start.3 = (bf16[1280,384]{1,0:T(8,128)(2,1)S(1)}, bf16[1280,384]{1,0:T(8,128)(2,1)S(1)}, u32[]{:S(2)}, u32[]{:S(2)}) collective-permute-start(bf16[1280,384]{1,0:T(8,128)(2,1)S(1)} %get-tuple-element.21), channel_id=1, source_target_pairs={{0,4},{4,0},{1,5},{5,1},{2,6},{6,2},{3,7},{7,3},{8,12},{12,8},{9,1... | collective-permute-start | bytes 2949128 | tf_op jit(solution)/shard_map/ppermute | solution.py:323
  5.7 3.7 %collective-permute-start = (f32[8,512]{1,0:T(8,128)S(1)}, f32[8,512]{1,0:T(8,128)S(1)}, u32[]{:S(2)}, u32[]{:S(2)}) collective-permute-start(f32[8,512]{1,0:T(8,128)S(1)} %get-tuple-element.17), channel_id=1, source_target_pairs={{0,1},{1,0},{2,3},{3,2},{4,5},{5,4},{6,7},{7,6},{8,9},{9,8},{10,11... | collective-permute-start | bytes 49160 | tf_op jit(solution)/shard_map/ppermute | solution.py:324
  9.5 4.6 %collective-permute-start.1 = (f32[8,512]{1,0:T(8,128)S(1)}, f32[8,512]{1,0:T(8,128)S(1)}, u32[]{:S(2)}, u32[]{:S(2)}) collective-permute-start(f32[8,512]{1,0:T(8,128)S(1)} %add.7.near_ref), channel_id=1, source_target_pairs={{0,2},{1,3},{2,0},{3,1},{4,6},{5,7},{6,4},{7,5},{8,10},{9,11},{10,... | collective-permute-start | bytes 49160 | tf_op jit(solution)/shard_map/ppermute | solution.py:333
  14.1 6.6 %copy-start.2 = (f32[640]{0:T(1024)S(1)}, f32[640]{0:T(1024)}, u32[]{:S(2)}) copy-start(f32[640]{0:T(1024)} %param.13) | copy-start | bytes 7684
  14.1 6.6 %copy-start.3 = (f32[640]{0:T(1024)S(1)}, f32[640]{0:T(1024)}, u32[]{:S(2)}) copy-start(f32[640]{0:T(1024)} %param.14) | copy-start | bytes 7684
  15.9 20.2 %collective-permute-start.7 = (bf16[160,1280]{1,0:T(8,128)(2,1)S(1)}, bf16[160,1280]{1,0:T(8,128)(2,1)S(1)}, u32[]{:S(2)}, u32[]{:S(2)}) collective-permute-start(bf16[160,1280]{1,0:T(8,128)(2,1)S(1)} %get-tuple-element.23), channel_id=1, source_target_pairs={{0,1},{1,0},{2,3},{3,2},{4,5},{5,4},{6,7},{7,6},{8,9},{9,8},{10,11... | collective-permute-start | bytes 1228808 | tf_op jit(solution)/shard_map/ppermute | solution.py:346
  17.5 18.5 %collective-permute-start.8 = (bf16[80,1280]{1,0:T(8,128)(2,1)S(1)}, bf16[80,1280]{1,0:T(8,128)(2,1)S(1)}, u32[]{:S(2)}, u32[]{:S(2)}) collective-permute-start(bf16[80,1280]{1,0:T(8,128)(2,1)S(1)} %get-tuple-element.24), channel_id=1, source_target_pairs={{0,2},{1,3},{2,0},{3,1},{4,6},{5,7},{6,4},{7,5},{8,10},{9,11},{10,... | collective-permute-start | bytes 614408 | tf_op jit(solution)/shard_map/ppermute | solution.py:346
  20.2 15.9 %collective-permute-start.9 = (bf16[80,1280]{1,0:T(8,128)(2,1)S(1)}, bf16[80,1280]{1,0:T(8,128)(2,1)S(1)}, u32[]{:S(2)}, u32[]{:S(2)}) collective-permute-start(bf16[80,1280]{1,0:T(8,128)(2,1)S(1)} %get-tuple-element.25), channel_id=1, source_target_pairs={{0,3},{1,2},{2,1},{3,0},{4,7},{5,6},{6,5},{7,4},{8,11},{9,10},{10,... | collective-permute-start | bytes 614408 | tf_op jit(solution)/shard_map/ppermute | solution.py:346
  20.3 7.5 %collective-permute-start.2 = (f32[8,512]{1,0:T(8,128)S(1)}, f32[8,512]{1,0:T(8,128)S(1)}, u32[]{:S(2)}, u32[]{:S(2)}) collective-permute-start(f32[8,512]{1,0:T(8,128)S(1)} %settle.1.near_ref.after_ref), channel_id=1, source_target_pairs={{0,4},{4,0},{1,5},{5,1},{2,6},{6,2},{3,7},{7,3},{8,12},{12,8},{9,1... | collective-permute-start | bytes 49160 | tf_op jit(solution)/shard_map/ppermute | solution.py:334
  31.5 21.7 %collective-permute-start.4 = (bf16[512,384]{1,0:T(8,128)(2,1)S(1)}, bf16[512,384]{1,0:T(8,128)(2,1)S(1)}, u32[]{:S(2)}, u32[]{:S(2)}) collective-permute-start(bf16[512,384]{1,0:T(8,128)(2,1)S(1)} %attend.2.refs_0_), channel_id=1, source_target_pairs={{0,1},{1,0},{2,3},{3,2},{4,5},{5,4},{6,7},{7,6},{8,9},{9,8},{10,11... | collective-permute-start | bytes 1179656 | tf_op jit(solution)/shard_map/ppermute | solution.py:363
  33.4 19.5 %collective-permute-start.5 = (bf16[512,384]{1,0:T(8,128)(2,1)S(1)}, bf16[512,384]{1,0:T(8,128)(2,1)S(1)}, u32[]{:S(2)}, u32[]{:S(2)}) collective-permute-start(bf16[512,384]{1,0:T(8,128)(2,1)S(1)} %attend.2.refs_0_), channel_id=1, source_target_pairs={{0,2},{1,3},{2,0},{3,1},{4,6},{5,7},{6,4},{7,5},{8,10},{9,11},{10,... | collective-permute-start | bytes 1179656 | tf_op jit(solution)/shard_map/ppermute | solution.py:364
  36.1 17.7 %collective-permute-start.10 = (bf16[1280,256]{1,0:T(8,128)(2,1)S(1)}, bf16[1280,256]{1,0:T(8,128)(2,1)S(1)}, u32[]{:S(2)}, u32[]{:S(2)}) collective-permute-start(bf16[1280,256]{1,0:T(8,128)(2,1)S(1)} %pack.1.refs_3_.refs_2_), channel_id=1, source_target_pairs={{0,4},{4,0},{1,5},{5,1},{2,6},{6,2},{3,7},{7,3},{8,12},{12,8},{9,1... | collective-permute-start | bytes 1966088 | tf_op jit(solution)/shard_map/ppermute | solution.py:379
  37.7 22.3 %collective-permute-start.12 = (bf16[160,1280]{1,0:T(8,128)(2,1)S(1)}, bf16[160,1280]{1,0:T(8,128)(2,1)S(1)}, u32[]{:S(2)}, u32[]{:S(2)}) collective-permute-start(bf16[160,1280]{1,0:T(8,128)(2,1)S(1)} %join_two.1), channel_id=1, source_target_pairs={{0,4},{4,0},{1,5},{5,1},{2,6},{6,2},{3,7},{7,3},{8,12},{12,8},{9,1... | collective-permute-start | bytes 1228808 | tf_op jit(solution)/shard_map/ppermute | solution.py:382
  38.3 21.6 %collective-permute-start.11 = (bf16[320,1280]{1,0:T(8,128)(2,1)S(1)}, bf16[320,1280]{1,0:T(8,128)(2,1)S(1)}, u32[]{:S(2)}, u32[]{:S(2)}) collective-permute-start(bf16[320,1280]{1,0:T(8,128)(2,1)S(1)} %join_all.1.refs_5_), channel_id=1, source_target_pairs={{0,16},{16,0},{8,24},{24,8},{1,17},{17,1},{9,25},{25,9},{2,18},{18... | collective-permute-start | bytes 2457608 | tf_op jit(solution)/shard_map/ppermute | solution.py:383
  52.8 16.5 %collective-permute-start.6 = (bf16[512,384]{1,0:T(8,128)(2,1)S(1)}, bf16[512,384]{1,0:T(8,128)(2,1)S(1)}, u32[]{:S(2)}, u32[]{:S(2)}) collective-permute-start(bf16[512,384]{1,0:T(8,128)(2,1)S(1)} %collective-permute-done.5.refs_1_.refs_2_), channel_id=1, source_target_pairs={{0,1},{1,0},{2,3},{3,2},{4,5},{5,4},{6,7},{7,6},{8,9},{9,8},{10,11... | collective-permute-start | bytes 1179656 | tf_op jit(solution)/shard_map/ppermute | solution.py:365
  56.8 15.4 %collective-permute-start.14 = (bf16[512,256]{1,0:T(8,128)(2,1)S(1)}, bf16[512,256]{1,0:T(8,128)(2,1)S(1)}, u32[]{:S(2)}, u32[]{:S(2)}) collective-permute-start(bf16[512,256]{1,0:T(8,128)(2,1)S(1)} %attend.3.refs_1_.refs_4_), channel_id=1, source_target_pairs={{0,1},{1,0},{2,3},{3,2},{4,5},{5,4},{6,7},{7,6},{8,9},{9,8},{10,11... | collective-permute-start | bytes 786440 | tf_op jit(solution)/shard_map/ppermute | solution.py:363
  57.9 14.3 %collective-permute-start.15 = (bf16[512,256]{1,0:T(8,128)(2,1)S(1)}, bf16[512,256]{1,0:T(8,128)(2,1)S(1)}, u32[]{:S(2)}, u32[]{:S(2)}) collective-permute-start(bf16[512,256]{1,0:T(8,128)(2,1)S(1)} %attend.3.refs_1_.refs_4_), channel_id=1, source_target_pairs={{0,2},{1,3},{2,0},{3,1},{4,6},{5,7},{6,4},{7,5},{8,10},{9,11},{10,... | collective-permute-start | bytes 786440 | tf_op jit(solution)/shard_map/ppermute | solution.py:364
  59.9 14.0 %collective-permute-start.16 = (bf16[320,1280]{1,0:T(8,128)(2,1)S(1)}, bf16[320,1280]{1,0:T(8,128)(2,1)S(1)}, u32[]{:S(2)}, u32[]{:S(2)}) collective-permute-start(bf16[320,1280]{1,0:T(8,128)(2,1)S(1)} %join_all.1.refs_5_), channel_id=1, source_target_pairs={{0,8},{8,0},{16,24},{24,16},{1,9},{9,1},{17,25},{25,17},{2,10},{10... | collective-permute-start | bytes 2457608 | tf_op jit(solution)/shard_map/ppermute | solution.py:393
  60.0 14.7 %copy-start = (f32[50,1280]{1,0:T(8,128)S(1)}, f32[50,1280]{1,0:T(8,128)}, u32[]{:S(2)}) copy-start(f32[50,1280]{1,0:T(8,128)} %gate_ref.1) | copy-start | bytes 768004
  60.0 14.7 %copy-start.1 = (s32[6]{0:T(128)S(1)}, s32[6]{0:T(128)}, u32[]{:S(2)}) copy-start(s32[6]{0:T(128)} %times.1) | copy-start | bytes 76
  60.0 12.2 %collective-permute-start.13 = (bf16[160,1280]{1,0:T(8,128)(2,1)S(1)}, bf16[160,1280]{1,0:T(8,128)(2,1)S(1)}, u32[]{:S(2)}, u32[]{:S(2)}) collective-permute-start(bf16[160,1280]{1,0:T(8,128)(2,1)S(1)} %hold.1.refs_0_), channel_id=1, source_target_pairs={{0,16},{16,0},{8,24},{24,8},{1,17},{17,1},{9,25},{25,9},{2,18},{18... | collective-permute-start | bytes 1228808 | tf_op jit(solution)/shard_map/ppermute | solution.py:388
  69.4 4.6 %collective-permute-start.17 = (bf16[320,1280]{1,0:T(8,128)(2,1)S(1)}, bf16[320,1280]{1,0:T(8,128)(2,1)S(1)}, u32[]{:S(2)}, u32[]{:S(2)}) collective-permute-start(bf16[320,1280]{1,0:T(8,128)(2,1)S(1)} %collective-permute-done.11.refs_2_.refs_6_), channel_id=1, source_target_pairs={{0,8},{8,0},{16,24},{24,16},{1,9},{9,1},{17,25},{25,17},{2,10},{10... | collective-permute-start | bytes 2457608 | tf_op jit(solution)/shard_map/ppermute | solution.py:393
  72.2 2.4 %collective-permute-start.18 = (bf16[320,1280]{1,0:T(8,128)(2,1)S(1)}, bf16[320,1280]{1,0:T(8,128)(2,1)S(1)}, u32[]{:S(2)}, u32[]{:S(2)}) collective-permute-start(bf16[320,1280]{1,0:T(8,128)(2,1)S(1)} %join_y.1.refs_7_), channel_id=1, source_target_pairs={{0,8},{8,0},{16,24},{24,16},{1,9},{9,1},{17,25},{25,17},{2,10},{10... | collective-permute-start | bytes 2457608 | tf_op jit(solution)/shard_map/ppermute | solution.py:393
  72.3 8.7 %collective-permute-start.19 = (bf16[512,256]{1,0:T(8,128)(2,1)S(1)}, bf16[512,256]{1,0:T(8,128)(2,1)S(1)}, u32[]{:S(2)}, u32[]{:S(2)}) collective-permute-start(bf16[512,256]{1,0:T(8,128)(2,1)S(1)} %collective-permute-done.15.refs_2_.two), channel_id=1, source_target_pairs={{0,1},{1,0},{2,3},{3,2},{4,5},{5,4},{6,7},{7,6},{8,9},{9,8},{10,11... | collective-permute-start | bytes 786440 | tf_op jit(solution)/shard_map/ppermute | solution.py:365

commit v5 on v4

--- a/solution.py
+++ b/solution.py
@@ -64,11 +64,16 @@
 
 
 def prepare_kernel(
-    cut, place, q_hbm, k_hbm, v_hbm, dest_hbm, seg_hbm,
-    own_ref, other_ref, packed_ref, stats_ref, k_ref, v_ref,
+    cut, place, q_hbm, k_hbm, v_hbm, dest_hbm, seg_hbm, weight_ref,
+    own_ref, other_ref, packed_ref, stats_ref, k_ref, v_ref, one_ref, two_ref, three_ref,
     q_ref, dest_ref, seg_ref, sems,
 ):
     pairs = [(dest_hbm, dest_ref), (seg_hbm, seg_ref), (q_hbm, q_ref), (k_hbm, k_ref), (v_hbm, v_ref)]
+    for step, (ref, index) in enumerate(((one_ref, place[3]), (two_ref, place[2]), (three_ref, place[2]))):
+        count, columns = ref.shape
+        first = pl.multiple_of(index * count, count)
+        start = pl.multiple_of((place[1] ^ (step + 1)) * columns, columns)
+        pairs.append((weight_ref.at[pl.ds(first, count), pl.ds(start, columns)], ref))
     copies = load(pairs, sems)
     rows = q_ref.shape[0]
     half = rows // 2
@@ -100,21 +105,12 @@
     )
     copies[4].wait()
     packed_ref[half + rows :, :] = v_ref[:, low:high]
-
-
-def settle_kernel(near_ref, far_ref, out_ref):
-    out_ref[...] = near_ref[...] + far_ref[...]
-
-
-def cut_kernel(place, weight_ref, after_ref, one_ref, two_ref, three_ref, sems):
-    pairs = []
-    for step, (ref, index) in enumerate(((one_ref, place[3]), (two_ref, place[2]), (three_ref, place[2]))):
-        count, columns = ref.shape
-        first = pl.multiple_of(index * count, count)
-        start = pl.multiple_of((place[1] ^ (step + 1)) * columns, columns)
-        pairs.append((weight_ref.at[pl.ds(first, count), pl.ds(start, columns)], ref))
-    for copy in load(pairs, sems):
+    for copy in copies[5:]:
         copy.wait()
+
+
+def settle_kernel(own_ref, one_ref, two_ref, three_ref, out_ref):
+    out_ref[...] = (own_ref[...] + one_ref[...]) + (two_ref[...] + three_ref[...])
 
 
 def pack_kernel(cut, other_ref, k_ref, v_ref, *refs):
@@ -127,12 +123,11 @@
 
 
 def attend_kernel(
-    cut, total_width, place, near_ref, far_ref, q_ref, k_ref, v_ref, qg_ref, kg_ref, remote_ref, *refs
+    cut, total_width, near_ref, far_ref, q_ref, k_ref, v_ref, qg_ref, kg_ref, remote_ref, *refs
 ):
     out_ref = refs[-1]
     rows = k_ref.shape[0]
     half = rows // 2
-    me = place[0]
     near, far = near_ref[...], far_ref[...]
     near_factors = lax.rsqrt(near[0:2] / total_width + 1e-06)
     far_factors = lax.rsqrt(far[0:2] / total_width + 1e-06)
@@ -166,9 +161,7 @@
             weights = jnp.exp2((scores - largest) * scale).astype(BF16)
             mixed = jnp.dot(weights, values, preferred_element_type=F32)
             mixed, totals = mixed[:, :HD], mixed[:, HD:]
-            start = me * half if part == 0 else (1 - me) * half
-            at = pl.ds(pl.multiple_of(start, half), half)
-            out_ref[at, here] = (mixed / totals).astype(BF16)
+            out_ref[piece, here] = (mixed / totals).astype(BF16)
 
 
 def join_kernel(count, *refs):
@@ -207,19 +200,21 @@
 
 
 def project_kernel(place, times, gate_ref, weight_ref, *refs):
-    first, own_last, shares = refs[:4], refs[4], refs[5:11]
-    total, tail_ref, gates_ref, rows_all, w_all, sems = refs[11:]
+    parts, shares = refs[:7], refs[7:13]
+    total, tail_ref, gates_ref, rows_all, w_all, sems = refs[13:]
     width = total.shape[1]
-    group = w_all.shape[1]
+    group = w_all.shape[0] // 4
     share = group // 8
-    early = first[0].shape[1]
-    head, mine = place[1], place[2]
-    own_start = pl.multiple_of(head * width, width)
-    own_copy = pltpu.make_async_copy(weight_ref.at[:, pl.ds(own_start, width)], w_all.at[0], sems.at[0])
+    mine = place[2]
+    own_start = pl.multiple_of(place[1] * width, width)
+    own_copy = pltpu.make_async_copy(
+        weight_ref.at[:, pl.ds(own_start, width)], w_all.at[pl.ds(0, group), :], sems.at[0]
+    )
     own_copy.start()
-    for slot in range(4):
-        rows_all[:, slot * early : (slot + 1) * early] = first[slot][...]
-    rows_all[:, 4 * early :] = own_last[...]
+    used = 0
+    for part in parts:
+        rows_all[:, used : used + part.shape[1]] = part[...]
+        used += part.shape[1]
     gates_ref[...] = jnp.zeros(gates_ref.shape, BF16)
     for video in range(times.shape[0]):
         for index, piece in enumerate(three_pieces(gate_ref[pl.ds(times[video], 1), :])):
@@ -237,40 +232,38 @@
         for ref, low, step, flip in pieces:
             count = share if step else 2 * share
             index = mine ^ (flip + 2 * core) if step else place[3] ^ (flip // 2 + core)
-            w_all[1 + step, pl.ds(pl.multiple_of(index * count, count), count), :] = ref[low : low + count, :]
-    for step in range(3):
-        tail_ref[step * (group - early) : (step + 1) * (group - early), :] = w_all[1 + step, early:group, :]
+            start = pl.multiple_of((1 + step) * group + index * count, share)
+            w_all[pl.ds(start, count), :] = ref[low : low + count, :]
+    tail_ref[...] = w_all[used:, :]
     own_copy.wait()
     for low in range(0, width, 256):
         block = slice(low, low + 256)
-        mixed = jnp.dot(rows_all[:, 4 * early :], w_all[0, early:group, block], preferred_element_type=F32)
-        for slot in range(4):
-            mixed += jnp.dot(
-                rows_all[:, slot * early : (slot + 1) * early], w_all[slot, 0:early, block],
-                preferred_element_type=F32,
-            )
-        total[:, block] = mixed
-
-
-def finish_kernel(place, near_ref, far_ref, total, tail_ref, gates_ref, one, two, three, out_hbm, out_ref, sems):
+        total[:, block] = jnp.dot(rows_all[...], w_all[0:used, block], preferred_element_type=F32)
+
+
+def finish_kernel(place, near_ref, far_ref, total, tail_ref, gates_ref, late_ref, out_hbm, out_ref, sems):
     rows, width = out_ref.shape
     half = rows // 2
     me = place[0]
     videos = lax.rem(lax.broadcasted_iota(jnp.int32, (rows, gates_ref.shape[0]), 1), 16).astype(F32)
-    own_mark, other_mark = near_ref[2:3, :half], far_ref[2:3, half:]
-    marks = jnp.concatenate(
-        [jnp.where(me == 0, own_mark, other_mark), jnp.where(me == 0, other_mark, own_mark)], axis=1
-    )
+    marks = jnp.concatenate([near_ref[2:3, :half], far_ref[2:3, half:]], axis=1)
     picked = (column(marks) == 4.0 * videos).astype(BF16)
-    late = jnp.concatenate([one[...], two[...], three[...]], axis=1)
     copies = []
-    for index, low in enumerate(range(0, width, 256)):
+    for low in range(0, width, 256):
         block = slice(low, low + 256)
         gates = jnp.dot(picked, gates_ref[:, block], preferred_element_type=F32)
-        mixed = total[:, block] + jnp.dot(late, tail_ref[:, block], preferred_element_type=F32)
+        mixed = total[:, block] + jnp.dot(late_ref[...], tail_ref[:, block], preferred_element_type=F32)
         out_ref[:, block] = (mixed * gates).astype(BF16)
-        copies.append(pltpu.make_async_copy(out_ref.at[:, block], out_hbm.at[:, block], sems.at[index]))
-        copies[-1].start()
+        for part in range(2):
+            start = me * half if part == 0 else (1 - me) * half
+            copies.append(
+                pltpu.make_async_copy(
+                    out_ref.at[pl.ds(part * half, half), block],
+                    out_hbm.at[pl.ds(pl.multiple_of(start, half), half), block],
+                    sems.at[len(copies)],
+                )
+            )
+            copies[-1].start()
     for copy in copies:
         copy.wait()
 
@@ -295,10 +288,10 @@
     in_hbm = functools.partial(pltpu.with_memory_space_constraint, memory_space=pltpu.HBM)
     weight_hbm = in_hbm(out_weight)
 
-    own_queries, other_queries, packed, stats, keys, values = pl.pallas_call(
+    own_queries, other_queries, packed, stats, keys, values, *cut_weights = pl.pallas_call(
         functools.partial(prepare_kernel, cuts[0]),
-        in_specs=[SMEM] + [HBM] * 5,
-        out_specs=[VMEM] * 6,
+        in_specs=[SMEM] + [HBM] * 6,
+        out_specs=[VMEM] * 9,
         out_shape=[
             jax.ShapeDtypeStruct((half, width), BF16),
             jax.ShapeDtypeStruct((half, width), BF16),
@@ -306,56 +299,47 @@
             jax.ShapeDtypeStruct((8, rows), F32),
             jax.ShapeDtypeStruct((rows, width), BF16),
             jax.ShapeDtypeStruct((rows, width), BF16),
+            jax.ShapeDtypeStruct((2 * share, out_width), BF16),
+            jax.ShapeDtypeStruct((share, out_width), BF16),
+            jax.ShapeDtypeStruct((share, out_width), BF16),
         ],
         scratch_shapes=[
             pltpu.VMEM((rows, width), BF16),
             pltpu.VMEM((1, rows), jnp.int32),
             pltpu.VMEM((1, rows), jnp.int32),
-            pltpu.SemaphoreType.DMA((5,)),
+            pltpu.SemaphoreType.DMA((8,)),
         ],
         compiler_params=params(16),
         cost_estimate=cost(2),
         name="prepare",
     )(
         place, in_hbm(query_raw), in_hbm(key_raw), in_hbm(value_rows),
-        in_hbm(destination.reshape(1, rows)), in_hbm(segment.reshape(1, rows)),
-    )
+        in_hbm(destination.reshape(1, rows)), in_hbm(segment.reshape(1, rows)), weight_hbm,
+    )
+    from_head = [lax.ppermute(cut_weights[s - 1], "head", xor_pairs(4, s)) for s in (1, 2, 3)]
     arrived = [lax.ppermute(packed, "ctx", SWAP_CTX)]
-    stats = stats + lax.ppermute(stats, "head", xor_pairs(4, 1))
     near = pl.pallas_call(
         settle_kernel,
-        in_specs=[VMEM] * 2,
+        in_specs=[VMEM] * 4,
         out_specs=VMEM,
         out_shape=jax.ShapeDtypeStruct((8, rows), F32),
         compiler_params=params(4),
         cost_estimate=cost(1),
         name="settle",
-    )(stats, lax.ppermute(stats, "head", xor_pairs(4, 2)))
+    )(stats, *[lax.ppermute(stats, "head", xor_pairs(4, step)) for step in (1, 2, 3)])
     far = lax.ppermute(near, "ctx", SWAP_CTX)
-
-    cut_weights = pl.pallas_call(
-        cut_kernel,
-        in_specs=[SMEM, HBM, AFTER],
-        out_specs=[VMEM] * 3,
-        out_shape=[jax.ShapeDtypeStruct((count * share, out_width), BF16) for count in (2, 1, 1)],
-        scratch_shapes=[pltpu.SemaphoreType.DMA((3,))],
-        compiler_params=params(4),
-        cost_estimate=cost(1),
-        name="cut_weights",
-    )(place, weight_hbm, near)
-    from_head = [lax.ppermute(cut_weights[s - 1], "head", xor_pairs(4, s)) for s in (1, 2, 3)]
 
     def attend(cut, piece, after):
         return pl.pallas_call(
             functools.partial(attend_kernel, cut, total_width),
-            in_specs=[SMEM] + [VMEM] * 8 + [AFTER] * len(after),
+            in_specs=[VMEM] * 8 + [AFTER] * len(after),
             out_specs=VMEM,
             out_shape=jax.ShapeDtypeStruct((rows, cut[1] - cut[0]), BF16),
             compiler_params=params(14),
             cost_estimate=cost(8),
             name="attend",
         )(
-            place, near, far, own_queries, keys, values, query_gain.reshape(1, width),
+            near, far, own_queries, keys, values, query_gain.reshape(1, width),
             key_gain.reshape(1, width), piece, *after,
         )
 
@@ -365,18 +349,19 @@
         three = lax.ppermute(two, "head", xor_pairs(4, 1))
         return [attended, one, two, three]
 
-    first = spread(attend(cuts[0], arrived[0], []))
-    landed = gate(from_head, 10, "landed")
+    first = spread(attend(cuts[0], arrived[0], [gate([far, arrived[0]], 10, "ready")]))
+    clear = gate([from_head[1], first[0]], 10, "clear")
     packed = pl.pallas_call(
         functools.partial(pack_kernel, cuts[1]),
-        in_specs=[VMEM] * 3 + [AFTER] * 2,
+        in_specs=[VMEM] * 3 + [AFTER],
         out_specs=VMEM,
         out_shape=packed_shapes[1],
         compiler_params=params(4),
         cost_estimate=cost(1),
         name="pack",
-    )(other_queries, keys, values, first[0], landed)
+    )(other_queries, keys, values, clear)
     arrived.append(lax.ppermute(packed, "ctx", SWAP_CTX))
+    landed = gate([*from_head, packed], 10, "landed")
     two_three = join(from_head[1:], [packed], "join_two")
     share0 = join(from_head, [packed], "join_all")
     share_y = lax.ppermute(two_three, "ctx", SWAP_CTX)
@@ -392,38 +377,39 @@
     shares = [share0, share_x, share_yxy]
     shares += [lax.ppermute(value, "batch", SWAP_CORE) for value in shares]
 
-    tail = width - cuts[0][1]
+    parts = [first[0], last[0], first[1], last[1], first[2], last[2], first[3]]
+    used = 3 * width + cuts[0][1]
     total, tail_weights, gates = pl.pallas_call(
         project_kernel,
-        in_specs=[SMEM, SMEM, VMEM, HBM] + [VMEM] * 11,
+        in_specs=[SMEM, SMEM, VMEM, HBM] + [VMEM] * (len(parts) + len(shares)),
         out_specs=[VMEM] * 3,
         out_shape=[
             jax.ShapeDtypeStruct((rows, out_width), F32),
-            jax.ShapeDtypeStruct((3 * tail, out_width), BF16),
+            jax.ShapeDtypeStruct((4 * width - used, out_width), BF16),
             jax.ShapeDtypeStruct((48, out_width), BF16),
         ],
         scratch_shapes=[
-            pltpu.VMEM((rows, 3 * cuts[0][1] + width), BF16),
-            pltpu.VMEM((4, width, out_width), BF16),
+            pltpu.VMEM((rows, used), BF16),
+            pltpu.VMEM((4 * width, out_width), BF16),
             pltpu.SemaphoreType.DMA((1,)),
         ],
         compiler_params=params(24),
         cost_estimate=cost(0),
         name="project",
-    )(place, timestep, gate_table, weight_hbm, *first, last[0], *shares)
+    )(place, timestep, gate_table, weight_hbm, *parts, *shares)
     return pl.pallas_call(
         finish_kernel,
-        in_specs=[SMEM] + [VMEM] * 8,
+        in_specs=[SMEM] + [VMEM] * 6,
         out_specs=ANY,
         out_shape=jax.ShapeDtypeStruct((rows, out_width), BF16),
         scratch_shapes=[
             pltpu.VMEM((rows, out_width), BF16),
-            pltpu.SemaphoreType.DMA((out_width // 256,)),
+            pltpu.SemaphoreType.DMA((2 * out_width // 256,)),
         ],
         compiler_params=params(14),
         cost_estimate=cost(0),
         name="finish",
-    )(place, near, far, total, tail_weights, gates, *last[1:])
+    )(place, near, far, total, tail_weights, gates, last[3])
 
 
 def for_sending(array):

time: 84.5 us -> 82.9 us (0.981)
  Pallas kernels: 19.7 us -> 16.1 us
  waiting for transfers between devices: 38.3 us -> 41.6 us
  starting transfers between devices: 26.1 us -> 24.8 us
    ppermute x2, waiting for transfers between devices: 12.9 us -> 6.39 us  [spread(): two = lax.ppermute(attended, 'head', xor_pairs(4, 2))]
    ppermute x3, waiting for transfers between devices: 0.06 us -> 6.34 us  [fast_local(): lax.ppermute(cut_weights[s - 1], 'head', xor_pairs(4, s))]
    pallas_call x3 -> x2, Pallas kernels: 5.01 us -> 2.45 us  [the longest x1 2.44 us: fast_local(): pl.pallas_call(finish_kernel, in_specs=[SMEM] + [VMEM] * 6, out_specs=ANY...]
    ppermute x1, waiting for transfers between devices: 7.15 us -> 8.31 us  [fast_local(): far = lax.ppermute(near, 'ctx', SWAP_CTX)]
    ppermute x2, starting transfers between devices: 2.99 us -> 1.87 us  [spread(): one = lax.ppermute(attended, 'head', xor_pairs(4, 1))]
    ppermute x2 -> x3, waiting for transfers between devices: 4.21 us -> 5.31 us  [fast_local(): lax.ppermute(stats, 'head', xor_pairs(4, step))]
    pallas_call x2, Pallas kernels: 6.65 us -> 5.61 us  [attend(): pl.pallas_call(functools.partial(attend_kernel, cut, total_width), in_spe...]
    ppermute x3, starting transfers between devices: 4.45 us -> 3.49 us  [fast_local(): lax.ppermute(cut_weights[s - 1], 'head', xor_pairs(4, s))]
  transfers between devices with their start and end apart: 20 -> 21, of which waited for: 10 -> 11; matrix products, arithmetic and copies ran while one was open for 0% -> 0% of each run, Pallas kernels for 16% -> 13%
where the time goes in v5:
time: 82.9 us; the launch traced here: 82.8 us
  waiting for transfers between devices  41.6 us (50%)
  starting transfers between devices  24.8 us (30%)
  Pallas kernels  16.1 us (19%)
    ppermute x2, waiting for transfers between devices, spread(): three = lax.ppermute(two, 'head', xor_pairs(4, 1))  8.79 us
    ppermute x1, waiting for transfers between devices, fast_local(): far = lax.ppermute(near, 'ctx', SWAP_CTX)  8.31 us
    ppermute x2, waiting for transfers between devices, spread(): two = lax.ppermute(attended, 'head', xor_pairs(4, 2))  6.39 us
    ppermute x3, waiting for transfers between devices, fast_local(): lax.ppermute(cut_weights[s - 1], 'head', xor_pairs(4, s))  6.34 us
    pallas_call x2, Pallas kernels, attend(): pl.pallas_call(functools.partial(attend_kernel, cut, total_width), in_spe...  5.61 us
    ppermute x3, waiting for transfers between devices, fast_local(): lax.ppermute(stats, 'head', xor_pairs(4, step))  5.31 us
    pallas_call x1, Pallas kernels, fast_local(): pl.pallas_call(project_kernel, in_specs=[SMEM, SMEM, VMEM, HBM] + [VMEM]...  5.2 us
    ppermute x2, starting transfers between devices, spread(): two = lax.ppermute(attended, 'head', xor_pairs(4, 2))  4.51 us
  transfers between devices with their start and end apart: 21, of which 11 were waited for; matrix products, arithmetic and copies ran while one was open for 0% of the time, Pallas kernels for 13%

profile of v5, /device:TPU:0, one launch (start us, length us, event | category | flops | bytes accessed | tf_op | source)
XLA Modules:
  0.0 82.8 jit_solution(15988962508510029480)
XLA Ops:
  0.0 0.1 pad_add_fusion.place
  0.1 0.0 copy-start.2
  0.1 0.0 copy-start.3
  0.1 2.6 %prepare.1 = (bf16[256,640]{1,0:T(8,128)(2,1)S(1)}, bf16[256,640]{1,0:T(8,128)(2,1)S(1)}, bf16[1280,384]{1,0:T(8,128)(2,1)S(1)}, f32[8,512]{1,0:T(8,128)S(1)}, b...) custom-call(s32[4]{0:T(128)S(1)} %pad_add_fusion.place, ...), custom_call_target="tpu_custom_call" | custom-call | bytes 7200000 | tf_op jit(solution)/shard_map/prepare/pallas_call | solution.py:291
  2.7 3.0 %collective-permute-start.4 = (bf16[1280,384]{1,0:T(8,128)(2,1)S(1)}, bf16[1280,384]{1,0:T(8,128)(2,1)S(1)}, u32[]{:S(2)}, u32[]{:S(2)}) collective-permute-start(bf16[1280,384]{1,0:T(8,128)(2,1)S(1)} %get-tuple-element.21), channel_id=1, source_target_pairs={{0,4},{4,0},{1,5},{5,1},{2,6},{6,2},{3,7},{7,3},{8,12},{12,8},{9,1... | collective-permute-start | bytes 2949128 | tf_op jit(solution)/shard_map/ppermute | solution.py:320
  5.8 1.6 %collective-permute-start = (f32[8,512]{1,0:T(8,128)S(1)}, f32[8,512]{1,0:T(8,128)S(1)}, u32[]{:S(2)}, u32[]{:S(2)}) collective-permute-start(f32[8,512]{1,0:T(8,128)S(1)} %get-tuple-element.17.own_ref), channel_id=1, source_target_pairs={{0,1},{1,0},{2,3},{3,2},{4,5},{5,4},{6,7},{7,6},{8,9},{9,8},{10,11... | collective-permute-start | bytes 49160 | tf_op jit(solution)/shard_map/ppermute | solution.py:329
  7.3 2.6 %collective-permute-start.1 = (f32[8,512]{1,0:T(8,128)S(1)}, f32[8,512]{1,0:T(8,128)S(1)}, u32[]{:S(2)}, u32[]{:S(2)}) collective-permute-start(f32[8,512]{1,0:T(8,128)S(1)} %get-tuple-element.17.own_ref), channel_id=1, source_target_pairs={{0,2},{1,3},{2,0},{3,1},{4,6},{5,7},{6,4},{7,5},{8,10},{9,11},{10,... | collective-permute-start | bytes 49160 | tf_op jit(solution)/shard_map/ppermute | solution.py:329
  9.9 0.2 collective-permute-start.2
  10.2 0.0 collective-permute-done.one_ref
  10.2 1.9 %collective-permute-done.1.two_ref = f32[8,512]{1,0:T(8,128)S(1)} collective-permute-done((f32[8,512]{1,0:T(8,128)S(1)}, f32[8,512]{1,0:T(8,128)S(1)}, u32[]{:S(2)}, u32[]{:S(2)}) %collective-permute-start.1) | collective-permute-done | bytes 16416 | tf_op jit(solution)/shard_map/ppermute | solution.py:329
  12.0 3.4 %collective-permute-done.2.three_ref = f32[8,512]{1,0:T(8,128)S(1)} collective-permute-done((f32[8,512]{1,0:T(8,128)S(1)}, f32[8,512]{1,0:T(8,128)S(1)}, u32[]{:S(2)}, u32[]{:S(2)}) %collective-permute-start.2) | collective-permute-done | bytes 16416 | tf_op jit(solution)/shard_map/ppermute | solution.py:329
  15.5 0.6 collective-permute-start.3
  16.0 0.0 collective-permute-start.5
  16.1 1.1 %collective-permute-start.13 = (bf16[80,1280]{1,0:T(8,128)(2,1)S(1)}, bf16[80,1280]{1,0:T(8,128)(2,1)S(1)}, u32[]{:S(2)}, u32[]{:S(2)}) collective-permute-start(bf16[80,1280]{1,0:T(8,128)(2,1)S(1)} %get-tuple-element.25), channel_id=1, source_target_pairs={{0,3},{1,2},{2,1},{3,0},{4,7},{5,6},{6,5},{7,4},{8,11},{9,10},{10,... | collective-permute-start | bytes 614408 | tf_op jit(solution)/shard_map/ppermute | solution.py:319
  17.2 2.4 %collective-permute-start.12 = (bf16[160,1280]{1,0:T(8,128)(2,1)S(1)}, bf16[160,1280]{1,0:T(8,128)(2,1)S(1)}, u32[]{:S(2)}, u32[]{:S(2)}) collective-permute-start(bf16[160,1280]{1,0:T(8,128)(2,1)S(1)} %get-tuple-element.24), channel_id=1, source_target_pairs={{0,1},{1,0},{2,3},{3,2},{4,5},{5,4},{6,7},{7,6},{8,9},{9,8},{10,11... | collective-permute-start | bytes 1228808 | tf_op jit(solution)/shard_map/ppermute | solution.py:319
  19.5 0.0 copy-done.2
  19.5 0.0 copy-done.3
  19.6 8.3 %collective-permute-done.3.refs_0_.far_ref = f32[8,512]{1,0:T(8,128)S(1)} collective-permute-done((f32[8,512]{1,0:T(8,128)S(1)}, f32[8,512]{1,0:T(8,128)S(1)}, u32[]{:S(2)}, u32[]{:S(2)}) %collective-permute-start.3) | collective-permute-done | bytes 16416 | tf_op jit(solution)/shard_map/ppermute | solution.py:330
  27.9 0.0 collective-permute-done.4.refs_1_.remote_ref
  27.9 3.1 %attend.2.refs_1_.refs_0_ = bf16[512,384]{1,0:T(8,128)(2,1)S(1)} custom-call(f32[8,512]{1,0:T(8,128)S(1)} %settle.1.near_ref, f32[8,512]{1,0:T(8,128)S(1)} %collective-permute-done.3.refs_0_.far_ref, bf16[256,640]{1,0:T(8,128)(2,1)S(1)} %get-tuple-element.18.q_ref, bf16[512,640]{1,0:T(8,128)(2,1)S(1)} %get-tuple-element.19.k_ref, ...), custom_call_target="tpu_custom_call" | custom-call | bytes 28800000 | tf_op jit(solution)/shard_map/attend/pallas_call | solution.py:333
  31.0 1.9 %collective-permute-start.7 = (bf16[512,384]{1,0:T(8,128)(2,1)S(1)}, bf16[512,384]{1,0:T(8,128)(2,1)S(1)}, u32[]{:S(2)}, u32[]{:S(2)}) collective-permute-start(bf16[512,384]{1,0:T(8,128)(2,1)S(1)} %attend.2.refs_1_.refs_0_), channel_id=1, source_target_pairs={{0,1},{1,0},{2,3},{3,2},{4,5},{5,4},{6,7},{7,6},{8,9},{9,8},{10,11... | collective-permute-start | bytes 1179656 | tf_op jit(solution)/shard_map/ppermute | solution.py:347
  32.9 2.6 %collective-permute-start.8 = (bf16[512,384]{1,0:T(8,128)(2,1)S(1)}, bf16[512,384]{1,0:T(8,128)(2,1)S(1)}, u32[]{:S(2)}, u32[]{:S(2)}) collective-permute-start(bf16[512,384]{1,0:T(8,128)(2,1)S(1)} %attend.2.refs_1_.refs_0_), channel_id=1, source_target_pairs={{0,2},{1,3},{2,0},{3,1},{4,6},{5,7},{6,4},{7,5},{8,10},{9,11},{10,... | collective-permute-start | bytes 1179656 | tf_op jit(solution)/shard_map/ppermute | solution.py:348
  35.5 0.0 collective-permute-done.5.refs_0_.refs_1_
  35.5 1.6 %collective-permute-start.6 = (bf16[1280,256]{1,0:T(8,128)(2,1)S(1)}, bf16[1280,256]{1,0:T(8,128)(2,1)S(1)}, u32[]{:S(2)}, u32[]{:S(2)}) collective-permute-start(bf16[1280,256]{1,0:T(8,128)(2,1)S(1)} %pack.1.refs_3_.refs_2_), channel_id=1, source_target_pairs={{0,4},{4,0},{1,5},{5,1},{2,6},{6,2},{3,7},{7,3},{8,12},{12,8},{9,1... | collective-permute-start | bytes 1966088 | tf_op jit(solution)/shard_map/ppermute | solution.py:363
  37.1 0.0 collective-permute-done.13.refs_2_.refs_1_
  37.1 0.6 collective-permute-start.15
  37.7 6.3 %collective-permute-done.12.refs_0_ = bf16[160,1280]{1,0:T(8,128)(2,1)S(1)} collective-permute-done((bf16[160,1280]{1,0:T(8,128)(2,1)S(1)}, bf16[160,1280]{1,0:T(8,128)(2,1)S(1)}, u32[]{:S(2)}, u32[]{:S(2)}) %collective-permute-start.12) | collective-permute-done | bytes 409632 | tf_op jit(solution)/shard_map/ppermute | solution.py:319
  44.1 0.1 join_all.1.refs_7_
  44.1 1.6 %collective-permute-start.14 = (bf16[320,1280]{1,0:T(8,128)(2,1)S(1)}, bf16[320,1280]{1,0:T(8,128)(2,1)S(1)}, u32[]{:S(2)}, u32[]{:S(2)}) collective-permute-start(bf16[320,1280]{1,0:T(8,128)(2,1)S(1)} %join_all.1.refs_7_), channel_id=1, source_target_pairs={{0,16},{16,0},{8,24},{24,8},{1,17},{17,1},{9,25},{25,9},{2,18},{18... | collective-permute-start | bytes 2457608 | tf_op jit(solution)/shard_map/ppermute | solution.py:368
  45.7 6.4 %collective-permute-done.8.refs_1_.refs_4_ = bf16[512,384]{1,0:T(8,128)(2,1)S(1)} collective-permute-done((bf16[512,384]{1,0:T(8,128)(2,1)S(1)}, bf16[512,384]{1,0:T(8,128)(2,1)S(1)}, u32[]{:S(2)}, u32[]{:S(2)}) %collective-permute-start.8) | collective-permute-done | bytes 393248 | tf_op jit(solution)/shard_map/ppermute | solution.py:348
  52.1 0.3 collective-permute-start.11
  52.4 0.0 collective-permute-done.7.refs_0_.refs_2_
  52.4 0.8 %collective-permute-done.6.remote_ref = bf16[1280,256]{1,0:T(8,128)(2,1)S(1)} collective-permute-done((bf16[1280,256]{1,0:T(8,128)(2,1)S(1)}, bf16[1280,256]{1,0:T(8,128)(2,1)S(1)}, u32[]{:S(2)}, u32[]{:S(2)}) %collective-permute-start.6) | collective-permute-done | bytes 655392 | tf_op jit(solution)/shard_map/ppermute | solution.py:363
  53.3 2.5 %attend.3.refs_1_ = bf16[512,256]{1,0:T(8,128)(2,1)S(1)} custom-call(f32[8,512]{1,0:T(8,128)S(1)} %settle.1.near_ref, f32[8,512]{1,0:T(8,128)S(1)} %collective-permute-done.3.refs_0_.far_ref, bf16[256,640]{1,0:T(8,128)(2,1)S(1)} %get-tuple-element.18.q_ref, bf16[512,640]{1,0:T(8,128)(2,1)S(1)} %get-tuple-element.19.k_ref, ...), custom_call_target="tpu_custom_call" | custom-call | bytes 28800000 | tf_op jit(solution)/shard_map/attend/pallas_call | solution.py:333
  55.7 1.9 %collective-permute-start.10 = (bf16[512,256]{1,0:T(8,128)(2,1)S(1)}, bf16[512,256]{1,0:T(8,128)(2,1)S(1)}, u32[]{:S(2)}, u32[]{:S(2)}) collective-permute-start(bf16[512,256]{1,0:T(8,128)(2,1)S(1)} %attend.3.refs_1_), channel_id=1, source_target_pairs={{0,2},{1,3},{2,0},{3,1},{4,6},{5,7},{6,4},{7,5},{8,10},{9,11},{10,... | collective-permute-start | bytes 786440 | tf_op jit(solution)/shard_map/ppermute | solution.py:348
  57.7 0.0 collective-permute-start.9
  57.7 1.7 %collective-permute-done.15.refs_0_ = bf16[160,1280]{1,0:T(8,128)(2,1)S(1)} collective-permute-done((bf16[160,1280]{1,0:T(8,128)(2,1)S(1)}, bf16[160,1280]{1,0:T(8,128)(2,1)S(1)}, u32[]{:S(2)}, u32[]{:S(2)}) %collective-permute-start.15) | collective-permute-done | bytes 409632 | tf_op jit(solution)/shard_map/ppermute | solution.py:367
  59.4 0.0 collective-permute-start.17
  59.4 0.0 collective-permute-done.14.refs_2_.refs_8_
  59.5 0.0 copy-start
  59.5 0.0 copy-start.1
  59.5 1.6 %collective-permute-start.16 = (bf16[160,1280]{1,0:T(8,128)(2,1)S(1)}, bf16[160,1280]{1,0:T(8,128)(2,1)S(1)}, u32[]{:S(2)}, u32[]{:S(2)}) collective-permute-start(bf16[160,1280]{1,0:T(8,128)(2,1)S(1)} %hold.1.refs_0_), channel_id=1, source_target_pairs={{0,16},{16,0},{8,24},{24,8},{1,17},{17,1},{9,25},{25,9},{2,18},{18... | collective-permute-start | bytes 1228808 | tf_op jit(solution)/shard_map/ppermute | solution.py:373
  61.0 7.6 %collective-permute-done.11.refs_0_.refs_6_ = bf16[512,384]{1,0:T(8,128)(2,1)S(1)} collective-permute-done((bf16[512,384]{1,0:T(8,128)(2,1)S(1)}, bf16[512,384]{1,0:T(8,128)(2,1)S(1)}, u32[]{:S(2)}, u32[]{:S(2)}) %collective-permute-start.11) | collective-permute-done | bytes 393248 | tf_op jit(solution)/shard_map/ppermute | solution.py:349
  68.6 0.0 collective-permute-start.18
  68.6 0.0 collective-permute-done.10.refs_2_.refs_5_
  68.6 2.8 %collective-permute-done.9.refs_1_.refs_3_ = bf16[512,256]{1,0:T(8,128)(2,1)S(1)} collective-permute-done((bf16[512,256]{1,0:T(8,128)(2,1)S(1)}, bf16[512,256]{1,0:T(8,128)(2,1)S(1)}, u32[]{:S(2)}, u32[]{:S(2)}) %collective-permute-start.9) | collective-permute-done | bytes 262176 | tf_op jit(solution)/shard_map/ppermute | solution.py:347
  71.5 0.0 collective-permute-done.16.refs_1_
  71.5 0.1 join_y.1.refs_9_
  71.5 0.1 collective-permute-start.19
  71.6 1.3 %collective-permute-start.20 = (bf16[512,256]{1,0:T(8,128)(2,1)S(1)}, bf16[512,256]{1,0:T(8,128)(2,1)S(1)}, u32[]{:S(2)}, u32[]{:S(2)}) collective-permute-start(bf16[512,256]{1,0:T(8,128)(2,1)S(1)} %collective-permute-done.10.refs_2_.refs_5_), channel_id=1, source_target_pairs={{0,1},{1,0},{2,3},{3,2},{4,5},{5,4},{6,7},{7,6},{8,9},{9,8},{10,11... | collective-permute-start | bytes 786440 | tf_op jit(solution)/shard_map/ppermute | solution.py:349
  72.9 0.0 collective-permute-done.17.refs_10_
  72.9 0.0 collective-permute-done.18.refs_11_
  72.9 1.0 %collective-permute-done.19.refs_12_ = bf16[320,1280]{1,0:T(8,128)(2,1)S(1)} collective-permute-done((bf16[320,1280]{1,0:T(8,128)(2,1)S(1)}, bf16[320,1280]{1,0:T(8,128)(2,1)S(1)}, u32[]{:S(2)}, u32[]{:S(2)}) %collective-permute-start.19) | collective-permute-done | bytes 819232 | tf_op jit(solution)/shard_map/ppermute | solution.py:378
  73.9 0.0 copy-done
  73.9 0.0 copy-done.1
  73.9 5.2 %project.1 = (f32[512,1280]{1,0:T(8,128)S(1)}, bf16[256,1280]{1,0:T(8,128)(2,1)S(1)}, bf16[48,1280]{1,0:T(8,128)(2,1)S(1)}) custom-call(s32[4]{0:T(128)S(1)} %pad_add_fusion.place, s32[6]{0:T(128)S(1)} %copy-done.1, f32[50,1280]{1,0:T(8,128)S(1)} %copy-done, bf16[640,5120]{1,0:T(8,128)(2,1)} %weight_ref.3, bf16[512,384]{1,0:T(8,128)(2,1)S(1)} %attend.2.refs_1_.refs_0_, ...), custom_call_target="tpu_custom_call" | custom-call | tf_op jit(solution)/shard_map/project/pallas_call | solution.py:382
  79.1 1.2 %collective-permute-done.20.late_ref = bf16[512,256]{1,0:T(8,128)(2,1)S(1)} collective-permute-done((bf16[512,256]{1,0:T(8,128)(2,1)S(1)}, bf16[512,256]{1,0:T(8,128)(2,1)S(1)}, u32[]{:S(2)}, u32[]{:S(2)}) %collective-permute-start.20) | collective-permute-done | bytes 262176 | tf_op jit(solution)/shard_map/ppermute | solution.py:349
  80.3 2.4 %finish.1 = bf16[512,1280]{1,0:T(8,128)(2,1)} custom-call(s32[4]{0:T(128)S(1)} %pad_add_fusion.place, f32[8,512]{1,0:T(8,128)S(1)} %settle.1.near_ref, f32[8,512]{1,0:T(8,128)S(1)} %collective-permute-done.3.refs_0_.far_ref, f32[512,1280]{1,0:T(8,128)S(1)} %get-tuple-element.26.total, bf16[256,1280]{1,0:T(8,128)(2,1)S(1)} %get-tuple-element.27.tail_ref, ...), custom_call_target="tpu_custom_call" | custom-call | tf_op jit(solution)/shard_map/finish/pallas_call | solution.py:400
  (10 shorter events, 0.1 us)
Async XLA Ops:
  0.1 19.5 %copy-start.2 = (f32[640]{0:T(1024)S(1)}, f32[640]{0:T(1024)}, u32[]{:S(2)}) copy-start(f32[640]{0:T(1024)} %param.13) | copy-start | bytes 7684
  0.1 19.5 %copy-start.3 = (f32[640]{0:T(1024)S(1)}, f32[640]{0:T(1024)}, u32[]{:S(2)}) copy-start(f32[640]{0:T(1024)} %param.14) | copy-start | bytes 7684
  2.7 25.1 %collective-permute-start.4 = (bf16[1280,384]{1,0:T(8,128)(2,1)S(1)}, bf16[1280,384]{1,0:T(8,128)(2,1)S(1)}, u32[]{:S(2)}, u32[]{:S(2)}) collective-permute-start(bf16[1280,384]{1,0:T(8,128)(2,1)S(1)} %get-tuple-element.21), channel_id=1, source_target_pairs={{0,4},{4,0},{1,5},{5,1},{2,6},{6,2},{3,7},{7,3},{8,12},{12,8},{9,1... | collective-permute-start | bytes 2949128 | tf_op jit(solution)/shard_map/ppermute | solution.py:320
  5.8 4.4 %collective-permute-start = (f32[8,512]{1,0:T(8,128)S(1)}, f32[8,512]{1,0:T(8,128)S(1)}, u32[]{:S(2)}, u32[]{:S(2)}) collective-permute-start(f32[8,512]{1,0:T(8,128)S(1)} %get-tuple-element.17.own_ref), channel_id=1, source_target_pairs={{0,1},{1,0},{2,3},{3,2},{4,5},{5,4},{6,7},{7,6},{8,9},{9,8},{10,11... | collective-permute-start | bytes 49160 | tf_op jit(solution)/shard_map/ppermute | solution.py:329
  7.3 4.7 %collective-permute-start.1 = (f32[8,512]{1,0:T(8,128)S(1)}, f32[8,512]{1,0:T(8,128)S(1)}, u32[]{:S(2)}, u32[]{:S(2)}) collective-permute-start(f32[8,512]{1,0:T(8,128)S(1)} %get-tuple-element.17.own_ref), channel_id=1, source_target_pairs={{0,2},{1,3},{2,0},{3,1},{4,6},{5,7},{6,4},{7,5},{8,10},{9,11},{10,... | collective-permute-start | bytes 49160 | tf_op jit(solution)/shard_map/ppermute | solution.py:329
  9.9 5.5 %collective-permute-start.2 = (f32[8,512]{1,0:T(8,128)S(1)}, f32[8,512]{1,0:T(8,128)S(1)}, u32[]{:S(2)}, u32[]{:S(2)}) collective-permute-start(f32[8,512]{1,0:T(8,128)S(1)} %get-tuple-element.17.own_ref), channel_id=1, source_target_pairs={{0,3},{1,2},{2,1},{3,0},{4,7},{5,6},{6,5},{7,4},{8,11},{9,10},{10,... | collective-permute-start | bytes 49160 | tf_op jit(solution)/shard_map/ppermute | solution.py:329
  15.5 12.4 %collective-permute-start.3 = (f32[8,512]{1,0:T(8,128)S(1)}, f32[8,512]{1,0:T(8,128)S(1)}, u32[]{:S(2)}, u32[]{:S(2)}) collective-permute-start(f32[8,512]{1,0:T(8,128)S(1)} %settle.1.near_ref), channel_id=1, source_target_pairs={{0,4},{4,0},{1,5},{5,1},{2,6},{6,2},{3,7},{7,3},{8,12},{12,8},{9,1... | collective-permute-start | bytes 49160 | tf_op jit(solution)/shard_map/ppermute | solution.py:330
  16.0 19.4 %collective-permute-start.5 = (bf16[80,1280]{1,0:T(8,128)(2,1)S(1)}, bf16[80,1280]{1,0:T(8,128)(2,1)S(1)}, u32[]{:S(2)}, u32[]{:S(2)}) collective-permute-start(bf16[80,1280]{1,0:T(8,128)(2,1)S(1)} %get-tuple-element.23), channel_id=1, source_target_pairs={{0,2},{1,3},{2,0},{3,1},{4,6},{5,7},{6,4},{7,5},{8,10},{9,11},{10,... | collective-permute-start | bytes 614408 | tf_op jit(solution)/shard_map/ppermute | solution.py:319
  16.1 21.1 %collective-permute-start.13 = (bf16[80,1280]{1,0:T(8,128)(2,1)S(1)}, bf16[80,1280]{1,0:T(8,128)(2,1)S(1)}, u32[]{:S(2)}, u32[]{:S(2)}) collective-permute-start(bf16[80,1280]{1,0:T(8,128)(2,1)S(1)} %get-tuple-element.25), channel_id=1, source_target_pairs={{0,3},{1,2},{2,1},{3,0},{4,7},{5,6},{6,5},{7,4},{8,11},{9,10},{10,... | collective-permute-start | bytes 614408 | tf_op jit(solution)/shard_map/ppermute | solution.py:319
  17.2 26.9 %collective-permute-start.12 = (bf16[160,1280]{1,0:T(8,128)(2,1)S(1)}, bf16[160,1280]{1,0:T(8,128)(2,1)S(1)}, u32[]{:S(2)}, u32[]{:S(2)}) collective-permute-start(bf16[160,1280]{1,0:T(8,128)(2,1)S(1)} %get-tuple-element.24), channel_id=1, source_target_pairs={{0,1},{1,0},{2,3},{3,2},{4,5},{5,4},{6,7},{7,6},{8,9},{9,8},{10,11... | collective-permute-start | bytes 1228808 | tf_op jit(solution)/shard_map/ppermute | solution.py:319
  31.0 21.4 %collective-permute-start.7 = (bf16[512,384]{1,0:T(8,128)(2,1)S(1)}, bf16[512,384]{1,0:T(8,128)(2,1)S(1)}, u32[]{:S(2)}, u32[]{:S(2)}) collective-permute-start(bf16[512,384]{1,0:T(8,128)(2,1)S(1)} %attend.2.refs_1_.refs_0_), channel_id=1, source_target_pairs={{0,1},{1,0},{2,3},{3,2},{4,5},{5,4},{6,7},{7,6},{8,9},{9,8},{10,11... | collective-permute-start | bytes 1179656 | tf_op jit(solution)/shard_map/ppermute | solution.py:347
  32.9 19.2 %collective-permute-start.8 = (bf16[512,384]{1,0:T(8,128)(2,1)S(1)}, bf16[512,384]{1,0:T(8,128)(2,1)S(1)}, u32[]{:S(2)}, u32[]{:S(2)}) collective-permute-start(bf16[512,384]{1,0:T(8,128)(2,1)S(1)} %attend.2.refs_1_.refs_0_), channel_id=1, source_target_pairs={{0,2},{1,3},{2,0},{3,1},{4,6},{5,7},{6,4},{7,5},{8,10},{9,11},{10,... | collective-permute-start | bytes 1179656 | tf_op jit(solution)/shard_map/ppermute | solution.py:348
  35.5 17.7 %collective-permute-start.6 = (bf16[1280,256]{1,0:T(8,128)(2,1)S(1)}, bf16[1280,256]{1,0:T(8,128)(2,1)S(1)}, u32[]{:S(2)}, u32[]{:S(2)}) collective-permute-start(bf16[1280,256]{1,0:T(8,128)(2,1)S(1)} %pack.1.refs_3_.refs_2_), channel_id=1, source_target_pairs={{0,4},{4,0},{1,5},{5,1},{2,6},{6,2},{3,7},{7,3},{8,12},{12,8},{9,1... | collective-permute-start | bytes 1966088 | tf_op jit(solution)/shard_map/ppermute | solution.py:363
  37.1 22.3 %collective-permute-start.15 = (bf16[160,1280]{1,0:T(8,128)(2,1)S(1)}, bf16[160,1280]{1,0:T(8,128)(2,1)S(1)}, u32[]{:S(2)}, u32[]{:S(2)}) collective-permute-start(bf16[160,1280]{1,0:T(8,128)(2,1)S(1)} %join_two.1), channel_id=1, source_target_pairs={{0,4},{4,0},{1,5},{5,1},{2,6},{6,2},{3,7},{7,3},{8,12},{12,8},{9,1... | collective-permute-start | bytes 1228808 | tf_op jit(solution)/shard_map/ppermute | solution.py:367
  44.1 15.3 %collective-permute-start.14 = (bf16[320,1280]{1,0:T(8,128)(2,1)S(1)}, bf16[320,1280]{1,0:T(8,128)(2,1)S(1)}, u32[]{:S(2)}, u32[]{:S(2)}) collective-permute-start(bf16[320,1280]{1,0:T(8,128)(2,1)S(1)} %join_all.1.refs_7_), channel_id=1, source_target_pairs={{0,16},{16,0},{8,24},{24,8},{1,17},{17,1},{9,25},{25,9},{2,18},{18... | collective-permute-start | bytes 2457608 | tf_op jit(solution)/shard_map/ppermute | solution.py:368
  52.1 16.6 %collective-permute-start.11 = (bf16[512,384]{1,0:T(8,128)(2,1)S(1)}, bf16[512,384]{1,0:T(8,128)(2,1)S(1)}, u32[]{:S(2)}, u32[]{:S(2)}) collective-permute-start(bf16[512,384]{1,0:T(8,128)(2,1)S(1)} %collective-permute-done.8.refs_1_.refs_4_), channel_id=1, source_target_pairs={{0,1},{1,0},{2,3},{3,2},{4,5},{5,4},{6,7},{7,6},{8,9},{9,8},{10,11... | collective-permute-start | bytes 1179656 | tf_op jit(solution)/shard_map/ppermute | solution.py:349
  55.7 12.9 %collective-permute-start.10 = (bf16[512,256]{1,0:T(8,128)(2,1)S(1)}, bf16[512,256]{1,0:T(8,128)(2,1)S(1)}, u32[]{:S(2)}, u32[]{:S(2)}) collective-permute-start(bf16[512,256]{1,0:T(8,128)(2,1)S(1)} %attend.3.refs_1_), channel_id=1, source_target_pairs={{0,2},{1,3},{2,0},{3,1},{4,6},{5,7},{6,4},{7,5},{8,10},{9,11},{10,... | collective-permute-start | bytes 786440 | tf_op jit(solution)/shard_map/ppermute | solution.py:348
  57.7 13.8 %collective-permute-start.9 = (bf16[512,256]{1,0:T(8,128)(2,1)S(1)}, bf16[512,256]{1,0:T(8,128)(2,1)S(1)}, u32[]{:S(2)}, u32[]{:S(2)}) collective-permute-start(bf16[512,256]{1,0:T(8,128)(2,1)S(1)} %attend.3.refs_1_), channel_id=1, source_target_pairs={{0,1},{1,0},{2,3},{3,2},{4,5},{5,4},{6,7},{7,6},{8,9},{9,8},{10,11... | collective-permute-start | bytes 786440 | tf_op jit(solution)/shard_map/ppermute | solution.py:347
  59.4 13.5 %collective-permute-start.17 = (bf16[320,1280]{1,0:T(8,128)(2,1)S(1)}, bf16[320,1280]{1,0:T(8,128)(2,1)S(1)}, u32[]{:S(2)}, u32[]{:S(2)}) collective-permute-start(bf16[320,1280]{1,0:T(8,128)(2,1)S(1)} %join_all.1.refs_7_), channel_id=1, source_target_pairs={{0,8},{8,0},{16,24},{24,16},{1,9},{9,1},{17,25},{25,17},{2,10},{10... | collective-permute-start | bytes 2457608 | tf_op jit(solution)/shard_map/ppermute | solution.py:378
  59.5 14.5 %copy-start = (f32[50,1280]{1,0:T(8,128)S(1)}, f32[50,1280]{1,0:T(8,128)}, u32[]{:S(2)}) copy-start(f32[50,1280]{1,0:T(8,128)} %gate_ref.1) | copy-start | bytes 768004
  59.5 14.4 %copy-start.1 = (s32[6]{0:T(128)S(1)}, s32[6]{0:T(128)}, u32[]{:S(2)}) copy-start(s32[6]{0:T(128)} %times.1) | copy-start | bytes 76
  59.5 12.0 %collective-permute-start.16 = (bf16[160,1280]{1,0:T(8,128)(2,1)S(1)}, bf16[160,1280]{1,0:T(8,128)(2,1)S(1)}, u32[]{:S(2)}, u32[]{:S(2)}) collective-permute-start(bf16[160,1280]{1,0:T(8,128)(2,1)S(1)} %hold.1.refs_0_), channel_id=1, source_target_pairs={{0,16},{16,0},{8,24},{24,8},{1,17},{17,1},{9,25},{25,9},{2,18},{18... | collective-permute-start | bytes 1228808 | tf_op jit(solution)/shard_map/ppermute | solution.py:373
  68.6 4.2 %collective-permute-start.18 = (bf16[320,1280]{1,0:T(8,128)(2,1)S(1)}, bf16[320,1280]{1,0:T(8,128)(2,1)S(1)}, u32[]{:S(2)}, u32[]{:S(2)}) collective-permute-start(bf16[320,1280]{1,0:T(8,128)(2,1)S(1)} %collective-permute-done.14.refs_2_.refs_8_), channel_id=1, source_target_pairs={{0,8},{8,0},{16,24},{24,16},{1,9},{9,1},{17,25},{25,17},{2,10},{10... | collective-permute-start | bytes 2457608 | tf_op jit(solution)/shard_map/ppermute | solution.py:378
  71.5 2.4 %collective-permute-start.19 = (bf16[320,1280]{1,0:T(8,128)(2,1)S(1)}, bf16[320,1280]{1,0:T(8,128)(2,1)S(1)}, u32[]{:S(2)}, u32[]{:S(2)}) collective-permute-start(bf16[320,1280]{1,0:T(8,128)(2,1)S(1)} %join_y.1.refs_9_), channel_id=1, source_target_pairs={{0,8},{8,0},{16,24},{24,16},{1,9},{9,1},{17,25},{25,17},{2,10},{10... | collective-permute-start | bytes 2457608 | tf_op jit(solution)/shard_map/ppermute | solution.py:378
  71.6 8.7 %collective-permute-start.20 = (bf16[512,256]{1,0:T(8,128)(2,1)S(1)}, bf16[512,256]{1,0:T(8,128)(2,1)S(1)}, u32[]{:S(2)}, u32[]{:S(2)}) collective-permute-start(bf16[512,256]{1,0:T(8,128)(2,1)S(1)} %collective-permute-done.10.refs_2_.refs_5_), channel_id=1, source_target_pairs={{0,1},{1,0},{2,3},{3,2},{4,5},{5,4},{6,7},{7,6},{8,9},{9,8},{10,11... | collective-permute-start | bytes 786440 | tf_op jit(solution)/shard_map/ppermute | solution.py:349

commit v6 on v5

--- a/solution.py
+++ b/solution.py
@@ -101,7 +101,7 @@
     packed_ref[half : half + rows, :] = k_ref[:, low:high]
     key_sums = row_sums(k_ref[...].astype(F32))
     stats_ref[...] = jnp.concatenate(
-        [query_sums, key_sums, moved_marks, marks, jnp.zeros((4, rows), F32)], axis=0
+        [query_sums, key_sums, moved_marks, marks, jnp.full((4, rows), me).astype(F32)], axis=0
     )
     copies[4].wait()
     packed_ref[half + rows :, :] = v_ref[:, low:high]
@@ -215,10 +215,10 @@
     for part in parts:
         rows_all[:, used : used + part.shape[1]] = part[...]
         used += part.shape[1]
-    gates_ref[...] = jnp.zeros(gates_ref.shape, BF16)
-    for video in range(times.shape[0]):
-        for index, piece in enumerate(three_pieces(gate_ref[pl.ds(times[video], 1), :])):
-            gates_ref[index * 16 + video : index * 16 + video + 1, :] = piece.astype(BF16)
+    chosen = [gate_ref[pl.ds(times[video], 1), :] for video in range(times.shape[0])]
+    chosen.append(jnp.zeros((16 - len(chosen), width), F32))
+    chosen = jnp.concatenate(chosen, axis=0)
+    gates_ref[...] = jnp.concatenate(three_pieces(chosen), axis=0).astype(BF16)
     for core in range(2):
         near, far, other = shares[3 * core : 3 * core + 3]
         pieces = [(near, 0, 0, 0), (far, 0, 0, 4)]
@@ -241,10 +241,10 @@
         total[:, block] = jnp.dot(rows_all[...], w_all[0:used, block], preferred_element_type=F32)
 
 
-def finish_kernel(place, near_ref, far_ref, total, tail_ref, gates_ref, late_ref, out_hbm, out_ref, sems):
+def finish_kernel(near_ref, far_ref, total, tail_ref, gates_ref, late_ref, out_hbm, out_ref, sems):
     rows, width = out_ref.shape
     half = rows // 2
-    me = place[0]
+    second = near_ref[4:5, 0:1] > 0.5
     videos = lax.rem(lax.broadcasted_iota(jnp.int32, (rows, gates_ref.shape[0]), 1), 16).astype(F32)
     marks = jnp.concatenate([near_ref[2:3, :half], far_ref[2:3, half:]], axis=1)
     picked = (column(marks) == 4.0 * videos).astype(BF16)
@@ -253,17 +253,11 @@
         block = slice(low, low + 256)
         gates = jnp.dot(picked, gates_ref[:, block], preferred_element_type=F32)
         mixed = total[:, block] + jnp.dot(late_ref[...], tail_ref[:, block], preferred_element_type=F32)
-        out_ref[:, block] = (mixed * gates).astype(BF16)
-        for part in range(2):
-            start = me * half if part == 0 else (1 - me) * half
-            copies.append(
-                pltpu.make_async_copy(
-                    out_ref.at[pl.ds(part * half, half), block],
-                    out_hbm.at[pl.ds(pl.multiple_of(start, half), half), block],
-                    sems.at[len(copies)],
-                )
-            )
-            copies[-1].start()
+        gated = mixed * gates
+        out_ref[0:half, block] = jnp.where(second, gated[half:], gated[:half]).astype(BF16)
+        out_ref[half:, block] = jnp.where(second, gated[:half], gated[half:]).astype(BF16)
+        copies.append(pltpu.make_async_copy(out_ref.at[:, block], out_hbm.at[:, block], sems.at[len(copies)]))
+        copies[-1].start()
     for copy in copies:
         copy.wait()
 
@@ -399,17 +393,17 @@
     )(place, timestep, gate_table, weight_hbm, *parts, *shares)
     return pl.pallas_call(
         finish_kernel,
-        in_specs=[SMEM] + [VMEM] * 6,
+        in_specs=[VMEM] * 6,
         out_specs=ANY,
         out_shape=jax.ShapeDtypeStruct((rows, out_width), BF16),
         scratch_shapes=[
             pltpu.VMEM((rows, out_width), BF16),
-            pltpu.SemaphoreType.DMA((2 * out_width // 256,)),
+            pltpu.SemaphoreType.DMA((out_width // 256,)),
         ],
         compiler_params=params(14),
         cost_estimate=cost(0),
         name="finish",
-    )(place, near, far, total, tail_weights, gates, last[3])
+    )(near, far, total, tail_weights, gates, last[3])
 
 
 def for_sending(array):

time: 82.9 us -> 82.3 us (level)
  no operation moved by 1% of the time
where the time goes in v6:
time: 82.3 us; the launch traced here: 82.2 us
  waiting for transfers between devices  41.6 us (51%)
  starting transfers between devices  24.8 us (30%)
  Pallas kernels  15.5 us (19%)
    ppermute x2, waiting for transfers between devices, spread(): three = lax.ppermute(two, 'head', xor_pairs(4, 1))  8.79 us
    ppermute x1, waiting for transfers between devices, fast_local(): far = lax.ppermute(near, 'ctx', SWAP_CTX)  8.31 us
    ppermute x2, waiting for transfers between devices, spread(): two = lax.ppermute(attended, 'head', xor_pairs(4, 2))  6.39 us
    ppermute x3, waiting for transfers between devices, fast_local(): lax.ppermute(cut_weights[s - 1], 'head', xor_pairs(4, s))  6.34 us
    pallas_call x2, Pallas kernels, attend(): pl.pallas_call(functools.partial(attend_kernel, cut, total_width), in_spe...  5.61 us
    ppermute x3, waiting for transfers between devices, fast_local(): lax.ppermute(stats, 'head', xor_pairs(4, step))  5.31 us
    pallas_call x1, Pallas kernels, fast_local(): pl.pallas_call(project_kernel, in_specs=[SMEM, SMEM, VMEM, HBM] + [VMEM]...  5.2 us
    ppermute x2, starting transfers between devices, spread(): two = lax.ppermute(attended, 'head', xor_pairs(4, 2))  4.51 us
  transfers between devices with their start and end apart: 21, of which 11 were waited for; matrix products, arithmetic and copies ran while one was open for 0% of the time, Pallas kernels for 13%

profile of v6, /device:TPU:0, one launch (start us, length us, event | category | flops | bytes accessed | tf_op | source)
XLA Modules:
  0.0 82.2 jit_solution(6878710806727869655)
XLA Ops:
  0.0 0.1 pad_add_fusion.place
  0.1 0.0 copy-start.2
  0.1 0.0 copy-start.3
  0.1 2.6 %prepare.1 = (bf16[256,640]{1,0:T(8,128)(2,1)S(1)}, bf16[256,640]{1,0:T(8,128)(2,1)S(1)}, bf16[1280,384]{1,0:T(8,128)(2,1)S(1)}, f32[8,512]{1,0:T(8,128)S(1)}, b...) custom-call(s32[4]{0:T(128)S(1)} %pad_add_fusion.place, ...), custom_call_target="tpu_custom_call" | custom-call | bytes 7200000 | tf_op jit(solution)/shard_map/prepare/pallas_call | solution.py:285
  2.7 3.0 %collective-permute-start.4 = (bf16[1280,384]{1,0:T(8,128)(2,1)S(1)}, bf16[1280,384]{1,0:T(8,128)(2,1)S(1)}, u32[]{:S(2)}, u32[]{:S(2)}) collective-permute-start(bf16[1280,384]{1,0:T(8,128)(2,1)S(1)} %get-tuple-element.21), channel_id=1, source_target_pairs={{0,4},{4,0},{1,5},{5,1},{2,6},{6,2},{3,7},{7,3},{8,12},{12,8},{9,1... | collective-permute-start | bytes 2949128 | tf_op jit(solution)/shard_map/ppermute | solution.py:314
  5.8 1.6 %collective-permute-start = (f32[8,512]{1,0:T(8,128)S(1)}, f32[8,512]{1,0:T(8,128)S(1)}, u32[]{:S(2)}, u32[]{:S(2)}) collective-permute-start(f32[8,512]{1,0:T(8,128)S(1)} %get-tuple-element.17.own_ref), channel_id=1, source_target_pairs={{0,1},{1,0},{2,3},{3,2},{4,5},{5,4},{6,7},{7,6},{8,9},{9,8},{10,11... | collective-permute-start | bytes 49160 | tf_op jit(solution)/shard_map/ppermute | solution.py:323
  7.3 2.6 %collective-permute-start.1 = (f32[8,512]{1,0:T(8,128)S(1)}, f32[8,512]{1,0:T(8,128)S(1)}, u32[]{:S(2)}, u32[]{:S(2)}) collective-permute-start(f32[8,512]{1,0:T(8,128)S(1)} %get-tuple-element.17.own_ref), channel_id=1, source_target_pairs={{0,2},{1,3},{2,0},{3,1},{4,6},{5,7},{6,4},{7,5},{8,10},{9,11},{10,... | collective-permute-start | bytes 49160 | tf_op jit(solution)/shard_map/ppermute | solution.py:323
  9.9 0.2 collective-permute-start.2
  10.2 0.0 collective-permute-done.one_ref
  10.2 1.9 %collective-permute-done.1.two_ref = f32[8,512]{1,0:T(8,128)S(1)} collective-permute-done((f32[8,512]{1,0:T(8,128)S(1)}, f32[8,512]{1,0:T(8,128)S(1)}, u32[]{:S(2)}, u32[]{:S(2)}) %collective-permute-start.1) | collective-permute-done | bytes 16416 | tf_op jit(solution)/shard_map/ppermute | solution.py:323
  12.0 3.4 %collective-permute-done.2.three_ref = f32[8,512]{1,0:T(8,128)S(1)} collective-permute-done((f32[8,512]{1,0:T(8,128)S(1)}, f32[8,512]{1,0:T(8,128)S(1)}, u32[]{:S(2)}, u32[]{:S(2)}) %collective-permute-start.2) | collective-permute-done | bytes 16416 | tf_op jit(solution)/shard_map/ppermute | solution.py:323
  15.5 0.6 collective-permute-start.3
  16.0 0.0 collective-permute-start.5
  16.1 1.1 %collective-permute-start.13 = (bf16[80,1280]{1,0:T(8,128)(2,1)S(1)}, bf16[80,1280]{1,0:T(8,128)(2,1)S(1)}, u32[]{:S(2)}, u32[]{:S(2)}) collective-permute-start(bf16[80,1280]{1,0:T(8,128)(2,1)S(1)} %get-tuple-element.25), channel_id=1, source_target_pairs={{0,3},{1,2},{2,1},{3,0},{4,7},{5,6},{6,5},{7,4},{8,11},{9,10},{10,... | collective-permute-start | bytes 614408 | tf_op jit(solution)/shard_map/ppermute | solution.py:313
  17.2 2.4 %collective-permute-start.12 = (bf16[160,1280]{1,0:T(8,128)(2,1)S(1)}, bf16[160,1280]{1,0:T(8,128)(2,1)S(1)}, u32[]{:S(2)}, u32[]{:S(2)}) collective-permute-start(bf16[160,1280]{1,0:T(8,128)(2,1)S(1)} %get-tuple-element.24), channel_id=1, source_target_pairs={{0,1},{1,0},{2,3},{3,2},{4,5},{5,4},{6,7},{7,6},{8,9},{9,8},{10,11... | collective-permute-start | bytes 1228808 | tf_op jit(solution)/shard_map/ppermute | solution.py:313
  19.5 0.0 copy-done.2
  19.5 0.0 copy-done.3
  19.6 8.3 %collective-permute-done.3.refs_0_.far_ref = f32[8,512]{1,0:T(8,128)S(1)} collective-permute-done((f32[8,512]{1,0:T(8,128)S(1)}, f32[8,512]{1,0:T(8,128)S(1)}, u32[]{:S(2)}, u32[]{:S(2)}) %collective-permute-start.3) | collective-permute-done | bytes 16416 | tf_op jit(solution)/shard_map/ppermute | solution.py:324
  27.9 0.0 collective-permute-done.4.refs_1_.remote_ref
  27.9 3.1 %attend.2.refs_1_.refs_0_ = bf16[512,384]{1,0:T(8,128)(2,1)S(1)} custom-call(f32[8,512]{1,0:T(8,128)S(1)} %settle.1.near_ref, f32[8,512]{1,0:T(8,128)S(1)} %collective-permute-done.3.refs_0_.far_ref, bf16[256,640]{1,0:T(8,128)(2,1)S(1)} %get-tuple-element.18.q_ref, bf16[512,640]{1,0:T(8,128)(2,1)S(1)} %get-tuple-element.19.k_ref, ...), custom_call_target="tpu_custom_call" | custom-call | bytes 28800000 | tf_op jit(solution)/shard_map/attend/pallas_call | solution.py:327
  31.0 1.9 %collective-permute-start.7 = (bf16[512,384]{1,0:T(8,128)(2,1)S(1)}, bf16[512,384]{1,0:T(8,128)(2,1)S(1)}, u32[]{:S(2)}, u32[]{:S(2)}) collective-permute-start(bf16[512,384]{1,0:T(8,128)(2,1)S(1)} %attend.2.refs_1_.refs_0_), channel_id=1, source_target_pairs={{0,1},{1,0},{2,3},{3,2},{4,5},{5,4},{6,7},{7,6},{8,9},{9,8},{10,11... | collective-permute-start | bytes 1179656 | tf_op jit(solution)/shard_map/ppermute | solution.py:341
  32.9 2.6 %collective-permute-start.8 = (bf16[512,384]{1,0:T(8,128)(2,1)S(1)}, bf16[512,384]{1,0:T(8,128)(2,1)S(1)}, u32[]{:S(2)}, u32[]{:S(2)}) collective-permute-start(bf16[512,384]{1,0:T(8,128)(2,1)S(1)} %attend.2.refs_1_.refs_0_), channel_id=1, source_target_pairs={{0,2},{1,3},{2,0},{3,1},{4,6},{5,7},{6,4},{7,5},{8,10},{9,11},{10,... | collective-permute-start | bytes 1179656 | tf_op jit(solution)/shard_map/ppermute | solution.py:342
  35.5 0.0 collective-permute-done.5.refs_0_.refs_1_
  35.5 1.6 %collective-permute-start.6 = (bf16[1280,256]{1,0:T(8,128)(2,1)S(1)}, bf16[1280,256]{1,0:T(8,128)(2,1)S(1)}, u32[]{:S(2)}, u32[]{:S(2)}) collective-permute-start(bf16[1280,256]{1,0:T(8,128)(2,1)S(1)} %pack.1.refs_3_.refs_2_), channel_id=1, source_target_pairs={{0,4},{4,0},{1,5},{5,1},{2,6},{6,2},{3,7},{7,3},{8,12},{12,8},{9,1... | collective-permute-start | bytes 1966088 | tf_op jit(solution)/shard_map/ppermute | solution.py:357
  37.1 0.0 collective-permute-done.13.refs_2_.refs_1_
  37.1 0.6 collective-permute-start.15
  37.7 6.3 %collective-permute-done.12.refs_0_ = bf16[160,1280]{1,0:T(8,128)(2,1)S(1)} collective-permute-done((bf16[160,1280]{1,0:T(8,128)(2,1)S(1)}, bf16[160,1280]{1,0:T(8,128)(2,1)S(1)}, u32[]{:S(2)}, u32[]{:S(2)}) %collective-permute-start.12) | collective-permute-done | bytes 409632 | tf_op jit(solution)/shard_map/ppermute | solution.py:313
  44.1 0.1 join_all.1.refs_7_
  44.1 1.6 %collective-permute-start.14 = (bf16[320,1280]{1,0:T(8,128)(2,1)S(1)}, bf16[320,1280]{1,0:T(8,128)(2,1)S(1)}, u32[]{:S(2)}, u32[]{:S(2)}) collective-permute-start(bf16[320,1280]{1,0:T(8,128)(2,1)S(1)} %join_all.1.refs_7_), channel_id=1, source_target_pairs={{0,16},{16,0},{8,24},{24,8},{1,17},{17,1},{9,25},{25,9},{2,18},{18... | collective-permute-start | bytes 2457608 | tf_op jit(solution)/shard_map/ppermute | solution.py:362
  45.7 6.4 %collective-permute-done.8.refs_1_.refs_4_ = bf16[512,384]{1,0:T(8,128)(2,1)S(1)} collective-permute-done((bf16[512,384]{1,0:T(8,128)(2,1)S(1)}, bf16[512,384]{1,0:T(8,128)(2,1)S(1)}, u32[]{:S(2)}, u32[]{:S(2)}) %collective-permute-start.8) | collective-permute-done | bytes 393248 | tf_op jit(solution)/shard_map/ppermute | solution.py:342
  52.1 0.3 collective-permute-start.11
  52.4 0.0 collective-permute-done.7.refs_0_.refs_2_
  52.4 0.8 %collective-permute-done.6.remote_ref = bf16[1280,256]{1,0:T(8,128)(2,1)S(1)} collective-permute-done((bf16[1280,256]{1,0:T(8,128)(2,1)S(1)}, bf16[1280,256]{1,0:T(8,128)(2,1)S(1)}, u32[]{:S(2)}, u32[]{:S(2)}) %collective-permute-start.6) | collective-permute-done | bytes 655392 | tf_op jit(solution)/shard_map/ppermute | solution.py:357
  53.3 2.5 %attend.3.refs_1_ = bf16[512,256]{1,0:T(8,128)(2,1)S(1)} custom-call(f32[8,512]{1,0:T(8,128)S(1)} %settle.1.near_ref, f32[8,512]{1,0:T(8,128)S(1)} %collective-permute-done.3.refs_0_.far_ref, bf16[256,640]{1,0:T(8,128)(2,1)S(1)} %get-tuple-element.18.q_ref, bf16[512,640]{1,0:T(8,128)(2,1)S(1)} %get-tuple-element.19.k_ref, ...), custom_call_target="tpu_custom_call" | custom-call | bytes 28800000 | tf_op jit(solution)/shard_map/attend/pallas_call | solution.py:327
  55.7 1.9 %collective-permute-start.10 = (bf16[512,256]{1,0:T(8,128)(2,1)S(1)}, bf16[512,256]{1,0:T(8,128)(2,1)S(1)}, u32[]{:S(2)}, u32[]{:S(2)}) collective-permute-start(bf16[512,256]{1,0:T(8,128)(2,1)S(1)} %attend.3.refs_1_), channel_id=1, source_target_pairs={{0,2},{1,3},{2,0},{3,1},{4,6},{5,7},{6,4},{7,5},{8,10},{9,11},{10,... | collective-permute-start | bytes 786440 | tf_op jit(solution)/shard_map/ppermute | solution.py:342
  57.7 0.0 collective-permute-start.9
  57.7 1.7 %collective-permute-done.15.refs_0_ = bf16[160,1280]{1,0:T(8,128)(2,1)S(1)} collective-permute-done((bf16[160,1280]{1,0:T(8,128)(2,1)S(1)}, bf16[160,1280]{1,0:T(8,128)(2,1)S(1)}, u32[]{:S(2)}, u32[]{:S(2)}) %collective-permute-start.15) | collective-permute-done | bytes 409632 | tf_op jit(solution)/shard_map/ppermute | solution.py:361
  59.4 0.0 collective-permute-start.17
  59.4 0.0 collective-permute-done.14.refs_2_.refs_8_
  59.5 0.0 copy-start
  59.5 0.0 copy-start.1
  59.5 1.6 %collective-permute-start.16 = (bf16[160,1280]{1,0:T(8,128)(2,1)S(1)}, bf16[160,1280]{1,0:T(8,128)(2,1)S(1)}, u32[]{:S(2)}, u32[]{:S(2)}) collective-permute-start(bf16[160,1280]{1,0:T(8,128)(2,1)S(1)} %hold.1.refs_0_), channel_id=1, source_target_pairs={{0,16},{16,0},{8,24},{24,8},{1,17},{17,1},{9,25},{25,9},{2,18},{18... | collective-permute-start | bytes 1228808 | tf_op jit(solution)/shard_map/ppermute | solution.py:367
  61.0 7.6 %collective-permute-done.11.refs_0_.refs_6_ = bf16[512,384]{1,0:T(8,128)(2,1)S(1)} collective-permute-done((bf16[512,384]{1,0:T(8,128)(2,1)S(1)}, bf16[512,384]{1,0:T(8,128)(2,1)S(1)}, u32[]{:S(2)}, u32[]{:S(2)}) %collective-permute-start.11) | collective-permute-done | bytes 393248 | tf_op jit(solution)/shard_map/ppermute | solution.py:343
  68.6 0.0 collective-permute-start.18
  68.6 0.0 collective-permute-done.10.refs_2_.refs_5_
  68.6 2.8 %collective-permute-done.9.refs_1_.refs_3_ = bf16[512,256]{1,0:T(8,128)(2,1)S(1)} collective-permute-done((bf16[512,256]{1,0:T(8,128)(2,1)S(1)}, bf16[512,256]{1,0:T(8,128)(2,1)S(1)}, u32[]{:S(2)}, u32[]{:S(2)}) %collective-permute-start.9) | collective-permute-done | bytes 262176 | tf_op jit(solution)/shard_map/ppermute | solution.py:341
  71.5 0.0 collective-permute-done.16.refs_1_
  71.5 0.1 join_y.1.refs_9_
  71.5 0.1 collective-permute-start.19
  71.6 1.3 %collective-permute-start.20 = (bf16[512,256]{1,0:T(8,128)(2,1)S(1)}, bf16[512,256]{1,0:T(8,128)(2,1)S(1)}, u32[]{:S(2)}, u32[]{:S(2)}) collective-permute-start(bf16[512,256]{1,0:T(8,128)(2,1)S(1)} %collective-permute-done.10.refs_2_.refs_5_), channel_id=1, source_target_pairs={{0,1},{1,0},{2,3},{3,2},{4,5},{5,4},{6,7},{7,6},{8,9},{9,8},{10,11... | collective-permute-start | bytes 786440 | tf_op jit(solution)/shard_map/ppermute | solution.py:343
  72.9 0.0 collective-permute-done.17.refs_10_
  72.9 0.0 collective-permute-done.18.refs_11_
  72.9 1.0 %collective-permute-done.19.refs_12_ = bf16[320,1280]{1,0:T(8,128)(2,1)S(1)} collective-permute-done((bf16[320,1280]{1,0:T(8,128)(2,1)S(1)}, bf16[320,1280]{1,0:T(8,128)(2,1)S(1)}, u32[]{:S(2)}, u32[]{:S(2)}) %collective-permute-start.19) | collective-permute-done | bytes 819232 | tf_op jit(solution)/shard_map/ppermute | solution.py:372
  73.9 0.0 copy-done
  73.9 0.0 copy-done.1
  73.9 5.2 %project.1 = (f32[512,1280]{1,0:T(8,128)S(1)}, bf16[256,1280]{1,0:T(8,128)(2,1)S(1)}, bf16[48,1280]{1,0:T(8,128)(2,1)S(1)}) custom-call(s32[4]{0:T(128)S(1)} %pad_add_fusion.place, s32[6]{0:T(128)S(1)} %copy-done.1, f32[50,1280]{1,0:T(8,128)S(1)} %copy-done, bf16[640,5120]{1,0:T(8,128)(2,1)} %weight_ref.3, bf16[512,384]{1,0:T(8,128)(2,1)S(1)} %attend.2.refs_1_.refs_0_, ...), custom_call_target="tpu_custom_call" | custom-call | tf_op jit(solution)/shard_map/project/pallas_call | solution.py:376
  79.1 1.2 %collective-permute-done.20.late_ref = bf16[512,256]{1,0:T(8,128)(2,1)S(1)} collective-permute-done((bf16[512,256]{1,0:T(8,128)(2,1)S(1)}, bf16[512,256]{1,0:T(8,128)(2,1)S(1)}, u32[]{:S(2)}, u32[]{:S(2)}) %collective-permute-start.20) | collective-permute-done | bytes 262176 | tf_op jit(solution)/shard_map/ppermute | solution.py:343
  80.3 1.9 %finish.1 = bf16[512,1280]{1,0:T(8,128)(2,1)} custom-call(f32[8,512]{1,0:T(8,128)S(1)} %settle.1.near_ref, f32[8,512]{1,0:T(8,128)S(1)} %collective-permute-done.3.refs_0_.far_ref, f32[512,1280]{1,0:T(8,128)S(1)} %get-tuple-element.26.total, bf16[256,1280]{1,0:T(8,128)(2,1)S(1)} %get-tuple-element.27.tail_ref, ...), custom_call_target="tpu_custom_call" | custom-call | tf_op jit(solution)/shard_map/finish/pallas_call | solution.py:394
  (10 shorter events, 0.1 us)
Async XLA Ops:
  0.1 19.5 %copy-start.2 = (f32[640]{0:T(1024)S(1)}, f32[640]{0:T(1024)}, u32[]{:S(2)}) copy-start(f32[640]{0:T(1024)} %param.13) | copy-start | bytes 7684
  0.1 19.5 %copy-start.3 = (f32[640]{0:T(1024)S(1)}, f32[640]{0:T(1024)}, u32[]{:S(2)}) copy-start(f32[640]{0:T(1024)} %param.14) | copy-start | bytes 7684
  2.7 25.1 %collective-permute-start.4 = (bf16[1280,384]{1,0:T(8,128)(2,1)S(1)}, bf16[1280,384]{1,0:T(8,128)(2,1)S(1)}, u32[]{:S(2)}, u32[]{:S(2)}) collective-permute-start(bf16[1280,384]{1,0:T(8,128)(2,1)S(1)} %get-tuple-element.21), channel_id=1, source_target_pairs={{0,4},{4,0},{1,5},{5,1},{2,6},{6,2},{3,7},{7,3},{8,12},{12,8},{9,1... | collective-permute-start | bytes 2949128 | tf_op jit(solution)/shard_map/ppermute | solution.py:314
  5.8 4.4 %collective-permute-start = (f32[8,512]{1,0:T(8,128)S(1)}, f32[8,512]{1,0:T(8,128)S(1)}, u32[]{:S(2)}, u32[]{:S(2)}) collective-permute-start(f32[8,512]{1,0:T(8,128)S(1)} %get-tuple-element.17.own_ref), channel_id=1, source_target_pairs={{0,1},{1,0},{2,3},{3,2},{4,5},{5,4},{6,7},{7,6},{8,9},{9,8},{10,11... | collective-permute-start | bytes 49160 | tf_op jit(solution)/shard_map/ppermute | solution.py:323
  7.3 4.7 %collective-permute-start.1 = (f32[8,512]{1,0:T(8,128)S(1)}, f32[8,512]{1,0:T(8,128)S(1)}, u32[]{:S(2)}, u32[]{:S(2)}) collective-permute-start(f32[8,512]{1,0:T(8,128)S(1)} %get-tuple-element.17.own_ref), channel_id=1, source_target_pairs={{0,2},{1,3},{2,0},{3,1},{4,6},{5,7},{6,4},{7,5},{8,10},{9,11},{10,... | collective-permute-start | bytes 49160 | tf_op jit(solution)/shard_map/ppermute | solution.py:323
  9.9 5.5 %collective-permute-start.2 = (f32[8,512]{1,0:T(8,128)S(1)}, f32[8,512]{1,0:T(8,128)S(1)}, u32[]{:S(2)}, u32[]{:S(2)}) collective-permute-start(f32[8,512]{1,0:T(8,128)S(1)} %get-tuple-element.17.own_ref), channel_id=1, source_target_pairs={{0,3},{1,2},{2,1},{3,0},{4,7},{5,6},{6,5},{7,4},{8,11},{9,10},{10,... | collective-permute-start | bytes 49160 | tf_op jit(solution)/shard_map/ppermute | solution.py:323
  15.5 12.4 %collective-permute-start.3 = (f32[8,512]{1,0:T(8,128)S(1)}, f32[8,512]{1,0:T(8,128)S(1)}, u32[]{:S(2)}, u32[]{:S(2)}) collective-permute-start(f32[8,512]{1,0:T(8,128)S(1)} %settle.1.near_ref), channel_id=1, source_target_pairs={{0,4},{4,0},{1,5},{5,1},{2,6},{6,2},{3,7},{7,3},{8,12},{12,8},{9,1... | collective-permute-start | bytes 49160 | tf_op jit(solution)/shard_map/ppermute | solution.py:324
  16.0 19.4 %collective-permute-start.5 = (bf16[80,1280]{1,0:T(8,128)(2,1)S(1)}, bf16[80,1280]{1,0:T(8,128)(2,1)S(1)}, u32[]{:S(2)}, u32[]{:S(2)}) collective-permute-start(bf16[80,1280]{1,0:T(8,128)(2,1)S(1)} %get-tuple-element.23), channel_id=1, source_target_pairs={{0,2},{1,3},{2,0},{3,1},{4,6},{5,7},{6,4},{7,5},{8,10},{9,11},{10,... | collective-permute-start | bytes 614408 | tf_op jit(solution)/shard_map/ppermute | solution.py:313
  16.1 21.1 %collective-permute-start.13 = (bf16[80,1280]{1,0:T(8,128)(2,1)S(1)}, bf16[80,1280]{1,0:T(8,128)(2,1)S(1)}, u32[]{:S(2)}, u32[]{:S(2)}) collective-permute-start(bf16[80,1280]{1,0:T(8,128)(2,1)S(1)} %get-tuple-element.25), channel_id=1, source_target_pairs={{0,3},{1,2},{2,1},{3,0},{4,7},{5,6},{6,5},{7,4},{8,11},{9,10},{10,... | collective-permute-start | bytes 614408 | tf_op jit(solution)/shard_map/ppermute | solution.py:313
  17.2 26.9 %collective-permute-start.12 = (bf16[160,1280]{1,0:T(8,128)(2,1)S(1)}, bf16[160,1280]{1,0:T(8,128)(2,1)S(1)}, u32[]{:S(2)}, u32[]{:S(2)}) collective-permute-start(bf16[160,1280]{1,0:T(8,128)(2,1)S(1)} %get-tuple-element.24), channel_id=1, source_target_pairs={{0,1},{1,0},{2,3},{3,2},{4,5},{5,4},{6,7},{7,6},{8,9},{9,8},{10,11... | collective-permute-start | bytes 1228808 | tf_op jit(solution)/shard_map/ppermute | solution.py:313
  31.0 21.4 %collective-permute-start.7 = (bf16[512,384]{1,0:T(8,128)(2,1)S(1)}, bf16[512,384]{1,0:T(8,128)(2,1)S(1)}, u32[]{:S(2)}, u32[]{:S(2)}) collective-permute-start(bf16[512,384]{1,0:T(8,128)(2,1)S(1)} %attend.2.refs_1_.refs_0_), channel_id=1, source_target_pairs={{0,1},{1,0},{2,3},{3,2},{4,5},{5,4},{6,7},{7,6},{8,9},{9,8},{10,11... | collective-permute-start | bytes 1179656 | tf_op jit(solution)/shard_map/ppermute | solution.py:341
  32.9 19.2 %collective-permute-start.8 = (bf16[512,384]{1,0:T(8,128)(2,1)S(1)}, bf16[512,384]{1,0:T(8,128)(2,1)S(1)}, u32[]{:S(2)}, u32[]{:S(2)}) collective-permute-start(bf16[512,384]{1,0:T(8,128)(2,1)S(1)} %attend.2.refs_1_.refs_0_), channel_id=1, source_target_pairs={{0,2},{1,3},{2,0},{3,1},{4,6},{5,7},{6,4},{7,5},{8,10},{9,11},{10,... | collective-permute-start | bytes 1179656 | tf_op jit(solution)/shard_map/ppermute | solution.py:342
  35.5 17.7 %collective-permute-start.6 = (bf16[1280,256]{1,0:T(8,128)(2,1)S(1)}, bf16[1280,256]{1,0:T(8,128)(2,1)S(1)}, u32[]{:S(2)}, u32[]{:S(2)}) collective-permute-start(bf16[1280,256]{1,0:T(8,128)(2,1)S(1)} %pack.1.refs_3_.refs_2_), channel_id=1, source_target_pairs={{0,4},{4,0},{1,5},{5,1},{2,6},{6,2},{3,7},{7,3},{8,12},{12,8},{9,1... | collective-permute-start | bytes 1966088 | tf_op jit(solution)/shard_map/ppermute | solution.py:357
  37.1 22.3 %collective-permute-start.15 = (bf16[160,1280]{1,0:T(8,128)(2,1)S(1)}, bf16[160,1280]{1,0:T(8,128)(2,1)S(1)}, u32[]{:S(2)}, u32[]{:S(2)}) collective-permute-start(bf16[160,1280]{1,0:T(8,128)(2,1)S(1)} %join_two.1), channel_id=1, source_target_pairs={{0,4},{4,0},{1,5},{5,1},{2,6},{6,2},{3,7},{7,3},{8,12},{12,8},{9,1... | collective-permute-start | bytes 1228808 | tf_op jit(solution)/shard_map/ppermute | solution.py:361
  44.1 15.3 %collective-permute-start.14 = (bf16[320,1280]{1,0:T(8,128)(2,1)S(1)}, bf16[320,1280]{1,0:T(8,128)(2,1)S(1)}, u32[]{:S(2)}, u32[]{:S(2)}) collective-permute-start(bf16[320,1280]{1,0:T(8,128)(2,1)S(1)} %join_all.1.refs_7_), channel_id=1, source_target_pairs={{0,16},{16,0},{8,24},{24,8},{1,17},{17,1},{9,25},{25,9},{2,18},{18... | collective-permute-start | bytes 2457608 | tf_op jit(solution)/shard_map/ppermute | solution.py:362
  52.1 16.6 %collective-permute-start.11 = (bf16[512,384]{1,0:T(8,128)(2,1)S(1)}, bf16[512,384]{1,0:T(8,128)(2,1)S(1)}, u32[]{:S(2)}, u32[]{:S(2)}) collective-permute-start(bf16[512,384]{1,0:T(8,128)(2,1)S(1)} %collective-permute-done.8.refs_1_.refs_4_), channel_id=1, source_target_pairs={{0,1},{1,0},{2,3},{3,2},{4,5},{5,4},{6,7},{7,6},{8,9},{9,8},{10,11... | collective-permute-start | bytes 1179656 | tf_op jit(solution)/shard_map/ppermute | solution.py:343
  55.7 12.9 %collective-permute-start.10 = (bf16[512,256]{1,0:T(8,128)(2,1)S(1)}, bf16[512,256]{1,0:T(8,128)(2,1)S(1)}, u32[]{:S(2)}, u32[]{:S(2)}) collective-permute-start(bf16[512,256]{1,0:T(8,128)(2,1)S(1)} %attend.3.refs_1_), channel_id=1, source_target_pairs={{0,2},{1,3},{2,0},{3,1},{4,6},{5,7},{6,4},{7,5},{8,10},{9,11},{10,... | collective-permute-start | bytes 786440 | tf_op jit(solution)/shard_map/ppermute | solution.py:342
  57.7 13.8 %collective-permute-start.9 = (bf16[512,256]{1,0:T(8,128)(2,1)S(1)}, bf16[512,256]{1,0:T(8,128)(2,1)S(1)}, u32[]{:S(2)}, u32[]{:S(2)}) collective-permute-start(bf16[512,256]{1,0:T(8,128)(2,1)S(1)} %attend.3.refs_1_), channel_id=1, source_target_pairs={{0,1},{1,0},{2,3},{3,2},{4,5},{5,4},{6,7},{7,6},{8,9},{9,8},{10,11... | collective-permute-start | bytes 786440 | tf_op jit(solution)/shard_map/ppermute | solution.py:341
  59.4 13.5 %collective-permute-start.17 = (bf16[320,1280]{1,0:T(8,128)(2,1)S(1)}, bf16[320,1280]{1,0:T(8,128)(2,1)S(1)}, u32[]{:S(2)}, u32[]{:S(2)}) collective-permute-start(bf16[320,1280]{1,0:T(8,128)(2,1)S(1)} %join_all.1.refs_7_), channel_id=1, source_target_pairs={{0,8},{8,0},{16,24},{24,16},{1,9},{9,1},{17,25},{25,17},{2,10},{10... | collective-permute-start | bytes 2457608 | tf_op jit(solution)/shard_map/ppermute | solution.py:372
  59.5 14.5 %copy-start = (f32[50,1280]{1,0:T(8,128)S(1)}, f32[50,1280]{1,0:T(8,128)}, u32[]{:S(2)}) copy-start(f32[50,1280]{1,0:T(8,128)} %gate_ref.1) | copy-start | bytes 768004
  59.5 14.4 %copy-start.1 = (s32[6]{0:T(128)S(1)}, s32[6]{0:T(128)}, u32[]{:S(2)}) copy-start(s32[6]{0:T(128)} %times.1) | copy-start | bytes 76
  59.5 12.0 %collective-permute-start.16 = (bf16[160,1280]{1,0:T(8,128)(2,1)S(1)}, bf16[160,1280]{1,0:T(8,128)(2,1)S(1)}, u32[]{:S(2)}, u32[]{:S(2)}) collective-permute-start(bf16[160,1280]{1,0:T(8,128)(2,1)S(1)} %hold.1.refs_0_), channel_id=1, source_target_pairs={{0,16},{16,0},{8,24},{24,8},{1,17},{17,1},{9,25},{25,9},{2,18},{18... | collective-permute-start | bytes 1228808 | tf_op jit(solution)/shard_map/ppermute | solution.py:367
  68.6 4.2 %collective-permute-start.18 = (bf16[320,1280]{1,0:T(8,128)(2,1)S(1)}, bf16[320,1280]{1,0:T(8,128)(2,1)S(1)}, u32[]{:S(2)}, u32[]{:S(2)}) collective-permute-start(bf16[320,1280]{1,0:T(8,128)(2,1)S(1)} %collective-permute-done.14.refs_2_.refs_8_), channel_id=1, source_target_pairs={{0,8},{8,0},{16,24},{24,16},{1,9},{9,1},{17,25},{25,17},{2,10},{10... | collective-permute-start | bytes 2457608 | tf_op jit(solution)/shard_map/ppermute | solution.py:372
  71.5 2.4 %collective-permute-start.19 = (bf16[320,1280]{1,0:T(8,128)(2,1)S(1)}, bf16[320,1280]{1,0:T(8,128)(2,1)S(1)}, u32[]{:S(2)}, u32[]{:S(2)}) collective-permute-start(bf16[320,1280]{1,0:T(8,128)(2,1)S(1)} %join_y.1.refs_9_), channel_id=1, source_target_pairs={{0,8},{8,0},{16,24},{24,16},{1,9},{9,1},{17,25},{25,17},{2,10},{10... | collective-permute-start | bytes 2457608 | tf_op jit(solution)/shard_map/ppermute | solution.py:372
  71.6 8.7 %collective-permute-start.20 = (bf16[512,256]{1,0:T(8,128)(2,1)S(1)}, bf16[512,256]{1,0:T(8,128)(2,1)S(1)}, u32[]{:S(2)}, u32[]{:S(2)}) collective-permute-start(bf16[512,256]{1,0:T(8,128)(2,1)S(1)} %collective-permute-done.10.refs_2_.refs_5_), channel_id=1, source_target_pairs={{0,1},{1,0},{2,3},{3,2},{4,5},{5,4},{6,7},{7,6},{8,9},{9,8},{10,11... | collective-permute-start | bytes 786440 | tf_op jit(solution)/shard_map/ppermute | solution.py:343

commit v7 on v6

--- a/solution.py
+++ b/solution.py
@@ -64,21 +64,22 @@
 
 
 def prepare_kernel(
-    cut, place, q_hbm, k_hbm, v_hbm, dest_hbm, seg_hbm, weight_ref,
+    cut, after_ref, q_hbm, k_hbm, v_hbm, dest_hbm, seg_hbm, weight_ref,
     own_ref, other_ref, packed_ref, stats_ref, k_ref, v_ref, one_ref, two_ref, three_ref,
     q_ref, dest_ref, seg_ref, sems,
 ):
+    me, head, batch = lax.axis_index("ctx"), lax.axis_index("head"), lax.axis_index("batch")
+    mine = batch * 2 + me
     pairs = [(dest_hbm, dest_ref), (seg_hbm, seg_ref), (q_hbm, q_ref), (k_hbm, k_ref), (v_hbm, v_ref)]
-    for step, (ref, index) in enumerate(((one_ref, place[3]), (two_ref, place[2]), (three_ref, place[2]))):
+    for step, (ref, index) in enumerate(((one_ref, batch), (two_ref, mine), (three_ref, mine))):
         count, columns = ref.shape
         first = pl.multiple_of(index * count, count)
-        start = pl.multiple_of((place[1] ^ (step + 1)) * columns, columns)
+        start = pl.multiple_of((head ^ (step + 1)) * columns, columns)
         pairs.append((weight_ref.at[pl.ds(first, count), pl.ds(start, columns)], ref))
     copies = load(pairs, sems)
     rows = q_ref.shape[0]
     half = rows // 2
     low, high = cut
-    me = place[0]
     copies[0].wait()
     copies[1].wait()
     dest = dest_ref[...]
@@ -284,7 +285,7 @@
 
     own_queries, other_queries, packed, stats, keys, values, *cut_weights = pl.pallas_call(
         functools.partial(prepare_kernel, cuts[0]),
-        in_specs=[SMEM] + [HBM] * 6,
+        in_specs=[ANY] + [HBM] * 6,
         out_specs=[VMEM] * 9,
         out_shape=[
             jax.ShapeDtypeStruct((half, width), BF16),

time: 82.3 us -> 81.8 us (level)
  no operation moved by 1% of the time
where the time goes in v7:
time: 81.8 us; the launch traced here: 81.7 us
  waiting for transfers between devices  41.6 us (51%)
  starting transfers between devices  24.8 us (30%)
  Pallas kernels  15 us (18%)
    ppermute x2, waiting for transfers between devices, spread(): three = lax.ppermute(two, 'head', xor_pairs(4, 1))  8.79 us
    ppermute x1, waiting for transfers between devices, fast_local(): far = lax.ppermute(near, 'ctx', SWAP_CTX)  8.31 us
    ppermute x2, waiting for transfers between devices, spread(): two = lax.ppermute(attended, 'head', xor_pairs(4, 2))  6.38 us
    ppermute x3, waiting for transfers between devices, fast_local(): lax.ppermute(cut_weights[s - 1], 'head', xor_pairs(4, s))  6.34 us
    pallas_call x2, Pallas kernels, attend(): pl.pallas_call(functools.partial(attend_kernel, cut, total_width), in_spe...  5.6 us
    ppermute x3, waiting for transfers between devices, fast_local(): lax.ppermute(stats, 'head', xor_pairs(4, step))  5.31 us
    pallas_call x1, Pallas kernels, fast_local(): pl.pallas_call(project_kernel, in_specs=[SMEM, SMEM, VMEM, HBM] + [VMEM]...  5.2 us
    ppermute x2, starting transfers between devices, spread(): two = lax.ppermute(attended, 'head', xor_pairs(4, 2))  4.52 us
  transfers between devices with their start and end apart: 21, of which 11 were waited for; matrix products, arithmetic and copies ran while one was open for 0% of the time, Pallas kernels for 13%

profile of v7, /device:TPU:0, one launch (start us, length us, event | category | flops | bytes accessed | tf_op | source)
XLA Modules:
  0.0 81.7 jit_solution(17557518881414833240)
XLA Ops:
  0.0 0.1 pad_add_fusion.after_ref.place
  0.1 0.0 copy-start.2
  0.1 0.0 copy-start.3
  0.1 2.1 %prepare.1 = (bf16[256,640]{1,0:T(8,128)(2,1)S(1)}, bf16[256,640]{1,0:T(8,128)(2,1)S(1)}, bf16[1280,384]{1,0:T(8,128)(2,1)S(1)}, f32[8,512]{1,0:T(8,128)S(1)}, b...) custom-call(s32[4]{0:T(128)S(1)} %pad_add_fusion.after_ref.place, ...), custom_call_target="tpu_custom_call" | custom-call | bytes 7200000 | tf_op jit(solution)/shard_map/prepare/pallas_call | solution.py:286
  2.2 3.0 %collective-permute-start.4 = (bf16[1280,384]{1,0:T(8,128)(2,1)S(1)}, bf16[1280,384]{1,0:T(8,128)(2,1)S(1)}, u32[]{:S(2)}, u32[]{:S(2)}) collective-permute-start(bf16[1280,384]{1,0:T(8,128)(2,1)S(1)} %get-tuple-element.21), channel_id=1, source_target_pairs={{0,4},{4,0},{1,5},{5,1},{2,6},{6,2},{3,7},{7,3},{8,12},{12,8},{9,1... | collective-permute-start | bytes 2949128 | tf_op jit(solution)/shard_map/ppermute | solution.py:315
  5.3 1.6 %collective-permute-start = (f32[8,512]{1,0:T(8,128)S(1)}, f32[8,512]{1,0:T(8,128)S(1)}, u32[]{:S(2)}, u32[]{:S(2)}) collective-permute-start(f32[8,512]{1,0:T(8,128)S(1)} %get-tuple-element.17.own_ref), channel_id=1, source_target_pairs={{0,1},{1,0},{2,3},{3,2},{4,5},{5,4},{6,7},{7,6},{8,9},{9,8},{10,11... | collective-permute-start | bytes 49160 | tf_op jit(solution)/shard_map/ppermute | solution.py:324
  6.8 2.6 %collective-permute-start.1 = (f32[8,512]{1,0:T(8,128)S(1)}, f32[8,512]{1,0:T(8,128)S(1)}, u32[]{:S(2)}, u32[]{:S(2)}) collective-permute-start(f32[8,512]{1,0:T(8,128)S(1)} %get-tuple-element.17.own_ref), channel_id=1, source_target_pairs={{0,2},{1,3},{2,0},{3,1},{4,6},{5,7},{6,4},{7,5},{8,10},{9,11},{10,... | collective-permute-start | bytes 49160 | tf_op jit(solution)/shard_map/ppermute | solution.py:324
  9.4 0.2 collective-permute-start.2
  9.6 0.0 collective-permute-done.one_ref
  9.6 1.9 %collective-permute-done.1.two_ref = f32[8,512]{1,0:T(8,128)S(1)} collective-permute-done((f32[8,512]{1,0:T(8,128)S(1)}, f32[8,512]{1,0:T(8,128)S(1)}, u32[]{:S(2)}, u32[]{:S(2)}) %collective-permute-start.1) | collective-permute-done | bytes 16416 | tf_op jit(solution)/shard_map/ppermute | solution.py:324
  11.5 3.4 %collective-permute-done.2.three_ref = f32[8,512]{1,0:T(8,128)S(1)} collective-permute-done((f32[8,512]{1,0:T(8,128)S(1)}, f32[8,512]{1,0:T(8,128)S(1)}, u32[]{:S(2)}, u32[]{:S(2)}) %collective-permute-start.2) | collective-permute-done | bytes 16416 | tf_op jit(solution)/shard_map/ppermute | solution.py:324
  15.0 0.6 collective-permute-start.3
  15.5 0.0 collective-permute-start.5
  15.5 1.1 %collective-permute-start.13 = (bf16[80,1280]{1,0:T(8,128)(2,1)S(1)}, bf16[80,1280]{1,0:T(8,128)(2,1)S(1)}, u32[]{:S(2)}, u32[]{:S(2)}) collective-permute-start(bf16[80,1280]{1,0:T(8,128)(2,1)S(1)} %get-tuple-element.25), channel_id=1, source_target_pairs={{0,3},{1,2},{2,1},{3,0},{4,7},{5,6},{6,5},{7,4},{8,11},{9,10},{10,... | collective-permute-start | bytes 614408 | tf_op jit(solution)/shard_map/ppermute | solution.py:314
  16.7 2.4 %collective-permute-start.12 = (bf16[160,1280]{1,0:T(8,128)(2,1)S(1)}, bf16[160,1280]{1,0:T(8,128)(2,1)S(1)}, u32[]{:S(2)}, u32[]{:S(2)}) collective-permute-start(bf16[160,1280]{1,0:T(8,128)(2,1)S(1)} %get-tuple-element.24), channel_id=1, source_target_pairs={{0,1},{1,0},{2,3},{3,2},{4,5},{5,4},{6,7},{7,6},{8,9},{9,8},{10,11... | collective-permute-start | bytes 1228808 | tf_op jit(solution)/shard_map/ppermute | solution.py:314
  19.0 0.0 copy-done.2
  19.0 0.0 copy-done.3
  19.0 8.3 %collective-permute-done.3.refs_0_.far_ref = f32[8,512]{1,0:T(8,128)S(1)} collective-permute-done((f32[8,512]{1,0:T(8,128)S(1)}, f32[8,512]{1,0:T(8,128)S(1)}, u32[]{:S(2)}, u32[]{:S(2)}) %collective-permute-start.3) | collective-permute-done | bytes 16416 | tf_op jit(solution)/shard_map/ppermute | solution.py:325
  27.4 0.0 collective-permute-done.4.refs_1_.remote_ref
  27.4 3.1 %attend.2.refs_1_.refs_0_ = bf16[512,384]{1,0:T(8,128)(2,1)S(1)} custom-call(f32[8,512]{1,0:T(8,128)S(1)} %settle.1.near_ref, f32[8,512]{1,0:T(8,128)S(1)} %collective-permute-done.3.refs_0_.far_ref, bf16[256,640]{1,0:T(8,128)(2,1)S(1)} %get-tuple-element.18.q_ref, bf16[512,640]{1,0:T(8,128)(2,1)S(1)} %get-tuple-element.19.k_ref, ...), custom_call_target="tpu_custom_call" | custom-call | bytes 28800000 | tf_op jit(solution)/shard_map/attend/pallas_call | solution.py:328
  30.5 1.9 %collective-permute-start.7 = (bf16[512,384]{1,0:T(8,128)(2,1)S(1)}, bf16[512,384]{1,0:T(8,128)(2,1)S(1)}, u32[]{:S(2)}, u32[]{:S(2)}) collective-permute-start(bf16[512,384]{1,0:T(8,128)(2,1)S(1)} %attend.2.refs_1_.refs_0_), channel_id=1, source_target_pairs={{0,1},{1,0},{2,3},{3,2},{4,5},{5,4},{6,7},{7,6},{8,9},{9,8},{10,11... | collective-permute-start | bytes 1179656 | tf_op jit(solution)/shard_map/ppermute | solution.py:342
  32.4 2.6 %collective-permute-start.8 = (bf16[512,384]{1,0:T(8,128)(2,1)S(1)}, bf16[512,384]{1,0:T(8,128)(2,1)S(1)}, u32[]{:S(2)}, u32[]{:S(2)}) collective-permute-start(bf16[512,384]{1,0:T(8,128)(2,1)S(1)} %attend.2.refs_1_.refs_0_), channel_id=1, source_target_pairs={{0,2},{1,3},{2,0},{3,1},{4,6},{5,7},{6,4},{7,5},{8,10},{9,11},{10,... | collective-permute-start | bytes 1179656 | tf_op jit(solution)/shard_map/ppermute | solution.py:343
  35.0 0.0 collective-permute-done.5.refs_0_.refs_1_
  35.0 1.6 %collective-permute-start.6 = (bf16[1280,256]{1,0:T(8,128)(2,1)S(1)}, bf16[1280,256]{1,0:T(8,128)(2,1)S(1)}, u32[]{:S(2)}, u32[]{:S(2)}) collective-permute-start(bf16[1280,256]{1,0:T(8,128)(2,1)S(1)} %pack.1.refs_3_.refs_2_), channel_id=1, source_target_pairs={{0,4},{4,0},{1,5},{5,1},{2,6},{6,2},{3,7},{7,3},{8,12},{12,8},{9,1... | collective-permute-start | bytes 1966088 | tf_op jit(solution)/shard_map/ppermute | solution.py:358
  36.6 0.0 collective-permute-done.13.refs_2_.refs_1_
  36.6 0.6 collective-permute-start.15
  37.2 6.3 %collective-permute-done.12.refs_0_ = bf16[160,1280]{1,0:T(8,128)(2,1)S(1)} collective-permute-done((bf16[160,1280]{1,0:T(8,128)(2,1)S(1)}, bf16[160,1280]{1,0:T(8,128)(2,1)S(1)}, u32[]{:S(2)}, u32[]{:S(2)}) %collective-permute-start.12) | collective-permute-done | bytes 409632 | tf_op jit(solution)/shard_map/ppermute | solution.py:314
  43.5 0.1 join_all.1.refs_7_
  43.6 1.6 %collective-permute-start.14 = (bf16[320,1280]{1,0:T(8,128)(2,1)S(1)}, bf16[320,1280]{1,0:T(8,128)(2,1)S(1)}, u32[]{:S(2)}, u32[]{:S(2)}) collective-permute-start(bf16[320,1280]{1,0:T(8,128)(2,1)S(1)} %join_all.1.refs_7_), channel_id=1, source_target_pairs={{0,16},{16,0},{8,24},{24,8},{1,17},{17,1},{9,25},{25,9},{2,18},{18... | collective-permute-start | bytes 2457608 | tf_op jit(solution)/shard_map/ppermute | solution.py:363
  45.2 6.4 %collective-permute-done.8.refs_1_.refs_4_ = bf16[512,384]{1,0:T(8,128)(2,1)S(1)} collective-permute-done((bf16[512,384]{1,0:T(8,128)(2,1)S(1)}, bf16[512,384]{1,0:T(8,128)(2,1)S(1)}, u32[]{:S(2)}, u32[]{:S(2)}) %collective-permute-start.8) | collective-permute-done | bytes 393248 | tf_op jit(solution)/shard_map/ppermute | solution.py:343
  51.6 0.3 collective-permute-start.11
  51.9 0.0 collective-permute-done.7.refs_0_.refs_2_
  51.9 0.8 %collective-permute-done.6.remote_ref = bf16[1280,256]{1,0:T(8,128)(2,1)S(1)} collective-permute-done((bf16[1280,256]{1,0:T(8,128)(2,1)S(1)}, bf16[1280,256]{1,0:T(8,128)(2,1)S(1)}, u32[]{:S(2)}, u32[]{:S(2)}) %collective-permute-start.6) | collective-permute-done | bytes 655392 | tf_op jit(solution)/shard_map/ppermute | solution.py:358
  52.8 2.5 %attend.3.refs_1_ = bf16[512,256]{1,0:T(8,128)(2,1)S(1)} custom-call(f32[8,512]{1,0:T(8,128)S(1)} %settle.1.near_ref, f32[8,512]{1,0:T(8,128)S(1)} %collective-permute-done.3.refs_0_.far_ref, bf16[256,640]{1,0:T(8,128)(2,1)S(1)} %get-tuple-element.18.q_ref, bf16[512,640]{1,0:T(8,128)(2,1)S(1)} %get-tuple-element.19.k_ref, ...), custom_call_target="tpu_custom_call" | custom-call | bytes 28800000 | tf_op jit(solution)/shard_map/attend/pallas_call | solution.py:328
  55.2 1.9 %collective-permute-start.10 = (bf16[512,256]{1,0:T(8,128)(2,1)S(1)}, bf16[512,256]{1,0:T(8,128)(2,1)S(1)}, u32[]{:S(2)}, u32[]{:S(2)}) collective-permute-start(bf16[512,256]{1,0:T(8,128)(2,1)S(1)} %attend.3.refs_1_), channel_id=1, source_target_pairs={{0,2},{1,3},{2,0},{3,1},{4,6},{5,7},{6,4},{7,5},{8,10},{9,11},{10,... | collective-permute-start | bytes 786440 | tf_op jit(solution)/shard_map/ppermute | solution.py:343
  57.1 0.0 collective-permute-start.9
  57.2 1.7 %collective-permute-done.15.refs_0_ = bf16[160,1280]{1,0:T(8,128)(2,1)S(1)} collective-permute-done((bf16[160,1280]{1,0:T(8,128)(2,1)S(1)}, bf16[160,1280]{1,0:T(8,128)(2,1)S(1)}, u32[]{:S(2)}, u32[]{:S(2)}) %collective-permute-start.15) | collective-permute-done | bytes 409632 | tf_op jit(solution)/shard_map/ppermute | solution.py:362
  58.9 0.0 collective-permute-start.17
  58.9 0.0 collective-permute-done.14.refs_2_.refs_8_
  58.9 0.0 copy-start
  59.0 0.0 copy-start.1
  59.0 1.6 %collective-permute-start.16 = (bf16[160,1280]{1,0:T(8,128)(2,1)S(1)}, bf16[160,1280]{1,0:T(8,128)(2,1)S(1)}, u32[]{:S(2)}, u32[]{:S(2)}) collective-permute-start(bf16[160,1280]{1,0:T(8,128)(2,1)S(1)} %hold.1.refs_0_), channel_id=1, source_target_pairs={{0,16},{16,0},{8,24},{24,8},{1,17},{17,1},{9,25},{25,9},{2,18},{18... | collective-permute-start | bytes 1228808 | tf_op jit(solution)/shard_map/ppermute | solution.py:368
  60.5 7.6 %collective-permute-done.11.refs_0_.refs_6_ = bf16[512,384]{1,0:T(8,128)(2,1)S(1)} collective-permute-done((bf16[512,384]{1,0:T(8,128)(2,1)S(1)}, bf16[512,384]{1,0:T(8,128)(2,1)S(1)}, u32[]{:S(2)}, u32[]{:S(2)}) %collective-permute-start.11) | collective-permute-done | bytes 393248 | tf_op jit(solution)/shard_map/ppermute | solution.py:344
  68.1 0.0 collective-permute-start.18
  68.1 0.0 collective-permute-done.10.refs_2_.refs_5_
  68.1 2.8 %collective-permute-done.9.refs_1_.refs_3_ = bf16[512,256]{1,0:T(8,128)(2,1)S(1)} collective-permute-done((bf16[512,256]{1,0:T(8,128)(2,1)S(1)}, bf16[512,256]{1,0:T(8,128)(2,1)S(1)}, u32[]{:S(2)}, u32[]{:S(2)}) %collective-permute-start.9) | collective-permute-done | bytes 262176 | tf_op jit(solution)/shard_map/ppermute | solution.py:342
  70.9 0.0 collective-permute-done.16.refs_1_
  70.9 0.1 join_y.1.refs_9_
  71.0 0.1 collective-permute-start.19
  71.1 1.3 %collective-permute-start.20 = (bf16[512,256]{1,0:T(8,128)(2,1)S(1)}, bf16[512,256]{1,0:T(8,128)(2,1)S(1)}, u32[]{:S(2)}, u32[]{:S(2)}) collective-permute-start(bf16[512,256]{1,0:T(8,128)(2,1)S(1)} %collective-permute-done.10.refs_2_.refs_5_), channel_id=1, source_target_pairs={{0,1},{1,0},{2,3},{3,2},{4,5},{5,4},{6,7},{7,6},{8,9},{9,8},{10,11... | collective-permute-start | bytes 786440 | tf_op jit(solution)/shard_map/ppermute | solution.py:344
  72.4 0.0 collective-permute-done.17.refs_10_
  72.4 0.0 collective-permute-done.18.refs_11_
  72.4 1.0 %collective-permute-done.19.refs_12_ = bf16[320,1280]{1,0:T(8,128)(2,1)S(1)} collective-permute-done((bf16[320,1280]{1,0:T(8,128)(2,1)S(1)}, bf16[320,1280]{1,0:T(8,128)(2,1)S(1)}, u32[]{:S(2)}, u32[]{:S(2)}) %collective-permute-start.19) | collective-permute-done | bytes 819232 | tf_op jit(solution)/shard_map/ppermute | solution.py:373
  73.4 0.0 copy-done
  73.4 0.0 copy-done.1
  73.4 5.2 %project.1 = (f32[512,1280]{1,0:T(8,128)S(1)}, bf16[256,1280]{1,0:T(8,128)(2,1)S(1)}, bf16[48,1280]{1,0:T(8,128)(2,1)S(1)}) custom-call(s32[4]{0:T(128)S(1)} %pad_add_fusion.after_ref.place, s32[6]{0:T(128)S(1)} %copy-done.1, f32[50,1280]{1,0:T(8,128)S(1)} %copy-done, bf16[640,5120]{1,0:T(8,128)(2,1)} %weight_ref.3, ...), custom_call_target="tpu_custom_call" | custom-call | tf_op jit(solution)/shard_map/project/pallas_call | solution.py:377
  78.6 1.2 %collective-permute-done.20.late_ref = bf16[512,256]{1,0:T(8,128)(2,1)S(1)} collective-permute-done((bf16[512,256]{1,0:T(8,128)(2,1)S(1)}, bf16[512,256]{1,0:T(8,128)(2,1)S(1)}, u32[]{:S(2)}, u32[]{:S(2)}) %collective-permute-start.20) | collective-permute-done | bytes 262176 | tf_op jit(solution)/shard_map/ppermute | solution.py:344
  79.8 1.9 %finish.1 = bf16[512,1280]{1,0:T(8,128)(2,1)} custom-call(f32[8,512]{1,0:T(8,128)S(1)} %settle.1.near_ref, f32[8,512]{1,0:T(8,128)S(1)} %collective-permute-done.3.refs_0_.far_ref, f32[512,1280]{1,0:T(8,128)S(1)} %get-tuple-element.26.total, bf16[256,1280]{1,0:T(8,128)(2,1)S(1)} %get-tuple-element.27.tail_ref, ...), custom_call_target="tpu_custom_call" | custom-call | tf_op jit(solution)/shard_map/finish/pallas_call | solution.py:395
  (10 shorter events, 0.1 us)
Async XLA Ops:
  0.1 18.9 %copy-start.2 = (f32[640]{0:T(1024)S(1)}, f32[640]{0:T(1024)}, u32[]{:S(2)}) copy-start(f32[640]{0:T(1024)} %param.13) | copy-start | bytes 7684
  0.1 19.0 %copy-start.3 = (f32[640]{0:T(1024)S(1)}, f32[640]{0:T(1024)}, u32[]{:S(2)}) copy-start(f32[640]{0:T(1024)} %param.14) | copy-start | bytes 7684
  2.2 25.1 %collective-permute-start.4 = (bf16[1280,384]{1,0:T(8,128)(2,1)S(1)}, bf16[1280,384]{1,0:T(8,128)(2,1)S(1)}, u32[]{:S(2)}, u32[]{:S(2)}) collective-permute-start(bf16[1280,384]{1,0:T(8,128)(2,1)S(1)} %get-tuple-element.21), channel_id=1, source_target_pairs={{0,4},{4,0},{1,5},{5,1},{2,6},{6,2},{3,7},{7,3},{8,12},{12,8},{9,1... | collective-permute-start | bytes 2949128 | tf_op jit(solution)/shard_map/ppermute | solution.py:315
  5.3 4.4 %collective-permute-start = (f32[8,512]{1,0:T(8,128)S(1)}, f32[8,512]{1,0:T(8,128)S(1)}, u32[]{:S(2)}, u32[]{:S(2)}) collective-permute-start(f32[8,512]{1,0:T(8,128)S(1)} %get-tuple-element.17.own_ref), channel_id=1, source_target_pairs={{0,1},{1,0},{2,3},{3,2},{4,5},{5,4},{6,7},{7,6},{8,9},{9,8},{10,11... | collective-permute-start | bytes 49160 | tf_op jit(solution)/shard_map/ppermute | solution.py:324
  6.8 4.7 %collective-permute-start.1 = (f32[8,512]{1,0:T(8,128)S(1)}, f32[8,512]{1,0:T(8,128)S(1)}, u32[]{:S(2)}, u32[]{:S(2)}) collective-permute-start(f32[8,512]{1,0:T(8,128)S(1)} %get-tuple-element.17.own_ref), channel_id=1, source_target_pairs={{0,2},{1,3},{2,0},{3,1},{4,6},{5,7},{6,4},{7,5},{8,10},{9,11},{10,... | collective-permute-start | bytes 49160 | tf_op jit(solution)/shard_map/ppermute | solution.py:324
  9.4 5.5 %collective-permute-start.2 = (f32[8,512]{1,0:T(8,128)S(1)}, f32[8,512]{1,0:T(8,128)S(1)}, u32[]{:S(2)}, u32[]{:S(2)}) collective-permute-start(f32[8,512]{1,0:T(8,128)S(1)} %get-tuple-element.17.own_ref), channel_id=1, source_target_pairs={{0,3},{1,2},{2,1},{3,0},{4,7},{5,6},{6,5},{7,4},{8,11},{9,10},{10,... | collective-permute-start | bytes 49160 | tf_op jit(solution)/shard_map/ppermute | solution.py:324
  15.0 12.4 %collective-permute-start.3 = (f32[8,512]{1,0:T(8,128)S(1)}, f32[8,512]{1,0:T(8,128)S(1)}, u32[]{:S(2)}, u32[]{:S(2)}) collective-permute-start(f32[8,512]{1,0:T(8,128)S(1)} %settle.1.near_ref), channel_id=1, source_target_pairs={{0,4},{4,0},{1,5},{5,1},{2,6},{6,2},{3,7},{7,3},{8,12},{12,8},{9,1... | collective-permute-start | bytes 49160 | tf_op jit(solution)/shard_map/ppermute | solution.py:325
  15.5 19.4 %collective-permute-start.5 = (bf16[80,1280]{1,0:T(8,128)(2,1)S(1)}, bf16[80,1280]{1,0:T(8,128)(2,1)S(1)}, u32[]{:S(2)}, u32[]{:S(2)}) collective-permute-start(bf16[80,1280]{1,0:T(8,128)(2,1)S(1)} %get-tuple-element.23), channel_id=1, source_target_pairs={{0,2},{1,3},{2,0},{3,1},{4,6},{5,7},{6,4},{7,5},{8,10},{9,11},{10,... | collective-permute-start | bytes 614408 | tf_op jit(solution)/shard_map/ppermute | solution.py:314
  15.5 21.1 %collective-permute-start.13 = (bf16[80,1280]{1,0:T(8,128)(2,1)S(1)}, bf16[80,1280]{1,0:T(8,128)(2,1)S(1)}, u32[]{:S(2)}, u32[]{:S(2)}) collective-permute-start(bf16[80,1280]{1,0:T(8,128)(2,1)S(1)} %get-tuple-element.25), channel_id=1, source_target_pairs={{0,3},{1,2},{2,1},{3,0},{4,7},{5,6},{6,5},{7,4},{8,11},{9,10},{10,... | collective-permute-start | bytes 614408 | tf_op jit(solution)/shard_map/ppermute | solution.py:314
  16.7 26.9 %collective-permute-start.12 = (bf16[160,1280]{1,0:T(8,128)(2,1)S(1)}, bf16[160,1280]{1,0:T(8,128)(2,1)S(1)}, u32[]{:S(2)}, u32[]{:S(2)}) collective-permute-start(bf16[160,1280]{1,0:T(8,128)(2,1)S(1)} %get-tuple-element.24), channel_id=1, source_target_pairs={{0,1},{1,0},{2,3},{3,2},{4,5},{5,4},{6,7},{7,6},{8,9},{9,8},{10,11... | collective-permute-start | bytes 1228808 | tf_op jit(solution)/shard_map/ppermute | solution.py:314
  30.5 21.4 %collective-permute-start.7 = (bf16[512,384]{1,0:T(8,128)(2,1)S(1)}, bf16[512,384]{1,0:T(8,128)(2,1)S(1)}, u32[]{:S(2)}, u32[]{:S(2)}) collective-permute-start(bf16[512,384]{1,0:T(8,128)(2,1)S(1)} %attend.2.refs_1_.refs_0_), channel_id=1, source_target_pairs={{0,1},{1,0},{2,3},{3,2},{4,5},{5,4},{6,7},{7,6},{8,9},{9,8},{10,11... | collective-permute-start | bytes 1179656 | tf_op jit(solution)/shard_map/ppermute | solution.py:342
  32.4 19.2 %collective-permute-start.8 = (bf16[512,384]{1,0:T(8,128)(2,1)S(1)}, bf16[512,384]{1,0:T(8,128)(2,1)S(1)}, u32[]{:S(2)}, u32[]{:S(2)}) collective-permute-start(bf16[512,384]{1,0:T(8,128)(2,1)S(1)} %attend.2.refs_1_.refs_0_), channel_id=1, source_target_pairs={{0,2},{1,3},{2,0},{3,1},{4,6},{5,7},{6,4},{7,5},{8,10},{9,11},{10,... | collective-permute-start | bytes 1179656 | tf_op jit(solution)/shard_map/ppermute | solution.py:343
  35.0 17.7 %collective-permute-start.6 = (bf16[1280,256]{1,0:T(8,128)(2,1)S(1)}, bf16[1280,256]{1,0:T(8,128)(2,1)S(1)}, u32[]{:S(2)}, u32[]{:S(2)}) collective-permute-start(bf16[1280,256]{1,0:T(8,128)(2,1)S(1)} %pack.1.refs_3_.refs_2_), channel_id=1, source_target_pairs={{0,4},{4,0},{1,5},{5,1},{2,6},{6,2},{3,7},{7,3},{8,12},{12,8},{9,1... | collective-permute-start | bytes 1966088 | tf_op jit(solution)/shard_map/ppermute | solution.py:358
  36.6 22.3 %collective-permute-start.15 = (bf16[160,1280]{1,0:T(8,128)(2,1)S(1)}, bf16[160,1280]{1,0:T(8,128)(2,1)S(1)}, u32[]{:S(2)}, u32[]{:S(2)}) collective-permute-start(bf16[160,1280]{1,0:T(8,128)(2,1)S(1)} %join_two.1), channel_id=1, source_target_pairs={{0,4},{4,0},{1,5},{5,1},{2,6},{6,2},{3,7},{7,3},{8,12},{12,8},{9,1... | collective-permute-start | bytes 1228808 | tf_op jit(solution)/shard_map/ppermute | solution.py:362
  43.6 15.3 %collective-permute-start.14 = (bf16[320,1280]{1,0:T(8,128)(2,1)S(1)}, bf16[320,1280]{1,0:T(8,128)(2,1)S(1)}, u32[]{:S(2)}, u32[]{:S(2)}) collective-permute-start(bf16[320,1280]{1,0:T(8,128)(2,1)S(1)} %join_all.1.refs_7_), channel_id=1, source_target_pairs={{0,16},{16,0},{8,24},{24,8},{1,17},{17,1},{9,25},{25,9},{2,18},{18... | collective-permute-start | bytes 2457608 | tf_op jit(solution)/shard_map/ppermute | solution.py:363
  51.6 16.6 %collective-permute-start.11 = (bf16[512,384]{1,0:T(8,128)(2,1)S(1)}, bf16[512,384]{1,0:T(8,128)(2,1)S(1)}, u32[]{:S(2)}, u32[]{:S(2)}) collective-permute-start(bf16[512,384]{1,0:T(8,128)(2,1)S(1)} %collective-permute-done.8.refs_1_.refs_4_), channel_id=1, source_target_pairs={{0,1},{1,0},{2,3},{3,2},{4,5},{5,4},{6,7},{7,6},{8,9},{9,8},{10,11... | collective-permute-start | bytes 1179656 | tf_op jit(solution)/shard_map/ppermute | solution.py:344
  55.2 12.9 %collective-permute-start.10 = (bf16[512,256]{1,0:T(8,128)(2,1)S(1)}, bf16[512,256]{1,0:T(8,128)(2,1)S(1)}, u32[]{:S(2)}, u32[]{:S(2)}) collective-permute-start(bf16[512,256]{1,0:T(8,128)(2,1)S(1)} %attend.3.refs_1_), channel_id=1, source_target_pairs={{0,2},{1,3},{2,0},{3,1},{4,6},{5,7},{6,4},{7,5},{8,10},{9,11},{10,... | collective-permute-start | bytes 786440 | tf_op jit(solution)/shard_map/ppermute | solution.py:343
  57.1 13.8 %collective-permute-start.9 = (bf16[512,256]{1,0:T(8,128)(2,1)S(1)}, bf16[512,256]{1,0:T(8,128)(2,1)S(1)}, u32[]{:S(2)}, u32[]{:S(2)}) collective-permute-start(bf16[512,256]{1,0:T(8,128)(2,1)S(1)} %attend.3.refs_1_), channel_id=1, source_target_pairs={{0,1},{1,0},{2,3},{3,2},{4,5},{5,4},{6,7},{7,6},{8,9},{9,8},{10,11... | collective-permute-start | bytes 786440 | tf_op jit(solution)/shard_map/ppermute | solution.py:342
  58.9 13.5 %collective-permute-start.17 = (bf16[320,1280]{1,0:T(8,128)(2,1)S(1)}, bf16[320,1280]{1,0:T(8,128)(2,1)S(1)}, u32[]{:S(2)}, u32[]{:S(2)}) collective-permute-start(bf16[320,1280]{1,0:T(8,128)(2,1)S(1)} %join_all.1.refs_7_), channel_id=1, source_target_pairs={{0,8},{8,0},{16,24},{24,16},{1,9},{9,1},{17,25},{25,17},{2,10},{10... | collective-permute-start | bytes 2457608 | tf_op jit(solution)/shard_map/ppermute | solution.py:373
  58.9 14.5 %copy-start = (f32[50,1280]{1,0:T(8,128)S(1)}, f32[50,1280]{1,0:T(8,128)}, u32[]{:S(2)}) copy-start(f32[50,1280]{1,0:T(8,128)} %gate_ref.1) | copy-start | bytes 768004
  59.0 14.4 %copy-start.1 = (s32[6]{0:T(128)S(1)}, s32[6]{0:T(128)}, u32[]{:S(2)}) copy-start(s32[6]{0:T(128)} %times.1) | copy-start | bytes 76
  59.0 12.0 %collective-permute-start.16 = (bf16[160,1280]{1,0:T(8,128)(2,1)S(1)}, bf16[160,1280]{1,0:T(8,128)(2,1)S(1)}, u32[]{:S(2)}, u32[]{:S(2)}) collective-permute-start(bf16[160,1280]{1,0:T(8,128)(2,1)S(1)} %hold.1.refs_0_), channel_id=1, source_target_pairs={{0,16},{16,0},{8,24},{24,8},{1,17},{17,1},{9,25},{25,9},{2,18},{18... | collective-permute-start | bytes 1228808 | tf_op jit(solution)/shard_map/ppermute | solution.py:368
  68.1 4.2 %collective-permute-start.18 = (bf16[320,1280]{1,0:T(8,128)(2,1)S(1)}, bf16[320,1280]{1,0:T(8,128)(2,1)S(1)}, u32[]{:S(2)}, u32[]{:S(2)}) collective-permute-start(bf16[320,1280]{1,0:T(8,128)(2,1)S(1)} %collective-permute-done.14.refs_2_.refs_8_), channel_id=1, source_target_pairs={{0,8},{8,0},{16,24},{24,16},{1,9},{9,1},{17,25},{25,17},{2,10},{10... | collective-permute-start | bytes 2457608 | tf_op jit(solution)/shard_map/ppermute | solution.py:373
  71.0 2.4 %collective-permute-start.19 = (bf16[320,1280]{1,0:T(8,128)(2,1)S(1)}, bf16[320,1280]{1,0:T(8,128)(2,1)S(1)}, u32[]{:S(2)}, u32[]{:S(2)}) collective-permute-start(bf16[320,1280]{1,0:T(8,128)(2,1)S(1)} %join_y.1.refs_9_), channel_id=1, source_target_pairs={{0,8},{8,0},{16,24},{24,16},{1,9},{9,1},{17,25},{25,17},{2,10},{10... | collective-permute-start | bytes 2457608 | tf_op jit(solution)/shard_map/ppermute | solution.py:373
  71.1 8.7 %collective-permute-start.20 = (bf16[512,256]{1,0:T(8,128)(2,1)S(1)}, bf16[512,256]{1,0:T(8,128)(2,1)S(1)}, u32[]{:S(2)}, u32[]{:S(2)}) collective-permute-start(bf16[512,256]{1,0:T(8,128)(2,1)S(1)} %collective-permute-done.10.refs_2_.refs_5_), channel_id=1, source_target_pairs={{0,1},{1,0},{2,3},{3,2},{4,5},{5,4},{6,7},{7,6},{8,9},{9,8},{10,11... | collective-permute-start | bytes 786440 | tf_op jit(solution)/shard_map/ppermute | solution.py:344

commit v8 on v7

--- a/solution.py
+++ b/solution.py
@@ -200,18 +200,26 @@
     )(*pieces, *after)
 
 
-def project_kernel(place, times, gate_ref, weight_ref, *refs):
-    parts, shares = refs[:7], refs[7:13]
-    total, tail_ref, gates_ref, rows_all, w_all, sems = refs[13:]
+def own_kernel(after_ref, later_ref, weight_ref, first_ref, last_ref, out_ref, own_w, sems):
+    width = out_ref.shape[1]
+    start = pl.multiple_of(lax.axis_index("head") * width, width)
+    copy = pltpu.make_async_copy(weight_ref.at[:, pl.ds(start, width)], own_w, sems.at[0])
+    copy.start()
+    rows = jnp.concatenate([first_ref[...], last_ref[...]], axis=1)
+    copy.wait()
+    for low in range(0, width, 256):
+        block = slice(low, low + 256)
+        out_ref[:, block] = jnp.dot(rows, own_w[:, block], preferred_element_type=F32)
+
+
+def project_kernel(after_ref, times, gate_ref, own_total, *refs):
+    parts, shares = refs[:5], refs[5:11]
+    total, tail_ref, gates_ref, rows_all, w_all = refs[11:]
     width = total.shape[1]
-    group = w_all.shape[0] // 4
+    group = w_all.shape[0] // 3
     share = group // 8
-    mine = place[2]
-    own_start = pl.multiple_of(place[1] * width, width)
-    own_copy = pltpu.make_async_copy(
-        weight_ref.at[:, pl.ds(own_start, width)], w_all.at[pl.ds(0, group), :], sems.at[0]
-    )
-    own_copy.start()
+    batch = lax.axis_index("batch")
+    mine = batch * 2 + lax.axis_index("ctx")
     used = 0
     for part in parts:
         rows_all[:, used : used + part.shape[1]] = part[...]
@@ -232,14 +240,13 @@
             ]
         for ref, low, step, flip in pieces:
             count = share if step else 2 * share
-            index = mine ^ (flip + 2 * core) if step else place[3] ^ (flip // 2 + core)
-            start = pl.multiple_of((1 + step) * group + index * count, share)
+            index = mine ^ (flip + 2 * core) if step else batch ^ (flip // 2 + core)
+            start = pl.multiple_of(step * group + index * count, share)
             w_all[pl.ds(start, count), :] = ref[low : low + count, :]
     tail_ref[...] = w_all[used:, :]
-    own_copy.wait()
     for low in range(0, width, 256):
         block = slice(low, low + 256)
-        total[:, block] = jnp.dot(rows_all[...], w_all[0:used, block], preferred_element_type=F32)
+        total[:, block] = own_total[:, block] + jnp.dot(rows_all[...], w_all[0:used, block], preferred_element_type=F32)
 
 
 def finish_kernel(near_ref, far_ref, total, tail_ref, gates_ref, late_ref, out_hbm, out_ref, sems):
@@ -367,31 +374,40 @@
     share_y = join([share_y], [attended, share_x], "hold")
     share_xy = lax.ppermute(share_y, "batch", SWAP_X)
     last = spread(attended)
-    passed = gate([first[3], *last[1:3]], 10, "passed")
+    own_total = pl.pallas_call(
+        own_kernel,
+        in_specs=[AFTER, AFTER, HBM, VMEM, VMEM],
+        out_specs=VMEM,
+        out_shape=jax.ShapeDtypeStruct((rows, out_width), F32),
+        scratch_shapes=[pltpu.VMEM((width, out_width), BF16), pltpu.SemaphoreType.DMA((1,))],
+        compiler_params=params(14),
+        cost_estimate=cost(0),
+        name="own",
+    )(first[3], share_y, weight_hbm, first[0], last[0])
+    passed = gate([first[3], *last[1:3], own_total], 10, "passed")
     share_yxy = join([share_y, share_xy], [passed], "join_y")
     shares = [share0, share_x, share_yxy]
     shares += [lax.ppermute(value, "batch", SWAP_CORE) for value in shares]
 
-    parts = [first[0], last[0], first[1], last[1], first[2], last[2], first[3]]
-    used = 3 * width + cuts[0][1]
+    parts = [first[1], last[1], first[2], last[2], first[3]]
+    used = 2 * width + cuts[0][1]
     total, tail_weights, gates = pl.pallas_call(
         project_kernel,
-        in_specs=[SMEM, SMEM, VMEM, HBM] + [VMEM] * (len(parts) + len(shares)),
+        in_specs=[ANY, SMEM, VMEM, VMEM] + [VMEM] * (len(parts) + len(shares)),
         out_specs=[VMEM] * 3,
         out_shape=[
             jax.ShapeDtypeStruct((rows, out_width), F32),
-            jax.ShapeDtypeStruct((4 * width - used, out_width), BF16),
+            jax.ShapeDtypeStruct((3 * width - used, out_width), BF16),
             jax.ShapeDtypeStruct((48, out_width), BF16),
         ],
         scratch_shapes=[
             pltpu.VMEM((rows, used), BF16),
-            pltpu.VMEM((4 * width, out_width), BF16),
-            pltpu.SemaphoreType.DMA((1,)),
+            pltpu.VMEM((3 * width, out_width), BF16),
         ],
         compiler_params=params(24),
         cost_estimate=cost(0),
         name="project",
-    )(place, timestep, gate_table, weight_hbm, *parts, *shares)
+    )(place, timestep, gate_table, own_total, *parts, *shares)
     return pl.pallas_call(
         finish_kernel,
         in_specs=[VMEM] * 6,

time: 81.8 us -> 81.8 us (level)
  waiting for transfers between devices: 41.6 us -> 39.7 us
  Pallas kernels: 15 us -> 16 us
  starting transfers between devices: 24.8 us -> 25.8 us
    ppermute x2, waiting for transfers between devices: 2.8 us -> 0.14 us  [spread(): one = lax.ppermute(attended, 'head', xor_pairs(4, 1))]
    ppermute x2, waiting for transfers between devices: 8.79 us -> 10.4 us  [spread(): three = lax.ppermute(two, 'head', xor_pairs(4, 1))]
    ppermute x2, waiting for transfers between devices: 6.38 us -> 4.75 us  [spread(): two = lax.ppermute(attended, 'head', xor_pairs(4, 2))]
    ppermute x1, starting transfers between devices: 0.57 us -> 1.59 us  [fast_local(): share_y = lax.ppermute(two_three, 'ctx', SWAP_CTX)]
    pallas_call x1 -> x2, Pallas kernels: 5.2 us -> 6.16 us  [the longest x1 3.53 us: fast_local(): pl.pallas_call(project_kernel, in_specs=[ANY, SMEM, VMEM, VMEM] + [VMEM]...]
    ppermute x2, starting transfers between devices: 1.87 us -> 2.77 us  [spread(): one = lax.ppermute(attended, 'head', xor_pairs(4, 1))]
    ppermute x2, starting transfers between devices: 4.52 us -> 3.69 us  [spread(): two = lax.ppermute(attended, 'head', xor_pairs(4, 2))]
  transfers between devices with their start and end apart: 21 -> 21, of which waited for: 11 -> 11; matrix products, arithmetic and copies ran while one was open for 0% -> 0% of each run, Pallas kernels for 13% -> 15%
where the time goes in v8:
time: 81.8 us; the launch traced here: 81.7 us
  waiting for transfers between devices  39.7 us (49%)
  starting transfers between devices  25.8 us (32%)
  Pallas kernels  16 us (20%)
    ppermute x2, waiting for transfers between devices, spread(): three = lax.ppermute(two, 'head', xor_pairs(4, 1))  10.4 us
    ppermute x1, waiting for transfers between devices, fast_local(): far = lax.ppermute(near, 'ctx', SWAP_CTX)  8.31 us
    ppermute x3, waiting for transfers between devices, fast_local(): lax.ppermute(cut_weights[s - 1], 'head', xor_pairs(4, s))  6.95 us
    pallas_call x2, Pallas kernels, attend(): pl.pallas_call(functools.partial(attend_kernel, cut, total_width), in_spe...  5.57 us
    ppermute x3, waiting for transfers between devices, fast_local(): lax.ppermute(stats, 'head', xor_pairs(4, step))  5.31 us
    ppermute x2, waiting for transfers between devices, spread(): two = lax.ppermute(attended, 'head', xor_pairs(4, 2))  4.75 us
    ppermute x3, starting transfers between devices, fast_local(): lax.ppermute(stats, 'head', xor_pairs(4, step))  4.39 us
    ppermute x2, starting transfers between devices, spread(): two = lax.ppermute(attended, 'head', xor_pairs(4, 2))  3.69 us
  transfers between devices with their start and end apart: 21, of which 11 were waited for; matrix products, arithmetic and copies ran while one was open for 0% of the time, Pallas kernels for 15%

profile of v8, /device:TPU:0, one launch (start us, length us, event | category | flops | bytes accessed | tf_op | source)
XLA Modules:
  0.0 81.7 jit_solution(4005948569802115898)
XLA Ops:
  0.0 0.1 pad_add_fusion.after_ref
  0.1 0.0 copy-start.2
  0.1 0.0 copy-start.3
  0.1 2.1 %prepare.1 = (bf16[256,640]{1,0:T(8,128)(2,1)S(1)}, bf16[256,640]{1,0:T(8,128)(2,1)S(1)}, bf16[1280,384]{1,0:T(8,128)(2,1)S(1)}, f32[8,512]{1,0:T(8,128)S(1)}, b...) custom-call(s32[4]{0:T(128)S(1)} %pad_add_fusion.after_ref, ...), custom_call_target="tpu_custom_call" | custom-call | bytes 7200000 | tf_op jit(solution)/shard_map/prepare/pallas_call | solution.py:293
  2.2 3.0 %collective-permute-start.4 = (bf16[1280,384]{1,0:T(8,128)(2,1)S(1)}, bf16[1280,384]{1,0:T(8,128)(2,1)S(1)}, u32[]{:S(2)}, u32[]{:S(2)}) collective-permute-start(bf16[1280,384]{1,0:T(8,128)(2,1)S(1)} %get-tuple-element.21), channel_id=1, source_target_pairs={{0,4},{4,0},{1,5},{5,1},{2,6},{6,2},{3,7},{7,3},{8,12},{12,8},{9,1... | collective-permute-start | bytes 2949128 | tf_op jit(solution)/shard_map/ppermute | solution.py:322
  5.3 1.6 %collective-permute-start = (f32[8,512]{1,0:T(8,128)S(1)}, f32[8,512]{1,0:T(8,128)S(1)}, u32[]{:S(2)}, u32[]{:S(2)}) collective-permute-start(f32[8,512]{1,0:T(8,128)S(1)} %get-tuple-element.17.own_ref), channel_id=1, source_target_pairs={{0,1},{1,0},{2,3},{3,2},{4,5},{5,4},{6,7},{7,6},{8,9},{9,8},{10,11... | collective-permute-start | bytes 49160 | tf_op jit(solution)/shard_map/ppermute | solution.py:331
  6.8 2.6 %collective-permute-start.1 = (f32[8,512]{1,0:T(8,128)S(1)}, f32[8,512]{1,0:T(8,128)S(1)}, u32[]{:S(2)}, u32[]{:S(2)}) collective-permute-start(f32[8,512]{1,0:T(8,128)S(1)} %get-tuple-element.17.own_ref), channel_id=1, source_target_pairs={{0,2},{1,3},{2,0},{3,1},{4,6},{5,7},{6,4},{7,5},{8,10},{9,11},{10,... | collective-permute-start | bytes 49160 | tf_op jit(solution)/shard_map/ppermute | solution.py:331
  9.4 0.2 collective-permute-start.2
  9.6 0.0 collective-permute-done.one_ref
  9.6 1.9 %collective-permute-done.1.two_ref = f32[8,512]{1,0:T(8,128)S(1)} collective-permute-done((f32[8,512]{1,0:T(8,128)S(1)}, f32[8,512]{1,0:T(8,128)S(1)}, u32[]{:S(2)}, u32[]{:S(2)}) %collective-permute-start.1) | collective-permute-done | bytes 16416 | tf_op jit(solution)/shard_map/ppermute | solution.py:331
  11.5 3.4 %collective-permute-done.2.three_ref = f32[8,512]{1,0:T(8,128)S(1)} collective-permute-done((f32[8,512]{1,0:T(8,128)S(1)}, f32[8,512]{1,0:T(8,128)S(1)}, u32[]{:S(2)}, u32[]{:S(2)}) %collective-permute-start.2) | collective-permute-done | bytes 16416 | tf_op jit(solution)/shard_map/ppermute | solution.py:331
  15.0 0.6 collective-permute-start.3
  15.5 0.0 collective-permute-start.7
  15.5 1.1 %collective-permute-start.8 = (bf16[80,1280]{1,0:T(8,128)(2,1)S(1)}, bf16[80,1280]{1,0:T(8,128)(2,1)S(1)}, u32[]{:S(2)}, u32[]{:S(2)}) collective-permute-start(bf16[80,1280]{1,0:T(8,128)(2,1)S(1)} %get-tuple-element.23), channel_id=1, source_target_pairs={{0,3},{1,2},{2,1},{3,0},{4,7},{5,6},{6,5},{7,4},{8,11},{9,10},{10,... | collective-permute-start | bytes 614408 | tf_op jit(solution)/shard_map/ppermute | solution.py:321
  16.7 2.4 %collective-permute-start.12 = (bf16[160,1280]{1,0:T(8,128)(2,1)S(1)}, bf16[160,1280]{1,0:T(8,128)(2,1)S(1)}, u32[]{:S(2)}, u32[]{:S(2)}) collective-permute-start(bf16[160,1280]{1,0:T(8,128)(2,1)S(1)} %get-tuple-element.25), channel_id=1, source_target_pairs={{0,1},{1,0},{2,3},{3,2},{4,5},{5,4},{6,7},{7,6},{8,9},{9,8},{10,11... | collective-permute-start | bytes 1228808 | tf_op jit(solution)/shard_map/ppermute | solution.py:321
  19.0 0.0 copy-done.2
  19.0 0.0 copy-done.3
  19.0 8.3 %collective-permute-done.3.refs_0_.far_ref = f32[8,512]{1,0:T(8,128)S(1)} collective-permute-done((f32[8,512]{1,0:T(8,128)S(1)}, f32[8,512]{1,0:T(8,128)S(1)}, u32[]{:S(2)}, u32[]{:S(2)}) %collective-permute-start.3) | collective-permute-done | bytes 16416 | tf_op jit(solution)/shard_map/ppermute | solution.py:332
  27.4 0.0 collective-permute-done.4.refs_1_.remote_ref
  27.4 3.1 %attend.2.refs_1_.first_ref = bf16[512,384]{1,0:T(8,128)(2,1)S(1)} custom-call(f32[8,512]{1,0:T(8,128)S(1)} %settle.1.near_ref, f32[8,512]{1,0:T(8,128)S(1)} %collective-permute-done.3.refs_0_.far_ref, bf16[256,640]{1,0:T(8,128)(2,1)S(1)} %get-tuple-element.18.q_ref, bf16[512,640]{1,0:T(8,128)(2,1)S(1)} %get-tuple-element.19.k_ref, ...), custom_call_target="tpu_custom_call" | custom-call | bytes 28800000 | tf_op jit(solution)/shard_map/attend/pallas_call | solution.py:335
  30.5 1.9 %collective-permute-start.11 = (bf16[512,384]{1,0:T(8,128)(2,1)S(1)}, bf16[512,384]{1,0:T(8,128)(2,1)S(1)}, u32[]{:S(2)}, u32[]{:S(2)}) collective-permute-start(bf16[512,384]{1,0:T(8,128)(2,1)S(1)} %attend.2.refs_1_.first_ref), channel_id=1, source_target_pairs={{0,1},{1,0},{2,3},{3,2},{4,5},{5,4},{6,7},{7,6},{8,9},{9,8},{10,11... | collective-permute-start | bytes 1179656 | tf_op jit(solution)/shard_map/ppermute | solution.py:349
  32.4 2.6 %collective-permute-start.5 = (bf16[512,384]{1,0:T(8,128)(2,1)S(1)}, bf16[512,384]{1,0:T(8,128)(2,1)S(1)}, u32[]{:S(2)}, u32[]{:S(2)}) collective-permute-start(bf16[512,384]{1,0:T(8,128)(2,1)S(1)} %attend.2.refs_1_.first_ref), channel_id=1, source_target_pairs={{0,2},{1,3},{2,0},{3,1},{4,6},{5,7},{6,4},{7,5},{8,10},{9,11},{10,... | collective-permute-start | bytes 1179656 | tf_op jit(solution)/shard_map/ppermute | solution.py:350
  35.0 0.0 collective-permute-done.7.refs_0_.refs_1_
  35.0 1.6 %collective-permute-start.10 = (bf16[1280,256]{1,0:T(8,128)(2,1)S(1)}, bf16[1280,256]{1,0:T(8,128)(2,1)S(1)}, u32[]{:S(2)}, u32[]{:S(2)}) collective-permute-start(bf16[1280,256]{1,0:T(8,128)(2,1)S(1)} %pack.1.refs_2_.refs_3_), channel_id=1, source_target_pairs={{0,4},{4,0},{1,5},{5,1},{2,6},{6,2},{3,7},{7,3},{8,12},{12,8},{9,1... | collective-permute-start | bytes 1966088 | tf_op jit(solution)/shard_map/ppermute | solution.py:365
  36.6 0.0 collective-permute-done.8.refs_1_.refs_2_
  36.6 6.9 %collective-permute-done.12.refs_0_ = bf16[160,1280]{1,0:T(8,128)(2,1)S(1)} collective-permute-done((bf16[160,1280]{1,0:T(8,128)(2,1)S(1)}, bf16[160,1280]{1,0:T(8,128)(2,1)S(1)}, u32[]{:S(2)}, u32[]{:S(2)}) %collective-permute-start.12) | collective-permute-done | bytes 409632 | tf_op jit(solution)/shard_map/ppermute | solution.py:321
  43.5 0.1 join_all.1.refs_5_
  43.6 1.6 %collective-permute-start.13 = (bf16[320,1280]{1,0:T(8,128)(2,1)S(1)}, bf16[320,1280]{1,0:T(8,128)(2,1)S(1)}, u32[]{:S(2)}, u32[]{:S(2)}) collective-permute-start(bf16[320,1280]{1,0:T(8,128)(2,1)S(1)} %join_all.1.refs_5_), channel_id=1, source_target_pairs={{0,16},{16,0},{8,24},{24,8},{1,17},{17,1},{9,25},{25,9},{2,18},{18... | collective-permute-start | bytes 2457608 | tf_op jit(solution)/shard_map/ppermute | solution.py:370
  45.2 1.6 %collective-permute-start.9 = (bf16[160,1280]{1,0:T(8,128)(2,1)S(1)}, bf16[160,1280]{1,0:T(8,128)(2,1)S(1)}, u32[]{:S(2)}, u32[]{:S(2)}) collective-permute-start(bf16[160,1280]{1,0:T(8,128)(2,1)S(1)} %join_two.1), channel_id=1, source_target_pairs={{0,4},{4,0},{1,5},{5,1},{2,6},{6,2},{3,7},{7,3},{8,12},{12,8},{9,1... | collective-permute-start | bytes 1228808 | tf_op jit(solution)/shard_map/ppermute | solution.py:369
  46.8 4.8 %collective-permute-done.5.refs_1_.refs_2_ = bf16[512,384]{1,0:T(8,128)(2,1)S(1)} collective-permute-done((bf16[512,384]{1,0:T(8,128)(2,1)S(1)}, bf16[512,384]{1,0:T(8,128)(2,1)S(1)}, u32[]{:S(2)}, u32[]{:S(2)}) %collective-permute-start.5) | collective-permute-done | bytes 393248 | tf_op jit(solution)/shard_map/ppermute | solution.py:350
  51.6 0.3 collective-permute-start.6
  51.9 0.0 collective-permute-done.11.refs_0_
  51.9 0.8 %collective-permute-done.10.remote_ref = bf16[1280,256]{1,0:T(8,128)(2,1)S(1)} collective-permute-done((bf16[1280,256]{1,0:T(8,128)(2,1)S(1)}, bf16[1280,256]{1,0:T(8,128)(2,1)S(1)}, u32[]{:S(2)}, u32[]{:S(2)}) %collective-permute-start.10) | collective-permute-done | bytes 655392 | tf_op jit(solution)/shard_map/ppermute | solution.py:365
  52.8 2.4 %attend.3.refs_1_.last_ref = bf16[512,256]{1,0:T(8,128)(2,1)S(1)} custom-call(f32[8,512]{1,0:T(8,128)S(1)} %settle.1.near_ref, f32[8,512]{1,0:T(8,128)S(1)} %collective-permute-done.3.refs_0_.far_ref, bf16[256,640]{1,0:T(8,128)(2,1)S(1)} %get-tuple-element.18.q_ref, bf16[512,640]{1,0:T(8,128)(2,1)S(1)} %get-tuple-element.19.k_ref, ...), custom_call_target="tpu_custom_call" | custom-call | bytes 28800000 | tf_op jit(solution)/shard_map/attend/pallas_call | solution.py:335
  55.2 0.9 %collective-permute-start.14 = (bf16[512,256]{1,0:T(8,128)(2,1)S(1)}, bf16[512,256]{1,0:T(8,128)(2,1)S(1)}, u32[]{:S(2)}, u32[]{:S(2)}) collective-permute-start(bf16[512,256]{1,0:T(8,128)(2,1)S(1)} %attend.3.refs_1_.last_ref), channel_id=1, source_target_pairs={{0,1},{1,0},{2,3},{3,2},{4,5},{5,4},{6,7},{7,6},{8,9},{9,8},{10,11... | collective-permute-start | bytes 786440 | tf_op jit(solution)/shard_map/ppermute | solution.py:349
  56.1 1.1 %collective-permute-start.15 = (bf16[512,256]{1,0:T(8,128)(2,1)S(1)}, bf16[512,256]{1,0:T(8,128)(2,1)S(1)}, u32[]{:S(2)}, u32[]{:S(2)}) collective-permute-start(bf16[512,256]{1,0:T(8,128)(2,1)S(1)} %attend.3.refs_1_.last_ref), channel_id=1, source_target_pairs={{0,2},{1,3},{2,0},{3,1},{4,6},{5,7},{6,4},{7,5},{8,10},{9,11},{10,... | collective-permute-start | bytes 786440 | tf_op jit(solution)/shard_map/ppermute | solution.py:350
  57.2 1.7 %collective-permute-done.9.refs_0_ = bf16[160,1280]{1,0:T(8,128)(2,1)S(1)} collective-permute-done((bf16[160,1280]{1,0:T(8,128)(2,1)S(1)}, bf16[160,1280]{1,0:T(8,128)(2,1)S(1)}, u32[]{:S(2)}, u32[]{:S(2)}) %collective-permute-start.9) | collective-permute-done | bytes 409632 | tf_op jit(solution)/shard_map/ppermute | solution.py:369
  58.9 0.0 collective-permute-start.17
  58.9 0.0 collective-permute-done.13.refs_2_.refs_6_
  58.9 1.6 %collective-permute-start.16 = (bf16[160,1280]{1,0:T(8,128)(2,1)S(1)}, bf16[160,1280]{1,0:T(8,128)(2,1)S(1)}, u32[]{:S(2)}, u32[]{:S(2)}) collective-permute-start(bf16[160,1280]{1,0:T(8,128)(2,1)S(1)} %hold.1.later_ref.refs_0_), channel_id=1, source_target_pairs={{0,16},{16,0},{8,24},{24,8},{1,17},{17,1},{9,25},{25,9},{2,18},{18... | collective-permute-start | bytes 1228808 | tf_op jit(solution)/shard_map/ppermute | solution.py:375
  60.5 7.6 %collective-permute-done.6.after_ref.refs_0_.refs_4_ = bf16[512,384]{1,0:T(8,128)(2,1)S(1)} collective-permute-done((bf16[512,384]{1,0:T(8,128)(2,1)S(1)}, bf16[512,384]{1,0:T(8,128)(2,1)S(1)}, u32[]{:S(2)}, u32[]{:S(2)}) %collective-permute-start.6) | collective-permute-done | bytes 393248 | tf_op jit(solution)/shard_map/ppermute | solution.py:351
  68.1 0.0 collective-permute-start.18
  68.1 2.6 %own.1.refs_3_.own_total = f32[512,1280]{1,0:T(8,128)S(1)} custom-call(bf16[512,384]{1,0:T(8,128)(2,1)S(1)} %collective-permute-done.6.after_ref.refs_0_.refs_4_, bf16[160,1280]{1,0:T(8,128)(2,1)S(1)} %hold.1.later_ref.refs_0_, bf16[640,5120]{1,0:T(8,128)(2,1)} %weight_ref.3, bf16[512,384]{1,0:T(8,128)(2,1)S(1)} %attend.2.refs_1_.first_ref, ...), custom_call_target="tpu_custom_call" | custom-call | tf_op jit(solution)/shard_map/own/pallas_call | solution.py:377
  70.8 0.0 copy-start
  70.8 0.0 copy-start.1
  70.8 0.1 collective-permute-done.14.refs_1_
  70.9 0.0 collective-permute-done.15.refs_2_.refs_3_
  70.9 0.0 collective-permute-done.16.refs_1_
  70.9 0.1 join_y.1.refs_7_
  71.0 0.5 collective-permute-start.19
  71.5 0.8 collective-permute-start.20
  72.2 0.0 collective-permute-done.17.refs_8_
  72.2 0.0 collective-permute-done.18.refs_9_
  72.2 1.2 %collective-permute-done.19.refs_10_ = bf16[320,1280]{1,0:T(8,128)(2,1)S(1)} collective-permute-done((bf16[320,1280]{1,0:T(8,128)(2,1)S(1)}, bf16[320,1280]{1,0:T(8,128)(2,1)S(1)}, u32[]{:S(2)}, u32[]{:S(2)}) %collective-permute-start.19) | collective-permute-done | bytes 819232 | tf_op jit(solution)/shard_map/ppermute | solution.py:390
  73.4 0.0 copy-done
  73.4 0.0 copy-done.1
  73.4 3.5 %project.1 = (f32[512,1280]{1,0:T(8,128)S(1)}, bf16[256,1280]{1,0:T(8,128)(2,1)S(1)}, bf16[48,1280]{1,0:T(8,128)(2,1)S(1)}) custom-call(s32[4]{0:T(128)S(1)} %pad_add_fusion.after_ref, s32[6]{0:T(128)S(1)} %copy-done.1, f32[50,1280]{1,0:T(8,128)S(1)} %copy-done, f32[512,1280]{1,0:T(8,128)S(1)} %own.1.refs_3_.own_total, ...), custom_call_target="tpu_custom_call" | custom-call | tf_op jit(solution)/shard_map/project/pallas_call | solution.py:394
  77.0 2.8 %collective-permute-done.20.late_ref = bf16[512,256]{1,0:T(8,128)(2,1)S(1)} collective-permute-done((bf16[512,256]{1,0:T(8,128)(2,1)S(1)}, bf16[512,256]{1,0:T(8,128)(2,1)S(1)}, u32[]{:S(2)}, u32[]{:S(2)}) %collective-permute-start.20) | collective-permute-done | bytes 262176 | tf_op jit(solution)/shard_map/ppermute | solution.py:351
  79.8 1.9 %finish.1 = bf16[512,1280]{1,0:T(8,128)(2,1)} custom-call(f32[8,512]{1,0:T(8,128)S(1)} %settle.1.near_ref, f32[8,512]{1,0:T(8,128)S(1)} %collective-permute-done.3.refs_0_.far_ref, f32[512,1280]{1,0:T(8,128)S(1)} %get-tuple-element.26.total, bf16[256,1280]{1,0:T(8,128)(2,1)S(1)} %get-tuple-element.27.tail_ref, ...), custom_call_target="tpu_custom_call" | custom-call | tf_op jit(solution)/shard_map/finish/pallas_call | solution.py:411
  (10 shorter events, 0.1 us)
Async XLA Ops:
  0.1 18.9 %copy-start.2 = (f32[640]{0:T(1024)S(1)}, f32[640]{0:T(1024)}, u32[]{:S(2)}) copy-start(f32[640]{0:T(1024)} %param.13) | copy-start | bytes 7684
  0.1 19.0 %copy-start.3 = (f32[640]{0:T(1024)S(1)}, f32[640]{0:T(1024)}, u32[]{:S(2)}) copy-start(f32[640]{0:T(1024)} %param.14) | copy-start | bytes 7684
  2.2 25.1 %collective-permute-start.4 = (bf16[1280,384]{1,0:T(8,128)(2,1)S(1)}, bf16[1280,384]{1,0:T(8,128)(2,1)S(1)}, u32[]{:S(2)}, u32[]{:S(2)}) collective-permute-start(bf16[1280,384]{1,0:T(8,128)(2,1)S(1)} %get-tuple-element.21), channel_id=1, source_target_pairs={{0,4},{4,0},{1,5},{5,1},{2,6},{6,2},{3,7},{7,3},{8,12},{12,8},{9,1... | collective-permute-start | bytes 2949128 | tf_op jit(solution)/shard_map/ppermute | solution.py:322
  5.3 4.4 %collective-permute-start = (f32[8,512]{1,0:T(8,128)S(1)}, f32[8,512]{1,0:T(8,128)S(1)}, u32[]{:S(2)}, u32[]{:S(2)}) collective-permute-start(f32[8,512]{1,0:T(8,128)S(1)} %get-tuple-element.17.own_ref), channel_id=1, source_target_pairs={{0,1},{1,0},{2,3},{3,2},{4,5},{5,4},{6,7},{7,6},{8,9},{9,8},{10,11... | collective-permute-start | bytes 49160 | tf_op jit(solution)/shard_map/ppermute | solution.py:331
  6.8 4.7 %collective-permute-start.1 = (f32[8,512]{1,0:T(8,128)S(1)}, f32[8,512]{1,0:T(8,128)S(1)}, u32[]{:S(2)}, u32[]{:S(2)}) collective-permute-start(f32[8,512]{1,0:T(8,128)S(1)} %get-tuple-element.17.own_ref), channel_id=1, source_target_pairs={{0,2},{1,3},{2,0},{3,1},{4,6},{5,7},{6,4},{7,5},{8,10},{9,11},{10,... | collective-permute-start | bytes 49160 | tf_op jit(solution)/shard_map/ppermute | solution.py:331
  9.4 5.5 %collective-permute-start.2 = (f32[8,512]{1,0:T(8,128)S(1)}, f32[8,512]{1,0:T(8,128)S(1)}, u32[]{:S(2)}, u32[]{:S(2)}) collective-permute-start(f32[8,512]{1,0:T(8,128)S(1)} %get-tuple-element.17.own_ref), channel_id=1, source_target_pairs={{0,3},{1,2},{2,1},{3,0},{4,7},{5,6},{6,5},{7,4},{8,11},{9,10},{10,... | collective-permute-start | bytes 49160 | tf_op jit(solution)/shard_map/ppermute | solution.py:331
  15.0 12.4 %collective-permute-start.3 = (f32[8,512]{1,0:T(8,128)S(1)}, f32[8,512]{1,0:T(8,128)S(1)}, u32[]{:S(2)}, u32[]{:S(2)}) collective-permute-start(f32[8,512]{1,0:T(8,128)S(1)} %settle.1.near_ref), channel_id=1, source_target_pairs={{0,4},{4,0},{1,5},{5,1},{2,6},{6,2},{3,7},{7,3},{8,12},{12,8},{9,1... | collective-permute-start | bytes 49160 | tf_op jit(solution)/shard_map/ppermute | solution.py:332
  15.5 19.4 %collective-permute-start.7 = (bf16[80,1280]{1,0:T(8,128)(2,1)S(1)}, bf16[80,1280]{1,0:T(8,128)(2,1)S(1)}, u32[]{:S(2)}, u32[]{:S(2)}) collective-permute-start(bf16[80,1280]{1,0:T(8,128)(2,1)S(1)} %get-tuple-element.22), channel_id=1, source_target_pairs={{0,2},{1,3},{2,0},{3,1},{4,6},{5,7},{6,4},{7,5},{8,10},{9,11},{10,... | collective-permute-start | bytes 614408 | tf_op jit(solution)/shard_map/ppermute | solution.py:321
  15.5 21.1 %collective-permute-start.8 = (bf16[80,1280]{1,0:T(8,128)(2,1)S(1)}, bf16[80,1280]{1,0:T(8,128)(2,1)S(1)}, u32[]{:S(2)}, u32[]{:S(2)}) collective-permute-start(bf16[80,1280]{1,0:T(8,128)(2,1)S(1)} %get-tuple-element.23), channel_id=1, source_target_pairs={{0,3},{1,2},{2,1},{3,0},{4,7},{5,6},{6,5},{7,4},{8,11},{9,10},{10,... | collective-permute-start | bytes 614408 | tf_op jit(solution)/shard_map/ppermute | solution.py:321
  16.7 26.9 %collective-permute-start.12 = (bf16[160,1280]{1,0:T(8,128)(2,1)S(1)}, bf16[160,1280]{1,0:T(8,128)(2,1)S(1)}, u32[]{:S(2)}, u32[]{:S(2)}) collective-permute-start(bf16[160,1280]{1,0:T(8,128)(2,1)S(1)} %get-tuple-element.25), channel_id=1, source_target_pairs={{0,1},{1,0},{2,3},{3,2},{4,5},{5,4},{6,7},{7,6},{8,9},{9,8},{10,11... | collective-permute-start | bytes 1228808 | tf_op jit(solution)/shard_map/ppermute | solution.py:321
  30.5 21.4 %collective-permute-start.11 = (bf16[512,384]{1,0:T(8,128)(2,1)S(1)}, bf16[512,384]{1,0:T(8,128)(2,1)S(1)}, u32[]{:S(2)}, u32[]{:S(2)}) collective-permute-start(bf16[512,384]{1,0:T(8,128)(2,1)S(1)} %attend.2.refs_1_.first_ref), channel_id=1, source_target_pairs={{0,1},{1,0},{2,3},{3,2},{4,5},{5,4},{6,7},{7,6},{8,9},{9,8},{10,11... | collective-permute-start | bytes 1179656 | tf_op jit(solution)/shard_map/ppermute | solution.py:349
  32.4 19.2 %collective-permute-start.5 = (bf16[512,384]{1,0:T(8,128)(2,1)S(1)}, bf16[512,384]{1,0:T(8,128)(2,1)S(1)}, u32[]{:S(2)}, u32[]{:S(2)}) collective-permute-start(bf16[512,384]{1,0:T(8,128)(2,1)S(1)} %attend.2.refs_1_.first_ref), channel_id=1, source_target_pairs={{0,2},{1,3},{2,0},{3,1},{4,6},{5,7},{6,4},{7,5},{8,10},{9,11},{10,... | collective-permute-start | bytes 1179656 | tf_op jit(solution)/shard_map/ppermute | solution.py:350
  35.0 17.7 %collective-permute-start.10 = (bf16[1280,256]{1,0:T(8,128)(2,1)S(1)}, bf16[1280,256]{1,0:T(8,128)(2,1)S(1)}, u32[]{:S(2)}, u32[]{:S(2)}) collective-permute-start(bf16[1280,256]{1,0:T(8,128)(2,1)S(1)} %pack.1.refs_2_.refs_3_), channel_id=1, source_target_pairs={{0,4},{4,0},{1,5},{5,1},{2,6},{6,2},{3,7},{7,3},{8,12},{12,8},{9,1... | collective-permute-start | bytes 1966088 | tf_op jit(solution)/shard_map/ppermute | solution.py:365
  43.6 15.3 %collective-permute-start.13 = (bf16[320,1280]{1,0:T(8,128)(2,1)S(1)}, bf16[320,1280]{1,0:T(8,128)(2,1)S(1)}, u32[]{:S(2)}, u32[]{:S(2)}) collective-permute-start(bf16[320,1280]{1,0:T(8,128)(2,1)S(1)} %join_all.1.refs_5_), channel_id=1, source_target_pairs={{0,16},{16,0},{8,24},{24,8},{1,17},{17,1},{9,25},{25,9},{2,18},{18... | collective-permute-start | bytes 2457608 | tf_op jit(solution)/shard_map/ppermute | solution.py:370
  45.2 13.7 %collective-permute-start.9 = (bf16[160,1280]{1,0:T(8,128)(2,1)S(1)}, bf16[160,1280]{1,0:T(8,128)(2,1)S(1)}, u32[]{:S(2)}, u32[]{:S(2)}) collective-permute-start(bf16[160,1280]{1,0:T(8,128)(2,1)S(1)} %join_two.1), channel_id=1, source_target_pairs={{0,4},{4,0},{1,5},{5,1},{2,6},{6,2},{3,7},{7,3},{8,12},{12,8},{9,1... | collective-permute-start | bytes 1228808 | tf_op jit(solution)/shard_map/ppermute | solution.py:369
  51.6 16.6 %collective-permute-start.6 = (bf16[512,384]{1,0:T(8,128)(2,1)S(1)}, bf16[512,384]{1,0:T(8,128)(2,1)S(1)}, u32[]{:S(2)}, u32[]{:S(2)}) collective-permute-start(bf16[512,384]{1,0:T(8,128)(2,1)S(1)} %collective-permute-done.5.refs_1_.refs_2_), channel_id=1, source_target_pairs={{0,1},{1,0},{2,3},{3,2},{4,5},{5,4},{6,7},{7,6},{8,9},{9,8},{10,11... | collective-permute-start | bytes 1179656 | tf_op jit(solution)/shard_map/ppermute | solution.py:351
  55.2 15.7 %collective-permute-start.14 = (bf16[512,256]{1,0:T(8,128)(2,1)S(1)}, bf16[512,256]{1,0:T(8,128)(2,1)S(1)}, u32[]{:S(2)}, u32[]{:S(2)}) collective-permute-start(bf16[512,256]{1,0:T(8,128)(2,1)S(1)} %attend.3.refs_1_.last_ref), channel_id=1, source_target_pairs={{0,1},{1,0},{2,3},{3,2},{4,5},{5,4},{6,7},{7,6},{8,9},{9,8},{10,11... | collective-permute-start | bytes 786440 | tf_op jit(solution)/shard_map/ppermute | solution.py:349
  56.1 14.8 %collective-permute-start.15 = (bf16[512,256]{1,0:T(8,128)(2,1)S(1)}, bf16[512,256]{1,0:T(8,128)(2,1)S(1)}, u32[]{:S(2)}, u32[]{:S(2)}) collective-permute-start(bf16[512,256]{1,0:T(8,128)(2,1)S(1)} %attend.3.refs_1_.last_ref), channel_id=1, source_target_pairs={{0,2},{1,3},{2,0},{3,1},{4,6},{5,7},{6,4},{7,5},{8,10},{9,11},{10,... | collective-permute-start | bytes 786440 | tf_op jit(solution)/shard_map/ppermute | solution.py:350
  58.9 13.3 %collective-permute-start.17 = (bf16[320,1280]{1,0:T(8,128)(2,1)S(1)}, bf16[320,1280]{1,0:T(8,128)(2,1)S(1)}, u32[]{:S(2)}, u32[]{:S(2)}) collective-permute-start(bf16[320,1280]{1,0:T(8,128)(2,1)S(1)} %join_all.1.refs_5_), channel_id=1, source_target_pairs={{0,8},{8,0},{16,24},{24,16},{1,9},{9,1},{17,25},{25,17},{2,10},{10... | collective-permute-start | bytes 2457608 | tf_op jit(solution)/shard_map/ppermute | solution.py:390
  58.9 12.0 %collective-permute-start.16 = (bf16[160,1280]{1,0:T(8,128)(2,1)S(1)}, bf16[160,1280]{1,0:T(8,128)(2,1)S(1)}, u32[]{:S(2)}, u32[]{:S(2)}) collective-permute-start(bf16[160,1280]{1,0:T(8,128)(2,1)S(1)} %hold.1.later_ref.refs_0_), channel_id=1, source_target_pairs={{0,16},{16,0},{8,24},{24,8},{1,17},{17,1},{9,25},{25,9},{2,18},{18... | collective-permute-start | bytes 1228808 | tf_op jit(solution)/shard_map/ppermute | solution.py:375
  68.1 4.1 %collective-permute-start.18 = (bf16[320,1280]{1,0:T(8,128)(2,1)S(1)}, bf16[320,1280]{1,0:T(8,128)(2,1)S(1)}, u32[]{:S(2)}, u32[]{:S(2)}) collective-permute-start(bf16[320,1280]{1,0:T(8,128)(2,1)S(1)} %collective-permute-done.13.refs_2_.refs_6_), channel_id=1, source_target_pairs={{0,8},{8,0},{16,24},{24,16},{1,9},{9,1},{17,25},{25,17},{2,10},{10... | collective-permute-start | bytes 2457608 | tf_op jit(solution)/shard_map/ppermute | solution.py:390
  70.8 2.7 %copy-start = (f32[50,1280]{1,0:T(8,128)S(1)}, f32[50,1280]{1,0:T(8,128)}, u32[]{:S(2)}) copy-start(f32[50,1280]{1,0:T(8,128)} %gate_ref.1) | copy-start | bytes 768004
  70.8 2.7 %copy-start.1 = (s32[6]{0:T(128)S(1)}, s32[6]{0:T(128)}, u32[]{:S(2)}) copy-start(s32[6]{0:T(128)} %times.1) | copy-start | bytes 76
  71.0 2.4 %collective-permute-start.19 = (bf16[320,1280]{1,0:T(8,128)(2,1)S(1)}, bf16[320,1280]{1,0:T(8,128)(2,1)S(1)}, u32[]{:S(2)}, u32[]{:S(2)}) collective-permute-start(bf16[320,1280]{1,0:T(8,128)(2,1)S(1)} %join_y.1.refs_7_), channel_id=1, source_target_pairs={{0,8},{8,0},{16,24},{24,16},{1,9},{9,1},{17,25},{25,17},{2,10},{10... | collective-permute-start | bytes 2457608 | tf_op jit(solution)/shard_map/ppermute | solution.py:390
  71.5 8.3 %collective-permute-start.20 = (bf16[512,256]{1,0:T(8,128)(2,1)S(1)}, bf16[512,256]{1,0:T(8,128)(2,1)S(1)}, u32[]{:S(2)}, u32[]{:S(2)}) collective-permute-start(bf16[512,256]{1,0:T(8,128)(2,1)S(1)} %collective-permute-done.15.refs_2_.refs_3_), channel_id=1, source_target_pairs={{0,1},{1,0},{2,3},{3,2},{4,5},{5,4},{6,7},{7,6},{8,9},{9,8},{10,11... | collective-permute-start | bytes 786440 | tf_op jit(solution)/shard_map/ppermute | solution.py:351
